TPU v7x, 32 devices: a whole 2x2x4 slice. The times are simulated.
32 devices in a mesh: groups: 2 (over y), blk: 4 (over z), sub: 2 (over x), inner: 2 (over core).
Axes of the slice: x: 2, y: 2, z: 4, core: 2. Of those that a mesh axis runs over, the one named last changes fastest.
Arguments:
- mass_profile_vectors: bfloat16 [10240, 1024], P(('groups', 'blk', 'sub', 'inner')), parts along dimension 0, may hold values from -6 to 6
- sugar_tree_vectors: bfloat16 [10240, 1024], P(('groups', 'blk', 'sub', 'inner')), parts along dimension 0, may hold values from -6 to 6
- matching_glycan_rows: int32 [10240], P(('groups', 'blk', 'sub', 'inner')), parts along dimension 0, may hold values from 0 to 5119, as said below
- sharpness_factor: float32 [1], replicated, may hold values from 0.03 to 0.08
- offset_shift_term: float32 [1], replicated, may hold values from -2 to 0
Outputs:
- grad_spectra: bfloat16 [10240, 1024], P(('groups', 'blk', 'sub', 'inner')), parts along dimension 0
- grad_structures: bfloat16 [10240, 1024], P(('groups', 'blk', 'sub', 'inner')), parts along dimension 0
There are 2 independent parts, one for each index of `groups`. A program takes and returns all parts, laid end to end along the dimension named above; an argument that names none is the same for every part. Nothing has to cross between parts.
Inputs may be any that keep to these rules, and one draw needn't show every extreme that they name: `matching_glycan_rows`: labels_i names a glycan row in node w(n, s) for some s in 0 .. 3, where n is the node of spectrum row i; several spectra may share one glycan.
All inputs are finite; a program needn't handle non-finite values.
Results may differ from a plain program's by a relative error of at most 0.0095.
Values may be sent and summed in bfloat16 or wider, within the bound.
No kernel may reach another device: no remote copies, remote signals or barrier semaphores. Data moves between devices by JAX's collectives and lax.ppermute only.
A program may use at most 64 MiB of HBM per device.

v0:
```python
import jax
import jax.numpy as jnp
from jax import lax
from jax.sharding import PartitionSpec as P

STEPS = 4


def from_behind(block, axis, distance):
    devices = range(lax.axis_size(axis))
    route = [((i - distance) % len(devices), i) for i in devices]
    return lax.ppermute(block, axis, route)


def local(
    mass_profile_vectors,
    sugar_tree_vectors,
    matching_glycan_rows,
    sharpness_factor,
    offset_shift_term,
):
    similarity_multiplier = sharpness_factor[0]
    shift_b = offset_shift_term[0]
    rows_here = mass_profile_vectors.shape[0]
    width = mass_profile_vectors.shape[1]
    n_inner = lax.axis_size("inner")
    node_rows = rows_here * n_inner
    loop_count = lax.axis_size("blk")
    lane_count = lax.axis_size("sub")
    position = lax.axis_index("blk")
    lane = lax.axis_index("sub")
    columns = jnp.arange(node_rows, dtype=jnp.int32)
    spectrum_total = jnp.zeros((rows_here, width), jnp.float32)
    glyc_total = jnp.zeros((node_rows, width), jnp.float32)
    held_shard = sugar_tree_vectors
    for step in range(STEPS):
        if step > 0:
            held_shard = from_behind(held_shard, "blk", 1)
        block = lax.all_gather(held_shard, "inner", axis=0, tiled=True)
        source = (position - step) % loop_count * lane_count + lane
        targets = source * node_rows + columns
        logits = (
            similarity_multiplier
            * lax.dot_general(
                mass_profile_vectors,
                block,
                (((1,), (1,)), ((), ())),
                preferred_element_type=jnp.float32,
            )
            + shift_b
        )
        positive = (matching_glycan_rows[:, None] == targets[None, :]).astype(jnp.float32)
        coef = (jax.nn.sigmoid(logits) - positive).astype(jnp.bfloat16)
        spectrum_total = spectrum_total + jnp.dot(coef, block, preferred_element_type=jnp.float32)
        partial_value = (
            similarity_multiplier
            * lax.dot_general(
                coef,
                mass_profile_vectors,
                (((0,), (0,)), ((), ())),
                preferred_element_type=jnp.float32,
            )
        ).astype(jnp.bfloat16)
        if step > 0:
            partial_value = from_behind(partial_value, "blk", -step)
        glyc_total = glyc_total + partial_value.astype(jnp.float32)
    grad_structures = lax.psum_scatter(
        glyc_total.astype(jnp.bfloat16), "inner", scatter_dimension=0, tiled=True
    )
    grad_spectra = (similarity_multiplier * spectrum_total).astype(jnp.bfloat16)
    return (grad_spectra, grad_structures)


def solution(mesh):
    placed = (
        P(("groups", "blk", "sub", "inner"), None),
        P(("groups", "blk", "sub", "inner"), None),
        P(("groups", "blk", "sub", "inner")),
        P(),
        P(),
    )
    return jax.shard_map(
        local,
        mesh=mesh,
        in_specs=placed,
        out_specs=(
            P(("groups", "blk", "sub", "inner"), None),
            P(("groups", "blk", "sub", "inner"), None),
        ),
        check_vma=False,
    )
```

profile of v0, /device:TPU:0, one launch (start us, length us, event | category | flops | bytes accessed | tf_op | source)
XLA Modules:
  0.0 201.6 jit_solution(4673739439838691657)
XLA Ops:
  7.2 3.1 %collective-permute-start = (bf16[320,1024]{1,0:T(8,128)(2,1)}, bf16[320,1024]{1,0:T(8,128)(2,1)S(1)}, u32[]{:S(2)}, u32[]{:S(2)}) collective-permute-start(bf16[320,1024]{1,0:T(8,128)(2,1)} %param.6), channel_id=1, source_target_pairs={{12,0},{0,4},{4,8},{8,12},{13,1},{1,5},{5,9},{9,13},{14,2},{2,6},{... | collective-permute-start | bytes 1966088 | tf_op jit(solution)/shard_map/ppermute | solution.py:12
  10.3 17.0 %collective-permute-done = bf16[320,1024]{1,0:T(8,128)(2,1)S(1)} collective-permute-done((bf16[320,1024]{1,0:T(8,128)(2,1)}, bf16[320,1024]{1,0:T(8,128)(2,1)S(1)}, u32[]{:S(2)}, u32[]{:S(2)}) %collective-permute-start) | collective-permute-done | bytes 655392 | tf_op jit(solution)/shard_map/ppermute | solution.py:12
  27.3 0.8 copy-done.5
  28.1 0.0 all-gather.9.cloned.1.call-start
  28.2 0.1 collective-permute-start.1
  28.2 17.9 %collective-permute-done.1 = bf16[320,1024]{1,0:T(8,128)(2,1)S(1)} collective-permute-done((bf16[320,1024]{1,0:T(8,128)(2,1)}, bf16[320,1024]{1,0:T(8,128)(2,1)S(1)}, u32[]{:S(2)}, u32[]{:S(2)}) %collective-permute-start.1) | collective-permute-done | bytes 655392 | tf_op jit(solution)/shard_map/ppermute | solution.py:12
  46.2 0.8 copy-done.6
  47.0 0.0 all-gather.11.cloned.1.call-start
  47.1 0.1 collective-permute-start.2
  47.1 17.0 %collective-permute-done.2 = bf16[320,1024]{1,0:T(8,128)(2,1)S(1)} collective-permute-done((bf16[320,1024]{1,0:T(8,128)(2,1)}, bf16[320,1024]{1,0:T(8,128)(2,1)S(1)}, u32[]{:S(2)}, u32[]{:S(2)}) %collective-permute-start.2) | collective-permute-done | bytes 655392 | tf_op jit(solution)/shard_map/ppermute | solution.py:12
  64.1 0.9 copy-done.7
  65.1 0.5 all-gather.5.cloned.1.call-update
  67.1 2.1 %fusion.28 = bf16[320,640]{1,0:T(8,128)(2,1)S(1)} fusion(bf16[320,1024]{1,0:T(8,128)(2,1)S(1)} %copy-done, bf16[640,1024]{1,0:T(8,128)(2,1)} %all-gather.7.cloned.1.call-done, s32[640]{0:T(1024)S(1)} %iota_add_fusion.2, f32[]{:T(128)} %bitcast.38, f32[]{:T(128)} %bitcast.34, s32[320]{0:T(512)S(1)} %copy-done.9), kind=kOutput, calls=%fused_computation.40 | convolution fusion | flops 421273600 | bytes 2379528 | tf_op jit(solution)/shard_map/dot_general | solution.py:44
  69.2 2.0 multiply_convert_fusion.2
  71.2 2.1 %fusion.27 = bf16[320,640]{1,0:T(8,128)(2,1)S(1)} fusion(bf16[320,1024]{1,0:T(8,128)(2,1)S(1)} %copy-done, bf16[640,1024]{1,0:T(8,128)(2,1)} %all-gather.9.cloned.1.call-done, s32[640]{0:T(1024)S(1)} %iota_add_fusion.1, f32[]{:T(128)} %bitcast.37, f32[]{:T(128)} %bitcast.33, s32[320]{0:T(512)S(1)} %copy-done.9), kind=kOutput, calls=%fused_computation.39 | convolution fusion | flops 421273600 | bytes 2379528 | tf_op jit(solution)/shard_map/dot_general | solution.py:44
  73.3 2.0 multiply_convert_fusion.1
  75.3 2.1 %fusion.26 = bf16[320,640]{1,0:T(8,128)(2,1)S(1)} fusion(bf16[320,1024]{1,0:T(8,128)(2,1)S(1)} %copy-done, bf16[640,1024]{1,0:T(8,128)(2,1)} %all-gather.11.cloned.1.call-done, s32[640]{0:T(1024)S(1)} %iota_add_fusion, f32[]{:T(128)} %bitcast.36, f32[]{:T(128)} %bitcast.32, s32[320]{0:T(512)S(1)} %copy-done.9), kind=kOutput, calls=%fused_computation.38 | convolution fusion | flops 421273600 | bytes 2379528 | tf_op jit(solution)/shard_map/dot_general | solution.py:44
  77.4 1.9 multiply_convert_fusion
  79.3 2.0 collective-permute-start.5
  81.3 3.0 %all-gather.5.cloned.1.call-done = bf16[640,1024]{1,0:T(8,128)(2,1)} async-done(((bf16[320,1024]{1,0:T(8,128)(2,1)}), bf16[640,1024]{1,0:T(8,128)(2,1)}) %all-gather.5.cloned.1.call-update) | async-done | bytes 1310736 | tf_op jit(solution)/shard_map/all_gather | solution.py:39
  84.4 2.1 %fusion.29 = bf16[320,640]{1,0:T(8,128)(2,1)S(1)} fusion(bf16[320,1024]{1,0:T(8,128)(2,1)S(1)} %copy-done, bf16[640,1024]{1,0:T(8,128)(2,1)} %all-gather.5.cloned.1.call-done, s32[640]{0:T(1024)S(1)} %iota_add_fusion.3, f32[]{:T(128)} %bitcast.35, f32[]{:T(128)} %bitcast.27, s32[320]{0:T(512)S(1)} %copy-done.9), kind=kOutput, calls=%fused_computation.41 | convolution fusion | flops 421273600 | bytes 2379528 | tf_op jit(solution)/shard_map/dot_general | solution.py:44
  86.5 14.6 %collective-permute-done.3 = bf16[640,1024]{1,0:T(8,128)(2,1)S(1)} collective-permute-done((bf16[640,1024]{1,0:T(8,128)(2,1)}, bf16[640,1024]{1,0:T(8,128)(2,1)S(1)}, u32[]{:S(2)}, u32[]{:S(2)}) %collective-permute-start.3) | collective-permute-done | bytes 1310752 | tf_op jit(solution)/shard_map/ppermute | solution.py:12
  101.1 81.0 %collective-permute-done.4 = bf16[640,1024]{1,0:T(8,128)(2,1)} collective-permute-done((bf16[640,1024]{1,0:T(8,128)(2,1)}, bf16[640,1024]{1,0:T(8,128)(2,1)}, u32[]{:S(2)}, u32[]{:S(2)}) %collective-permute-start.4) | collective-permute-done | bytes 1310752 | tf_op jit(solution)/shard_map/ppermute | solution.py:12
  182.1 4.1 %add_convert_fusion = bf16[640,1024]{1,0:T(8,128)(2,1)} fusion(bf16[640,1024]{1,0:T(8,128)(2,1)} %collective-permute-done.5, bf16[640,1024]{1,0:T(8,128)(2,1)} %collective-permute-done.4, bf16[640,1024]{1,0:T(8,128)(2,1)S(1)} %collective-permute-done.3, bf16[320,640]{1,0:T(8,128)(2,1)S(1)} %fusion.29, bf16[320,1024]{1,0:T(8,128)(2,1)S(1)} %copy-done, f32[]{:T(128)} %bitcast.28), kind=kOutput, calls=%fused_computation | convolution fusion | flops 425984000 | bytes 6307844 | tf_op jit(solution)/shard_map/dot_general | solution.py:57
  186.2 1.3 copy-done.4
  187.5 1.8 fusion.30
  189.3 0.7 convolution_add_fusion.2
  190.0 0.6 copy-done.2
  190.6 0.7 convolution_add_fusion.1
  191.3 0.6 copy-done.3
  191.9 1.5 fusion.1
  193.4 1.6 reduce-scatter.2.cloned.1.call-done
  (31 shorter events, 0.3 us)
Async XLA Ops:
  7.2 59.9 %copy-start = (bf16[320,1024]{1,0:T(8,128)(2,1)S(1)}, bf16[320,1024]{1,0:T(8,128)(2,1)}, u32[]{:S(2)}) copy-start(bf16[320,1024]{1,0:T(8,128)(2,1)} %param.5) | copy-start | bytes 1966084
  7.2 59.9 %all-gather.7.cloned.1.call-start = ((), (), s32[]{:S(2)}) async-start(), calls=%async_computation.2 | async-start | bytes 1966080 | tf_op jit(solution)/shard_map/all_gather | solution.py:39
  7.2 20.0 %collective-permute-start = (bf16[320,1024]{1,0:T(8,128)(2,1)}, bf16[320,1024]{1,0:T(8,128)(2,1)S(1)}, u32[]{:S(2)}, u32[]{:S(2)}) collective-permute-start(bf16[320,1024]{1,0:T(8,128)(2,1)} %param.6), channel_id=1, source_target_pairs={{12,0},{0,4},{4,8},{8,12},{13,1},{1,5},{5,9},{9,13},{14,2},{2,6},{... | collective-permute-start | bytes 1966088 | tf_op jit(solution)/shard_map/ppermute | solution.py:12
  27.3 0.8 copy-start.5
  27.3 39.8 %copy-start.9 = (s32[320]{0:T(512)S(1)}, s32[320]{0:T(512)}, u32[]{:S(2)}) copy-start(s32[320]{0:T(512)} %param.7) | copy-start | bytes 3844
  28.1 43.1 %all-gather.9.cloned.1.call-start = ((), (), s32[]{:S(2)}) async-start(), calls=%async_computation.3 | async-start | bytes 1966080 | tf_op jit(solution)/shard_map/all_gather | solution.py:39
  28.2 18.0 %collective-permute-start.1 = (bf16[320,1024]{1,0:T(8,128)(2,1)}, bf16[320,1024]{1,0:T(8,128)(2,1)S(1)}, u32[]{:S(2)}, u32[]{:S(2)}) collective-permute-start(bf16[320,1024]{1,0:T(8,128)(2,1)} %copy-done.5), channel_id=1, source_target_pairs={{12,0},{0,4},{4,8},{8,12},{13,1},{1,5},{5,9},{9,13},{14,2},{2,6},{... | collective-permute-start | bytes 1966088 | tf_op jit(solution)/shard_map/ppermute | solution.py:12
  46.2 0.8 copy-start.6
  47.0 28.3 %all-gather.11.cloned.1.call-start = ((), (), s32[]{:S(2)}) async-start(), calls=%async_computation.4 | async-start | bytes 1966080 | tf_op jit(solution)/shard_map/all_gather | solution.py:39
  47.1 17.1 %collective-permute-start.2 = (bf16[320,1024]{1,0:T(8,128)(2,1)}, bf16[320,1024]{1,0:T(8,128)(2,1)S(1)}, u32[]{:S(2)}, u32[]{:S(2)}) collective-permute-start(bf16[320,1024]{1,0:T(8,128)(2,1)} %copy-done.6), channel_id=1, source_target_pairs={{12,0},{0,4},{4,8},{8,12},{13,1},{1,5},{5,9},{9,13},{14,2},{2,6},{... | collective-permute-start | bytes 1966088 | tf_op jit(solution)/shard_map/ppermute | solution.py:12
  64.1 0.9 copy-start.7
  65.1 19.3 %all-gather.5.cloned.1.call-start = ((), (), s32[]{:S(2)}) async-start(), calls=%async_computation.1 | async-start | bytes 1966080 | tf_op jit(solution)/shard_map/all_gather | solution.py:39
  65.6 129.4 %reduce-scatter.2.cloned.1.call-start = ((), (), s32[]{:S(2)}) async-start(), calls=%async_computation.5 | async-start | bytes 1966080 | tf_op jit(solution)/shard_map/reduce_scatter | solution.py:67
  71.2 29.9 %collective-permute-start.3 = (bf16[640,1024]{1,0:T(8,128)(2,1)}, bf16[640,1024]{1,0:T(8,128)(2,1)S(1)}, u32[]{:S(2)}, u32[]{:S(2)}) collective-permute-start(bf16[640,1024]{1,0:T(8,128)(2,1)} %multiply_convert_fusion.2), channel_id=1, source_target_pairs={{4,0},{8,4},{12,8},{0,12},{5,1},{9,5},{13,9},{1,13},{6,2},{10,6},{... | collective-permute-start | bytes 3932168 | tf_op jit(solution)/shard_map/ppermute | solution.py:12
  75.3 106.8 %collective-permute-start.4 = (bf16[640,1024]{1,0:T(8,128)(2,1)}, bf16[640,1024]{1,0:T(8,128)(2,1)}, u32[]{:S(2)}, u32[]{:S(2)}) collective-permute-start(bf16[640,1024]{1,0:T(8,128)(2,1)} %multiply_convert_fusion.1), channel_id=1, source_target_pairs={{8,0},{12,4},{0,8},{4,12},{9,1},{13,5},{1,9},{5,13},{10,2},{14,6},... | collective-permute-start | bytes 3932168 | tf_op jit(solution)/shard_map/ppermute | solution.py:12
  79.3 102.8 %collective-permute-start.5 = (bf16[640,1024]{1,0:T(8,128)(2,1)}, bf16[640,1024]{1,0:T(8,128)(2,1)}, u32[]{:S(2)}, u32[]{:S(2)}) collective-permute-start(bf16[640,1024]{1,0:T(8,128)(2,1)} %multiply_convert_fusion), channel_id=1, source_target_pairs={{12,0},{0,4},{4,8},{8,12},{13,1},{1,5},{5,9},{9,13},{14,2},{2,6},{... | collective-permute-start | bytes 3932168 | tf_op jit(solution)/shard_map/ppermute | solution.py:12
  86.5 95.6 %copy-start.8 = (bf16[320,640]{1,0:T(8,128)(2,1)}, bf16[320,640]{1,0:T(8,128)(2,1)S(1)}, u32[]{:S(2)}) copy-start(bf16[320,640]{1,0:T(8,128)(2,1)S(1)} %fusion.29) | copy-start | bytes 1228804
  186.2 1.3 copy-start.4
  187.5 1.8 copy-start.1
  189.3 1.3 copy-start.2
  190.6 1.3 copy-start.3
Sparse Core Ops, SparseCore 0:
  28.3 8.7 all-gather.6
  47.1 7.3 all-gather.8
  65.2 7.1 all-gather.10
  73.7 10.5 all-gather.4
  186.3 8.7 reduce-scatter.1
where the time goes:
time: 202 us
  waiting for transfers between devices  153 us (76%)
  matrix products  23 us (11%)
  between operations  15.3 us (8%)
  starting transfers between devices  5.41 us (3%)
  local copies, waits for them, and re-layouts  5.14 us (3%)
    ppermute x6, waiting for transfers between devices, from_behind(): return lax.ppermute(block, axis, route)  147 us
    dot_general x4, matrix products, local(): lax.dot_general(coef, mass_profile_vectors, (((0,), (0,)), ((), ())), pre...  9.93 us
    dot_general x4, matrix products, local(): lax.dot_general(mass_profile_vectors, block, (((1,), (1,)), ((), ())), pr...  8.39 us
    ppermute x6, starting transfers between devices, from_behind(): return lax.ppermute(block, axis, route)  5.22 us
    unnamed x20, local copies, waits for them, and re-layouts  5.14 us
    dot_general x4, matrix products, local(): jnp.dot(coef, block, preferred_element_type=jnp.float32)  4.64 us
  transfers between devices with their start and end apart: 11, of which 7 were waited for; matrix products, arithmetic and copies ran while one was open for 9% of the time, Pallas kernels for 0%

commit v1 on v0

v1 whole, which is shorter than its diff:
```python
import jax
import jax.numpy as jnp
from jax import lax
from jax.sharding import PartitionSpec as P

STEPS = 4
LINE = 4


def from_behind(block, axis, distance):
    devices = range(lax.axis_size(axis))
    route = [((i - distance) % len(devices), i) for i in devices]
    return lax.ppermute(block, axis, route)


def swap_inner(block):
    return from_behind(block, "inner", 1)


def coefficients(spectra, glycans, labels, first_target, scale, shift):
    logits = (
        scale
        * lax.dot_general(
            spectra, glycans, (((1,), (1,)), ((), ())), preferred_element_type=jnp.float32
        )
        + shift
    )
    targets = first_target + jnp.arange(glycans.shape[0], dtype=jnp.int32)
    positive = (labels[:, None] == targets[None, :]).astype(jnp.float32)
    return (jax.nn.sigmoid(logits) - positive).astype(jnp.bfloat16)


def toward_spectra(coef, glycans):
    return jnp.dot(coef, glycans, preferred_element_type=jnp.float32)


def toward_glycans(coef, spectra):
    return lax.dot_general(
        coef, spectra, (((0,), (0,)), ((), ())), preferred_element_type=jnp.float32
    )


def merge_spectra(total, rows_here, scale):
    other = swap_inner((scale * total[rows_here:]).astype(jnp.bfloat16))
    return (scale * total[:rows_here] + other.astype(jnp.float32)).astype(jnp.bfloat16)


def around_ring(spectra, glycans, labels, scale, shift):
    rows_here = spectra.shape[0]
    node_rows = rows_here * lax.axis_size("inner")
    loop_count = lax.axis_size("blk")
    position = lax.axis_index("blk")
    core_first = lax.axis_index("sub") * node_rows + lax.axis_index("inner") * rows_here
    lane_rows = lax.axis_size("sub") * node_rows
    node_spectra = jnp.concatenate([spectra, swap_inner(spectra)])
    node_labels = jnp.concatenate([labels, swap_inner(labels)])
    spectrum_total = 0.0
    glycan_total = 0.0
    held = glycans
    for step in range(STEPS):
        if step > 0:
            held = from_behind(held, "blk", 1)
        first_target = (position - step) % loop_count * lane_rows + core_first
        coef = coefficients(node_spectra, held, node_labels, first_target, scale, shift)
        spectrum_total += toward_spectra(coef, held)
        partial_value = scale * toward_glycans(coef, node_spectra)
        if step > 0:
            back = from_behind(partial_value.astype(jnp.bfloat16), "blk", -step)
            partial_value = back.astype(jnp.float32)
        glycan_total += partial_value
    return (
        merge_spectra(spectrum_total, rows_here, scale),
        glycan_total.astype(jnp.bfloat16),
    )


def along_line(spectra, glycans, labels, scale, shift):
    rows_here = spectra.shape[0]
    node_rows = rows_here * lax.axis_size("inner")
    position = lax.axis_index("blk")
    outer = (position == 0) | (position == LINE - 1)
    core_first = lax.axis_index("sub") * node_rows + lax.axis_index("inner") * rows_here
    lane_rows = lax.axis_size("sub") * node_rows

    def permute(block, pairs):
        return lax.ppermute(block, "blk", pairs)

    def first_of(block_position):
        return block_position * lane_rows + core_first

    sides = [(0, 1), (1, 0), (2, 3), (3, 2)]
    middle = [(1, 2), (2, 1)]
    inward = [(0, 1), (3, 2)]
    outward = [(1, 0), (2, 3)]

    side = permute(glycans, sides)
    across = permute(glycans, middle)
    node_spectra = jnp.concatenate([spectra, swap_inner(spectra)])
    node_labels = jnp.concatenate([labels, swap_inner(labels)])
    end_labels = permute(node_labels, inward)

    far = permute(side, middle)
    next_out = permute(across, outward)
    end_half = permute(spectra, inward)
    last_out = permute(far, outward)
    end_spectra = jnp.concatenate([end_half, swap_inner(end_half)])

    here_at = first_of(position)
    side_at = first_of(position ^ 1)
    across_at = first_of(LINE - 1 - position)
    far_at = first_of((LINE - 1 - position) ^ 1)

    def own(block, at):
        coef = coefficients(node_spectra, block, node_labels, at, scale, shift)
        return toward_spectra(coef, block), toward_glycans(coef, node_spectra)

    def ends(block, at):
        coef = coefficients(end_spectra, block, end_labels, at, scale, shift)
        return toward_glycans(coef, end_spectra)

    here_s, here_g = own(glycans, here_at)
    side_s, side_g = own(side, side_at)
    across_s, across_g = own(across, across_at)
    far_s, far_g = own(far, far_at)

    far_back = permute((scale * (far_g + ends(far, far_at))).astype(jnp.bfloat16), middle)
    across_back = permute(
        (scale * (across_g + ends(across, across_at))).astype(jnp.bfloat16), middle
    )
    side_total = scale * (side_g + ends(side, side_at)) + far_back.astype(jnp.float32)
    from_inside = permute(side_total.astype(jnp.bfloat16), outward)
    here_total = scale * (here_g + ends(glycans, here_at)) + across_back.astype(jnp.float32)
    grad_structures = jnp.where(outer, from_inside, here_total.astype(jnp.bfloat16))

    next_s, _ = own(next_out, far_at)
    last_s, _ = own(last_out, across_at)
    spectrum_total = here_s + side_s + across_s + far_s + next_s + last_s
    return merge_spectra(spectrum_total, rows_here, scale), grad_structures


def local(
    mass_profile_vectors,
    sugar_tree_vectors,
    matching_glycan_rows,
    sharpness_factor,
    offset_shift_term,
):
    work = along_line if lax.axis_size("blk") == STEPS == LINE else around_ring
    return work(
        mass_profile_vectors,
        sugar_tree_vectors,
        matching_glycan_rows,
        sharpness_factor[0],
        offset_shift_term[0],
    )


def solution(mesh):
    placed = (
        P(("groups", "blk", "sub", "inner"), None),
        P(("groups", "blk", "sub", "inner"), None),
        P(("groups", "blk", "sub", "inner")),
        P(),
        P(),
    )
    return jax.shard_map(
        local,
        mesh=mesh,
        in_specs=placed,
        out_specs=(
            P(("groups", "blk", "sub", "inner"), None),
            P(("groups", "blk", "sub", "inner"), None),
        ),
        check_vma=False,
    )
```

time: 202 us -> 133 us (0.66)
  waiting for transfers between devices: 153 us -> 41.1 us
  matrix products: 23 us -> 57.3 us
  starting transfers between devices: 5.41 us -> 22 us
  between operations: 15.3 us -> 2.14 us
  other arithmetic: 0.02 us -> 6.67 us
    ppermute x6 -> x4, waiting for transfers between devices: 147 us -> 0.01 us  [from_behind(): return lax.ppermute(block, axis, route)]
    ppermute x0 -> x10, waiting for transfers between devices: none -> 41.1 us  [permute(): return lax.ppermute(block, 'blk', pairs)]
    dot_general x12 -> x18, matrix products: 23 us -> 57.3 us  [the longest x6 26.2 us: toward_spectra(): return jnp.dot(coef, glycans, preferred_element_type=jnp.float32)]
    ppermute x0 -> x10, starting transfers between devices: none -> 21.3 us  [permute(): return lax.ppermute(block, 'blk', pairs)]
    convert_element_type x0 -> x2, other arithmetic: none -> 4.58 us  [the longest x1 2.38 us: merge_spectra(): other = swap_inner((scale * total[rows_here:]).astype(jnp.bfloat16))]
    ppermute x6 -> x4, starting transfers between devices: 5.22 us -> 0.73 us  [from_behind(): return lax.ppermute(block, axis, route)]
    all_gather x4 -> x0, waiting for transfers between devices: 3.06 us -> none  [local(): block = lax.all_gather(held_shard, 'inner', axis=0, tiled=True)]
    unnamed x20 -> x14, local copies, waits for them, and re-layouts: 5.14 us -> 3.41 us
  transfers between devices with their start and end apart: 11 -> 14, of which waited for: 7 -> 3; matrix products, arithmetic and copies ran while one was open for 9% -> 49% of each run, Pallas kernels for 0% -> 0%
where the time goes in v1:
time: 133 us
  matrix products  57.3 us (43%)
  waiting for transfers between devices  41.1 us (31%)
  starting transfers between devices  22 us (17%)
  other arithmetic  6.67 us (5%)
  local copies, waits for them, and re-layouts  3.5 us (3%)
  between operations  2.14 us (2%)
    ppermute x10, waiting for transfers between devices, permute(): return lax.ppermute(block, 'blk', pairs)  41.1 us
    dot_general x6, matrix products, toward_spectra(): return jnp.dot(coef, glycans, preferred_element_type=jnp.float32)  26.2 us
    dot_general x8, matrix products, toward_glycans(): lax.dot_general(coef, spectra, (((0,), (0,)), ((), ())), preferred_elemen...  24.6 us
    ppermute x10, starting transfers between devices, permute(): return lax.ppermute(block, 'blk', pairs)  21.3 us
    dot_general x4, matrix products, coefficients(): lax.dot_general(spectra, glycans, (((1,), (1,)), ((), ())), preferred_ele...  6.39 us
    unnamed x14, local copies, waits for them, and re-layouts  3.41 us
  transfers between devices with their start and end apart: 14, of which 3 were waited for; matrix products, arithmetic and copies ran while one was open for 49% of the time, Pallas kernels for 0%

profile of v1, /device:TPU:0, one launch (start us, length us, event | category | flops | bytes accessed | tf_op | source)
XLA Modules:
  0.0 132.6 jit_solution(5935843121567269891)
XLA Ops:
  1.2 5.4 %collective-permute-start.8 = (bf16[320,1024]{1,0:T(8,128)(2,1)}, bf16[320,1024]{1,0:T(8,128)(2,1)}, u32[]{:S(2)}, u32[]{:S(2)}) collective-permute-start(bf16[320,1024]{1,0:T(8,128)(2,1)} %param.5), channel_id=1, source_target_pairs={{0,4},{12,8},{1,5},{13,9},{2,6},{14,10},{3,7},{15,11},{16,20},{28,... | collective-permute-start | bytes 1966088 | tf_op jit(solution)/shard_map/ppermute | solution.py:86
  6.5 1.5 %collective-permute-start.3 = (bf16[320,1024]{1,0:T(8,128)(2,1)}, bf16[320,1024]{1,0:T(8,128)(2,1)}, u32[]{:S(2)}, u32[]{:S(2)}) collective-permute-start(bf16[320,1024]{1,0:T(8,128)(2,1)} %param.6), channel_id=1, source_target_pairs={{4,8},{8,4},{5,9},{9,5},{6,10},{10,6},{7,11},{11,7},{20,24},{24,20... | collective-permute-start | bytes 1966088 | tf_op jit(solution)/shard_map/ppermute | solution.py:86
  8.3 1.2 constant_dynamic-update-slice_fusion.1
  10.9 5.8 %collective-permute-start.10 = (s32[640]{0:T(1024)S(1)}, s32[640]{0:T(1024)S(1)}, u32[]{:S(2)}, u32[]{:S(2)}) collective-permute-start(s32[640]{0:T(1024)S(1)} %pad_add_fusion), channel_id=1, source_target_pairs={{0,4},{12,8},{1,5},{13,9},{2,6},{14,10},{3,7},{15,11},{16,20},{28,... | collective-permute-start | bytes 7688 | tf_op jit(solution)/shard_map/ppermute | solution.py:86
  17.6 1.7 %fusion.136 = f32[320,1024]{1,0:T(8,128)} fusion(bf16[640,320]{0,1:T(8,128)(2,1)S(1)} %fusion.82, bf16[640,1024]{1,0:T(8,128)(2,1)S(1)} %constant_dynamic-update-slice_fusion), kind=kOutput, calls=%fused_computation.163 | convolution fusion | flops 419430400 | bytes 3031040 | tf_op jit(solution)/shard_map/dot_general | solution.py:38
  19.3 15.4 %collective-permute-done.2 = bf16[320,1024]{1,0:T(8,128)(2,1)} collective-permute-done((bf16[320,1024]{1,0:T(8,128)(2,1)}, bf16[320,1024]{1,0:T(8,128)(2,1)}, u32[]{:S(2)}, u32[]{:S(2)}) %collective-permute-start.2) | collective-permute-done | bytes 655392 | tf_op jit(solution)/shard_map/ppermute | solution.py:86
  34.7 1.9 %fusion.81 = bf16[640,320]{0,1:T(8,128)(2,1)S(1)} fusion(bf16[640,1024]{1,0:T(8,128)(2,1)S(1)} %constant_dynamic-update-slice_fusion, bf16[320,1024]{1,0:T(8,128)(2,1)} %collective-permute-done.2, s32[640]{0:T(1024)S(1)} %pad_add_fusion, f32[]{:T(128)} %bitcast.65, f32[]{:T(128)} %bitcast.55, s32[320]{0:T(512)S(1)} %iota_add_fusion.2), kind=kOutput, calls=%fused_computation.98 | convolution fusion | flops 421273600 | bytes 2379528 | tf_op jit(solution)/shard_map/dot_general | solution.py:23
  36.6 1.7 %fusion.134 = f32[320,1024]{1,0:T(8,128)} fusion(bf16[640,320]{0,1:T(8,128)(2,1)S(1)} %fusion.81, bf16[640,1024]{1,0:T(8,128)(2,1)S(1)} %constant_dynamic-update-slice_fusion), kind=kOutput, calls=%fused_computation.161 | convolution fusion | flops 419430400 | bytes 3031040 | tf_op jit(solution)/shard_map/dot_general | solution.py:38
  38.3 1.5 %collective-permute-start.4 = (bf16[320,1024]{1,0:T(8,128)(2,1)}, bf16[320,1024]{1,0:T(8,128)(2,1)}, u32[]{:S(2)}, u32[]{:S(2)}) collective-permute-start(bf16[320,1024]{1,0:T(8,128)(2,1)} %collective-permute-done.2), channel_id=1, source_target_pairs={{4,8},{8,4},{5,9},{9,5},{6,10},{10,6},{7,11},{11,7},{20,24},{24,20... | collective-permute-start | bytes 1966088 | tf_op jit(solution)/shard_map/ppermute | solution.py:86
  39.8 2.4 %fusion.130 = f32[640,1024]{1,0:T(8,128)} fusion(bf16[640,320]{0,1:T(8,128)(2,1)S(1)} %fusion.82, bf16[320,1024]{1,0:T(8,128)(2,1)S(1)} %copy-done.2), kind=kOutput, calls=%fused_computation.157 | convolution fusion | flops 419430400 | bytes 3686400 | tf_op jit(solution)/shard_map/dot_general | solution.py:34
  42.2 3.5 %fusion.131 = f32[640,1024]{1,0:T(8,128)} fusion(bf16[640,320]{0,1:T(8,128)(2,1)S(1)} %fusion.81, bf16[320,1024]{1,0:T(8,128)(2,1)} %collective-permute-done.2), kind=kOutput, calls=%fused_computation.158 | convolution fusion | flops 419430400 | bytes 3686400 | tf_op jit(solution)/shard_map/dot_general | solution.py:34
  45.7 1.3 collective-permute-start.5
  47.0 1.9 %fusion.80 = bf16[640,320]{0,1:T(8,128)(2,1)S(1)} fusion(bf16[640,1024]{1,0:T(8,128)(2,1)S(1)} %constant_dynamic-update-slice_fusion, bf16[320,1024]{1,0:T(8,128)(2,1)} %collective-permute-done.3, s32[640]{0:T(1024)S(1)} %pad_add_fusion, f32[]{:T(128)} %bitcast.64, f32[]{:T(128)} %bitcast.54, s32[320]{0:T(512)S(1)} %iota_add_fusion.1), kind=kOutput, calls=%fused_computation.97 | convolution fusion | flops 421273600 | bytes 2379528 | tf_op jit(solution)/shard_map/dot_general | solution.py:23
  49.5 3.4 %fusion.132 = f32[640,1024]{1,0:T(8,128)} fusion(bf16[640,320]{0,1:T(8,128)(2,1)S(1)} %fusion.80, bf16[320,1024]{1,0:T(8,128)(2,1)} %collective-permute-done.3), kind=kOutput, calls=%fused_computation.159 | convolution fusion | flops 419430400 | bytes 3686400 | tf_op jit(solution)/shard_map/dot_general | solution.py:34
  55.2 4.4 %fusion.6 = bf16[320,1024]{1,0:T(8,128)(2,1)} fusion(f32[320,1024]{1,0:T(8,128)S(1)} %fusion.137, bf16[640,1024]{1,0:T(8,128)(2,1)} %copy-done.4, bf16[320,1024]{1,0:T(8,128)(2,1)} %collective-permute-done.3, f32[]{:T(128)} %bitcast.46, s32[640]{0:T(1024)S(1)} %collective-permute-done.10, f32[]{:T(128)} %bitcast.57, s32[320]{0:T(512)S(1)} %iota_add_fusion.1), kind=kOutput, calls=%fused_computation.11 | convolution fusion | flops 841687040 | bytes 3936008 | tf_op jit(solution)/shard_map/dot_general | solution.py:38
  59.6 1.5 %collective-permute-start.13 = (bf16[320,1024]{1,0:T(8,128)(2,1)}, bf16[320,1024]{1,0:T(8,128)(2,1)}, u32[]{:S(2)}, u32[]{:S(2)}) collective-permute-start(bf16[320,1024]{1,0:T(8,128)(2,1)} %fusion.6), channel_id=1, source_target_pairs={{4,8},{8,4},{5,9},{9,5},{6,10},{10,6},{7,11},{11,7},{20,24},{24,20... | collective-permute-start | bytes 1966088 | tf_op jit(solution)/shard_map/ppermute | solution.py:86
  61.1 1.9 %fusion.79 = bf16[640,320]{0,1:T(8,128)(2,1)S(1)} fusion(bf16[640,1024]{1,0:T(8,128)(2,1)S(1)} %constant_dynamic-update-slice_fusion, bf16[320,1024]{1,0:T(8,128)(2,1)} %collective-permute-done.4, s32[640]{0:T(1024)S(1)} %pad_add_fusion, f32[]{:T(128)} %bitcast.63, f32[]{:T(128)} %bitcast.53, s32[320]{0:T(512)S(1)} %iota_add_fusion), kind=kOutput, calls=%fused_computation.96 | convolution fusion | flops 421273600 | bytes 2379528 | tf_op jit(solution)/shard_map/dot_general | solution.py:23
  63.0 1.8 %fusion.135 = f32[320,1024]{1,0:T(8,128)} fusion(bf16[640,320]{0,1:T(8,128)(2,1)S(1)} %fusion.79, bf16[640,1024]{1,0:T(8,128)(2,1)S(1)} %constant_dynamic-update-slice_fusion), kind=kOutput, calls=%fused_computation.162 | convolution fusion | flops 419430400 | bytes 3031040 | tf_op jit(solution)/shard_map/dot_general | solution.py:38
  64.8 4.8 %fusion.8 = bf16[320,1024]{1,0:T(8,128)(2,1)} fusion(f32[320,1024]{1,0:T(8,128)} %fusion.135, bf16[640,1024]{1,0:T(8,128)(2,1)} %copy-done.4, bf16[320,1024]{1,0:T(8,128)(2,1)} %collective-permute-done.4, f32[]{:T(128)} %bitcast.48, s32[640]{0:T(1024)S(1)} %collective-permute-done.10, f32[]{:T(128)} %bitcast.59, s32[320]{0:T(512)S(1)} %iota_add_fusion), kind=kOutput, calls=%fused_computation.13 | convolution fusion | flops 841687040 | bytes 3936008 | tf_op jit(solution)/shard_map/dot_general | solution.py:38
  69.6 1.5 %collective-permute-start.11 = (bf16[320,1024]{1,0:T(8,128)(2,1)}, bf16[320,1024]{1,0:T(8,128)(2,1)}, u32[]{:S(2)}, u32[]{:S(2)}) collective-permute-start(bf16[320,1024]{1,0:T(8,128)(2,1)} %fusion.8), channel_id=1, source_target_pairs={{4,8},{8,4},{5,9},{9,5},{6,10},{10,6},{7,11},{11,7},{20,24},{24,20... | collective-permute-start | bytes 1966088 | tf_op jit(solution)/shard_map/ppermute | solution.py:86
  71.1 1.5 %collective-permute-start.6 = (bf16[320,1024]{1,0:T(8,128)(2,1)}, bf16[320,1024]{1,0:T(8,128)(2,1)S(1)}, u32[]{:S(2)}, u32[]{:S(2)}) collective-permute-start(bf16[320,1024]{1,0:T(8,128)(2,1)} %collective-permute-done.4), channel_id=1, source_target_pairs={{4,0},{8,12},{5,1},{9,13},{6,2},{10,14},{7,3},{11,15},{20,16},{24,... | collective-permute-start | bytes 1966088 | tf_op jit(solution)/shard_map/ppermute | solution.py:86
  72.6 3.5 %fusion.133 = f32[640,1024]{1,0:T(8,128)} fusion(bf16[640,320]{0,1:T(8,128)(2,1)S(1)} %fusion.79, bf16[320,1024]{1,0:T(8,128)(2,1)} %collective-permute-done.4), kind=kOutput, calls=%fused_computation.160 | convolution fusion | flops 419430400 | bytes 3686400 | tf_op jit(solution)/shard_map/dot_general | solution.py:34
  76.1 4.7 %fusion.83 = f32[640,1024]{1,0:T(8,128)} fusion(bf16[320,1024]{1,0:T(8,128)(2,1)} %collective-permute-done.5, bf16[640,1024]{1,0:T(8,128)(2,1)S(1)} %constant_dynamic-update-slice_fusion, s32[640]{0:T(1024)S(1)} %pad_add_fusion, f32[]{:T(128)} %bitcast.62, f32[]{:T(128)} %bitcast.52, s32[320]{0:T(512)S(1)} %iota_add_fusion), kind=kOutput, calls=%fused_computation.100 | convolution fusion | flops 840704000 | bytes 4591368 | tf_op jit(solution)/shard_map/dot_general | solution.py:34
  80.8 14.8 %collective-permute-done.6 = bf16[320,1024]{1,0:T(8,128)(2,1)S(1)} collective-permute-done((bf16[320,1024]{1,0:T(8,128)(2,1)}, bf16[320,1024]{1,0:T(8,128)(2,1)S(1)}, u32[]{:S(2)}, u32[]{:S(2)}) %collective-permute-start.6) | collective-permute-done | bytes 655392 | tf_op jit(solution)/shard_map/ppermute | solution.py:86
  95.6 8.7 %add_add_fusion = f32[640,1024]{1,0:T(8,128)} fusion(f32[640,1024]{1,0:T(8,128)} %fusion.83, f32[640,1024]{1,0:T(8,128)} %fusion.133, f32[640,1024]{1,0:T(8,128)} %fusion.132, f32[640,1024]{1,0:T(8,128)} %fusion.130, f32[640,1024]{1,0:T(8,128)} %fusion.131, bf16[320,1024]{1,0:T(8,128)(2,1)S(1)} %collective-permute-done.6, ...), kind=kOutput, calls=%fused_computation | convolution fusion | flops 843980800 | bytes 17698568 | tf_op jit(solution)/shard_map/dot_general | solution.py:34
  104.3 2.4 %fusion.10 = bf16[320,1024]{1,0:T(8,128)(2,1)} fusion(f32[640,1024]{1,0:T(8,128)} %add_add_fusion, f32[]{:T(128)} %bitcast.50), kind=kLoop, calls=%fused_computation.16 | loop fusion | flops 655360 | bytes 1966084 | tf_op jit(solution)/shard_map/convert_element_type | solution.py:44
  106.7 4.6 %fusion.9 = bf16[320,1024]{1,0:T(8,128)(2,1)} fusion(f32[320,1024]{1,0:T(8,128)S(1)} %copy-done.1, bf16[640,1024]{1,0:T(8,128)(2,1)} %copy-done.4, bf16[320,1024]{1,0:T(8,128)(2,1)} %collective-permute-done.11, bf16[320,1024]{1,0:T(8,128)(2,1)} %collective-permute-done.2, f32[]{:T(128)} %bitcast.49, s32[640]{0:T(1024)S(1)} %collective-permute-done.10, ...), kind=kOutput, calls=%fused_computation.14 | convolution fusion | flops 842342400 | bytes 4591368 | tf_op jit(solution)/shard_map/dot_general | solution.py:38
  111.3 1.3 collective-permute-start.12
  112.6 4.9 %fusion.7 = bf16[320,1024]{1,0:T(8,128)(2,1)} fusion(f32[320,1024]{1,0:T(8,128)} %fusion.136, bf16[640,1024]{1,0:T(8,128)(2,1)} %copy-done.4, bf16[320,1024]{1,0:T(8,128)(2,1)} %collective-permute-done.13, bf16[320,1024]{1,0:T(8,128)(2,1)S(1)} %copy-done.2, f32[]{:T(128)} %bitcast.47, s32[640]{0:T(1024)S(1)} %collective-permute-done.10, f32[]{:T(128)} %bitcast.58, ...), kind=kOutput, calls=%fused_computation.12 | convolution fusion | flops 842342400 | bytes 4591368 | tf_op jit(solution)/shard_map/dot_general | solution.py:38
  117.5 2.2 %fusion.12 = bf16[320,1024]{1,0:T(8,128)(2,1)} fusion(f32[640,1024]{1,0:T(8,128)S(1)} %copy-done, bf16[320,1024]{1,0:T(8,128)(2,1)} %collective-permute-done.7, f32[]{:T(128)} %bitcast.44), kind=kLoop, calls=%fused_computation.19 | loop fusion | flops 1310720 | bytes 2621444 | tf_op jit(solution)/shard_map/convert_element_type | solution.py:45
  119.7 10.9 %collective-permute-done.12 = bf16[320,1024]{1,0:T(8,128)(2,1)} collective-permute-done((bf16[320,1024]{1,0:T(8,128)(2,1)}, bf16[320,1024]{1,0:T(8,128)(2,1)}, u32[]{:S(2)}, u32[]{:S(2)}) %collective-permute-start.12) | collective-permute-done | bytes 655392 | tf_op jit(solution)/shard_map/ppermute | solution.py:86
  130.6 2.0 %broadcast_select_fusion = bf16[320,1024]{1,0:T(8,128)(2,1)} fusion(bf16[320,1024]{1,0:T(8,128)(2,1)} %collective-permute-done.12, bf16[320,1024]{1,0:T(8,128)(2,1)S(1)} %copy-done.3, pred[]{:T(512)S(6)} %or.3), kind=kLoop, calls=%fused_computation.111 | loop fusion | flops 327680 | bytes 1966081 | tf_op jit(solution)/shard_map/jit(_where)/select_n | solution.py:133
  (38 shorter events, 4.6 us)
Async XLA Ops:
  0.6 10.2 %copy-start.5 = (s32[320]{0:T(512)S(1)}, s32[320]{0:T(512)}, u32[]{:S(2)}) copy-start(s32[320]{0:T(512)} %param.7) | copy-start | bytes 3844
  0.6 16.1 %collective-permute-start = (bf16[320,1024]{1,0:T(8,128)(2,1)}, bf16[320,1024]{1,0:T(8,128)(2,1)S(1)}, u32[]{:S(2)}, u32[]{:S(2)}) collective-permute-start(bf16[320,1024]{1,0:T(8,128)(2,1)} %param.5), channel_id=1, source_target_pairs={{1,0},{0,1},{3,2},{2,3},{5,4},{4,5},{7,6},{6,7},{9,8},{8,9},{11,10... | collective-permute-start | bytes 1966088 | tf_op jit(solution)/shard_map/ppermute | solution.py:13
  1.2 38.7 %collective-permute-start.8 = (bf16[320,1024]{1,0:T(8,128)(2,1)}, bf16[320,1024]{1,0:T(8,128)(2,1)}, u32[]{:S(2)}, u32[]{:S(2)}) collective-permute-start(bf16[320,1024]{1,0:T(8,128)(2,1)} %param.5), channel_id=1, source_target_pairs={{0,4},{12,8},{1,5},{13,9},{2,6},{14,10},{3,7},{15,11},{16,20},{28,... | collective-permute-start | bytes 1966088 | tf_op jit(solution)/shard_map/ppermute | solution.py:86
  6.5 28.2 %collective-permute-start.2 = (bf16[320,1024]{1,0:T(8,128)(2,1)}, bf16[320,1024]{1,0:T(8,128)(2,1)}, u32[]{:S(2)}, u32[]{:S(2)}) collective-permute-start(bf16[320,1024]{1,0:T(8,128)(2,1)} %param.6), channel_id=1, source_target_pairs={{0,4},{4,0},{8,12},{12,8},{1,5},{5,1},{9,13},{13,9},{2,6},{6,2},{1... | collective-permute-start | bytes 1966088 | tf_op jit(solution)/shard_map/ppermute | solution.py:86
  6.5 39.1 %collective-permute-start.3 = (bf16[320,1024]{1,0:T(8,128)(2,1)}, bf16[320,1024]{1,0:T(8,128)(2,1)}, u32[]{:S(2)}, u32[]{:S(2)}) collective-permute-start(bf16[320,1024]{1,0:T(8,128)(2,1)} %param.6), channel_id=1, source_target_pairs={{4,8},{8,4},{5,9},{9,5},{6,10},{10,6},{7,11},{11,7},{20,24},{24,20... | collective-permute-start | bytes 1966088 | tf_op jit(solution)/shard_map/ppermute | solution.py:86
  8.0 2.7 %collective-permute-start.1 = (s32[320]{0:T(512)}, s32[320]{0:T(512)S(1)}, u32[]{:S(2)}, u32[]{:S(2)}) collective-permute-start(s32[320]{0:T(512)} %param.7), channel_id=1, source_target_pairs={{1,0},{0,1},{3,2},{2,3},{5,4},{4,5},{7,6},{6,7},{9,8},{8,9},{11,10... | collective-permute-start | bytes 3848 | tf_op jit(solution)/shard_map/ppermute | solution.py:13
  8.3 8.5 %copy-start.2 = (bf16[320,1024]{1,0:T(8,128)(2,1)S(1)}, bf16[320,1024]{1,0:T(8,128)(2,1)}, u32[]{:S(2)}) copy-start(bf16[320,1024]{1,0:T(8,128)(2,1)} %param.6) | copy-start | bytes 1966084
  10.9 44.3 %collective-permute-start.10 = (s32[640]{0:T(1024)S(1)}, s32[640]{0:T(1024)S(1)}, u32[]{:S(2)}, u32[]{:S(2)}) collective-permute-start(s32[640]{0:T(1024)S(1)} %pad_add_fusion), channel_id=1, source_target_pairs={{0,4},{12,8},{1,5},{13,9},{2,6},{14,10},{3,7},{15,11},{16,20},{28,... | collective-permute-start | bytes 7688 | tf_op jit(solution)/shard_map/ppermute | solution.py:86
  38.3 22.8 %collective-permute-start.4 = (bf16[320,1024]{1,0:T(8,128)(2,1)}, bf16[320,1024]{1,0:T(8,128)(2,1)}, u32[]{:S(2)}, u32[]{:S(2)}) collective-permute-start(bf16[320,1024]{1,0:T(8,128)(2,1)} %collective-permute-done.2), channel_id=1, source_target_pairs={{4,8},{8,4},{5,9},{9,5},{6,10},{10,6},{7,11},{11,7},{20,24},{24,20... | collective-permute-start | bytes 1966088 | tf_op jit(solution)/shard_map/ppermute | solution.py:86
  39.8 14.3 %collective-permute-start.9 = (bf16[320,1024]{1,0:T(8,128)(2,1)}, bf16[320,1024]{1,0:T(8,128)(2,1)S(1)}, u32[]{:S(2)}, u32[]{:S(2)}) collective-permute-start(bf16[320,1024]{1,0:T(8,128)(2,1)} %collective-permute-done.8), channel_id=1, source_target_pairs={{1,0},{0,1},{3,2},{2,3},{5,4},{4,5},{7,6},{6,7},{9,8},{8,9},{11,10... | collective-permute-start | bytes 1966088 | tf_op jit(solution)/shard_map/ppermute | solution.py:13
  45.7 30.5 %collective-permute-start.5 = (bf16[320,1024]{1,0:T(8,128)(2,1)}, bf16[320,1024]{1,0:T(8,128)(2,1)}, u32[]{:S(2)}, u32[]{:S(2)}) collective-permute-start(bf16[320,1024]{1,0:T(8,128)(2,1)} %collective-permute-done.3), channel_id=1, source_target_pairs={{4,0},{8,12},{5,1},{9,13},{6,2},{10,14},{7,3},{11,15},{20,16},{24,... | collective-permute-start | bytes 1966088 | tf_op jit(solution)/shard_map/ppermute | solution.py:86
  54.1 1.1 copy-start.4
  59.6 53.0 %collective-permute-start.13 = (bf16[320,1024]{1,0:T(8,128)(2,1)}, bf16[320,1024]{1,0:T(8,128)(2,1)}, u32[]{:S(2)}, u32[]{:S(2)}) collective-permute-start(bf16[320,1024]{1,0:T(8,128)(2,1)} %fusion.6), channel_id=1, source_target_pairs={{4,8},{8,4},{5,9},{9,5},{6,10},{10,6},{7,11},{11,7},{20,24},{24,20... | collective-permute-start | bytes 1966088 | tf_op jit(solution)/shard_map/ppermute | solution.py:86
  69.6 37.1 %collective-permute-start.11 = (bf16[320,1024]{1,0:T(8,128)(2,1)}, bf16[320,1024]{1,0:T(8,128)(2,1)}, u32[]{:S(2)}, u32[]{:S(2)}) collective-permute-start(bf16[320,1024]{1,0:T(8,128)(2,1)} %fusion.8), channel_id=1, source_target_pairs={{4,8},{8,4},{5,9},{9,5},{6,10},{10,6},{7,11},{11,7},{20,24},{24,20... | collective-permute-start | bytes 1966088 | tf_op jit(solution)/shard_map/ppermute | solution.py:86
  71.1 24.5 %collective-permute-start.6 = (bf16[320,1024]{1,0:T(8,128)(2,1)}, bf16[320,1024]{1,0:T(8,128)(2,1)S(1)}, u32[]{:S(2)}, u32[]{:S(2)}) collective-permute-start(bf16[320,1024]{1,0:T(8,128)(2,1)} %collective-permute-done.4), channel_id=1, source_target_pairs={{4,0},{8,12},{5,1},{9,13},{6,2},{10,14},{7,3},{11,15},{20,16},{24,... | collective-permute-start | bytes 1966088 | tf_op jit(solution)/shard_map/ppermute | solution.py:86
  104.3 2.4 %copy-start.1 = (f32[320,1024]{1,0:T(8,128)S(1)}, f32[320,1024]{1,0:T(8,128)}, u32[]{:S(2)}) copy-start(f32[320,1024]{1,0:T(8,128)} %fusion.134) | copy-start | bytes 3932164
  106.7 10.8 %collective-permute-start.7 = (bf16[320,1024]{1,0:T(8,128)(2,1)}, bf16[320,1024]{1,0:T(8,128)(2,1)}, u32[]{:S(2)}, u32[]{:S(2)}) collective-permute-start(bf16[320,1024]{1,0:T(8,128)(2,1)} %fusion.10), channel_id=1, source_target_pairs={{1,0},{0,1},{3,2},{2,3},{5,4},{4,5},{7,6},{6,7},{9,8},{8,9},{11,10... | collective-permute-start | bytes 1966088 | tf_op jit(solution)/shard_map/ppermute | solution.py:13
  111.3 19.3 %collective-permute-start.12 = (bf16[320,1024]{1,0:T(8,128)(2,1)}, bf16[320,1024]{1,0:T(8,128)(2,1)}, u32[]{:S(2)}, u32[]{:S(2)}) collective-permute-start(bf16[320,1024]{1,0:T(8,128)(2,1)} %fusion.9), channel_id=1, source_target_pairs={{4,0},{8,12},{5,1},{9,13},{6,2},{10,14},{7,3},{11,15},{20,16},{24,... | collective-permute-start | bytes 1966088 | tf_op jit(solution)/shard_map/ppermute | solution.py:86
  112.6 4.9 %copy-start = (f32[640,1024]{1,0:T(8,128)S(1)}, f32[640,1024]{1,0:T(8,128)}, u32[]{:S(2)}) copy-start(f32[640,1024]{1,0:T(8,128)} %add_add_fusion) | copy-start | bytes 7864324
  117.5 13.1 %copy-start.3 = (bf16[320,1024]{1,0:T(8,128)(2,1)S(1)}, bf16[320,1024]{1,0:T(8,128)(2,1)}, u32[]{:S(2)}) copy-start(bf16[320,1024]{1,0:T(8,128)(2,1)} %fusion.7) | copy-start | bytes 1966084

commit v2 on v1

v2 whole, which is shorter than its diff:
```python
import functools

import jax
import jax.numpy as jnp
from jax import lax
from jax.experimental import pallas as pl
from jax.experimental.pallas import tpu as pltpu
from jax.sharding import PartitionSpec as P

STEPS = 4
LINE = 4
VMEM_BYTES = 32 * 1024 * 1024


def from_behind(block, axis, distance):
    devices = range(lax.axis_size(axis))
    route = [((i - distance) % len(devices), i) for i in devices]
    return lax.ppermute(block, axis, route)


def swap_inner(block):
    return from_behind(block, "inner", 1)


def after(value, *earlier):
    return lax.optimization_barrier((value,) + earlier)[0]


def coefficients(spectra, glycans, labels, first_target, scale, shift):
    logits = (
        scale
        * lax.dot_general(
            spectra, glycans, (((1,), (1,)), ((), ())), preferred_element_type=jnp.float32
        )
        + shift
    )
    targets = first_target + jnp.arange(glycans.shape[0], dtype=jnp.int32)
    positive = (labels[:, None] == targets[None, :]).astype(jnp.float32)
    return (jax.nn.sigmoid(logits) - positive).astype(jnp.bfloat16)


def around_ring(spectra, glycans, labels, scale, shift):
    rows_here = spectra.shape[0]
    node_rows = rows_here * lax.axis_size("inner")
    loop_count = lax.axis_size("blk")
    position = lax.axis_index("blk")
    core_first = lax.axis_index("sub") * node_rows + lax.axis_index("inner") * rows_here
    lane_rows = lax.axis_size("sub") * node_rows
    node_spectra = jnp.concatenate([spectra, swap_inner(spectra)])
    node_labels = jnp.concatenate([labels, swap_inner(labels)])
    spectrum_total = 0.0
    glycan_total = 0.0
    held = glycans
    for step in range(STEPS):
        if step > 0:
            held = from_behind(held, "blk", 1)
        first_target = (position - step) % loop_count * lane_rows + core_first
        coef = coefficients(node_spectra, held, node_labels, first_target, scale, shift)
        spectrum_total += jnp.dot(coef, held, preferred_element_type=jnp.float32)
        partial_value = scale * lax.dot_general(
            coef, node_spectra, (((0,), (0,)), ((), ())), preferred_element_type=jnp.float32
        )
        if step > 0:
            back = from_behind(partial_value.astype(jnp.bfloat16), "blk", -step)
            partial_value = back.astype(jnp.float32)
        glycan_total += partial_value
    other = swap_inner((scale * spectrum_total[rows_here:]).astype(jnp.bfloat16))
    spectrum_total = scale * spectrum_total[:rows_here] + other.astype(jnp.float32)
    return spectrum_total.astype(jnp.bfloat16), glycan_total.astype(jnp.bfloat16)


def pair_body(plan, *refs):
    n_spectra, blocks, with_spectra, prior_spectra, round_glycans, half = plan
    refs = list(refs)
    factors, ints, labels = refs[:3]
    refs = refs[3:]
    spectra_in, refs = refs[:n_spectra], refs[n_spectra:]
    blocks_in, refs = refs[: len(blocks)], refs[len(blocks) :]
    priors_in = []
    for _, _, has_prior, _ in blocks:
        priors_in.append(refs.pop(0) if has_prior else None)
    prior_s_in = refs.pop(0) if prior_spectra else None
    glycans_out = []
    for _, _, _, wants in blocks:
        glycans_out.append(refs.pop(0) if wants else None)
    if with_spectra == "final":
        mine_out, other_out = refs.pop(0), refs.pop(0)
    elif with_spectra:
        spectra_out = refs.pop(0)
    spectra = refs.pop(0)
    held = [refs.pop(0) for _ in blocks]
    priors = [refs.pop(0) if b[2] else None for b in blocks]
    if with_spectra == "final":
        spectra_out = refs.pop(0)
    sems = refs.pop(0)

    scale, shift = factors[0], factors[1]
    rows = spectra.shape[0] // n_spectra
    at = 0
    moves = []

    def move(source, target):
        nonlocal at
        copy = pltpu.make_async_copy(source, target, sems.at[at])
        copy.start()
        at += 1
        return copy

    for i, ref in enumerate(spectra_in):
        moves.append(move(ref, spectra.at[pl.ds(i * rows, rows)]))
    block_moves = [
        move(ref.at[pl.ds(b[0], b[1])], held[i]) for i, (ref, b) in enumerate(zip(blocks_in, blocks))
    ]
    prior_moves = [
        move(ref.at[pl.ds(b[0], b[1])], priors[i]) if b[2] else None
        for i, (ref, b) in enumerate(zip(priors_in, blocks))
    ]
    prior_s_move = move(prior_s_in, spectra_out) if prior_spectra else None
    for copy in moves:
        copy.wait()
    waited = False
    for i, block in enumerate(blocks):
        block_moves[i].wait()
        if block[2]:
            prior_moves[i].wait()
        if with_spectra and prior_spectra and not waited:
            prior_s_move.wait()
            waited = True

        def work(i=i, block=block):
            glycans = held[i][...]
            logits = scale * lax.dot_general(
                glycans, spectra[...], (((1,), (1,)), ((), ())), preferred_element_type=jnp.float32
            )
            logits = logits + shift
            targets = ints[2 * i] + block[0] + lax.broadcasted_iota(jnp.int32, logits.shape, 0)
            positive = jnp.where(targets == labels[...], 1.0, 0.0)
            coef = (jax.nn.sigmoid(logits) - positive).astype(jnp.bfloat16)
            if block[3]:
                total = jnp.dot(coef, spectra[...], preferred_element_type=jnp.float32)
                if block[2]:
                    total = total + priors[i][...]
                if round_glycans:
                    glycans_out[i][...] = (scale * total).astype(jnp.bfloat16)
                else:
                    glycans_out[i][...] = total
            if with_spectra:
                part = lax.dot_general(
                    coef, glycans, (((0,), (0,)), ((), ())), preferred_element_type=jnp.float32
                )
                if prior_spectra or i > 0:
                    spectra_out[...] += part
                else:
                    spectra_out[...] = part

        if with_spectra == "final":
            pl.when(ints[2 * i + 1] != 0)(work)
        else:
            work()
    if with_spectra == "final":
        mine_out[...] = scale * spectra_out[pl.ds(0, half)]
        other_out[...] = (scale * spectra_out[pl.ds(half, half)]).astype(jnp.bfloat16)


def pair_work(
    factors, spectra, labels, blocks, with_spectra=False, prior_s=None, round_glycans=False
):
    rows, width = spectra[0].shape
    all_rows = rows * len(spectra)
    ints = []
    for b in blocks:
        ints += [jnp.int32(b[1]), jnp.int32(b[2])]
    shapes = tuple((b[3], b[4], b[5] is not None, b[6]) for b in blocks)
    plan = (len(spectra), shapes, with_spectra, prior_s is not None, round_glycans, rows)
    anywhere = pl.BlockSpec(memory_space=pl.ANY)
    in_vmem = pl.BlockSpec(memory_space=pltpu.VMEM)
    in_smem = pl.BlockSpec(memory_space=pltpu.SMEM)
    operands = [factors, jnp.stack(ints), labels] + list(spectra) + [b[0] for b in blocks]
    operands += [b[5] for b in blocks if b[5] is not None]
    if prior_s is not None:
        operands.append(prior_s)
    in_specs = [in_smem, in_smem, in_vmem] + [anywhere] * (len(operands) - 3)
    glycan_type = jnp.bfloat16 if round_glycans else jnp.float32
    outs = [jax.ShapeDtypeStruct((b[4], width), glycan_type) for b in blocks if b[6]]
    if with_spectra == "final":
        outs.append(jax.ShapeDtypeStruct((rows, width), jnp.float32))
        outs.append(jax.ShapeDtypeStruct((rows, width), jnp.bfloat16))
    elif with_spectra:
        outs.append(jax.ShapeDtypeStruct((all_rows, width), jnp.float32))
    scratch = [pltpu.VMEM((all_rows, width), jnp.bfloat16)]
    scratch += [pltpu.VMEM((b[4], width), jnp.bfloat16) for b in blocks]
    scratch += [pltpu.VMEM((b[4], width), jnp.float32) for b in blocks if b[5] is not None]
    if with_spectra == "final":
        scratch.append(pltpu.VMEM((all_rows, width), jnp.float32))
    scratch.append(pltpu.SemaphoreType.DMA((len(operands),)))
    return pl.pallas_call(
        functools.partial(pair_body, plan),
        out_shape=outs,
        in_specs=in_specs,
        out_specs=[in_vmem] * len(outs),
        scratch_shapes=scratch,
        cost_estimate=pl.CostEstimate(flops=1024, bytes_accessed=1024, transcendentals=0),
        compiler_params=pltpu.CompilerParams(vmem_limit_bytes=VMEM_BYTES),
    )(*operands)


def along_line(spectra, glycans, labels, scale, shift):
    rows = spectra.shape[0]
    half = rows // 2
    first_part = 3 * rows // 5
    node_rows = rows * lax.axis_size("inner")
    position = lax.axis_index("blk")
    outer = (position == 0) | (position == LINE - 1)
    core_first = lax.axis_index("sub") * node_rows + lax.axis_index("inner") * rows
    lane_rows = lax.axis_size("sub") * node_rows
    factors = jnp.stack([scale, shift])

    def permute(block, pairs):
        return lax.ppermute(block, "blk", pairs)

    def first_of(block_position):
        return block_position * lane_rows + core_first

    sides = [(0, 1), (1, 0), (2, 3), (3, 2)]
    middle = [(1, 2), (2, 1)]
    inward = [(0, 1), (3, 2)]
    outward = [(1, 0), (2, 3)]
    here_at = first_of(position)
    side_at = first_of(position ^ 1)
    across_at = first_of(LINE - 1 - position)
    far_at = first_of((LINE - 1 - position) ^ 1)

    side = permute(glycans, sides)
    across = permute(glycans, middle)
    partner = swap_inner(spectra)
    own_labels = labels.reshape(1, rows)
    node_labels = jnp.concatenate([own_labels, swap_inner(own_labels)], axis=1)
    end_labels = permute(node_labels, inward)
    node = [spectra, partner]
    here_g, own_s = pair_work(
        factors, node, node_labels, [(glycans, here_at, 1, 0, rows, None, True)], with_spectra=True
    )

    side, across, late_spectra, end_labels = lax.optimization_barrier(
        (side, across, spectra, end_labels, here_g)
    )[:4]
    far = permute(side, middle)
    end_mine = permute(late_spectra, inward)
    next_out = permute(across, outward)
    side_g, across_g, own_s = pair_work(
        factors,
        node,
        node_labels,
        [(side, side_at, 1, 0, rows, None, True), (across, across_at, 1, 0, rows, None, True)],
        with_spectra=True,
        prior_s=own_s,
    )

    end_mine, far, next_out = lax.optimization_barrier((end_mine, far, next_out, own_s))[:3]
    end_other = swap_inner(end_mine)
    last_out = permute(far, outward)
    three_labels = jnp.concatenate([node_labels, end_labels[:, :rows]], axis=1)
    (far_g,) = pair_work(
        factors,
        node + [end_mine],
        three_labels,
        [(far, far_at, 1, 0, rows, None, True)],
    )

    def far_part(first, count, *earlier):
        (out,) = pair_work(
            factors,
            [end_other],
            end_labels[:, rows:],
            [(after(far, far_g, *earlier), far_at, 1, first, count, far_g, True)],
            round_glycans=True,
        )
        return out

    ends = [end_mine, end_other]
    far_a = far_part(0, first_part)
    back_a = permute(far_a, middle)
    side_g, here_g = pair_work(
        factors,
        ends,
        end_labels,
        [
            (after(side, far_a), side_at, 1, 0, rows, side_g, True),
            (glycans, here_at, 1, 0, rows, here_g, True),
        ],
    )
    far_b = far_part(first_part, rows - first_part, side_g)
    back_b = permute(far_b, middle)
    (across_out,) = pair_work(
        factors,
        ends,
        end_labels,
        [(after(across, far_b), across_at, 1, 0, rows, across_g, True)],
        round_glycans=True,
    )
    across_back = permute(across_out, middle)

    total_a = (scale * side_g[:first_part] + back_a.astype(jnp.float32)).astype(jnp.bfloat16)
    inside_a = permute(total_a, outward)
    mine_s, other_s = pair_work(
        factors,
        node,
        node_labels,
        [
            (after(far, total_a), far_at, ~outer, 0, rows, None, False),
            (next_out, far_at, outer, 0, rows, None, False),
            (last_out, across_at, outer, 0, rows, None, False),
        ],
        with_spectra="final",
        prior_s=own_s,
    )
    other_back = jnp.concatenate([swap_inner(other_s[:half]), swap_inner(other_s[half:])])
    back_b = after(back_b, mine_s)
    total_b = (scale * side_g[first_part:] + back_b.astype(jnp.float32)).astype(jnp.bfloat16)
    inside_b = permute(total_b, outward)

    grad_spectra = (mine_s + other_back.astype(jnp.float32)).astype(jnp.bfloat16)
    here_total = (scale * here_g + across_back.astype(jnp.float32)).astype(jnp.bfloat16)
    grad_structures = jnp.where(outer, jnp.concatenate([inside_a, inside_b]), here_total)
    return grad_spectra, grad_structures


def local(
    mass_profile_vectors,
    sugar_tree_vectors,
    matching_glycan_rows,
    sharpness_factor,
    offset_shift_term,
):
    work = along_line if lax.axis_size("blk") == STEPS == LINE else around_ring
    return work(
        mass_profile_vectors,
        sugar_tree_vectors,
        matching_glycan_rows,
        sharpness_factor[0],
        offset_shift_term[0],
    )


def solution(mesh):
    placed = (
        P(("groups", "blk", "sub", "inner"), None),
        P(("groups", "blk", "sub", "inner"), None),
        P(("groups", "blk", "sub", "inner")),
        P(),
        P(),
    )
    return jax.shard_map(
        local,
        mesh=mesh,
        in_specs=placed,
        out_specs=(
            P(("groups", "blk", "sub", "inner"), None),
            P(("groups", "blk", "sub", "inner"), None),
        ),
        check_vma=False,
    )
```

time: 133 us -> 103 us (0.77)
  matrix products: 57.3 us -> 0 us
  Pallas kernels: 0 us -> 31.3 us
  waiting for transfers between devices: 41.1 us -> 20.1 us
  local copies, waits for them, and re-layouts: 3.5 us -> 15.6 us
  starting transfers between devices: 22 us -> 28.8 us
  other arithmetic: 6.67 us -> 4.01 us
    dot_general x18 -> x0, matrix products: 57.3 us -> none  [the longest x6 26.2 us: toward_spectra(): return jnp.dot(coef, glycans, preferred_element_type=jnp.float32)]
    pallas_call x0 -> x8, Pallas kernels: none -> 31.3 us  [pair_work(): pl.pallas_call(functools.partial(pair_body, plan), out_shape=outs, in_spe...]
    ppermute x10 -> x12, waiting for transfers between devices: 41.1 us -> 20.1 us  [permute(): return lax.ppermute(block, 'blk', pairs)]
    unnamed x14 -> x36, local copies, waits for them, and re-layouts: 3.41 us -> 14.7 us
    ppermute x10 -> x12, starting transfers between devices: 21.3 us -> 27.6 us  [permute(): return lax.ppermute(block, 'blk', pairs)]
    convert_element_type x2 -> x3, other arithmetic: 4.58 us -> 2.24 us  [the longest x1 1.12 us: along_line(): (scale * side_g[:first_part] + back_a.astype(jnp.float32)).astype(jnp.bfl...]
  transfers between devices with their start and end apart: 14 -> 17, of which waited for: 3 -> 3; matrix products, arithmetic and copies ran while one was open for 49% -> 4% of each run, Pallas kernels for 0% -> 28%
where the time goes in v2:
time: 103 us; the launch traced here: 102 us
  Pallas kernels  31.3 us (30%)
  starting transfers between devices  28.8 us (28%)
  waiting for transfers between devices  20.1 us (20%)
  local copies, waits for them, and re-layouts  15.6 us (15%)
  other arithmetic  4.01 us (4%)
  between operations  2.28 us (2%)
    pallas_call x8, Pallas kernels, pair_work(): pl.pallas_call(functools.partial(pair_body, plan), out_shape=outs, in_spe...  31.3 us
    ppermute x12, starting transfers between devices, permute(): return lax.ppermute(block, 'blk', pairs)  27.6 us
    ppermute x12, waiting for transfers between devices, permute(): return lax.ppermute(block, 'blk', pairs)  20.1 us
    unnamed x36, local copies, waits for them, and re-layouts  14.7 us
  transfers between devices with their start and end apart: 17, of which 3 were waited for; matrix products, arithmetic and copies ran while one was open for 4% of the time, Pallas kernels for 28%

profile of v2, /device:TPU:0, one launch (start us, length us, event | category | flops | bytes accessed | tf_op | source)
XLA Modules:
  0.0 102.1 jit_solution(3787533411956234521)
XLA Ops:
  1.1 2.7 %collective-permute-start.2 = (bf16[320,1024]{1,0:T(8,128)(2,1)}, bf16[320,1024]{1,0:T(8,128)(2,1)S(1)}, u32[]{:S(2)}, u32[]{:S(2)}) collective-permute-start(bf16[320,1024]{1,0:T(8,128)(2,1)} %refs_6_.1), channel_id=1, source_target_pairs={{0,4},{4,0},{8,12},{12,8},{1,5},{5,1},{9,13},{13,9},{2,6},{6,2},{1... | collective-permute-start | bytes 1966088 | tf_op jit(solution)/shard_map/ppermute | solution.py:219
  6.8 6.1 %collective-permute-start.4 = (s32[1,640]{1,0:T(1,128)S(1)}, s32[1,640]{1,0:T(1,128)S(1)}, u32[]{:S(2)}, u32[]{:S(2)}) collective-permute-start(s32[1,640]{1,0:T(1,128)S(1)} %pad_add_fusion.1.refs_2_), channel_id=1, source_target_pairs={{0,4},{12,8},{1,5},{13,9},{2,6},{14,10},{3,7},{15,11},{16,20},{28,... | collective-permute-start | bytes 7688 | tf_op jit(solution)/shard_map/ppermute | solution.py:219
  13.0 1.1 %copy-done.4 = bf16[320,1024]{1,0:T(8,128)(2,1)S(1)} copy-done((bf16[320,1024]{1,0:T(8,128)(2,1)S(1)}, bf16[320,1024]{1,0:T(8,128)(2,1)}, u32[]{:S(2)}) %copy-start.4) | copy-done | bytes 655384
  14.1 4.0 %shard_map.68 = (f32[320,1024]{1,0:T(8,128)S(1)}, f32[640,1024]{1,0:T(8,128)S(1)}) custom-call(f32[2]{0:T(128)S(1)} %pad_maximum_fusion.refs_0_, s32[2]{0:T(128)S(1)} %pad_add_fusion.4.refs_1_, s32[1,640]{1,0:T(1,128)S(1)} %pad_add_fusion.1.refs_2_, bf16[320,1024]{1,0:T(8,128)(2,1)} %refs_3_.7, bf16[320,1024]{1,0:T(8,128)(2,1)S(1)} %collective-permute-done.1.refs_4_, ...), custom_call_target="tpu_custom_call" | custom-call | flops 1024 | bytes 1024 | tf_op jit(solution)/shard_map/pallas_call | solution.py:196
  18.1 1.5 %copy-done.2 = f32[640,1024]{1,0:T(8,128)} copy-done((f32[640,1024]{1,0:T(8,128)}, f32[640,1024]{1,0:T(8,128)S(1)}, u32[]{:S(2)}) %copy-start.2) | copy-done | bytes 2621464
  19.5 1.1 %copy-done.12 = f32[320,1024]{1,0:T(8,128)} copy-done((f32[320,1024]{1,0:T(8,128)}, f32[320,1024]{1,0:T(8,128)S(1)}, u32[]{:S(2)}) %copy-start.12) | copy-done | bytes 1310744
  21.4 1.3 %collective-permute-start.7 = (bf16[320,1024]{1,0:T(8,128)(2,1)S(1)}, bf16[320,1024]{1,0:T(8,128)(2,1)S(1)}, u32[]{:S(2)}, u32[]{:S(2)}) collective-permute-start(bf16[320,1024]{1,0:T(8,128)(2,1)S(1)} %collective-permute-done.3.refs_6_.refs_5_), channel_id=1, source_target_pairs={{4,0},{8,12},{5,1},{9,13},{6,2},{10,14},{7,3},{11,15},{20,16},{24,... | collective-permute-start | bytes 1966088 | tf_op jit(solution)/shard_map/ppermute | solution.py:219
  22.7 9.2 %collective-permute-start.5 = (bf16[320,1024]{1,0:T(8,128)(2,1)}, bf16[320,1024]{1,0:T(8,128)(2,1)}, u32[]{:S(2)}, u32[]{:S(2)}) collective-permute-start(bf16[320,1024]{1,0:T(8,128)(2,1)} %refs_3_.7), channel_id=1, source_target_pairs={{0,4},{12,8},{1,5},{13,9},{2,6},{14,10},{3,7},{15,11},{16,20},{28,... | collective-permute-start | bytes 1966088 | tf_op jit(solution)/shard_map/ppermute | solution.py:219
  31.9 1.7 %copy-done.3 = f32[640,1024]{1,0:T(8,128)S(1)} copy-done((f32[640,1024]{1,0:T(8,128)S(1)}, f32[640,1024]{1,0:T(8,128)}, u32[]{:S(2)}) %copy-start.3) | copy-done | bytes 2621464
  33.7 5.9 %shard_map.69 = (f32[320,1024]{1,0:T(8,128)S(1)}, f32[320,1024]{1,0:T(8,128)S(1)}, f32[640,1024]{1,0:T(8,128)S(1)}) custom-call(f32[2]{0:T(128)S(1)} %pad_maximum_fusion.refs_0_, s32[4]{0:T(128)S(1)} %pad_add_fusion.6.refs_1_, s32[1,640]{1,0:T(1,128)S(1)} %pad_add_fusion.1.refs_2_, bf16[320,1024]{1,0:T(8,128)(2,1)} %refs_3_.7, ...), custom_call_target="tpu_custom_call" | custom-call | flops 1024 | bytes 1024 | tf_op jit(solution)/shard_map/pallas_call | solution.py:196
  39.6 1.5 %copy-done = f32[640,1024]{1,0:T(8,128)} copy-done((f32[640,1024]{1,0:T(8,128)}, f32[640,1024]{1,0:T(8,128)S(1)}, u32[]{:S(2)}) %copy-start) | copy-done | bytes 2621464
  41.1 1.1 %copy-done.10 = f32[320,1024]{1,0:T(8,128)} copy-done((f32[320,1024]{1,0:T(8,128)}, f32[320,1024]{1,0:T(8,128)S(1)}, u32[]{:S(2)}) %copy-start.10) | copy-done | bytes 1310744
  42.2 1.1 %copy-done.14 = f32[320,1024]{1,0:T(8,128)} copy-done((f32[320,1024]{1,0:T(8,128)}, f32[320,1024]{1,0:T(8,128)S(1)}, u32[]{:S(2)}) %copy-start.14) | copy-done | bytes 1310744
  44.7 3.5 %shard_map.70.refs_5_ = f32[320,1024]{1,0:T(8,128)S(1)} custom-call(f32[2]{0:T(128)S(1)} %pad_maximum_fusion.refs_0_, s32[2]{0:T(128)S(1)} %pad_add_fusion.3.refs_1_, s32[1,960]{1,0:T(1,128)S(1)} %pad_add_fusion.refs_2_, bf16[320,1024]{1,0:T(8,128)(2,1)} %refs_3_.7, bf16[320,1024]{1,0:T(8,128)(2,1)S(1)} %collective-permute-done.1.refs_4_, ...), custom_call_target="tpu_custom_call" | custom-call | flops 1024 | bytes 1024 | tf_op jit(solution)/shard_map/pallas_call | solution.py:196
  48.3 2.6 %shard_map.71 = bf16[192,1024]{1,0:T(8,128)(2,1)} custom-call(f32[2]{0:T(128)S(1)} %pad_maximum_fusion.refs_0_, s32[2]{0:T(128)S(1)} %pad_add_fusion.3.refs_1_, s32[1,320]{1,0:T(1,128)S(1)} %get-tuple-element.49.refs_2_, bf16[320,1024]{1,0:T(8,128)(2,1)S(1)} %collective-permute-done.8.refs_3_.refs_4_, ...), custom_call_target="tpu_custom_call" | custom-call | flops 1024 | bytes 1024 | tf_op jit(solution)/shard_map/pallas_call | solution.py:196
  51.0 1.4 %collective-permute-start.9 = (bf16[192,1024]{1,0:T(8,128)(2,1)}, bf16[192,1024]{1,0:T(8,128)(2,1)}, u32[]{:S(2)}, u32[]{:S(2)}) collective-permute-start(bf16[192,1024]{1,0:T(8,128)(2,1)} %shard_map.71), channel_id=1, source_target_pairs={{4,8},{8,4},{5,9},{9,5},{6,10},{10,6},{7,11},{11,7},{20,24},{24,20... | collective-permute-start | bytes 1179656 | tf_op jit(solution)/shard_map/ppermute | solution.py:219
  52.4 1.3 %collective-permute-start.10 = (bf16[320,1024]{1,0:T(8,128)(2,1)S(1)}, bf16[320,1024]{1,0:T(8,128)(2,1)}, u32[]{:S(2)}, u32[]{:S(2)}) collective-permute-start(bf16[320,1024]{1,0:T(8,128)(2,1)S(1)} %collective-permute-done.6.refs_6_.refs_4_.refs_5_), channel_id=1, source_target_pairs={{4,0},{8,12},{5,1},{9,13},{6,2},{10,14},{7,3},{11,15},{20,16},{24,... | collective-permute-start | bytes 1966088 | tf_op jit(solution)/shard_map/ppermute | solution.py:219
  53.9 1.1 %copy-done.5 = bf16[320,1024]{1,0:T(8,128)(2,1)S(1)} copy-done((bf16[320,1024]{1,0:T(8,128)(2,1)S(1)}, bf16[320,1024]{1,0:T(8,128)(2,1)}, u32[]{:S(2)}) %copy-start.5) | copy-done | bytes 655384
  55.0 1.1 %copy-done.9 = bf16[320,1024]{1,0:T(8,128)(2,1)S(1)} copy-done((bf16[320,1024]{1,0:T(8,128)(2,1)S(1)}, bf16[320,1024]{1,0:T(8,128)(2,1)}, u32[]{:S(2)}) %copy-start.9) | copy-done | bytes 655384
  56.1 1.3 %copy-done.13 = f32[320,1024]{1,0:T(8,128)S(1)} copy-done((f32[320,1024]{1,0:T(8,128)S(1)}, f32[320,1024]{1,0:T(8,128)}, u32[]{:S(2)}) %copy-start.13) | copy-done | bytes 1310744
  57.4 1.3 %copy-done.15 = f32[320,1024]{1,0:T(8,128)S(1)} copy-done((f32[320,1024]{1,0:T(8,128)S(1)}, f32[320,1024]{1,0:T(8,128)}, u32[]{:S(2)}) %copy-start.15) | copy-done | bytes 1310744
  58.7 4.6 %shard_map.72 = (f32[320,1024]{1,0:T(8,128)S(1)}, f32[320,1024]{1,0:T(8,128)S(1)}) custom-call(f32[2]{0:T(128)S(1)} %pad_maximum_fusion.refs_0_, s32[4]{0:T(128)S(1)} %pad_add_fusion.5.refs_1_, s32[1,640]{1,0:T(1,128)S(1)} %collective-permute-done.4.refs_2_, bf16[320,1024]{1,0:T(8,128)(2,1)} %collective-permute-done.5.refs_5_.refs_3_, ...), custom_call_target="tpu_custom_call" | custom-call | flops 1024 | bytes 1024 | tf_op jit(solution)/shard_map/pallas_call | solution.py:196
  63.3 1.6 %shard_map.74 = bf16[128,1024]{1,0:T(8,128)(2,1)S(1)} custom-call(f32[2]{0:T(128)S(1)} %pad_maximum_fusion.refs_0_, s32[2]{0:T(128)S(1)} %pad_add_fusion.3.refs_1_, s32[1,320]{1,0:T(1,128)S(1)} %get-tuple-element.49.refs_2_, bf16[320,1024]{1,0:T(8,128)(2,1)S(1)} %collective-permute-done.8.refs_3_.refs_4_, ...), custom_call_target="tpu_custom_call" | custom-call | flops 1024 | bytes 1024 | tf_op jit(solution)/shard_map/pallas_call | solution.py:196
  65.9 3.5 %shard_map.75 = bf16[320,1024]{1,0:T(8,128)(2,1)S(1)} custom-call(f32[2]{0:T(128)S(1)} %pad_maximum_fusion.refs_0_, s32[2]{0:T(128)S(1)} %pad_add_fusion.2.refs_1_, s32[1,640]{1,0:T(1,128)S(1)} %collective-permute-done.4.refs_2_, bf16[320,1024]{1,0:T(8,128)(2,1)} %collective-permute-done.5.refs_5_.refs_3_, ...), custom_call_target="tpu_custom_call" | custom-call | flops 1024 | bytes 1024 | tf_op jit(solution)/shard_map/pallas_call | solution.py:196
  70.3 1.1 %add_convert_fusion.2 = bf16[192,1024]{1,0:T(8,128)(2,1)S(1)} fusion(bf16[192,1024]{1,0:T(8,128)(2,1)} %collective-permute-done.9, f32[320,1024]{1,0:T(8,128)S(1)} %get-tuple-element.36, f32[]{:T(128)} %bitcast.7), kind=kLoop, calls=%fused_computation.2 | loop fusion | flops 786432 | bytes 1572868 | tf_op jit(solution)/shard_map/convert_element_type | solution.py:303
  71.4 1.1 %collective-permute-done.10.refs_7_ = bf16[320,1024]{1,0:T(8,128)(2,1)} collective-permute-done((bf16[320,1024]{1,0:T(8,128)(2,1)S(1)}, bf16[320,1024]{1,0:T(8,128)(2,1)}, u32[]{:S(2)}, u32[]{:S(2)}) %collective-permute-start.10) | collective-permute-done | bytes 655392 | tf_op jit(solution)/shard_map/ppermute | solution.py:219
  72.5 5.4 %shard_map.73 = (f32[320,1024]{1,0:T(8,128)S(1)}, bf16[320,1024]{1,0:T(8,128)(2,1)S(1)}) custom-call(f32[2]{0:T(128)S(1)} %pad_maximum_fusion.refs_0_, s32[6]{0:T(128)S(1)} %stack.63.refs_1_, s32[1,640]{1,0:T(1,128)S(1)} %pad_add_fusion.1.refs_2_, bf16[320,1024]{1,0:T(8,128)(2,1)} %refs_3_.7, bf16[320,1024]{1,0:T(8,128)(2,1)S(1)} %collective-permute-done.1.refs_4_, ...), custom_call_target="tpu_custom_call" | custom-call | flops 1024 | bytes 1024 | tf_op jit(solution)/shard_map/pallas_call | solution.py:196
  78.5 1.3 %collective-permute-start.13 = (bf16[192,1024]{1,0:T(8,128)(2,1)S(1)}, bf16[192,1024]{1,0:T(8,128)(2,1)S(1)}, u32[]{:S(2)}, u32[]{:S(2)}) collective-permute-start(bf16[192,1024]{1,0:T(8,128)(2,1)S(1)} %add_convert_fusion.2), channel_id=1, source_target_pairs={{4,0},{8,12},{5,1},{9,13},{6,2},{10,14},{7,3},{11,15},{20,16},{24,... | collective-permute-start | bytes 1179656 | tf_op jit(solution)/shard_map/ppermute | solution.py:219
  79.9 1.3 %collective-permute-start.15 = (bf16[128,1024]{1,0:T(8,128)(2,1)S(1)}, bf16[128,1024]{1,0:T(8,128)(2,1)S(1)}, u32[]{:S(2)}, u32[]{:S(2)}) collective-permute-start(bf16[128,1024]{1,0:T(8,128)(2,1)S(1)} %add_convert_fusion.3), channel_id=1, source_target_pairs={{4,0},{8,12},{5,1},{9,13},{6,2},{10,14},{7,3},{11,15},{20,16},{24,... | collective-permute-start | bytes 786440 | tf_op jit(solution)/shard_map/ppermute | solution.py:219
  81.2 1.0 %add_convert_fusion.1 = bf16[320,1024]{1,0:T(8,128)(2,1)} fusion(f32[320,1024]{1,0:T(8,128)S(1)} %get-tuple-element.39, bf16[160,1024]{1,0:T(8,128)(2,1)S(1)} %collective-permute-done.12, bf16[160,1024]{1,0:T(8,128)(2,1)S(1)} %collective-permute-done.11), kind=kLoop, calls=%fused_computation.1 | loop fusion | flops 1966080 | bytes 2621440 | tf_op jit(solution)/shard_map/convert_element_type | solution.py:322
  82.3 18.6 %collective-permute-done.15 = bf16[128,1024]{1,0:T(8,128)(2,1)S(1)} collective-permute-done((bf16[128,1024]{1,0:T(8,128)(2,1)S(1)}, bf16[128,1024]{1,0:T(8,128)(2,1)S(1)}, u32[]{:S(2)}, u32[]{:S(2)}) %collective-permute-start.15) | collective-permute-done | bytes 262176 | tf_op jit(solution)/shard_map/ppermute | solution.py:219
  100.9 1.2 %fusion = bf16[320,1024]{1,0:T(8,128)(2,1)} fusion(bf16[320,1024]{1,0:T(8,128)(2,1)S(1)} %collective-permute-done.16, f32[320,1024]{1,0:T(8,128)S(1)} %get-tuple-element.43, bf16[128,1024]{1,0:T(8,128)(2,1)S(1)} %collective-permute-done.15, bf16[192,1024]{1,0:T(8,128)(2,1)S(1)} %collective-permute-done.13, f32[]{:T(128)} %bitcast.9, pred[]{:T(512)S(6)} %or.3), kind=kLoop, calls=%fused_computation.3 | loop fusion | flops 2949120 | bytes 3276805 | tf_op jit(solution)/shard_map/jit(_where)/select_n | solution.py:324
  (62 shorter events, 7.2 us)
Async XLA Ops:
  0.6 12.4 %collective-permute-start.1 = (bf16[320,1024]{1,0:T(8,128)(2,1)}, bf16[320,1024]{1,0:T(8,128)(2,1)S(1)}, u32[]{:S(2)}, u32[]{:S(2)}) collective-permute-start(bf16[320,1024]{1,0:T(8,128)(2,1)} %refs_3_.7), channel_id=1, source_target_pairs={{1,0},{0,1},{3,2},{2,3},{5,4},{4,5},{7,6},{6,7},{9,8},{8,9},{11,10... | collective-permute-start | bytes 1966088 | tf_op jit(solution)/shard_map/ppermute | solution.py:18
  1.1 19.5 %collective-permute-start.2 = (bf16[320,1024]{1,0:T(8,128)(2,1)}, bf16[320,1024]{1,0:T(8,128)(2,1)S(1)}, u32[]{:S(2)}, u32[]{:S(2)}) collective-permute-start(bf16[320,1024]{1,0:T(8,128)(2,1)} %refs_6_.1), channel_id=1, source_target_pairs={{0,4},{4,0},{8,12},{12,8},{1,5},{5,1},{9,13},{13,9},{2,6},{6,2},{1... | collective-permute-start | bytes 1966088 | tf_op jit(solution)/shard_map/ppermute | solution.py:219
  3.8 16.8 %collective-permute-start.3 = (bf16[320,1024]{1,0:T(8,128)(2,1)}, bf16[320,1024]{1,0:T(8,128)(2,1)S(1)}, u32[]{:S(2)}, u32[]{:S(2)}) collective-permute-start(bf16[320,1024]{1,0:T(8,128)(2,1)} %refs_6_.1), channel_id=1, source_target_pairs={{4,8},{8,4},{5,9},{9,5},{6,10},{10,6},{7,11},{11,7},{20,24},{24,20... | collective-permute-start | bytes 1966088 | tf_op jit(solution)/shard_map/ppermute | solution.py:219
  5.2 1.5 %collective-permute-start = (s32[1,320]{1,0:T(1,128)S(1)}, s32[1,320]{1,0:T(1,128)S(1)}, u32[]{:S(2)}, u32[]{:S(2)}) collective-permute-start(s32[1,320]{1,0:T(1,128)S(1)} %reshape.7), channel_id=1, source_target_pairs={{1,0},{0,1},{3,2},{2,3},{5,4},{4,5},{7,6},{6,7},{9,8},{8,9},{11,10... | collective-permute-start | bytes 3848 | tf_op jit(solution)/shard_map/ppermute | solution.py:18
  6.8 13.8 %collective-permute-start.4 = (s32[1,640]{1,0:T(1,128)S(1)}, s32[1,640]{1,0:T(1,128)S(1)}, u32[]{:S(2)}, u32[]{:S(2)}) collective-permute-start(s32[1,640]{1,0:T(1,128)S(1)} %pad_add_fusion.1.refs_2_), channel_id=1, source_target_pairs={{0,4},{12,8},{1,5},{13,9},{2,6},{14,10},{3,7},{15,11},{16,20},{28,... | collective-permute-start | bytes 7688 | tf_op jit(solution)/shard_map/ppermute | solution.py:219
  13.0 1.1 %copy-start.4 = (bf16[320,1024]{1,0:T(8,128)(2,1)S(1)}, bf16[320,1024]{1,0:T(8,128)(2,1)}, u32[]{:S(2)}) copy-start(bf16[320,1024]{1,0:T(8,128)(2,1)} %refs_6_.1) | copy-start | bytes 1966084
  18.1 1.5 %copy-start.2 = (f32[640,1024]{1,0:T(8,128)}, f32[640,1024]{1,0:T(8,128)S(1)}, u32[]{:S(2)}) copy-start(f32[640,1024]{1,0:T(8,128)S(1)} %get-tuple-element.28.refs_7_) | copy-start | bytes 7864324
  20.6 19.0 %copy-start.8 = (bf16[320,1024]{1,0:T(8,128)(2,1)}, bf16[320,1024]{1,0:T(8,128)(2,1)S(1)}, u32[]{:S(2)}) copy-start(bf16[320,1024]{1,0:T(8,128)(2,1)S(1)} %collective-permute-done.2.refs_5_) | copy-start | bytes 1966084
  20.6 19.0 %copy-start.6 = (bf16[320,1024]{1,0:T(8,128)(2,1)}, bf16[320,1024]{1,0:T(8,128)(2,1)S(1)}, u32[]{:S(2)}) copy-start(bf16[320,1024]{1,0:T(8,128)(2,1)S(1)} %collective-permute-done.3.refs_6_.refs_5_) | copy-start | bytes 1966084
  20.6 22.6 %collective-permute-start.6 = (bf16[320,1024]{1,0:T(8,128)(2,1)S(1)}, bf16[320,1024]{1,0:T(8,128)(2,1)S(1)}, u32[]{:S(2)}, u32[]{:S(2)}) collective-permute-start(bf16[320,1024]{1,0:T(8,128)(2,1)S(1)} %collective-permute-done.2.refs_5_), channel_id=1, source_target_pairs={{4,8},{8,4},{5,9},{9,5},{6,10},{10,6},{7,11},{11,7},{20,24},{24,20... | collective-permute-start | bytes 1966088 | tf_op jit(solution)/shard_map/ppermute | solution.py:219
  21.4 21.9 %collective-permute-start.7 = (bf16[320,1024]{1,0:T(8,128)(2,1)S(1)}, bf16[320,1024]{1,0:T(8,128)(2,1)S(1)}, u32[]{:S(2)}, u32[]{:S(2)}) collective-permute-start(bf16[320,1024]{1,0:T(8,128)(2,1)S(1)} %collective-permute-done.3.refs_6_.refs_5_), channel_id=1, source_target_pairs={{4,0},{8,12},{5,1},{9,13},{6,2},{10,14},{7,3},{11,15},{20,16},{24,... | collective-permute-start | bytes 1966088 | tf_op jit(solution)/shard_map/ppermute | solution.py:219
  22.7 21.9 %collective-permute-start.5 = (bf16[320,1024]{1,0:T(8,128)(2,1)}, bf16[320,1024]{1,0:T(8,128)(2,1)}, u32[]{:S(2)}, u32[]{:S(2)}) collective-permute-start(bf16[320,1024]{1,0:T(8,128)(2,1)} %refs_3_.7), channel_id=1, source_target_pairs={{0,4},{12,8},{1,5},{13,9},{2,6},{14,10},{3,7},{15,11},{16,20},{28,... | collective-permute-start | bytes 1966088 | tf_op jit(solution)/shard_map/ppermute | solution.py:219
  31.9 1.7 %copy-start.3 = (f32[640,1024]{1,0:T(8,128)S(1)}, f32[640,1024]{1,0:T(8,128)}, u32[]{:S(2)}) copy-start(f32[640,1024]{1,0:T(8,128)} %copy-done.2) | copy-start | bytes 7864324
  39.6 1.5 %copy-start = (f32[640,1024]{1,0:T(8,128)}, f32[640,1024]{1,0:T(8,128)S(1)}, u32[]{:S(2)}) copy-start(f32[640,1024]{1,0:T(8,128)S(1)} %get-tuple-element.29.refs_8_) | copy-start | bytes 7864324
  41.1 1.1 %copy-start.10 = (f32[320,1024]{1,0:T(8,128)}, f32[320,1024]{1,0:T(8,128)S(1)}, u32[]{:S(2)}) copy-start(f32[320,1024]{1,0:T(8,128)S(1)} %get-tuple-element.45.refs_6_) | copy-start | bytes 3932164
  44.5 3.8 %collective-permute-start.8 = (bf16[320,1024]{1,0:T(8,128)(2,1)}, bf16[320,1024]{1,0:T(8,128)(2,1)S(1)}, u32[]{:S(2)}, u32[]{:S(2)}) collective-permute-start(bf16[320,1024]{1,0:T(8,128)(2,1)} %collective-permute-done.5.refs_5_.refs_3_), channel_id=1, source_target_pairs={{1,0},{0,1},{3,2},{2,3},{5,4},{4,5},{7,6},{6,7},{9,8},{8,9},{11,10... | collective-permute-start | bytes 1966088 | tf_op jit(solution)/shard_map/ppermute | solution.py:18
  51.0 19.3 %collective-permute-start.9 = (bf16[192,1024]{1,0:T(8,128)(2,1)}, bf16[192,1024]{1,0:T(8,128)(2,1)}, u32[]{:S(2)}, u32[]{:S(2)}) collective-permute-start(bf16[192,1024]{1,0:T(8,128)(2,1)} %shard_map.71), channel_id=1, source_target_pairs={{4,8},{8,4},{5,9},{9,5},{6,10},{10,6},{7,11},{11,7},{20,24},{24,20... | collective-permute-start | bytes 1179656 | tf_op jit(solution)/shard_map/ppermute | solution.py:219
  52.4 20.1 %collective-permute-start.10 = (bf16[320,1024]{1,0:T(8,128)(2,1)S(1)}, bf16[320,1024]{1,0:T(8,128)(2,1)}, u32[]{:S(2)}, u32[]{:S(2)}) collective-permute-start(bf16[320,1024]{1,0:T(8,128)(2,1)S(1)} %collective-permute-done.6.refs_6_.refs_4_.refs_5_), channel_id=1, source_target_pairs={{4,0},{8,12},{5,1},{9,13},{6,2},{10,14},{7,3},{11,15},{20,16},{24,... | collective-permute-start | bytes 1966088 | tf_op jit(solution)/shard_map/ppermute | solution.py:219
  53.9 1.1 %copy-start.5 = (bf16[320,1024]{1,0:T(8,128)(2,1)S(1)}, bf16[320,1024]{1,0:T(8,128)(2,1)}, u32[]{:S(2)}) copy-start(bf16[320,1024]{1,0:T(8,128)(2,1)} %refs_6_.1) | copy-start | bytes 1966084
  55.0 1.1 %copy-start.9 = (bf16[320,1024]{1,0:T(8,128)(2,1)S(1)}, bf16[320,1024]{1,0:T(8,128)(2,1)}, u32[]{:S(2)}) copy-start(bf16[320,1024]{1,0:T(8,128)(2,1)} %copy-done.8) | copy-start | bytes 1966084
  56.1 1.3 %copy-start.13 = (f32[320,1024]{1,0:T(8,128)S(1)}, f32[320,1024]{1,0:T(8,128)}, u32[]{:S(2)}) copy-start(f32[320,1024]{1,0:T(8,128)} %copy-done.12) | copy-start | bytes 3932164
  57.4 1.3 %copy-start.15 = (f32[320,1024]{1,0:T(8,128)S(1)}, f32[320,1024]{1,0:T(8,128)}, u32[]{:S(2)}) copy-start(f32[320,1024]{1,0:T(8,128)} %copy-done.14) | copy-start | bytes 3932164
  63.3 2.5 %copy-start.7 = (bf16[320,1024]{1,0:T(8,128)(2,1)S(1)}, bf16[320,1024]{1,0:T(8,128)(2,1)}, u32[]{:S(2)}) copy-start(bf16[320,1024]{1,0:T(8,128)(2,1)} %copy-done.6) | copy-start | bytes 1966084
  63.3 2.5 %copy-start.11 = (f32[320,1024]{1,0:T(8,128)S(1)}, f32[320,1024]{1,0:T(8,128)}, u32[]{:S(2)}) copy-start(f32[320,1024]{1,0:T(8,128)} %copy-done.10) | copy-start | bytes 3932164
  65.0 14.9 %collective-permute-start.14 = (bf16[128,1024]{1,0:T(8,128)(2,1)S(1)}, bf16[128,1024]{1,0:T(8,128)(2,1)S(1)}, u32[]{:S(2)}, u32[]{:S(2)}) collective-permute-start(bf16[128,1024]{1,0:T(8,128)(2,1)S(1)} %shard_map.74), channel_id=1, source_target_pairs={{4,8},{8,4},{5,9},{9,5},{6,10},{10,6},{7,11},{11,7},{20,24},{24,20... | collective-permute-start | bytes 786440 | tf_op jit(solution)/shard_map/ppermute | solution.py:219
  65.9 6.6 %copy-start.1 = (f32[640,1024]{1,0:T(8,128)S(1)}, f32[640,1024]{1,0:T(8,128)}, u32[]{:S(2)}) copy-start(f32[640,1024]{1,0:T(8,128)} %copy-done) | copy-start | bytes 7864324
  69.4 3.1 %copy-start.17 = (bf16[320,1024]{1,0:T(8,128)(2,1)S(1)}, bf16[320,1024]{1,0:T(8,128)(2,1)}, u32[]{:S(2)}) copy-start(bf16[320,1024]{1,0:T(8,128)(2,1)} %copy-done.16) | copy-start | bytes 1966084
  69.4 31.5 %collective-permute-start.16 = (bf16[320,1024]{1,0:T(8,128)(2,1)S(1)}, bf16[320,1024]{1,0:T(8,128)(2,1)S(1)}, u32[]{:S(2)}, u32[]{:S(2)}) collective-permute-start(bf16[320,1024]{1,0:T(8,128)(2,1)S(1)} %shard_map.75), channel_id=1, source_target_pairs={{4,8},{8,4},{5,9},{9,5},{6,10},{10,6},{7,11},{11,7},{20,24},{24,20... | collective-permute-start | bytes 1966088 | tf_op jit(solution)/shard_map/ppermute | solution.py:219
  78.0 3.3 %collective-permute-start.11 = (bf16[160,1024]{1,0:T(8,128)(2,1)S(1)}, bf16[160,1024]{1,0:T(8,128)(2,1)S(1)}, u32[]{:S(2)}, u32[]{:S(2)}) collective-permute-start(bf16[160,1024]{1,0:T(8,128)(2,1)S(1)} %get-tuple-element.46), channel_id=1, source_target_pairs={{1,0},{0,1},{3,2},{2,3},{5,4},{4,5},{7,6},{6,7},{9,8},{8,9},{11,10... | collective-permute-start | bytes 983048 | tf_op jit(solution)/shard_map/ppermute | solution.py:18
  78.0 3.2 %collective-permute-start.12 = (bf16[160,1024]{1,0:T(8,128)(2,1)S(1)}, bf16[160,1024]{1,0:T(8,128)(2,1)S(1)}, u32[]{:S(2)}, u32[]{:S(2)}) collective-permute-start(bf16[160,1024]{1,0:T(8,128)(2,1)S(1)} %get-tuple-element.47), channel_id=1, source_target_pairs={{1,0},{0,1},{3,2},{2,3},{5,4},{4,5},{7,6},{6,7},{9,8},{8,9},{11,10... | collective-permute-start | bytes 983048 | tf_op jit(solution)/shard_map/ppermute | solution.py:18
  78.5 22.4 %collective-permute-start.13 = (bf16[192,1024]{1,0:T(8,128)(2,1)S(1)}, bf16[192,1024]{1,0:T(8,128)(2,1)S(1)}, u32[]{:S(2)}, u32[]{:S(2)}) collective-permute-start(bf16[192,1024]{1,0:T(8,128)(2,1)S(1)} %add_convert_fusion.2), channel_id=1, source_target_pairs={{4,0},{8,12},{5,1},{9,13},{6,2},{10,14},{7,3},{11,15},{20,16},{24,... | collective-permute-start | bytes 1179656 | tf_op jit(solution)/shard_map/ppermute | solution.py:219
  79.9 21.0 %collective-permute-start.15 = (bf16[128,1024]{1,0:T(8,128)(2,1)S(1)}, bf16[128,1024]{1,0:T(8,128)(2,1)S(1)}, u32[]{:S(2)}, u32[]{:S(2)}) collective-permute-start(bf16[128,1024]{1,0:T(8,128)(2,1)S(1)} %add_convert_fusion.3), channel_id=1, source_target_pairs={{4,0},{8,12},{5,1},{9,13},{6,2},{10,14},{7,3},{11,15},{20,16},{24,... | collective-permute-start | bytes 786440 | tf_op jit(solution)/shard_map/ppermute | solution.py:219
  (3 other events, 3.0 us)

commit v3 on v1

v3 whole, which is shorter than its diff:
```python
import dataclasses
import functools

import jax
import jax.numpy as jnp
from jax import lax
from jax.experimental import pallas as pl
from jax.experimental.pallas import tpu as pltpu
from jax.sharding import PartitionSpec as P

STEPS = 4
LINE = 4
LABEL_ROWS = 16
VMEM_BYTES = 24 * 1024 * 1024


def from_behind(block, axis, distance):
    devices = range(lax.axis_size(axis))
    route = [((i - distance) % len(devices), i) for i in devices]
    return lax.ppermute(block, axis, route)


def swap_inner(block):
    return from_behind(block, "inner", 1)


def after(value, *earlier):
    return lax.optimization_barrier((value,) + earlier)[0]


def coefficients(spectra, glycans, labels, first_target, scale, shift):
    logits = (
        scale
        * lax.dot_general(
            spectra, glycans, (((1,), (1,)), ((), ())), preferred_element_type=jnp.float32
        )
        + shift
    )
    targets = first_target + jnp.arange(glycans.shape[0], dtype=jnp.int32)
    positive = (labels[:, None] == targets[None, :]).astype(jnp.float32)
    return (jax.nn.sigmoid(logits) - positive).astype(jnp.bfloat16)


def around_ring(spectra, glycans, labels, scale, shift):
    rows_here = spectra.shape[0]
    node_rows = rows_here * lax.axis_size("inner")
    loop_count = lax.axis_size("blk")
    position = lax.axis_index("blk")
    core_first = lax.axis_index("sub") * node_rows + lax.axis_index("inner") * rows_here
    lane_rows = lax.axis_size("sub") * node_rows
    node_spectra = jnp.concatenate([spectra, swap_inner(spectra)])
    node_labels = jnp.concatenate([labels, swap_inner(labels)])
    spectrum_total = 0.0
    glycan_total = 0.0
    held = glycans
    for step in range(STEPS):
        if step > 0:
            held = from_behind(held, "blk", 1)
        first_target = (position - step) % loop_count * lane_rows + core_first
        coef = coefficients(node_spectra, held, node_labels, first_target, scale, shift)
        spectrum_total += jnp.dot(coef, held, preferred_element_type=jnp.float32)
        partial_value = scale * lax.dot_general(
            coef, node_spectra, (((0,), (0,)), ((), ())), preferred_element_type=jnp.float32
        )
        if step > 0:
            back = from_behind(partial_value.astype(jnp.bfloat16), "blk", -step)
            partial_value = back.astype(jnp.float32)
        glycan_total += partial_value
    other = swap_inner((scale * spectrum_total[rows_here:]).astype(jnp.bfloat16))
    spectrum_total = scale * spectrum_total[:rows_here] + other.astype(jnp.float32)
    return spectrum_total.astype(jnp.bfloat16), glycan_total.astype(jnp.bfloat16)


def pair_body(plan, *refs):
    n_spectra, blocks, with_spectra, has_prior_s, rows = plan
    refs = list(refs)

    def take(count):
        taken = refs[:count]
        del refs[:count]
        return taken

    factors, ints, labels = take(3)
    spectra = take(n_spectra)
    held = take(len(blocks))
    priors = [take(1)[0] if b.has_prior else None for b in blocks]
    prior_s = take(1)[0] if has_prior_s else None
    glycans_out = [take(1)[0] if b.out else None for b in blocks]
    if with_spectra == "final":
        mine_out, other_out, spectra_out = take(3)
    elif with_spectra:
        (spectra_out,) = take(1)

    scale, shift = factors[0], factors[1]
    row_labels = []
    for j in range(n_spectra):
        if spectra[j].shape[0] > rows:
            digits = spectra[j][pl.ds(rows, LABEL_ROWS), pl.ds(0, rows)].astype(jnp.float32)
            label = digits[0:1] * 16384.0 + digits[1:2] * 128.0 + digits[2:3]
            row_labels.append(label.astype(jnp.int32))
        else:
            row_labels.append(labels[:, pl.ds(j * rows, rows)])
    if with_spectra == "final":
        spectra_out[...] = prior_s[...]
    for i, block in enumerate(blocks):

        def work(i=i, block=block):
            where = pl.ds(block.first, block.count)
            glycans = held[i][where]
            total = priors[i][where] if block.has_prior else None
            for j in range(block.first_spectra, n_spectra):
                here = spectra[j][pl.ds(0, rows)]
                logits = scale * lax.dot_general(
                    glycans, here, (((1,), (1,)), ((), ())), preferred_element_type=jnp.float32
                )
                logits = logits + shift
                targets = ints[2 * i] + block.first
                targets = targets + lax.broadcasted_iota(jnp.int32, logits.shape, 0)
                positive = jnp.where(targets == row_labels[j], 1.0, 0.0)
                coef = (jax.nn.sigmoid(logits) - positive).astype(jnp.bfloat16)
                if block.out:
                    part = jnp.dot(coef, here, preferred_element_type=jnp.float32)
                    total = part if total is None else total + part
                if with_spectra:
                    part = lax.dot_general(
                        coef, glycans, (((0,), (0,)), ((), ())), preferred_element_type=jnp.float32
                    )
                    at = pl.ds(j * rows, rows)
                    if i > 0 or block.optional:
                        spectra_out[at] += part
                    elif has_prior_s:
                        spectra_out[at] = prior_s[at] + part
                    else:
                        spectra_out[at] = part
            if block.out == "rounded":
                glycans_out[i][...] = (scale * total).astype(jnp.bfloat16)
            elif block.out:
                glycans_out[i][...] = total

        if block.optional:
            pl.when(ints[2 * i + 1] != 0)(work)
        else:
            work()
    if with_spectra == "final":
        mine_out[...] = scale * spectra_out[pl.ds(0, rows)]
        other_out[...] = (scale * spectra_out[pl.ds(rows, rows)]).astype(jnp.bfloat16)


@dataclasses.dataclass(frozen=True)
class Block:
    first: int
    count: int
    out: str = "total"
    has_prior: bool = False
    optional: bool = False
    first_spectra: int = 0


def in_vmem(array):
    return pltpu.with_memory_space_constraint(array, pltpu.VMEM)


def vmem_out(shape, kind):
    return pltpu.VMEM(shape, kind)


def pair_work(factors, spectra, labels, blocks, rows, with_spectra=False, prior_s=None):
    width = spectra[0].shape[1]
    all_rows = rows * len(spectra)
    ints = []
    for _, _, first_target, active, _ in blocks:
        ints += [jnp.int32(first_target), jnp.int32(active)]
    shapes = tuple(b[0] for b in blocks)
    plan = (len(spectra), shapes, with_spectra, prior_s is not None, rows)
    vmem = pl.BlockSpec(memory_space=pltpu.VMEM)
    smem = pl.BlockSpec(memory_space=pltpu.SMEM)
    arrays = list(spectra) + [b[1] for b in blocks]
    arrays += [b[4] for b in blocks if b[0].has_prior]
    if prior_s is not None:
        arrays.append(prior_s)
    outs = []
    for shape in shapes:
        if shape.out:
            kind = jnp.bfloat16 if shape.out == "rounded" else jnp.float32
            outs.append(vmem_out((shape.count, width), kind))
    scratch = []
    if with_spectra == "final":
        outs.append(vmem_out((rows, width), jnp.float32))
        outs.append(vmem_out((rows, width), jnp.bfloat16))
        scratch.append(pltpu.VMEM((all_rows, width), jnp.float32))
    elif with_spectra:
        outs.append(vmem_out((all_rows, width), jnp.float32))
    return pl.pallas_call(
        functools.partial(pair_body, plan),
        out_shape=outs,
        in_specs=[smem, smem] + [vmem] * (len(arrays) + 1),
        out_specs=[vmem] * len(outs),
        scratch_shapes=scratch,
        cost_estimate=pl.CostEstimate(flops=1024, bytes_accessed=1024, transcendentals=0),
        compiler_params=pltpu.CompilerParams(vmem_limit_bytes=VMEM_BYTES),
    )(factors, jnp.stack(ints), labels, *[in_vmem(a) for a in arrays])


def code_labels(labels, row_count, width):
    digits = jnp.stack([labels // 16384, labels // 128 % 128, labels % 128])
    spare = ((0, row_count - 3), (0, width - labels.shape[0]))
    return jnp.pad(digits.astype(jnp.bfloat16), spare)


def choose_body(flag, if_true, if_false, tail, out):
    rows = if_true.shape[0]

    @pl.when(flag[0] != 0)
    def _():
        out[pl.ds(0, rows)] = if_true[...]

    @pl.when(flag[0] == 0)
    def _():
        out[pl.ds(0, rows)] = if_false[...]

    out[pl.ds(rows, tail.shape[0])] = tail[...]


def choose(flag, if_true, if_false, tail):
    rows, width = if_true.shape
    vmem = pl.BlockSpec(memory_space=pltpu.VMEM)
    return pl.pallas_call(
        choose_body,
        out_shape=vmem_out((rows + tail.shape[0], width), if_true.dtype),
        in_specs=[pl.BlockSpec(memory_space=pltpu.SMEM)] + [vmem] * 3,
        out_specs=vmem,
        cost_estimate=pl.CostEstimate(flops=1024, bytes_accessed=1024, transcendentals=0),
        compiler_params=pltpu.CompilerParams(vmem_limit_bytes=VMEM_BYTES),
    )(jnp.int32(flag).reshape(1), in_vmem(if_true), in_vmem(if_false), in_vmem(tail))


def finish_body(flag, factors, mine_s, here_g, across_back, inside_a, inside_b, *rest):
    others, (spectra_out, glycans_out) = rest[:-2], rest[-2:]
    half = inside_a.shape[0]
    at = 0
    for other in others:
        where = pl.ds(at, other.shape[0])
        spectra_out[where] = (mine_s[where] + other[...].astype(jnp.float32)).astype(jnp.bfloat16)
        at += other.shape[0]

    @pl.when(flag[0] != 0)
    def _():
        glycans_out[pl.ds(0, half)] = inside_a[...]
        glycans_out[pl.ds(half, half)] = inside_b[...]

    @pl.when(flag[0] == 0)
    def _():
        total = factors[0] * here_g[...] + across_back[...].astype(jnp.float32)
        glycans_out[...] = total.astype(jnp.bfloat16)


def finish(flag, factors, mine_s, here_g, across_back, inside_a, inside_b, others):
    vmem = pl.BlockSpec(memory_space=pltpu.VMEM)
    smem = pl.BlockSpec(memory_space=pltpu.SMEM)
    arrays = [mine_s, here_g, across_back, inside_a, inside_b] + others
    out = jax.ShapeDtypeStruct(mine_s.shape, jnp.bfloat16)
    return pl.pallas_call(
        finish_body,
        out_shape=[out, out],
        in_specs=[smem, smem] + [vmem] * len(arrays),
        out_specs=[vmem, vmem],
        cost_estimate=pl.CostEstimate(flops=1024, bytes_accessed=1024, transcendentals=0),
        compiler_params=pltpu.CompilerParams(vmem_limit_bytes=VMEM_BYTES),
    )(jnp.int32(flag).reshape(1), factors, *[in_vmem(a) for a in arrays])


def along_line(spectra, glycans, labels, scale, shift):
    rows, width = spectra.shape
    half = rows // 2
    node_rows = rows * lax.axis_size("inner")
    position = lax.axis_index("blk")
    outer = (position == 0) | (position == LINE - 1)
    core_first = lax.axis_index("sub") * node_rows + lax.axis_index("inner") * rows
    lane_rows = lax.axis_size("sub") * node_rows
    factors = jnp.stack([scale, shift])

    def permute(block, pairs):
        return lax.ppermute(block, "blk", pairs)

    def first_of(block_position):
        return block_position * lane_rows + core_first

    sides = [(0, 1), (1, 0), (2, 3), (3, 2)]
    middle = [(1, 2), (2, 1)]
    outward = [(1, 0), (2, 3)]
    here_at = first_of(position)
    side_at = first_of(position ^ 1)
    across_at = first_of(LINE - 1 - position)
    far_at = first_of((LINE - 1 - position) ^ 1)
    whole = Block(0, rows)
    more = Block(0, rows, has_prior=True)

    side = permute(glycans, sides)
    across = permute(glycans, middle)
    partner = swap_inner(spectra)
    own_labels = labels.reshape(1, rows)
    node_labels = jnp.concatenate([own_labels, swap_inner(own_labels)], axis=1)
    node = [spectra, partner]
    here_g, own_s = pair_work(
        factors, node, node_labels, [(whole, glycans, here_at, 1, None)], rows, with_spectra=True
    )

    coded = code_labels(labels, LABEL_ROWS, width)
    side, across = lax.optimization_barrier((side, across, here_g))[:2]
    far = permute(side, middle)
    mixed = permute(choose(outer, spectra, across, coded), sides)
    side_g, across_g, own_s = pair_work(
        factors,
        node,
        node_labels,
        [(whole, side, side_at, 1, None), (whole, across, across_at, 1, None)],
        rows,
        with_spectra=True,
        prior_s=own_s,
    )

    mixed, far = lax.optimization_barrier((mixed, far, own_s))[:2]
    mixed_other = swap_inner(mixed)
    last_out = permute(far, outward)
    (far_g,) = pair_work(
        factors,
        node + [mixed],
        node_labels,
        [(whole, far, far_at, 1, None)],
        rows,
    )
    (far_a,) = pair_work(
        factors,
        [mixed_other],
        node_labels,
        [(Block(0, half, "rounded", True), far, far_at, 1, far_g)],
        rows,
    )
    back_a = permute(far_a, middle)
    far_b, across_out, side_g, here_g = pair_work(
        factors,
        [mixed, mixed_other],
        node_labels,
        [
            (Block(half, rows - half, "rounded", True, False, 1), far, far_at, 1, far_g),
            (Block(0, rows, "rounded", True), across, across_at, 1, across_g),
            (more, after(side, far_a), side_at, 1, side_g),
            (more, glycans, here_at, 1, here_g),
        ],
        rows,
    )
    back_b = permute(far_b, middle)
    total_a = (scale * side_g[:half] + back_a.astype(jnp.float32)).astype(jnp.bfloat16)
    inside_a = permute(total_a, outward)
    across_back = permute(after(across_out, total_a), middle)
    back_b = after(back_b, total_a)
    total_b = (scale * side_g[half:] + back_b.astype(jnp.float32)).astype(jnp.bfloat16)
    inside_b = permute(total_b, outward)

    only_s = Block(0, rows, "", False, True)
    mine_s, other_s = pair_work(
        factors,
        node,
        node_labels,
        [
            (only_s, after(far, total_b), far_at, ~outer, None),
            (only_s, mixed, far_at, outer, None),
            (only_s, last_out, across_at, outer, None),
        ],
        rows,
        with_spectra="final",
        prior_s=own_s,
    )
    piece = -(-rows // 48) * 16
    others = [swap_inner(other_s[at : at + piece]) for at in range(0, rows, piece)]
    return finish(outer, factors, mine_s, here_g, across_back, inside_a, inside_b, others)


def local(
    mass_profile_vectors,
    sugar_tree_vectors,
    matching_glycan_rows,
    sharpness_factor,
    offset_shift_term,
):
    work = along_line if lax.axis_size("blk") == STEPS == LINE else around_ring
    return work(
        mass_profile_vectors,
        sugar_tree_vectors,
        matching_glycan_rows,
        sharpness_factor[0],
        offset_shift_term[0],
    )


def solution(mesh):
    placed = (
        P(("groups", "blk", "sub", "inner"), None),
        P(("groups", "blk", "sub", "inner"), None),
        P(("groups", "blk", "sub", "inner")),
        P(),
        P(),
    )
    return jax.shard_map(
        local,
        mesh=mesh,
        in_specs=placed,
        out_specs=(
            P(("groups", "blk", "sub", "inner"), None),
            P(("groups", "blk", "sub", "inner"), None),
        ),
        check_vma=False,
    )
```

time: 133 us -> 101 us (0.76)
  the two profiles are of different devices: /device:TPU:0 before, /device:TPU:12 now
where the time goes in v3:
time: 101 us; the launch traced here: 99.9 us
  Pallas kernels  27.6 us (27%)
  starting transfers between devices  23.2 us (23%)
  local copies, waits for them, and re-layouts  22.3 us (22%)
  waiting for transfers between devices  20.7 us (20%)
  other arithmetic  3.8 us (4%)
  between operations  2.22 us (2%)
    pallas_call x6, Pallas kernels, pair_work(): pl.pallas_call(functools.partial(pair_body, plan), out_shape=outs, in_spe...  24.7 us
    ppermute x10, starting transfers between devices, permute(): return lax.ppermute(block, 'blk', pairs)  21.9 us
    unnamed x46, local copies, waits for them, and re-layouts  21.4 us
    ppermute x10, waiting for transfers between devices, permute(): return lax.ppermute(block, 'blk', pairs)  18.5 us
    ppermute x6, waiting for transfers between devices, from_behind(): return lax.ppermute(block, axis, route)  2.19 us
  transfers between devices with their start and end apart: 16, of which 8 were waited for; matrix products, arithmetic and copies ran while one was open for 5% of the time, Pallas kernels for 22%

profile of v3, /device:TPU:12, one launch (start us, length us, event | category | flops | bytes accessed | tf_op | source)
XLA Modules:
  0.0 99.9 jit_solution(9013149744366289010)
XLA Ops:
  1.1 4.6 %collective-permute-start.3 = (bf16[320,1024]{1,0:T(8,128)(2,1)}, bf16[320,1024]{1,0:T(8,128)(2,1)S(1)}, u32[]{:S(2)}, u32[]{:S(2)}) collective-permute-start(bf16[320,1024]{1,0:T(8,128)(2,1)} %refs_8_.1), channel_id=1, source_target_pairs={{4,8},{8,4},{5,9},{9,5},{6,10},{10,6},{7,11},{11,7},{20,24},{24,20... | collective-permute-start | bytes 1966088 | tf_op jit(solution)/shard_map/ppermute | solution.py:283
  9.3 1.1 %copy-done = bf16[320,1024]{1,0:T(8,128)(2,1)S(1)} copy-done((bf16[320,1024]{1,0:T(8,128)(2,1)S(1)}, bf16[320,1024]{1,0:T(8,128)(2,1)}, u32[]{:S(2)}) %copy-start) | copy-done | bytes 655384
  10.3 1.1 %copy-done.8 = bf16[320,1024]{1,0:T(8,128)(2,1)S(1)} copy-done((bf16[320,1024]{1,0:T(8,128)(2,1)S(1)}, bf16[320,1024]{1,0:T(8,128)(2,1)}, u32[]{:S(2)}) %copy-start.8) | copy-done | bytes 655384
  11.4 3.0 %shard_map.68 = (f32[320,1024]{1,0:T(8,128)S(1)}, f32[640,1024]{1,0:T(8,128)S(1)}) custom-call(f32[2]{0:T(128)S(1)} %pad_maximum_fusion.refs_0_.factors, s32[2]{0:T(128)S(1)} %pad_add_fusion.2.refs_1_, s32[1,640]{1,0:T(1,128)S(1)} %pad_add_fusion.refs_2_, bf16[320,1024]{1,0:T(8,128)(2,1)S(1)} %copy-done, ...), custom_call_target="tpu_custom_call" | custom-call | flops 1024 | bytes 1024 | tf_op jit(solution)/shard_map/pallas_call | solution.py:193
  14.5 1.5 %copy-done.6 = f32[640,1024]{1,0:T(8,128)} copy-done((f32[640,1024]{1,0:T(8,128)}, f32[640,1024]{1,0:T(8,128)S(1)}, u32[]{:S(2)}) %copy-start.6) | copy-done | bytes 2621464
  17.4 3.0 %collective-permute-done.3.if_false.refs_6_ = bf16[320,1024]{1,0:T(8,128)(2,1)S(1)} collective-permute-done((bf16[320,1024]{1,0:T(8,128)(2,1)}, bf16[320,1024]{1,0:T(8,128)(2,1)S(1)}, u32[]{:S(2)}, u32[]{:S(2)}) %collective-permute-start.3) | collective-permute-done | bytes 655392 | tf_op jit(solution)/shard_map/ppermute | solution.py:283
  21.4 3.6 %collective-permute-start.5 = (bf16[320,1024]{1,0:T(8,128)(2,1)}, bf16[320,1024]{1,0:T(8,128)(2,1)S(1)}, u32[]{:S(2)}, u32[]{:S(2)}) collective-permute-start(bf16[320,1024]{1,0:T(8,128)(2,1)} %copy-done.10), channel_id=1, source_target_pairs={{4,8},{8,4},{5,9},{9,5},{6,10},{10,6},{7,11},{11,7},{20,24},{24,20... | collective-permute-start | bytes 1966088 | tf_op jit(solution)/shard_map/ppermute | solution.py:283
  25.2 1.7 %copy-done.7 = f32[640,1024]{1,0:T(8,128)S(1)} copy-done((f32[640,1024]{1,0:T(8,128)S(1)}, f32[640,1024]{1,0:T(8,128)}, u32[]{:S(2)}) %copy-start.7) | copy-done | bytes 2621464
  28.0 5.3 %shard_map.70 = (f32[320,1024]{1,0:T(8,128)S(1)}, f32[320,1024]{1,0:T(8,128)S(1)}, f32[640,1024]{1,0:T(8,128)S(1)}) custom-call(f32[2]{0:T(128)S(1)} %pad_maximum_fusion.refs_0_.factors, s32[4]{0:T(128)S(1)} %pad_add_fusion.3.refs_1_, s32[1,640]{1,0:T(1,128)S(1)} %pad_add_fusion.refs_2_, bf16[320,1024]{1,0:T(8,128)(2,1)S(1)} %copy-done.1, ...), custom_call_target="tpu_custom_call" | custom-call | flops 1024 | bytes 1024 | tf_op jit(solution)/shard_map/pallas_call | solution.py:193
  33.4 1.5 %copy-done.4 = f32[640,1024]{1,0:T(8,128)} copy-done((f32[640,1024]{1,0:T(8,128)}, f32[640,1024]{1,0:T(8,128)S(1)}, u32[]{:S(2)}) %copy-start.4) | copy-done | bytes 2621464
  34.8 1.1 %copy-done.18 = f32[320,1024]{1,0:T(8,128)} copy-done((f32[320,1024]{1,0:T(8,128)}, f32[320,1024]{1,0:T(8,128)S(1)}, u32[]{:S(2)}) %copy-start.18) | copy-done | bytes 1310744
  37.0 2.1 %collective-permute-done.5.refs_6_.refs_4_.refs_5_ = bf16[320,1024]{1,0:T(8,128)(2,1)S(1)} collective-permute-done((bf16[320,1024]{1,0:T(8,128)(2,1)}, bf16[320,1024]{1,0:T(8,128)(2,1)S(1)}, u32[]{:S(2)}, u32[]{:S(2)}) %collective-permute-start.5) | collective-permute-done | bytes 655392 | tf_op jit(solution)/shard_map/ppermute | solution.py:283
  39.2 3.4 %shard_map.71.refs_5_.refs_9_ = f32[320,1024]{1,0:T(8,128)S(1)} custom-call(f32[2]{0:T(128)S(1)} %pad_maximum_fusion.refs_0_.factors, s32[2]{0:T(128)S(1)} %pad_add_fusion.1.refs_1_, s32[1,640]{1,0:T(1,128)S(1)} %pad_add_fusion.refs_2_, bf16[320,1024]{1,0:T(8,128)(2,1)S(1)} %copy-done.1, bf16[320,1024]{1,0:T(8,128)(2,1)S(1)} %collective-permute-done.1.refs_4_, ...), custom_call_target="tpu_custom_call" | custom-call | flops 1024 | bytes 1024 | tf_op jit(solution)/shard_map/pallas_call | solution.py:193
  42.7 2.7 %shard_map.72 = bf16[160,1024]{1,0:T(8,128)(2,1)} custom-call(f32[2]{0:T(128)S(1)} %pad_maximum_fusion.refs_0_.factors, s32[2]{0:T(128)S(1)} %pad_add_fusion.1.refs_1_, s32[1,640]{1,0:T(1,128)S(1)} %pad_add_fusion.refs_2_, bf16[336,1024]{1,0:T(8,128)(2,1)} %collective-permute-done.6.refs_3_.refs_4_, ...), custom_call_target="tpu_custom_call" | custom-call | flops 1024 | bytes 1024 | tf_op jit(solution)/shard_map/pallas_call | solution.py:193
  45.3 3.3 %collective-permute-start.8 = (bf16[160,1024]{1,0:T(8,128)(2,1)}, bf16[160,1024]{1,0:T(8,128)(2,1)}, u32[]{:S(2)}, u32[]{:S(2)}) collective-permute-start(bf16[160,1024]{1,0:T(8,128)(2,1)} %shard_map.72), channel_id=1, source_target_pairs={{4,8},{8,4},{5,9},{9,5},{6,10},{10,6},{7,11},{11,7},{20,24},{24,20... | collective-permute-start | bytes 983048 | tf_op jit(solution)/shard_map/ppermute | solution.py:283
  48.6 2.2 %collective-permute-start.9 = (bf16[320,1024]{1,0:T(8,128)(2,1)S(1)}, bf16[320,1024]{1,0:T(8,128)(2,1)}, u32[]{:S(2)}, u32[]{:S(2)}) collective-permute-start(bf16[320,1024]{1,0:T(8,128)(2,1)S(1)} %collective-permute-done.5.refs_6_.refs_4_.refs_5_), channel_id=1, source_target_pairs={{4,0},{8,12},{5,1},{9,13},{6,2},{10,14},{7,3},{11,15},{20,16},{24,... | collective-permute-start | bytes 1966088 | tf_op jit(solution)/shard_map/ppermute | solution.py:283
  50.9 1.1 %copy-done.3 = bf16[320,1024]{1,0:T(8,128)(2,1)S(1)} copy-done((bf16[320,1024]{1,0:T(8,128)(2,1)S(1)}, bf16[320,1024]{1,0:T(8,128)(2,1)}, u32[]{:S(2)}) %copy-start.3) | copy-done | bytes 655384
  54.2 1.3 %copy-done.17 = f32[320,1024]{1,0:T(8,128)S(1)} copy-done((f32[320,1024]{1,0:T(8,128)S(1)}, f32[320,1024]{1,0:T(8,128)}, u32[]{:S(2)}) %copy-start.17) | copy-done | bytes 1310744
  55.5 1.3 %copy-done.19 = f32[320,1024]{1,0:T(8,128)S(1)} copy-done((f32[320,1024]{1,0:T(8,128)S(1)}, f32[320,1024]{1,0:T(8,128)}, u32[]{:S(2)}) %copy-start.19) | copy-done | bytes 1310744
  56.8 1.3 %copy-done.21 = f32[320,1024]{1,0:T(8,128)S(1)} copy-done((f32[320,1024]{1,0:T(8,128)S(1)}, f32[320,1024]{1,0:T(8,128)}, u32[]{:S(2)}) %copy-start.21) | copy-done | bytes 1310744
  58.2 6.6 %shard_map.73 = (bf16[160,1024]{1,0:T(8,128)(2,1)}, bf16[320,1024]{1,0:T(8,128)(2,1)S(1)}, f32[320,1024]{1,0:T(8,128)S(1)}, f32[320,1024]{1,0:T(8,128)S(1)}) custom-call(f32[2]{0:T(128)S(1)} %pad_maximum_fusion.refs_0_.factors, s32[8]{0:T(128)S(1)} %stack.77.refs_1_, s32[1,640]{1,0:T(1,128)S(1)} %pad_add_fusion.refs_2_, ...), custom_call_target="tpu_custom_call" | custom-call | flops 1024 | bytes 1024 | tf_op jit(solution)/shard_map/pallas_call | solution.py:193
  67.8 2.5 %collective-permute-start.7 = (bf16[160,1024]{1,0:T(8,128)(2,1)}, bf16[160,1024]{1,0:T(8,128)(2,1)}, u32[]{:S(2)}, u32[]{:S(2)}) collective-permute-start(bf16[160,1024]{1,0:T(8,128)(2,1)} %get-tuple-element.32), channel_id=1, source_target_pairs={{4,8},{8,4},{5,9},{9,5},{6,10},{10,6},{7,11},{11,7},{20,24},{24,20... | collective-permute-start | bytes 983048 | tf_op jit(solution)/shard_map/ppermute | solution.py:283
  70.4 1.4 %add_convert_fusion.1 = bf16[160,1024]{1,0:T(8,128)(2,1)S(1)} fusion(bf16[160,1024]{1,0:T(8,128)(2,1)} %collective-permute-done.8, f32[320,1024]{1,0:T(8,128)} %copy-done.15, f32[]{:T(128)} %bitcast.8), kind=kLoop, calls=%fused_computation.1 | loop fusion | flops 655360 | bytes 1310724 | tf_op jit(solution)/shard_map/convert_element_type | solution.py:353
  71.8 1.3 %collective-permute-start.11 = (bf16[160,1024]{1,0:T(8,128)(2,1)S(1)}, bf16[160,1024]{1,0:T(8,128)(2,1)S(1)}, u32[]{:S(2)}, u32[]{:S(2)}) collective-permute-start(bf16[160,1024]{1,0:T(8,128)(2,1)S(1)} %add_convert_fusion.1), channel_id=1, source_target_pairs={{4,0},{8,12},{5,1},{9,13},{6,2},{10,14},{7,3},{11,15},{20,16},{24,... | collective-permute-start | bytes 983048 | tf_op jit(solution)/shard_map/ppermute | solution.py:283
  73.1 6.7 %collective-permute-done.7 = bf16[160,1024]{1,0:T(8,128)(2,1)} collective-permute-done((bf16[160,1024]{1,0:T(8,128)(2,1)}, bf16[160,1024]{1,0:T(8,128)(2,1)}, u32[]{:S(2)}, u32[]{:S(2)}) %collective-permute-start.7) | collective-permute-done | bytes 327712 | tf_op jit(solution)/shard_map/ppermute | solution.py:283
  79.8 2.5 %collective-permute-start.10 = (bf16[320,1024]{1,0:T(8,128)(2,1)}, bf16[320,1024]{1,0:T(8,128)(2,1)S(1)}, u32[]{:S(2)}, u32[]{:S(2)}) collective-permute-start(bf16[320,1024]{1,0:T(8,128)(2,1)} %copy-done.22), channel_id=1, source_target_pairs={{4,8},{8,4},{5,9},{9,5},{6,10},{10,6},{7,11},{11,7},{20,24},{24,20... | collective-permute-start | bytes 1966088 | tf_op jit(solution)/shard_map/ppermute | solution.py:283
  82.3 1.3 %add_convert_fusion = bf16[160,1024]{1,0:T(8,128)(2,1)S(1)} fusion(bf16[160,1024]{1,0:T(8,128)(2,1)} %collective-permute-done.7, f32[320,1024]{1,0:T(8,128)} %copy-done.15, f32[]{:T(128)} %bitcast.7), kind=kLoop, calls=%fused_computation | loop fusion | flops 655360 | bytes 1310724 | tf_op jit(solution)/shard_map/convert_element_type | solution.py:357
  83.6 1.3 %collective-permute-start.12 = (bf16[160,1024]{1,0:T(8,128)(2,1)S(1)}, bf16[160,1024]{1,0:T(8,128)(2,1)S(1)}, u32[]{:S(2)}, u32[]{:S(2)}) collective-permute-start(bf16[160,1024]{1,0:T(8,128)(2,1)S(1)} %add_convert_fusion), channel_id=1, source_target_pairs={{4,0},{8,12},{5,1},{9,13},{6,2},{10,14},{7,3},{11,15},{20,16},{24,... | collective-permute-start | bytes 983048 | tf_op jit(solution)/shard_map/ppermute | solution.py:283
  84.9 3.6 %shard_map.74 = (f32[320,1024]{1,0:T(8,128)S(1)}, bf16[320,1024]{1,0:T(8,128)(2,1)S(1)}) custom-call(f32[2]{0:T(128)S(1)} %pad_maximum_fusion.refs_0_.factors, s32[6]{0:T(128)S(1)} %stack.68.refs_1_, s32[1,640]{1,0:T(1,128)S(1)} %pad_add_fusion.refs_2_, bf16[320,1024]{1,0:T(8,128)(2,1)S(1)} %copy-done.1, ...), custom_call_target="tpu_custom_call" | custom-call | flops 1024 | bytes 1024 | tf_op jit(solution)/shard_map/pallas_call | solution.py:193
  90.4 1.2 %collective-permute-done.14.rest_1_ = bf16[112,1024]{1,0:T(8,128)(2,1)S(1)} collective-permute-done((bf16[112,1024]{1,0:T(8,128)(2,1)S(1)}, bf16[112,1024]{1,0:T(8,128)(2,1)S(1)}, u32[]{:S(2)}, u32[]{:S(2)}) %collective-permute-start.14) | collective-permute-done | bytes 229408 | tf_op jit(solution)/shard_map/ppermute | solution.py:20
  91.6 6.3 %collective-permute-done.10.across_back = bf16[320,1024]{1,0:T(8,128)(2,1)S(1)} collective-permute-done((bf16[320,1024]{1,0:T(8,128)(2,1)}, bf16[320,1024]{1,0:T(8,128)(2,1)S(1)}, u32[]{:S(2)}, u32[]{:S(2)}) %collective-permute-start.10) | collective-permute-done | bytes 655392 | tf_op jit(solution)/shard_map/ppermute | solution.py:283
  98.0 1.9 %shard_map.75 = (bf16[320,1024]{1,0:T(8,128)(2,1)}, bf16[320,1024]{1,0:T(8,128)(2,1)}) custom-call(s32[1]{0:T(128)} %bitcast.flag, f32[2]{0:T(128)S(1)} %pad_maximum_fusion.refs_0_.factors, f32[320,1024]{1,0:T(8,128)S(1)} %get-tuple-element.35.mine_s, f32[320,1024]{1,0:T(8,128)S(1)} %copy-done.14, bf16[320,1024]{1,0:T(8,128)(2,1)S(1)} %collective-permute-done.10.across_back, ...), custom_call_target="tpu_custom_call" | custom-call | flops 1024 | bytes 1024 | tf_op jit(solution)/shard_map/pallas_call | solution.py:262
  (71 shorter events, 14.7 us)
Async XLA Ops:
  0.6 16.7 %collective-permute-start.2 = (bf16[320,1024]{1,0:T(8,128)(2,1)}, bf16[320,1024]{1,0:T(8,128)(2,1)S(1)}, u32[]{:S(2)}, u32[]{:S(2)}) collective-permute-start(bf16[320,1024]{1,0:T(8,128)(2,1)} %refs_8_.1), channel_id=1, source_target_pairs={{0,4},{4,0},{8,12},{12,8},{1,5},{5,1},{9,13},{13,9},{2,6},{6,2},{1... | collective-permute-start | bytes 1966088 | tf_op jit(solution)/shard_map/ppermute | solution.py:283
  1.1 19.3 %collective-permute-start.3 = (bf16[320,1024]{1,0:T(8,128)(2,1)}, bf16[320,1024]{1,0:T(8,128)(2,1)S(1)}, u32[]{:S(2)}, u32[]{:S(2)}) collective-permute-start(bf16[320,1024]{1,0:T(8,128)(2,1)} %refs_8_.1), channel_id=1, source_target_pairs={{4,8},{8,4},{5,9},{9,5},{6,10},{10,6},{7,11},{11,7},{20,24},{24,20... | collective-permute-start | bytes 1966088 | tf_op jit(solution)/shard_map/ppermute | solution.py:283
  6.4 2.7 %collective-permute-start = (s32[1,320]{1,0:T(1,128)S(1)}, s32[1,320]{1,0:T(1,128)S(1)}, u32[]{:S(2)}, u32[]{:S(2)}) collective-permute-start(s32[1,320]{1,0:T(1,128)S(1)} %reshape.15), channel_id=1, source_target_pairs={{1,0},{0,1},{3,2},{2,3},{5,4},{4,5},{7,6},{6,7},{9,8},{8,9},{11,10... | collective-permute-start | bytes 3848 | tf_op jit(solution)/shard_map/ppermute | solution.py:20
  6.4 2.8 %collective-permute-start.1 = (bf16[320,1024]{1,0:T(8,128)(2,1)}, bf16[320,1024]{1,0:T(8,128)(2,1)S(1)}, u32[]{:S(2)}, u32[]{:S(2)}) collective-permute-start(bf16[320,1024]{1,0:T(8,128)(2,1)} %refs_3_.7), channel_id=1, source_target_pairs={{1,0},{0,1},{3,2},{2,3},{5,4},{4,5},{7,6},{6,7},{9,8},{8,9},{11,10... | collective-permute-start | bytes 1966088 | tf_op jit(solution)/shard_map/ppermute | solution.py:20
  9.3 1.1 %copy-start = (bf16[320,1024]{1,0:T(8,128)(2,1)S(1)}, bf16[320,1024]{1,0:T(8,128)(2,1)}, u32[]{:S(2)}) copy-start(bf16[320,1024]{1,0:T(8,128)(2,1)} %refs_3_.7) | copy-start | bytes 1966084
  10.3 1.1 %copy-start.8 = (bf16[320,1024]{1,0:T(8,128)(2,1)S(1)}, bf16[320,1024]{1,0:T(8,128)(2,1)}, u32[]{:S(2)}) copy-start(bf16[320,1024]{1,0:T(8,128)(2,1)} %refs_8_.1) | copy-start | bytes 1966084
  11.4 9.0 %copy-start.1 = (bf16[320,1024]{1,0:T(8,128)(2,1)S(1)}, bf16[320,1024]{1,0:T(8,128)(2,1)}, u32[]{:S(2)}) copy-start(bf16[320,1024]{1,0:T(8,128)(2,1)} %refs_3_.7) | copy-start | bytes 1966084
  14.5 1.5 %copy-start.6 = (f32[640,1024]{1,0:T(8,128)}, f32[640,1024]{1,0:T(8,128)S(1)}, u32[]{:S(2)}) copy-start(f32[640,1024]{1,0:T(8,128)S(1)} %get-tuple-element.24.refs_7_) | copy-start | bytes 7864324
  17.4 4.1 %copy-start.10 = (bf16[320,1024]{1,0:T(8,128)(2,1)}, bf16[320,1024]{1,0:T(8,128)(2,1)S(1)}, u32[]{:S(2)}) copy-start(bf16[320,1024]{1,0:T(8,128)(2,1)S(1)} %collective-permute-done.2.refs_5_.refs_7_) | copy-start | bytes 1966084
  20.4 12.9 %copy-start.2 = (bf16[320,1024]{1,0:T(8,128)(2,1)}, bf16[320,1024]{1,0:T(8,128)(2,1)S(1)}, u32[]{:S(2)}) copy-start(bf16[320,1024]{1,0:T(8,128)(2,1)S(1)} %collective-permute-done.3.if_false.refs_6_) | copy-start | bytes 1966084
  21.4 17.7 %collective-permute-start.4 = (bf16[336,1024]{1,0:T(8,128)(2,1)}, bf16[336,1024]{1,0:T(8,128)(2,1)}, u32[]{:S(2)}, u32[]{:S(2)}) collective-permute-start(bf16[336,1024]{1,0:T(8,128)(2,1)} %shard_map.69), channel_id=1, source_target_pairs={{0,4},{4,0},{8,12},{12,8},{1,5},{5,1},{9,13},{13,9},{2,6},{6,2},{1... | collective-permute-start | bytes 2064392 | tf_op jit(solution)/shard_map/ppermute | solution.py:283
  21.4 17.7 %collective-permute-start.5 = (bf16[320,1024]{1,0:T(8,128)(2,1)}, bf16[320,1024]{1,0:T(8,128)(2,1)S(1)}, u32[]{:S(2)}, u32[]{:S(2)}) collective-permute-start(bf16[320,1024]{1,0:T(8,128)(2,1)} %copy-done.10), channel_id=1, source_target_pairs={{4,8},{8,4},{5,9},{9,5},{6,10},{10,6},{7,11},{11,7},{20,24},{24,20... | collective-permute-start | bytes 1966088 | tf_op jit(solution)/shard_map/ppermute | solution.py:283
  25.2 1.7 %copy-start.7 = (f32[640,1024]{1,0:T(8,128)S(1)}, f32[640,1024]{1,0:T(8,128)}, u32[]{:S(2)}) copy-start(f32[640,1024]{1,0:T(8,128)} %copy-done.6) | copy-start | bytes 7864324
  33.4 1.5 %copy-start.4 = (f32[640,1024]{1,0:T(8,128)}, f32[640,1024]{1,0:T(8,128)S(1)}, u32[]{:S(2)}) copy-start(f32[640,1024]{1,0:T(8,128)S(1)} %get-tuple-element.25.refs_8_) | copy-start | bytes 7864324
  34.8 1.1 %copy-start.18 = (f32[320,1024]{1,0:T(8,128)}, f32[320,1024]{1,0:T(8,128)S(1)}, u32[]{:S(2)}) copy-start(f32[320,1024]{1,0:T(8,128)S(1)} %get-tuple-element.30.refs_11_) | copy-start | bytes 3932164
  39.1 3.5 %collective-permute-start.6 = (bf16[336,1024]{1,0:T(8,128)(2,1)}, bf16[336,1024]{1,0:T(8,128)(2,1)}, u32[]{:S(2)}, u32[]{:S(2)}) collective-permute-start(bf16[336,1024]{1,0:T(8,128)(2,1)} %collective-permute-done.4.refs_5_.refs_3_.refs_6_), channel_id=1, source_target_pairs={{1,0},{0,1},{3,2},{2,3},{5,4},{4,5},{7,6},{6,7},{9,8},{8,9},{11,10... | collective-permute-start | bytes 2064392 | tf_op jit(solution)/shard_map/ppermute | solution.py:20
  45.3 25.1 %collective-permute-start.8 = (bf16[160,1024]{1,0:T(8,128)(2,1)}, bf16[160,1024]{1,0:T(8,128)(2,1)}, u32[]{:S(2)}, u32[]{:S(2)}) collective-permute-start(bf16[160,1024]{1,0:T(8,128)(2,1)} %shard_map.72), channel_id=1, source_target_pairs={{4,8},{8,4},{5,9},{9,5},{6,10},{10,6},{7,11},{11,7},{20,24},{24,20... | collective-permute-start | bytes 983048 | tf_op jit(solution)/shard_map/ppermute | solution.py:283
  48.6 36.3 %collective-permute-start.9 = (bf16[320,1024]{1,0:T(8,128)(2,1)S(1)}, bf16[320,1024]{1,0:T(8,128)(2,1)}, u32[]{:S(2)}, u32[]{:S(2)}) collective-permute-start(bf16[320,1024]{1,0:T(8,128)(2,1)S(1)} %collective-permute-done.5.refs_6_.refs_4_.refs_5_), channel_id=1, source_target_pairs={{4,0},{8,12},{5,1},{9,13},{6,2},{10,14},{7,3},{11,15},{20,16},{24,... | collective-permute-start | bytes 1966088 | tf_op jit(solution)/shard_map/ppermute | solution.py:283
  50.9 1.1 %copy-start.3 = (bf16[320,1024]{1,0:T(8,128)(2,1)S(1)}, bf16[320,1024]{1,0:T(8,128)(2,1)}, u32[]{:S(2)}) copy-start(bf16[320,1024]{1,0:T(8,128)(2,1)} %copy-done.2) | copy-start | bytes 1966084
  53.1 1.1 %copy-start.12 = (bf16[320,1024]{1,0:T(8,128)(2,1)S(1)}, bf16[320,1024]{1,0:T(8,128)(2,1)}, u32[]{:S(2)}) copy-start(bf16[320,1024]{1,0:T(8,128)(2,1)} %copy-done.10) | copy-start | bytes 1966084
  54.2 1.3 %copy-start.17 = (f32[320,1024]{1,0:T(8,128)S(1)}, f32[320,1024]{1,0:T(8,128)}, u32[]{:S(2)}) copy-start(f32[320,1024]{1,0:T(8,128)} %copy-done.16) | copy-start | bytes 3932164
  55.5 1.3 %copy-start.19 = (f32[320,1024]{1,0:T(8,128)S(1)}, f32[320,1024]{1,0:T(8,128)}, u32[]{:S(2)}) copy-start(f32[320,1024]{1,0:T(8,128)} %copy-done.18) | copy-start | bytes 3932164
  56.8 1.3 %copy-start.21 = (f32[320,1024]{1,0:T(8,128)S(1)}, f32[320,1024]{1,0:T(8,128)}, u32[]{:S(2)}) copy-start(f32[320,1024]{1,0:T(8,128)} %copy-done.20) | copy-start | bytes 3932164
  67.8 12.0 %collective-permute-start.7 = (bf16[160,1024]{1,0:T(8,128)(2,1)}, bf16[160,1024]{1,0:T(8,128)(2,1)}, u32[]{:S(2)}, u32[]{:S(2)}) collective-permute-start(bf16[160,1024]{1,0:T(8,128)(2,1)} %get-tuple-element.32), channel_id=1, source_target_pairs={{4,8},{8,4},{5,9},{9,5},{6,10},{10,6},{7,11},{11,7},{20,24},{24,20... | collective-permute-start | bytes 983048 | tf_op jit(solution)/shard_map/ppermute | solution.py:283
  70.4 14.6 %copy-start.5 = (f32[640,1024]{1,0:T(8,128)S(1)}, f32[640,1024]{1,0:T(8,128)}, u32[]{:S(2)}) copy-start(f32[640,1024]{1,0:T(8,128)} %copy-done.4) | copy-start | bytes 7864324
  71.8 19.8 %collective-permute-start.11 = (bf16[160,1024]{1,0:T(8,128)(2,1)S(1)}, bf16[160,1024]{1,0:T(8,128)(2,1)S(1)}, u32[]{:S(2)}, u32[]{:S(2)}) collective-permute-start(bf16[160,1024]{1,0:T(8,128)(2,1)S(1)} %add_convert_fusion.1), channel_id=1, source_target_pairs={{4,0},{8,12},{5,1},{9,13},{6,2},{10,14},{7,3},{11,15},{20,16},{24,... | collective-permute-start | bytes 983048 | tf_op jit(solution)/shard_map/ppermute | solution.py:283
  79.8 18.1 %collective-permute-start.10 = (bf16[320,1024]{1,0:T(8,128)(2,1)}, bf16[320,1024]{1,0:T(8,128)(2,1)S(1)}, u32[]{:S(2)}, u32[]{:S(2)}) collective-permute-start(bf16[320,1024]{1,0:T(8,128)(2,1)} %copy-done.22), channel_id=1, source_target_pairs={{4,8},{8,4},{5,9},{9,5},{6,10},{10,6},{7,11},{11,7},{20,24},{24,20... | collective-permute-start | bytes 1966088 | tf_op jit(solution)/shard_map/ppermute | solution.py:283
  83.6 8.0 %collective-permute-start.12 = (bf16[160,1024]{1,0:T(8,128)(2,1)S(1)}, bf16[160,1024]{1,0:T(8,128)(2,1)S(1)}, u32[]{:S(2)}, u32[]{:S(2)}) collective-permute-start(bf16[160,1024]{1,0:T(8,128)(2,1)S(1)} %add_convert_fusion), channel_id=1, source_target_pairs={{4,0},{8,12},{5,1},{9,13},{6,2},{10,14},{7,3},{11,15},{20,16},{24,... | collective-permute-start | bytes 983048 | tf_op jit(solution)/shard_map/ppermute | solution.py:283
  88.6 9.4 %copy-start.14 = (f32[320,1024]{1,0:T(8,128)S(1)}, f32[320,1024]{1,0:T(8,128)}, u32[]{:S(2)}) copy-start(f32[320,1024]{1,0:T(8,128)} %copy-done.13) | copy-start | bytes 3932164
  88.6 1.5 %collective-permute-start.15 = (bf16[96,1024]{1,0:T(8,128)(2,1)S(1)}, bf16[96,1024]{1,0:T(8,128)(2,1)S(1)}, u32[]{:S(2)}, u32[]{:S(2)}) collective-permute-start(bf16[96,1024]{1,0:T(8,128)(2,1)S(1)} %slice.19), channel_id=1, source_target_pairs={{1,0},{0,1},{3,2},{2,3},{5,4},{4,5},{7,6},{6,7},{9,8},{8,9},{11,10... | collective-permute-start | bytes 589832 | tf_op jit(solution)/shard_map/ppermute | solution.py:20
  88.7 1.7 %collective-permute-start.13 = (bf16[112,1024]{1,0:T(8,128)(2,1)S(1)}, bf16[112,1024]{1,0:T(8,128)(2,1)S(1)}, u32[]{:S(2)}, u32[]{:S(2)}) collective-permute-start(bf16[112,1024]{1,0:T(8,128)(2,1)S(1)} %get-tuple-element.41), channel_id=1, source_target_pairs={{1,0},{0,1},{3,2},{2,3},{5,4},{4,5},{7,6},{6,7},{9,8},{8,9},{11,10... | collective-permute-start | bytes 688136 | tf_op jit(solution)/shard_map/ppermute | solution.py:20
  90.1 1.5 %collective-permute-start.14 = (bf16[112,1024]{1,0:T(8,128)(2,1)S(1)}, bf16[112,1024]{1,0:T(8,128)(2,1)S(1)}, u32[]{:S(2)}, u32[]{:S(2)}) collective-permute-start(bf16[112,1024]{1,0:T(8,128)(2,1)S(1)} %get-tuple-element.40), channel_id=1, source_target_pairs={{1,0},{0,1},{3,2},{2,3},{5,4},{4,5},{7,6},{6,7},{9,8},{8,9},{11,10... | collective-permute-start | bytes 688136 | tf_op jit(solution)/shard_map/ppermute | solution.py:20
  (7 other events, 7.3 us)

commit v4 on v3

v4 whole, which is shorter than its diff:
```python
import dataclasses
import functools

import jax
import jax.numpy as jnp
from jax import lax
from jax.experimental import pallas as pl
from jax.experimental.pallas import tpu as pltpu
from jax.sharding import PartitionSpec as P

STEPS = 4
LINE = 4
LABEL_ROWS = 16
KEEP_ROW = 6
VMEM_BYTES = 20 * 1024 * 1024


def from_behind(block, axis, distance):
    devices = range(lax.axis_size(axis))
    route = [((i - distance) % len(devices), i) for i in devices]
    return lax.ppermute(block, axis, route)


def swap_inner(block):
    return from_behind(block, "inner", 1)


def after(value, *earlier):
    return lax.optimization_barrier((value,) + earlier)[0]


def coefficients(spectra, glycans, labels, first_target, scale, shift):
    logits = (
        scale
        * lax.dot_general(
            spectra, glycans, (((1,), (1,)), ((), ())), preferred_element_type=jnp.float32
        )
        + shift
    )
    targets = first_target + jnp.arange(glycans.shape[0], dtype=jnp.int32)
    positive = (labels[:, None] == targets[None, :]).astype(jnp.float32)
    return (jax.nn.sigmoid(logits) - positive).astype(jnp.bfloat16)


def around_ring(spectra, glycans, labels, scale, shift):
    rows_here = spectra.shape[0]
    node_rows = rows_here * lax.axis_size("inner")
    loop_count = lax.axis_size("blk")
    position = lax.axis_index("blk")
    core_first = lax.axis_index("sub") * node_rows + lax.axis_index("inner") * rows_here
    lane_rows = lax.axis_size("sub") * node_rows
    node_spectra = jnp.concatenate([spectra, swap_inner(spectra)])
    node_labels = jnp.concatenate([labels, swap_inner(labels)])
    spectrum_total = 0.0
    glycan_total = 0.0
    held = glycans
    for step in range(STEPS):
        if step > 0:
            held = from_behind(held, "blk", 1)
        first_target = (position - step) % loop_count * lane_rows + core_first
        coef = coefficients(node_spectra, held, node_labels, first_target, scale, shift)
        spectrum_total += jnp.dot(coef, held, preferred_element_type=jnp.float32)
        partial_value = scale * lax.dot_general(
            coef, node_spectra, (((0,), (0,)), ((), ())), preferred_element_type=jnp.float32
        )
        if step > 0:
            back = from_behind(partial_value.astype(jnp.bfloat16), "blk", -step)
            partial_value = back.astype(jnp.float32)
        glycan_total += partial_value
    other = swap_inner((scale * spectrum_total[rows_here:]).astype(jnp.bfloat16))
    spectrum_total = scale * spectrum_total[:rows_here] + other.astype(jnp.float32)
    return spectrum_total.astype(jnp.bfloat16), glycan_total.astype(jnp.bfloat16)


@dataclasses.dataclass(frozen=True)
class Block:
    first: int
    count: int
    out: str
    prior: str = ""
    optional: str = ""
    first_spectra: int = 0


def pair_body(plan, *refs):
    n_spectra, blocks, with_spectra, has_prior_s, rows, row_of = plan
    refs = list(refs)

    def take(count):
        taken = refs[:count]
        del refs[:count]
        return taken

    def take_if(condition):
        return take(1)[0] if condition else None

    consts, labels = take(2)
    flags = take_if(any(b.optional == "all" for b in blocks))
    spectra = take(n_spectra)
    held = take(len(blocks))
    priors = [take_if(b.prior) for b in blocks]
    prior_s = take_if(has_prior_s)
    outs = [take_if(b.out) for b in blocks]
    if with_spectra == "final":
        mine_out, other_out = take(2)
    elif with_spectra:
        (s_out,) = take(1)
    prior_held = [take_if(b.prior == "kept") for b in blocks]
    out_held = [take_if(b.out == "kept") for b in blocks]
    s_held = take_if(with_spectra)
    (sems,) = take(1)
    used = 0

    def move(source, target):
        nonlocal used
        copy = pltpu.make_async_copy(source, target, sems.at[used])
        copy.start()
        used += 1
        return copy

    moving = [
        move(priors[i].at[pl.ds(b.first, b.count)], prior_held[i]) if b.prior == "kept" else None
        for i, b in enumerate(blocks)
    ]
    moving_s = move(prior_s, s_held) if has_prior_s else None
    leaving = []

    def const(row):
        return consts[pl.ds(row, 1), pl.ds(0, 1)]

    scale, shift = const(0), const(1)
    row_labels = []
    for j in range(n_spectra):
        if spectra[j].shape[0] > rows:
            digits = spectra[j][pl.ds(rows, LABEL_ROWS), pl.ds(0, rows)].astype(jnp.float32)
            row_labels.append(digits[0:1] * 16384.0 + digits[1:2] * 128.0 + digits[2:3])
        else:
            row_labels.append(labels[:, pl.ds(j * rows, rows)])
    if has_prior_s:
        moving_s.wait()
    for i, block in enumerate(blocks):

        def work(i=i, block=block):
            where = pl.ds(block.first, block.count)
            glycans = held[i][where]
            targets = lax.broadcasted_iota(jnp.int32, (block.count, 1), 0).astype(jnp.float32)
            targets = targets + (const(row_of[i]) + float(block.first))
            total = None
            for j in range(block.first_spectra, n_spectra):
                here = spectra[j][pl.ds(0, rows)]
                logits = lax.dot_general(
                    glycans, here, (((1,), (1,)), ((), ())), preferred_element_type=jnp.float32
                )
                logits = scale * logits + shift
                positive = jnp.where(targets == row_labels[j], 1.0, 0.0)
                coef = jax.nn.sigmoid(logits) - positive
                masked = coef * const(KEEP_ROW) if block.optional == "spectra" else coef
                coef = coef.astype(jnp.bfloat16)
                if block.out:
                    part = jnp.dot(coef, here, preferred_element_type=jnp.float32)
                    total = part if total is None else total + part
                if with_spectra:
                    part = lax.dot_general(
                        masked.astype(jnp.bfloat16),
                        glycans,
                        (((0,), (0,)), ((), ())),
                        preferred_element_type=jnp.float32,
                    )
                    at = pl.ds(j * rows, rows)
                    if i > 0 or has_prior_s:
                        s_held[at] += part
                    else:
                        s_held[at] = part
            if block.prior == "kept":
                moving[i].wait()
                total = total + prior_held[i][...]
            elif block.prior:
                total = total + priors[i][where]
            if block.out == "kept":
                out_held[i][...] = total
                leaving.append(move(out_held[i], outs[i]))
            elif block.out == "total":
                outs[i][...] = total
            elif block.out == "scaled":
                outs[i][...] = scale * total
            elif block.out:
                outs[i][...] = (scale * total).astype(jnp.bfloat16)

        if block.optional == "all":
            pl.when(flags[i] != 0)(work)
        else:
            work()
    if with_spectra == "final":
        mine_out[...] = scale * s_held[pl.ds(0, rows)]
        other_out[...] = (scale * s_held[pl.ds(rows, rows)]).astype(jnp.bfloat16)
    elif with_spectra:
        leaving.append(move(s_held, s_out))
    for copy in leaving:
        copy.wait()


def in_vmem(array):
    return pltpu.with_memory_space_constraint(array, pltpu.VMEM)


def in_hbm(array):
    return pltpu.with_memory_space_constraint(array, pltpu.HBM)


def vmem_out(shape, kind):
    return pltpu.VMEM(shape, kind)


def hbm_out(shape, kind):
    return pltpu.HBM(shape, kind)


VMEM_SPEC = pl.BlockSpec(memory_space=pltpu.VMEM)
SMEM_SPEC = pl.BlockSpec(memory_space=pltpu.SMEM)
HBM_SPEC = pl.BlockSpec(memory_space=pltpu.HBM)
SMALL_COST = pl.CostEstimate(flops=1024, bytes_accessed=1024, transcendentals=0)


def params():
    return pltpu.CompilerParams(vmem_limit_bytes=VMEM_BYTES)


def pair_work(consts, spectra, labels, blocks, rows, with_spectra=False, prior_s=None):
    width = spectra[0].shape[1]
    all_rows = rows * len(spectra)
    shapes = tuple(b[0] for b in blocks)
    row_of = tuple(b[2] for b in blocks)
    plan = (len(spectra), shapes, with_spectra, prior_s is not None, rows, row_of)
    operands = [in_vmem(consts), in_vmem(labels)]
    in_specs = [VMEM_SPEC, VMEM_SPEC]
    if any(b.optional == "all" for b in shapes):
        operands.append(jnp.stack([jnp.int32(b[3]) for b in blocks]))
        in_specs.append(SMEM_SPEC)
    for array in list(spectra) + [b[1] for b in blocks]:
        operands.append(in_vmem(array))
        in_specs.append(VMEM_SPEC)
    for shape, _, _, _, prior in blocks:
        if shape.prior:
            operands.append(in_hbm(prior) if shape.prior == "kept" else in_vmem(prior))
            in_specs.append(HBM_SPEC if shape.prior == "kept" else VMEM_SPEC)
    if prior_s is not None:
        operands.append(in_hbm(prior_s))
        in_specs.append(HBM_SPEC)
    outs = []
    out_specs = []
    scratch = []
    for shape in shapes:
        if shape.prior == "kept":
            scratch.append(pltpu.VMEM((shape.count, width), jnp.float32))
    for shape in shapes:
        if shape.out == "kept":
            outs.append(hbm_out((shape.count, width), jnp.float32))
            out_specs.append(HBM_SPEC)
            scratch.append(pltpu.VMEM((shape.count, width), jnp.float32))
        elif shape.out:
            kind = jnp.bfloat16 if shape.out == "rounded" else jnp.float32
            outs.append(vmem_out((shape.count, width), kind))
            out_specs.append(VMEM_SPEC)
    if with_spectra == "final":
        outs.append(vmem_out((rows, width), jnp.float32))
        outs.append(vmem_out((rows, width), jnp.bfloat16))
        out_specs += [VMEM_SPEC, VMEM_SPEC]
    elif with_spectra:
        outs.append(hbm_out((all_rows, width), jnp.float32))
        out_specs.append(HBM_SPEC)
    if with_spectra:
        scratch.append(pltpu.VMEM((all_rows, width), jnp.float32))
    scratch.append(pltpu.SemaphoreType.DMA((2 * len(blocks) + 2,)))
    return pl.pallas_call(
        functools.partial(pair_body, plan),
        out_shape=outs,
        in_specs=in_specs,
        out_specs=out_specs,
        scratch_shapes=scratch,
        cost_estimate=SMALL_COST,
        compiler_params=params(),
    )(*operands)


def code_labels(labels, row_count, width):
    digits = jnp.stack([labels // 16384, labels // 128 % 128, labels % 128])
    spare = ((0, row_count - 3), (0, width - labels.shape[0]))
    return jnp.pad(digits.astype(jnp.bfloat16), spare)


def choose_body(flag, if_true, if_false, tail, out):
    rows = if_true.shape[0]

    @pl.when(flag[0] != 0)
    def _():
        out[pl.ds(0, rows)] = if_true[...]

    @pl.when(flag[0] == 0)
    def _():
        out[pl.ds(0, rows)] = if_false[...]

    out[pl.ds(rows, tail.shape[0])] = tail[...]


def choose(flag, if_true, if_false, tail):
    rows, width = if_true.shape
    return pl.pallas_call(
        choose_body,
        out_shape=vmem_out((rows + tail.shape[0], width), if_true.dtype),
        in_specs=[SMEM_SPEC] + [VMEM_SPEC] * 3,
        out_specs=VMEM_SPEC,
        cost_estimate=SMALL_COST,
        compiler_params=params(),
    )(jnp.int32(flag).reshape(1), in_vmem(if_true), in_vmem(if_false), in_vmem(tail))


def add_body(first, total, arrived, out):
    where = pl.ds(first, out.shape[0])
    out[...] = (total[where] + arrived[...].astype(jnp.float32)).astype(jnp.bfloat16)


def add_rounded(total, first, arrived):
    return pl.pallas_call(
        functools.partial(add_body, first),
        out_shape=vmem_out(arrived.shape, jnp.bfloat16),
        in_specs=[VMEM_SPEC] * 2,
        out_specs=VMEM_SPEC,
        cost_estimate=SMALL_COST,
        compiler_params=params(),
    )(in_vmem(total), in_vmem(arrived))


def finish_body(flag, mine_s, here_total, across_back, inside_a, inside_b, *rest):
    others, (spectra_out, glycans_out) = rest[:-2], rest[-2:]
    at = 0
    for other in others:
        where = pl.ds(at, other.shape[0])
        spectra_out[where] = (mine_s[where] + other[...].astype(jnp.float32)).astype(jnp.bfloat16)
        at += other.shape[0]

    @pl.when(flag[0] != 0)
    def _():
        glycans_out[pl.ds(0, inside_a.shape[0])] = inside_a[...]
        glycans_out[pl.ds(inside_a.shape[0], inside_b.shape[0])] = inside_b[...]

    @pl.when(flag[0] == 0)
    def _():
        total = here_total[...] + across_back[...].astype(jnp.float32)
        glycans_out[...] = total.astype(jnp.bfloat16)


def finish(flag, mine_s, here_total, across_back, inside_a, inside_b, others):
    arrays = [mine_s, here_total, across_back, inside_a, inside_b] + others
    out = jax.ShapeDtypeStruct(mine_s.shape, jnp.bfloat16)
    return pl.pallas_call(
        finish_body,
        out_shape=[out, out],
        in_specs=[SMEM_SPEC] + [VMEM_SPEC] * len(arrays),
        out_specs=[VMEM_SPEC, VMEM_SPEC],
        cost_estimate=SMALL_COST,
        compiler_params=params(),
    )(jnp.int32(flag).reshape(1), *[in_vmem(a) for a in arrays])


def along_line(spectra, glycans, labels, scale, shift):
    rows, width = spectra.shape
    first_part = rows // 2 + 16
    node_rows = rows * lax.axis_size("inner")
    position = lax.axis_index("blk")
    outer = (position == 0) | (position == LINE - 1)
    core_first = lax.axis_index("sub") * node_rows + lax.axis_index("inner") * rows
    lane_rows = lax.axis_size("sub") * node_rows

    def permute(block, pairs):
        return lax.ppermute(block, "blk", pairs)

    def first_of(block_position):
        return (block_position * lane_rows + core_first).astype(jnp.float32)

    sides = [(0, 1), (1, 0), (2, 3), (3, 2)]
    middle = [(1, 2), (2, 1), (0, 0), (3, 3)]
    here_at, side_at, across_at, far_at = 2, 3, 4, 5
    rows_of_consts = [
        scale,
        shift,
        first_of(position),
        first_of(position ^ 1),
        first_of(LINE - 1 - position),
        first_of((LINE - 1 - position) ^ 1),
        jnp.where(outer, 0.0, 1.0),
    ]
    index = lax.broadcasted_iota(jnp.int32, (8, 128), 0)
    consts = jnp.zeros((8, 128), jnp.float32)
    for i, value in enumerate(rows_of_consts):
        consts = jnp.where(index == i, value, consts)

    across = permute(glycans, middle)
    side = permute(glycans, sides)
    partner = swap_inner(spectra)
    own_labels = labels.reshape(1, rows)
    node_labels = jnp.concatenate([own_labels, swap_inner(own_labels)], axis=1)
    node_labels = node_labels.astype(jnp.float32)
    node = [spectra, partner]
    kept = Block(0, rows, "kept")
    here_g, own_s = pair_work(
        consts, node, node_labels, [(kept, glycans, here_at, 1, None)], rows, with_spectra=True
    )

    coded = code_labels(labels, LABEL_ROWS, width)
    side = after(side, here_g)
    far = permute(side, middle)
    across = after(across, side)
    mixed = permute(choose(outer, spectra, across, coded), sides)
    side_g, across_g, own_s = pair_work(
        consts,
        node,
        node_labels,
        [
            (kept, side, side_at, 1, None),
            (Block(0, rows, "kept", optional="spectra"), across, across_at, 1, None),
        ],
        rows,
        with_spectra=True,
        prior_s=own_s,
    )

    mixed, far = lax.optimization_barrier((mixed, far, own_s))[:2]
    mixed_other = swap_inner(mixed)
    last_out = permute(far, sides)
    (far_g,) = pair_work(
        consts,
        node + [mixed],
        node_labels,
        [(Block(0, rows, "total"), far, far_at, 1, None)],
        rows,
    )
    (far_a,) = pair_work(
        consts,
        [mixed_other],
        node_labels,
        [(Block(0, first_part, "rounded", "near"), far, far_at, 1, far_g)],
        rows,
    )
    back_a = permute(far_a, middle)
    ends = [mixed, mixed_other]
    far_b, across_out = pair_work(
        consts,
        ends,
        node_labels,
        [
            (Block(first_part, rows - first_part, "rounded", "near", first_spectra=1), after(far, far_a), far_at, 1, far_g),
            (Block(0, rows, "rounded", "kept"), across, across_at, 1, across_g),
        ],
        rows,
    )
    back_b = permute(far_b, middle)
    side_total, here_total = pair_work(
        consts,
        ends,
        node_labels,
        [
            (Block(0, rows, "scaled", "kept"), after(side, far_b), side_at, 1, side_g),
            (Block(0, rows, "scaled", "kept"), glycans, here_at, 1, here_g),
        ],
        rows,
    )
    total_a = add_rounded(side_total, 0, back_a)
    inside_a = permute(total_a, sides)
    across_back = permute(after(across_out, total_a), middle)
    total_b = add_rounded(side_total, first_part, after(back_b, total_a))
    inside_b = permute(total_b, sides)

    only_s = Block(0, rows, "", optional="all")
    mine_s, other_s = pair_work(
        consts,
        node,
        node_labels,
        [
            (only_s, after(far, total_b), far_at, ~outer, None),
            (only_s, mixed, far_at, outer, None),
            (only_s, last_out, across_at, outer, None),
        ],
        rows,
        with_spectra="final",
        prior_s=own_s,
    )
    piece = -(-rows // 48) * 16
    others = [swap_inner(other_s[at : at + piece]) for at in range(0, rows, piece)]
    return finish(outer, mine_s, here_total, across_back, inside_a, inside_b, others)


def local(
    mass_profile_vectors,
    sugar_tree_vectors,
    matching_glycan_rows,
    sharpness_factor,
    offset_shift_term,
):
    work = along_line if lax.axis_size("blk") == STEPS == LINE else around_ring
    return work(
        mass_profile_vectors,
        sugar_tree_vectors,
        matching_glycan_rows,
        sharpness_factor[0],
        offset_shift_term[0],
    )


def solution(mesh):
    placed = (
        P(("groups", "blk", "sub", "inner"), None),
        P(("groups", "blk", "sub", "inner"), None),
        P(("groups", "blk", "sub", "inner")),
        P(),
        P(),
    )
    return jax.shard_map(
        local,
        mesh=mesh,
        in_specs=placed,
        out_specs=(
            P(("groups", "blk", "sub", "inner"), None),
            P(("groups", "blk", "sub", "inner"), None),
        ),
        check_vma=False,
    )
```

time: 101 us -> 85.3 us (0.84)
  the two profiles are of different devices: /device:TPU:12 before, /device:TPU:0 now
where the time goes in v4:
time: 85.3 us; the launch traced here: 84.2 us
  Pallas kernels  32.5 us (38%)
  starting transfers between devices  25.6 us (30%)
  waiting for transfers between devices  13.6 us (16%)
  local copies, waits for them, and re-layouts  9.32 us (11%)
  between operations  2.2 us (3%)
  other arithmetic  0.97 us (1%)
    pallas_call x7, Pallas kernels, pair_work(): pl.pallas_call(functools.partial(pair_body, plan), out_shape=outs, in_spe...  30 us
    ppermute x10, starting transfers between devices, permute(): return lax.ppermute(block, 'blk', pairs)  24.3 us
    ppermute x10, waiting for transfers between devices, permute(): return lax.ppermute(block, 'blk', pairs)  11.4 us
    unnamed x26, local copies, waits for them, and re-layouts  8.57 us
    pallas_call x1, Pallas kernels, finish(): pl.pallas_call(finish_body, out_shape=[out, out], in_specs=[SMEM_SPEC] +...  2.3 us
    ppermute x6, waiting for transfers between devices, from_behind(): return lax.ppermute(block, axis, route)  2.19 us
  transfers between devices with their start and end apart: 16, of which 6 were waited for; matrix products, arithmetic and copies ran while one was open for 2% of the time, Pallas kernels for 36%

profile of v4, /device:TPU:0, one launch (start us, length us, event | category | flops | bytes accessed | tf_op | source)
XLA Modules:
  0.0 84.2 jit_solution(12671587514440994552)
XLA Ops:
  0.6 3.1 %collective-permute-start.3 = (bf16[320,1024]{1,0:T(8,128)(2,1)}, bf16[320,1024]{1,0:T(8,128)(2,1)S(1)}, u32[]{:S(2)}, u32[]{:S(2)}) collective-permute-start(bf16[320,1024]{1,0:T(8,128)(2,1)} %refs_5_.1), channel_id=1, source_target_pairs={{0,4},{4,0},{8,12},{12,8},{1,5},{5,1},{9,13},{13,9},{2,6},{6,2},{1... | collective-permute-start | bytes 1966088 | tf_op jit(solution)/shard_map/ppermute | solution.py:375
  3.7 1.7 %collective-permute-start.2 = (bf16[320,1024]{1,0:T(8,128)(2,1)}, bf16[320,1024]{1,0:T(8,128)(2,1)S(1)}, u32[]{:S(2)}, u32[]{:S(2)}) collective-permute-start(bf16[320,1024]{1,0:T(8,128)(2,1)} %refs_5_.1), channel_id=1, source_target_pairs={{4,8},{8,4},{0,0},{12,12},{5,9},{9,5},{1,1},{13,13},{6,10},{10,6},... | collective-permute-start | bytes 1966088 | tf_op jit(solution)/shard_map/ppermute | solution.py:375
  5.5 0.7 concatenate.13
  6.7 0.7 fusion.10
  9.0 1.1 %copy-done = bf16[320,1024]{1,0:T(8,128)(2,1)S(1)} copy-done((bf16[320,1024]{1,0:T(8,128)(2,1)S(1)}, bf16[320,1024]{1,0:T(8,128)(2,1)}, u32[]{:S(2)}) %copy-start) | copy-done | bytes 655384
  10.0 1.1 %copy-done.4 = bf16[320,1024]{1,0:T(8,128)(2,1)S(1)} copy-done((bf16[320,1024]{1,0:T(8,128)(2,1)S(1)}, bf16[320,1024]{1,0:T(8,128)(2,1)}, u32[]{:S(2)}) %copy-start.4) | copy-done | bytes 655384
  11.1 4.2 %shard_map.68 = (f32[320,1024]{1,0:T(8,128)}, f32[640,1024]{1,0:T(8,128)}) custom-call(f32[8,128]{1,0:T(8,128)S(1)} %select_select_fusion.refs_0_, f32[1,640]{1,0:T(1,128)S(1)} %add_convert_fusion.refs_1_, bf16[320,1024]{1,0:T(8,128)(2,1)S(1)} %copy-done, bf16[320,1024]{1,0:T(8,128)(2,1)S(1)} %collective-permute-done.1.refs_3_.refs_4_, ...), custom_call_target="tpu_custom_call" | custom-call | flops 1024 | bytes 1024 | tf_op jit(solution)/shard_map/pallas_call | solution.py:274
  15.3 3.3 %collective-permute-done.3.refs_4_ = bf16[320,1024]{1,0:T(8,128)(2,1)S(1)} collective-permute-done((bf16[320,1024]{1,0:T(8,128)(2,1)}, bf16[320,1024]{1,0:T(8,128)(2,1)S(1)}, u32[]{:S(2)}, u32[]{:S(2)}) %collective-permute-start.3) | collective-permute-done | bytes 655392 | tf_op jit(solution)/shard_map/ppermute | solution.py:375
  18.7 0.8 copy-done.6
  19.6 4.0 %collective-permute-start.4 = (bf16[336,1024]{1,0:T(8,128)(2,1)S(1)}, bf16[336,1024]{1,0:T(8,128)(2,1)S(1)}, u32[]{:S(2)}, u32[]{:S(2)}) collective-permute-start(bf16[336,1024]{1,0:T(8,128)(2,1)S(1)} %shard_map.69), channel_id=1, source_target_pairs={{0,4},{4,0},{8,12},{12,8},{1,5},{5,1},{9,13},{13,9},{2,6},{6,2},{1... | collective-permute-start | bytes 2064392 | tf_op jit(solution)/shard_map/ppermute | solution.py:375
  23.5 1.7 %collective-permute-start.5 = (bf16[320,1024]{1,0:T(8,128)(2,1)}, bf16[320,1024]{1,0:T(8,128)(2,1)S(1)}, u32[]{:S(2)}, u32[]{:S(2)}) collective-permute-start(bf16[320,1024]{1,0:T(8,128)(2,1)} %copy-done.6), channel_id=1, source_target_pairs={{4,8},{8,4},{0,0},{12,12},{5,9},{9,5},{1,1},{13,13},{6,10},{10,6},... | collective-permute-start | bytes 1966088 | tf_op jit(solution)/shard_map/ppermute | solution.py:375
  25.3 1.1 %copy-done.7 = bf16[320,1024]{1,0:T(8,128)(2,1)S(1)} copy-done((bf16[320,1024]{1,0:T(8,128)(2,1)S(1)}, bf16[320,1024]{1,0:T(8,128)(2,1)}, u32[]{:S(2)}) %copy-start.7) | copy-done | bytes 655384
  26.4 8.3 %shard_map.70 = (f32[320,1024]{1,0:T(8,128)}, f32[320,1024]{1,0:T(8,128)}, f32[640,1024]{1,0:T(8,128)}) custom-call(f32[8,128]{1,0:T(8,128)S(1)} %select_select_fusion.refs_0_, f32[1,640]{1,0:T(1,128)S(1)} %add_convert_fusion.refs_1_, bf16[320,1024]{1,0:T(8,128)(2,1)S(1)} %copy-done.1, bf16[320,1024]{1,0:T(8,128)(2,1)S(1)} %collective-permute-done.1.refs_3_.refs_4_, ...), custom_call_target="tpu_custom_call" | custom-call | flops 1024 | bytes 1024 | tf_op jit(solution)/shard_map/pallas_call | solution.py:274
  34.7 3.5 %collective-permute-done.4.refs_4_.refs_2_.refs_6_ = bf16[336,1024]{1,0:T(8,128)(2,1)S(1)} collective-permute-done((bf16[336,1024]{1,0:T(8,128)(2,1)S(1)}, bf16[336,1024]{1,0:T(8,128)(2,1)S(1)}, u32[]{:S(2)}, u32[]{:S(2)}) %collective-permute-start.4) | collective-permute-done | bytes 688160 | tf_op jit(solution)/shard_map/ppermute | solution.py:375
  38.1 3.2 %collective-permute-start.9 = (bf16[320,1024]{1,0:T(8,128)(2,1)S(1)}, bf16[320,1024]{1,0:T(8,128)(2,1)}, u32[]{:S(2)}, u32[]{:S(2)}) collective-permute-start(bf16[320,1024]{1,0:T(8,128)(2,1)S(1)} %collective-permute-done.5.refs_5_.refs_3_.refs_4_), channel_id=1, source_target_pairs={{0,4},{4,0},{8,12},{12,8},{1,5},{5,1},{9,13},{13,9},{2,6},{6,2},{1... | collective-permute-start | bytes 1966088 | tf_op jit(solution)/shard_map/ppermute | solution.py:375
  41.3 2.4 %shard_map.71.refs_4_.refs_6_ = f32[320,1024]{1,0:T(8,128)S(1)} custom-call(f32[8,128]{1,0:T(8,128)S(1)} %select_select_fusion.refs_0_, f32[1,640]{1,0:T(1,128)S(1)} %add_convert_fusion.refs_1_, bf16[320,1024]{1,0:T(8,128)(2,1)S(1)} %copy-done.1, bf16[320,1024]{1,0:T(8,128)(2,1)S(1)} %collective-permute-done.1.refs_3_.refs_4_, ...), custom_call_target="tpu_custom_call" | custom-call | flops 1024 | bytes 1024 | tf_op jit(solution)/shard_map/pallas_call | solution.py:274
  43.7 0.9 %shard_map.72 = bf16[176,1024]{1,0:T(8,128)(2,1)S(1)} custom-call(f32[8,128]{1,0:T(8,128)S(1)} %select_select_fusion.refs_0_, f32[1,640]{1,0:T(1,128)S(1)} %add_convert_fusion.refs_1_, bf16[336,1024]{1,0:T(8,128)(2,1)S(1)} %collective-permute-done.6.refs_2_.refs_3_, bf16[320,1024]{1,0:T(8,128)(2,1)S(1)} %collective-permute-done.5.refs_5_.refs_3_.refs_4_, ...), custom_call_target="tpu_custom_call" | custom-call | flops 1024 | bytes 1024 | tf_op jit(solution)/shard_map/pallas_call | solution.py:274
  44.5 0.7 collective-permute-start.8
  45.2 3.6 %shard_map.73 = (bf16[144,1024]{1,0:T(8,128)(2,1)}, bf16[320,1024]{1,0:T(8,128)(2,1)}) custom-call(f32[8,128]{1,0:T(8,128)S(1)} %select_select_fusion.refs_0_, f32[1,640]{1,0:T(1,128)S(1)} %add_convert_fusion.refs_1_, bf16[336,1024]{1,0:T(8,128)(2,1)S(1)} %collective-permute-done.4.refs_4_.refs_2_.refs_6_, ...), custom_call_target="tpu_custom_call" | custom-call | flops 1024 | bytes 1024 | tf_op jit(solution)/shard_map/pallas_call | solution.py:274
  48.8 1.6 %collective-permute-start.7 = (bf16[144,1024]{1,0:T(8,128)(2,1)}, bf16[144,1024]{1,0:T(8,128)(2,1)S(1)}, u32[]{:S(2)}, u32[]{:S(2)}) collective-permute-start(bf16[144,1024]{1,0:T(8,128)(2,1)} %get-tuple-element.31), channel_id=1, source_target_pairs={{4,8},{8,4},{0,0},{12,12},{5,9},{9,5},{1,1},{13,13},{6,10},{10,6},... | collective-permute-start | bytes 884744 | tf_op jit(solution)/shard_map/ppermute | solution.py:375
  50.4 3.6 %shard_map.74 = (f32[320,1024]{1,0:T(8,128)S(1)}, f32[320,1024]{1,0:T(8,128)S(1)}) custom-call(f32[8,128]{1,0:T(8,128)S(1)} %select_select_fusion.refs_0_, f32[1,640]{1,0:T(1,128)S(1)} %add_convert_fusion.refs_1_, bf16[336,1024]{1,0:T(8,128)(2,1)S(1)} %collective-permute-done.4.refs_4_.refs_2_.refs_6_, ...), custom_call_target="tpu_custom_call" | custom-call | flops 1024 | bytes 1024 | tf_op jit(solution)/shard_map/pallas_call | solution.py:274
  54.1 1.0 %copy-done.9 = f32[320,1024]{1,0:T(8,128)} copy-done((f32[320,1024]{1,0:T(8,128)}, f32[320,1024]{1,0:T(8,128)S(1)}, u32[]{:S(2)}) %copy-start.9) | copy-done | bytes 1310744
  55.1 1.1 %copy-done.2 = f32[320,1024]{1,0:T(8,128)} copy-done((f32[320,1024]{1,0:T(8,128)}, f32[320,1024]{1,0:T(8,128)S(1)}, u32[]{:S(2)}) %copy-start.2) | copy-done | bytes 1310744
  56.2 0.7 copy-done.11
  56.9 6.6 %collective-permute-start.10 = (bf16[320,1024]{1,0:T(8,128)(2,1)}, bf16[320,1024]{1,0:T(8,128)(2,1)}, u32[]{:S(2)}, u32[]{:S(2)}) collective-permute-start(bf16[320,1024]{1,0:T(8,128)(2,1)} %get-tuple-element.40), channel_id=1, source_target_pairs={{4,8},{8,4},{0,0},{12,12},{5,9},{9,5},{1,1},{13,13},{6,10},{10,6},... | collective-permute-start | bytes 1966088 | tf_op jit(solution)/shard_map/ppermute | solution.py:375
  63.6 1.3 %copy-done.3 = f32[320,1024]{1,0:T(8,128)S(1)} copy-done((f32[320,1024]{1,0:T(8,128)S(1)}, f32[320,1024]{1,0:T(8,128)}, u32[]{:S(2)}) %copy-start.3) | copy-done | bytes 1310744
  65.9 1.2 %collective-permute-start.11 = (bf16[176,1024]{1,0:T(8,128)(2,1)S(1)}, bf16[176,1024]{1,0:T(8,128)(2,1)S(1)}, u32[]{:S(2)}, u32[]{:S(2)}) collective-permute-start(bf16[176,1024]{1,0:T(8,128)(2,1)S(1)} %copy-done.12), channel_id=1, source_target_pairs={{0,4},{4,0},{8,12},{12,8},{1,5},{5,1},{9,13},{13,9},{2,6},{6,2},{1... | collective-permute-start | bytes 1081352 | tf_op jit(solution)/shard_map/ppermute | solution.py:375
  67.0 7.2 %shard_map.77 = (f32[320,1024]{1,0:T(8,128)S(1)}, bf16[320,1024]{1,0:T(8,128)(2,1)S(1)}) custom-call(f32[8,128]{1,0:T(8,128)S(1)} %select_select_fusion.refs_0_, f32[1,640]{1,0:T(1,128)S(1)} %add_convert_fusion.refs_1_, s32[3]{0:T(128)S(1)} %pad_add_fusion.refs_2_, bf16[320,1024]{1,0:T(8,128)(2,1)S(1)} %copy-done.1, ...), custom_call_target="tpu_custom_call" | custom-call | flops 1024 | bytes 1024 | tf_op jit(solution)/shard_map/pallas_call | solution.py:274
  75.0 0.8 collective-permute-done.15.rest_2_
  76.1 1.2 %collective-permute-done.14.rest_1_ = bf16[112,1024]{1,0:T(8,128)(2,1)S(1)} collective-permute-done((bf16[112,1024]{1,0:T(8,128)(2,1)S(1)}, bf16[112,1024]{1,0:T(8,128)(2,1)S(1)}, u32[]{:S(2)}, u32[]{:S(2)}) %collective-permute-start.14) | collective-permute-done | bytes 229408 | tf_op jit(solution)/shard_map/ppermute | solution.py:21
  77.3 4.6 %collective-permute-done.11.inside_a = bf16[176,1024]{1,0:T(8,128)(2,1)S(1)} collective-permute-done((bf16[176,1024]{1,0:T(8,128)(2,1)S(1)}, bf16[176,1024]{1,0:T(8,128)(2,1)S(1)}, u32[]{:S(2)}, u32[]{:S(2)}) %collective-permute-start.11) | collective-permute-done | bytes 360480 | tf_op jit(solution)/shard_map/ppermute | solution.py:375
  81.9 2.3 %shard_map.78 = (bf16[320,1024]{1,0:T(8,128)(2,1)}, bf16[320,1024]{1,0:T(8,128)(2,1)}) custom-call(s32[1]{0:T(128)} %bitcast.flag, f32[320,1024]{1,0:T(8,128)S(1)} %get-tuple-element.37.mine_s, f32[320,1024]{1,0:T(8,128)S(1)} %copy-done.10, bf16[320,1024]{1,0:T(8,128)(2,1)} %collective-permute-done.10.across_back, ...), custom_call_target="tpu_custom_call" | custom-call | flops 1024 | bytes 1024 | tf_op jit(solution)/shard_map/pallas_call | solution.py:355
  (52 shorter events, 3.0 us)
Async XLA Ops:
  0.6 18.0 %collective-permute-start.3 = (bf16[320,1024]{1,0:T(8,128)(2,1)}, bf16[320,1024]{1,0:T(8,128)(2,1)S(1)}, u32[]{:S(2)}, u32[]{:S(2)}) collective-permute-start(bf16[320,1024]{1,0:T(8,128)(2,1)} %refs_5_.1), channel_id=1, source_target_pairs={{0,4},{4,0},{8,12},{12,8},{1,5},{5,1},{9,13},{13,9},{2,6},{6,2},{1... | collective-permute-start | bytes 1966088 | tf_op jit(solution)/shard_map/ppermute | solution.py:375
  3.7 14.9 %collective-permute-start.2 = (bf16[320,1024]{1,0:T(8,128)(2,1)}, bf16[320,1024]{1,0:T(8,128)(2,1)S(1)}, u32[]{:S(2)}, u32[]{:S(2)}) collective-permute-start(bf16[320,1024]{1,0:T(8,128)(2,1)} %refs_5_.1), channel_id=1, source_target_pairs={{4,8},{8,4},{0,0},{12,12},{5,9},{9,5},{1,1},{13,13},{6,10},{10,6},... | collective-permute-start | bytes 1966088 | tf_op jit(solution)/shard_map/ppermute | solution.py:375
  6.1 2.7 %collective-permute-start = (s32[1,320]{1,0:T(1,128)S(1)}, s32[1,320]{1,0:T(1,128)S(1)}, u32[]{:S(2)}, u32[]{:S(2)}) collective-permute-start(s32[1,320]{1,0:T(1,128)S(1)} %concatenate.13), channel_id=1, source_target_pairs={{1,0},{0,1},{3,2},{2,3},{5,4},{4,5},{7,6},{6,7},{9,8},{8,9},{11,10... | collective-permute-start | bytes 3848 | tf_op jit(solution)/shard_map/ppermute | solution.py:21
  6.1 2.8 %collective-permute-start.1 = (bf16[320,1024]{1,0:T(8,128)(2,1)}, bf16[320,1024]{1,0:T(8,128)(2,1)S(1)}, u32[]{:S(2)}, u32[]{:S(2)}) collective-permute-start(bf16[320,1024]{1,0:T(8,128)(2,1)} %refs_3_.1), channel_id=1, source_target_pairs={{1,0},{0,1},{3,2},{2,3},{5,4},{4,5},{7,6},{6,7},{9,8},{8,9},{11,10... | collective-permute-start | bytes 1966088 | tf_op jit(solution)/shard_map/ppermute | solution.py:21
  8.9 1.1 %copy-start = (bf16[320,1024]{1,0:T(8,128)(2,1)S(1)}, bf16[320,1024]{1,0:T(8,128)(2,1)}, u32[]{:S(2)}) copy-start(bf16[320,1024]{1,0:T(8,128)(2,1)} %refs_3_.1) | copy-start | bytes 1966084
  10.0 1.1 %copy-start.4 = (bf16[320,1024]{1,0:T(8,128)(2,1)S(1)}, bf16[320,1024]{1,0:T(8,128)(2,1)}, u32[]{:S(2)}) copy-start(bf16[320,1024]{1,0:T(8,128)(2,1)} %refs_5_.1) | copy-start | bytes 1966084
  11.1 8.4 %copy-start.1 = (bf16[320,1024]{1,0:T(8,128)(2,1)S(1)}, bf16[320,1024]{1,0:T(8,128)(2,1)}, u32[]{:S(2)}) copy-start(bf16[320,1024]{1,0:T(8,128)(2,1)} %refs_3_.1) | copy-start | bytes 1966084
  18.7 0.8 copy-start.6
  19.6 18.5 %collective-permute-start.4 = (bf16[336,1024]{1,0:T(8,128)(2,1)S(1)}, bf16[336,1024]{1,0:T(8,128)(2,1)S(1)}, u32[]{:S(2)}, u32[]{:S(2)}) collective-permute-start(bf16[336,1024]{1,0:T(8,128)(2,1)S(1)} %shard_map.69), channel_id=1, source_target_pairs={{0,4},{4,0},{8,12},{12,8},{1,5},{5,1},{9,13},{13,9},{2,6},{6,2},{1... | collective-permute-start | bytes 2064392 | tf_op jit(solution)/shard_map/ppermute | solution.py:375
  23.5 11.1 %collective-permute-start.5 = (bf16[320,1024]{1,0:T(8,128)(2,1)}, bf16[320,1024]{1,0:T(8,128)(2,1)S(1)}, u32[]{:S(2)}, u32[]{:S(2)}) collective-permute-start(bf16[320,1024]{1,0:T(8,128)(2,1)} %copy-done.6), channel_id=1, source_target_pairs={{4,8},{8,4},{0,0},{12,12},{5,9},{9,5},{1,1},{13,13},{6,10},{10,6},... | collective-permute-start | bytes 1966088 | tf_op jit(solution)/shard_map/ppermute | solution.py:375
  25.3 1.1 %copy-start.7 = (bf16[320,1024]{1,0:T(8,128)(2,1)S(1)}, bf16[320,1024]{1,0:T(8,128)(2,1)}, u32[]{:S(2)}) copy-start(bf16[320,1024]{1,0:T(8,128)(2,1)} %copy-done.6) | copy-start | bytes 1966084
  38.1 5.5 %collective-permute-start.6 = (bf16[336,1024]{1,0:T(8,128)(2,1)S(1)}, bf16[336,1024]{1,0:T(8,128)(2,1)S(1)}, u32[]{:S(2)}, u32[]{:S(2)}) collective-permute-start(bf16[336,1024]{1,0:T(8,128)(2,1)S(1)} %collective-permute-done.4.refs_4_.refs_2_.refs_6_), channel_id=1, source_target_pairs={{1,0},{0,1},{3,2},{2,3},{5,4},{4,5},{7,6},{6,7},{9,8},{8,9},{11,10... | collective-permute-start | bytes 2064392 | tf_op jit(solution)/shard_map/ppermute | solution.py:21
  38.1 28.9 %collective-permute-start.9 = (bf16[320,1024]{1,0:T(8,128)(2,1)S(1)}, bf16[320,1024]{1,0:T(8,128)(2,1)}, u32[]{:S(2)}, u32[]{:S(2)}) collective-permute-start(bf16[320,1024]{1,0:T(8,128)(2,1)S(1)} %collective-permute-done.5.refs_5_.refs_3_.refs_4_), channel_id=1, source_target_pairs={{0,4},{4,0},{8,12},{12,8},{1,5},{5,1},{9,13},{13,9},{2,6},{6,2},{1... | collective-permute-start | bytes 1966088 | tf_op jit(solution)/shard_map/ppermute | solution.py:375
  44.5 9.5 %collective-permute-start.8 = (bf16[176,1024]{1,0:T(8,128)(2,1)S(1)}, bf16[176,1024]{1,0:T(8,128)(2,1)S(1)}, u32[]{:S(2)}, u32[]{:S(2)}) collective-permute-start(bf16[176,1024]{1,0:T(8,128)(2,1)S(1)} %shard_map.72), channel_id=1, source_target_pairs={{4,8},{8,4},{0,0},{12,12},{5,9},{9,5},{1,1},{13,13},{6,10},{10,6},... | collective-permute-start | bytes 1081352 | tf_op jit(solution)/shard_map/ppermute | solution.py:375
  45.2 5.2 %copy-start.5 = (bf16[320,1024]{1,0:T(8,128)(2,1)S(1)}, bf16[320,1024]{1,0:T(8,128)(2,1)}, u32[]{:S(2)}) copy-start(bf16[320,1024]{1,0:T(8,128)(2,1)} %refs_5_.1) | copy-start | bytes 1966084
  45.2 5.2 %copy-start.8 = (bf16[320,1024]{1,0:T(8,128)(2,1)S(1)}, bf16[320,1024]{1,0:T(8,128)(2,1)}, u32[]{:S(2)}) copy-start(bf16[320,1024]{1,0:T(8,128)(2,1)} %copy-done.6) | copy-start | bytes 1966084
  48.8 14.7 %collective-permute-start.7 = (bf16[144,1024]{1,0:T(8,128)(2,1)}, bf16[144,1024]{1,0:T(8,128)(2,1)S(1)}, u32[]{:S(2)}, u32[]{:S(2)}) collective-permute-start(bf16[144,1024]{1,0:T(8,128)(2,1)} %get-tuple-element.31), channel_id=1, source_target_pairs={{4,8},{8,4},{0,0},{12,12},{5,9},{9,5},{1,1},{13,13},{6,10},{10,6},... | collective-permute-start | bytes 884744 | tf_op jit(solution)/shard_map/ppermute | solution.py:375
  54.0 1.1 %copy-start.9 = (f32[320,1024]{1,0:T(8,128)}, f32[320,1024]{1,0:T(8,128)S(1)}, u32[]{:S(2)}) copy-start(f32[320,1024]{1,0:T(8,128)S(1)} %get-tuple-element.38.here_total) | copy-start | bytes 3932164
  55.1 1.1 %copy-start.2 = (f32[320,1024]{1,0:T(8,128)}, f32[320,1024]{1,0:T(8,128)S(1)}, u32[]{:S(2)}) copy-start(f32[320,1024]{1,0:T(8,128)S(1)} %get-tuple-element.34.total) | copy-start | bytes 3932164
  56.2 0.7 copy-start.11
  56.9 25.0 %collective-permute-start.10 = (bf16[320,1024]{1,0:T(8,128)(2,1)}, bf16[320,1024]{1,0:T(8,128)(2,1)}, u32[]{:S(2)}, u32[]{:S(2)}) collective-permute-start(bf16[320,1024]{1,0:T(8,128)(2,1)} %get-tuple-element.40), channel_id=1, source_target_pairs={{4,8},{8,4},{0,0},{12,12},{5,9},{9,5},{1,1},{13,13},{6,10},{10,6},... | collective-permute-start | bytes 1966088 | tf_op jit(solution)/shard_map/ppermute | solution.py:375
  63.6 1.3 %copy-start.3 = (f32[320,1024]{1,0:T(8,128)S(1)}, f32[320,1024]{1,0:T(8,128)}, u32[]{:S(2)}) copy-start(f32[320,1024]{1,0:T(8,128)} %copy-done.2) | copy-start | bytes 3932164
  64.9 1.0 %copy-start.12 = (bf16[176,1024]{1,0:T(8,128)(2,1)S(1)}, bf16[176,1024]{1,0:T(8,128)(2,1)}, u32[]{:S(2)}) copy-start(bf16[176,1024]{1,0:T(8,128)(2,1)} %copy-done.11) | copy-start | bytes 1081348
  64.9 12.3 %collective-permute-start.12 = (bf16[144,1024]{1,0:T(8,128)(2,1)S(1)}, bf16[144,1024]{1,0:T(8,128)(2,1)S(1)}, u32[]{:S(2)}, u32[]{:S(2)}) collective-permute-start(bf16[144,1024]{1,0:T(8,128)(2,1)S(1)} %shard_map.76), channel_id=1, source_target_pairs={{0,4},{4,0},{8,12},{12,8},{1,5},{5,1},{9,13},{13,9},{2,6},{6,2},{1... | collective-permute-start | bytes 884744 | tf_op jit(solution)/shard_map/ppermute | solution.py:375
  65.9 16.0 %collective-permute-start.11 = (bf16[176,1024]{1,0:T(8,128)(2,1)S(1)}, bf16[176,1024]{1,0:T(8,128)(2,1)S(1)}, u32[]{:S(2)}, u32[]{:S(2)}) collective-permute-start(bf16[176,1024]{1,0:T(8,128)(2,1)S(1)} %copy-done.12), channel_id=1, source_target_pairs={{0,4},{4,0},{8,12},{12,8},{1,5},{5,1},{9,13},{13,9},{2,6},{6,2},{1... | collective-permute-start | bytes 1081352 | tf_op jit(solution)/shard_map/ppermute | solution.py:375
  74.2 7.6 %copy-start.10 = (f32[320,1024]{1,0:T(8,128)S(1)}, f32[320,1024]{1,0:T(8,128)}, u32[]{:S(2)}) copy-start(f32[320,1024]{1,0:T(8,128)} %copy-done.9) | copy-start | bytes 3932164
  74.3 1.5 %collective-permute-start.15 = (bf16[96,1024]{1,0:T(8,128)(2,1)S(1)}, bf16[96,1024]{1,0:T(8,128)(2,1)S(1)}, u32[]{:S(2)}, u32[]{:S(2)}) collective-permute-start(bf16[96,1024]{1,0:T(8,128)(2,1)S(1)} %slice.11), channel_id=1, source_target_pairs={{1,0},{0,1},{3,2},{2,3},{5,4},{4,5},{7,6},{6,7},{9,8},{8,9},{11,10... | collective-permute-start | bytes 589832 | tf_op jit(solution)/shard_map/ppermute | solution.py:21
  74.4 1.7 %collective-permute-start.13 = (bf16[112,1024]{1,0:T(8,128)(2,1)S(1)}, bf16[112,1024]{1,0:T(8,128)(2,1)S(1)}, u32[]{:S(2)}, u32[]{:S(2)}) collective-permute-start(bf16[112,1024]{1,0:T(8,128)(2,1)S(1)} %get-tuple-element.43), channel_id=1, source_target_pairs={{1,0},{0,1},{3,2},{2,3},{5,4},{4,5},{7,6},{6,7},{9,8},{8,9},{11,10... | collective-permute-start | bytes 688136 | tf_op jit(solution)/shard_map/ppermute | solution.py:21
  75.8 1.5 %collective-permute-start.14 = (bf16[112,1024]{1,0:T(8,128)(2,1)S(1)}, bf16[112,1024]{1,0:T(8,128)(2,1)S(1)}, u32[]{:S(2)}, u32[]{:S(2)}) collective-permute-start(bf16[112,1024]{1,0:T(8,128)(2,1)S(1)} %get-tuple-element.42), channel_id=1, source_target_pairs={{1,0},{0,1},{3,2},{2,3},{5,4},{4,5},{7,6},{6,7},{9,8},{8,9},{11,10... | collective-permute-start | bytes 688136 | tf_op jit(solution)/shard_map/ppermute | solution.py:21

commit v5 on v4

--- a/solution.py
+++ b/solution.py
@@ -82,8 +82,14 @@
     first_spectra: int = 0
 
 
+@dataclasses.dataclass(frozen=True)
+class Away:
+    array: jax.Array
+
+
 def pair_body(plan, *refs):
-    n_spectra, blocks, with_spectra, has_prior_s, rows, row_of = plan
+    blocks, with_spectra, has_prior_s, rows, row_of, away = plan
+    n_spectra = len(away) - len(blocks)
     refs = list(refs)
 
     def take(count):
@@ -106,8 +112,9 @@
     elif with_spectra:
         (s_out,) = take(1)
     prior_held = [take_if(b.prior == "kept") for b in blocks]
-    out_held = [take_if(b.out == "kept") for b in blocks]
+    out_held = [take_if(b.out.startswith("kept")) for b in blocks]
     s_held = take_if(with_spectra)
+    near = [take_if(flag) for flag in away]
     (sems,) = take(1)
     used = 0
 
@@ -118,6 +125,20 @@
         used += 1
         return copy
 
+    arriving = [None] * len(away)
+    for j in range(n_spectra):
+        if away[j]:
+            arriving[j] = move(spectra[j], near[j])
+            spectra[j] = near[j]
+    for i, b in enumerate(blocks):
+        if away[n_spectra + i]:
+            arriving[n_spectra + i] = move(held[i].at[pl.ds(b.first, b.count)], near[n_spectra + i])
+
+    def arrive(at):
+        if arriving[at] is not None:
+            arriving[at].wait()
+            arriving[at] = None
+
     moving = [
         move(priors[i].at[pl.ds(b.first, b.count)], prior_held[i]) if b.prior == "kept" else None
         for i, b in enumerate(blocks)
@@ -130,23 +151,29 @@
 
     scale, shift = const(0), const(1)
     row_labels = []
+    plain = 0
     for j in range(n_spectra):
         if spectra[j].shape[0] > rows:
             digits = spectra[j][pl.ds(rows, LABEL_ROWS), pl.ds(0, rows)].astype(jnp.float32)
             row_labels.append(digits[0:1] * 16384.0 + digits[1:2] * 128.0 + digits[2:3])
         else:
-            row_labels.append(labels[:, pl.ds(j * rows, rows)])
-    if has_prior_s:
+            row_labels.append(labels[:, pl.ds(plain * rows, rows)])
+            plain += 1
+    if with_spectra == "final":
+        for at in range(len(away)):
+            arrive(at)
         moving_s.wait()
     for i, block in enumerate(blocks):
 
         def work(i=i, block=block):
             where = pl.ds(block.first, block.count)
-            glycans = held[i][where]
+            arrive(n_spectra + i)
+            glycans = near[n_spectra + i][...] if away[n_spectra + i] else held[i][where]
             targets = lax.broadcasted_iota(jnp.int32, (block.count, 1), 0).astype(jnp.float32)
             targets = targets + (const(row_of[i]) + float(block.first))
             total = None
             for j in range(block.first_spectra, n_spectra):
+                arrive(j)
                 here = spectra[j][pl.ds(0, rows)]
                 logits = lax.dot_general(
                     glycans, here, (((1,), (1,)), ((), ())), preferred_element_type=jnp.float32
@@ -167,6 +194,8 @@
                         preferred_element_type=jnp.float32,
                     )
                     at = pl.ds(j * rows, rows)
+                    if i == 0 and j == 0 and with_spectra != "final" and has_prior_s:
+                        moving_s.wait()
                     if i > 0 or has_prior_s:
                         s_held[at] += part
                     else:
@@ -176,8 +205,8 @@
                 total = total + prior_held[i][...]
             elif block.prior:
                 total = total + priors[i][where]
-            if block.out == "kept":
-                out_held[i][...] = total
+            if block.out in ("kept", "kept scaled"):
+                out_held[i][...] = scale * total if block.out == "kept scaled" else total
                 leaving.append(move(out_held[i], outs[i]))
             elif block.out == "total":
                 outs[i][...] = total
@@ -225,20 +254,25 @@
     return pltpu.CompilerParams(vmem_limit_bytes=VMEM_BYTES)
 
 
-def pair_work(consts, spectra, labels, blocks, rows, with_spectra=False, prior_s=None):
-    width = spectra[0].shape[1]
+def pair_work(
+    consts, spectra, labels, blocks, rows, with_spectra=False, prior_s=None, cost=SMALL_COST
+):
+    placed = list(spectra) + [b[1] for b in blocks]
+    away = tuple(isinstance(a, Away) for a in placed)
+    placed = [a.array if isinstance(a, Away) else a for a in placed]
+    width = placed[0].shape[1]
     all_rows = rows * len(spectra)
     shapes = tuple(b[0] for b in blocks)
     row_of = tuple(b[2] for b in blocks)
-    plan = (len(spectra), shapes, with_spectra, prior_s is not None, rows, row_of)
+    plan = (shapes, with_spectra, prior_s is not None, rows, row_of, away)
     operands = [in_vmem(consts), in_vmem(labels)]
     in_specs = [VMEM_SPEC, VMEM_SPEC]
     if any(b.optional == "all" for b in shapes):
         operands.append(jnp.stack([jnp.int32(b[3]) for b in blocks]))
         in_specs.append(SMEM_SPEC)
-    for array in list(spectra) + [b[1] for b in blocks]:
-        operands.append(in_vmem(array))
-        in_specs.append(VMEM_SPEC)
+    for array, flag in zip(placed, away):
+        operands.append(in_hbm(array) if flag else in_vmem(array))
+        in_specs.append(HBM_SPEC if flag else VMEM_SPEC)
     for shape, _, _, _, prior in blocks:
         if shape.prior:
             operands.append(in_hbm(prior) if shape.prior == "kept" else in_vmem(prior))
@@ -253,7 +287,7 @@
         if shape.prior == "kept":
             scratch.append(pltpu.VMEM((shape.count, width), jnp.float32))
     for shape in shapes:
-        if shape.out == "kept":
+        if shape.out.startswith("kept"):
             outs.append(hbm_out((shape.count, width), jnp.float32))
             out_specs.append(HBM_SPEC)
             scratch.append(pltpu.VMEM((shape.count, width), jnp.float32))
@@ -270,14 +304,16 @@
         out_specs.append(HBM_SPEC)
     if with_spectra:
         scratch.append(pltpu.VMEM((all_rows, width), jnp.float32))
-    scratch.append(pltpu.SemaphoreType.DMA((2 * len(blocks) + 2,)))
+    counts = [rows] * len(spectra) + [shape.count for shape in shapes]
+    scratch += [pltpu.VMEM((n, width), jnp.bfloat16) for n, flag in zip(counts, away) if flag]
+    scratch.append(pltpu.SemaphoreType.DMA((len(away) + 2 * len(blocks) + 2,)))
     return pl.pallas_call(
         functools.partial(pair_body, plan),
         out_shape=outs,
         in_specs=in_specs,
         out_specs=out_specs,
         scratch_shapes=scratch,
-        cost_estimate=SMALL_COST,
+        cost_estimate=cost,
         compiler_params=params(),
     )(*operands)
 
@@ -288,12 +324,14 @@
     return jnp.pad(digits.astype(jnp.bfloat16), spare)
 
 
-def choose_body(flag, if_true, if_false, tail, out):
+def choose_body(flag, if_true, if_false, tail, out, sem):
     rows = if_true.shape[0]
 
     @pl.when(flag[0] != 0)
     def _():
-        out[pl.ds(0, rows)] = if_true[...]
+        copy = pltpu.make_async_copy(if_true, out.at[pl.ds(0, rows)], sem)
+        copy.start()
+        copy.wait()
 
     @pl.when(flag[0] == 0)
     def _():
@@ -307,56 +345,77 @@
     return pl.pallas_call(
         choose_body,
         out_shape=vmem_out((rows + tail.shape[0], width), if_true.dtype),
-        in_specs=[SMEM_SPEC] + [VMEM_SPEC] * 3,
+        in_specs=[SMEM_SPEC, HBM_SPEC, VMEM_SPEC, VMEM_SPEC],
+        out_specs=VMEM_SPEC,
+        scratch_shapes=[pltpu.SemaphoreType.DMA],
+        cost_estimate=SMALL_COST,
+        compiler_params=params(),
+    )(jnp.int32(flag).reshape(1), in_hbm(if_true), in_vmem(if_false), in_vmem(tail))
+
+
+def add_body(total, arrived, out, *scratch):
+    if scratch:
+        near, sem = scratch
+        copy = pltpu.make_async_copy(total, near, sem)
+        copy.start()
+        copy.wait()
+        total = near
+    out[...] = (total[...] + arrived[...].astype(jnp.float32)).astype(jnp.bfloat16)
+
+
+def add_rounded(total, arrived):
+    away = isinstance(total, Away)
+    scratch = [pltpu.VMEM(arrived.shape, jnp.float32), pltpu.SemaphoreType.DMA] if away else []
+    return pl.pallas_call(
+        add_body,
+        out_shape=vmem_out(arrived.shape, jnp.bfloat16),
+        in_specs=[HBM_SPEC if away else VMEM_SPEC, VMEM_SPEC],
+        out_specs=VMEM_SPEC,
+        scratch_shapes=scratch,
+        cost_estimate=SMALL_COST,
+        compiler_params=params(),
+    )(in_hbm(total.array) if away else in_vmem(total), in_vmem(arrived))
+
+
+def finish_spectra_body(mine_s, *rest):
+    others, out = rest[:-1], rest[-1]
+    at = 0
+    for other in others:
+        where = pl.ds(at, other.shape[0])
+        out[where] = (mine_s[where] + other[...].astype(jnp.float32)).astype(jnp.bfloat16)
+        at += other.shape[0]
+
+
+def finish_spectra(mine_s, others):
+    return pl.pallas_call(
+        finish_spectra_body,
+        out_shape=jax.ShapeDtypeStruct(mine_s.shape, jnp.bfloat16),
+        in_specs=[VMEM_SPEC] * (1 + len(others)),
         out_specs=VMEM_SPEC,
         cost_estimate=SMALL_COST,
         compiler_params=params(),
-    )(jnp.int32(flag).reshape(1), in_vmem(if_true), in_vmem(if_false), in_vmem(tail))
-
-
-def add_body(first, total, arrived, out):
-    where = pl.ds(first, out.shape[0])
-    out[...] = (total[where] + arrived[...].astype(jnp.float32)).astype(jnp.bfloat16)
-
-
-def add_rounded(total, first, arrived):
-    return pl.pallas_call(
-        functools.partial(add_body, first),
-        out_shape=vmem_out(arrived.shape, jnp.bfloat16),
-        in_specs=[VMEM_SPEC] * 2,
-        out_specs=VMEM_SPEC,
-        cost_estimate=SMALL_COST,
-        compiler_params=params(),
-    )(in_vmem(total), in_vmem(arrived))
-
-
-def finish_body(flag, mine_s, here_total, across_back, inside_a, inside_b, *rest):
-    others, (spectra_out, glycans_out) = rest[:-2], rest[-2:]
-    at = 0
-    for other in others:
-        where = pl.ds(at, other.shape[0])
-        spectra_out[where] = (mine_s[where] + other[...].astype(jnp.float32)).astype(jnp.bfloat16)
-        at += other.shape[0]
-
+    )(*[in_vmem(a) for a in [mine_s] + others])
+
+
+def finish_structures_body(flag, here_total, across_back, inside_a, inside_b, out):
     @pl.when(flag[0] != 0)
     def _():
-        glycans_out[pl.ds(0, inside_a.shape[0])] = inside_a[...]
-        glycans_out[pl.ds(inside_a.shape[0], inside_b.shape[0])] = inside_b[...]
+        out[pl.ds(0, inside_a.shape[0])] = inside_a[...]
+        out[pl.ds(inside_a.shape[0], inside_b.shape[0])] = inside_b[...]
 
     @pl.when(flag[0] == 0)
     def _():
         total = here_total[...] + across_back[...].astype(jnp.float32)
-        glycans_out[...] = total.astype(jnp.bfloat16)
-
-
-def finish(flag, mine_s, here_total, across_back, inside_a, inside_b, others):
-    arrays = [mine_s, here_total, across_back, inside_a, inside_b] + others
-    out = jax.ShapeDtypeStruct(mine_s.shape, jnp.bfloat16)
+        out[...] = total.astype(jnp.bfloat16)
+
+
+def finish_structures(flag, here_total, across_back, inside_a, inside_b):
+    arrays = [here_total, across_back, inside_a, inside_b]
     return pl.pallas_call(
-        finish_body,
-        out_shape=[out, out],
+        finish_structures_body,
+        out_shape=jax.ShapeDtypeStruct(here_total.shape, jnp.bfloat16),
         in_specs=[SMEM_SPEC] + [VMEM_SPEC] * len(arrays),
-        out_specs=[VMEM_SPEC, VMEM_SPEC],
+        out_specs=VMEM_SPEC,
         cost_estimate=SMALL_COST,
         compiler_params=params(),
     )(jnp.int32(flag).reshape(1), *[in_vmem(a) for a in arrays])
@@ -372,21 +431,30 @@
     lane_rows = lax.axis_size("sub") * node_rows
 
     def permute(block, pairs):
-        return lax.ppermute(block, "blk", pairs)
+        return lax.ppermute(block, ("blk", "inner"), pairs)
 
     def first_of(block_position):
         return (block_position * lane_rows + core_first).astype(jnp.float32)
 
-    sides = [(0, 1), (1, 0), (2, 3), (3, 2)]
-    middle = [(1, 2), (2, 1), (0, 0), (3, 3)]
+    n_inner = lax.axis_size("inner")
+    last = LINE - 1
+    sides = []
+    middle = []
+    for core in range(n_inner):
+        for at in range(LINE):
+            sides.append((at * n_inner + core, (at ^ 1) * n_inner + core))
+        for at in range(1, last):
+            middle.append((at * n_inner + core, (last - at) * n_inner + core))
+        for at in (0, last):
+            middle.append((at * n_inner + core, at * n_inner + (core + 1) % n_inner))
     here_at, side_at, across_at, far_at = 2, 3, 4, 5
     rows_of_consts = [
         scale,
         shift,
         first_of(position),
         first_of(position ^ 1),
-        first_of(LINE - 1 - position),
-        first_of((LINE - 1 - position) ^ 1),
+        first_of(last - position),
+        first_of((last - position) ^ 1),
         jnp.where(outer, 0.0, 1.0),
     ]
     index = lax.broadcasted_iota(jnp.int32, (8, 128), 0)
@@ -398,12 +466,15 @@
     side = permute(glycans, sides)
     partner = swap_inner(spectra)
     own_labels = labels.reshape(1, rows)
-    node_labels = jnp.concatenate([own_labels, swap_inner(own_labels)], axis=1)
-    node_labels = node_labels.astype(jnp.float32)
-    node = [spectra, partner]
+    partner_labels = swap_inner(own_labels).astype(jnp.float32)
+    own_labels = own_labels.astype(jnp.float32)
+    node_labels = jnp.concatenate([own_labels, partner_labels], axis=1)
+    other_first_labels = jnp.concatenate([partner_labels, own_labels], axis=1)
+    node = [Away(spectra), partner]
+    mine = Away(glycans)
     kept = Block(0, rows, "kept")
     here_g, own_s = pair_work(
-        consts, node, node_labels, [(kept, glycans, here_at, 1, None)], rows, with_spectra=True
+        consts, node, node_labels, [(kept, mine, here_at, 1, None)], rows, with_spectra=True
     )
 
     coded = code_labels(labels, LABEL_ROWS, width)
@@ -416,7 +487,7 @@
         node,
         node_labels,
         [
-            (kept, side, side_at, 1, None),
+            (kept, Away(side), side_at, 1, None),
             (Block(0, rows, "kept", optional="spectra"), across, across_at, 1, None),
         ],
         rows,
@@ -429,8 +500,8 @@
     last_out = permute(far, sides)
     (far_g,) = pair_work(
         consts,
-        node + [mixed],
-        node_labels,
+        [mixed, partner, Away(spectra)],
+        other_first_labels,
         [(Block(0, rows, "total"), far, far_at, 1, None)],
         rows,
     )
@@ -448,26 +519,39 @@
         ends,
         node_labels,
         [
-            (Block(first_part, rows - first_part, "rounded", "near", first_spectra=1), after(far, far_a), far_at, 1, far_g),
+            (
+                Block(first_part, rows - first_part, "rounded", "near", first_spectra=1),
+                after(far, far_a),
+                far_at,
+                1,
+                far_g,
+            ),
             (Block(0, rows, "rounded", "kept"), across, across_at, 1, across_g),
         ],
         rows,
     )
     back_b = permute(far_b, middle)
-    side_total, here_total = pair_work(
+    late_side = Away(after(side, far_b))
+    side_total_a, side_total_b = pair_work(
         consts,
         ends,
         node_labels,
         [
-            (Block(0, rows, "scaled", "kept"), after(side, far_b), side_at, 1, side_g),
-            (Block(0, rows, "scaled", "kept"), glycans, here_at, 1, here_g),
+            (Block(0, first_part, "scaled", "kept"), late_side, side_at, 1, side_g),
+            (
+                Block(first_part, rows - first_part, "kept scaled", "kept"),
+                late_side,
+                side_at,
+                1,
+                side_g,
+            ),
         ],
         rows,
     )
-    total_a = add_rounded(side_total, 0, back_a)
+    total_a = add_rounded(side_total_a, back_a)
     inside_a = permute(total_a, sides)
     across_back = permute(after(across_out, total_a), middle)
-    total_b = add_rounded(side_total, first_part, after(back_b, total_a))
+    total_b = add_rounded(Away(side_total_b), after(back_b, total_a))
     inside_b = permute(total_b, sides)
 
     only_s = Block(0, rows, "", optional="all")
@@ -486,7 +570,20 @@
     )
     piece = -(-rows // 48) * 16
     others = [swap_inner(other_s[at : at + piece]) for at in range(0, rows, piece)]
-    return finish(outer, mine_s, here_total, across_back, inside_a, inside_b, others)
+    inside_a, late_mine = lax.optimization_barrier((inside_a, glycans))
+    flops = 2 * 2 * 2 * rows * rows * width
+    (here_total,) = pair_work(
+        consts,
+        ends,
+        node_labels,
+        [(Block(0, rows, "scaled", "kept"), Away(late_mine), here_at, 1, here_g)],
+        rows,
+        cost=pl.CostEstimate(flops=flops, bytes_accessed=8 * rows * width, transcendentals=0),
+    )
+    others[0] = after(others[0], inside_b, here_total)
+    grad_spectra = finish_spectra(mine_s, others)
+    across_back = after(across_back, grad_spectra)
+    return grad_spectra, finish_structures(outer, here_total, across_back, inside_a, inside_b)
 
 
 def local(

time: 85.3 us -> 77.1 us (0.904)
  starting transfers between devices: 25.6 us -> 17.2 us
  Pallas kernels: 32.5 us -> 40.6 us
  local copies, waits for them, and re-layouts: 9.32 us -> 2.31 us
    ppermute x10, starting transfers between devices: 24.3 us -> 16 us  [permute(): return lax.ppermute(block, ('blk', 'inner'), pairs)]
    unnamed x26 -> x6, local copies, waits for them, and re-layouts: 8.57 us -> 1.57 us
    pallas_call x7 -> x8, Pallas kernels: 30 us -> 35.5 us  [pair_work(): pl.pallas_call(functools.partial(pair_body, plan), out_shape=outs, in_spe...]
    ppermute x6, waiting for transfers between devices: 2.19 us -> 0.02 us  [from_behind(): return lax.ppermute(block, axis, route)]
    ppermute x10, waiting for transfers between devices: 11.4 us -> 13.2 us  [permute(): return lax.ppermute(block, ('blk', 'inner'), pairs)]
    pallas_call x3 -> x4, Pallas kernels: 2.43 us -> 4 us  [the longest x2 2.17 us: add_rounded(): pl.pallas_call(add_body, out_shape=vmem_out(arrived.shape, jnp.bfloat16),...]
    pallas_call x1, Pallas kernels: 0.05 us -> 1.16 us  [choose(): pl.pallas_call(choose_body, out_shape=vmem_out((rows + tail.shape[0], wid...]
  transfers between devices with their start and end apart: 16 -> 16, of which waited for: 6 -> 2; matrix products, arithmetic and copies ran while one was open for 2% -> 2% of each run, Pallas kernels for 36% -> 50%
where the time goes in v5:
time: 77.1 us; the launch traced here: 76.6 us
  Pallas kernels  40.6 us (53%)
  starting transfers between devices  17.2 us (22%)
  waiting for transfers between devices  13.2 us (17%)
  local copies, waits for them, and re-layouts  2.31 us (3%)
  between operations  2.22 us (3%)
  other arithmetic  1.05 us (1%)
    pallas_call x8, Pallas kernels, pair_work(): pl.pallas_call(functools.partial(pair_body, plan), out_shape=outs, in_spe...  35.5 us
    ppermute x10, starting transfers between devices, permute(): return lax.ppermute(block, ('blk', 'inner'), pairs)  16 us
    ppermute x10, waiting for transfers between devices, permute(): return lax.ppermute(block, ('blk', 'inner'), pairs)  13.2 us
    pallas_call x2, Pallas kernels, add_rounded(): pl.pallas_call(add_body, out_shape=vmem_out(arrived.shape, jnp.bfloat16),...  2.17 us
    unnamed x6, local copies, waits for them, and re-layouts  1.57 us
  transfers between devices with their start and end apart: 16, of which 2 were waited for; matrix products, arithmetic and copies ran while one was open for 2% of the time, Pallas kernels for 50%

profile of v5, /device:TPU:0, one launch (start us, length us, event | category | flops | bytes accessed | tf_op | source)
XLA Modules:
  0.0 76.6 jit_solution(2953548455681520638)
XLA Ops:
  0.6 3.1 %collective-permute-start.3 = (bf16[320,1024]{1,0:T(8,128)(2,1)}, bf16[320,1024]{1,0:T(8,128)(2,1)S(1)}, u32[]{:S(2)}, u32[]{:S(2)}) collective-permute-start(bf16[320,1024]{1,0:T(8,128)(2,1)} %refs_4_.4), channel_id=1, source_target_pairs={{0,4},{4,0},{8,12},{12,8},{1,5},{5,1},{9,13},{13,9},{2,6},{6,2},{1... | collective-permute-start | bytes 1966088 | tf_op jit(solution)/shard_map/ppermute | solution.py:434
  3.7 0.7 reshape.10
  4.4 0.5 collective-permute-start
  4.9 0.8 %fusion.10 = (bf16[320]{0:T(512)(128)(2,1)S(1)}, bf16[320]{0:T(512)(128)(2,1)S(1)}, f32[320]{0:T(512)S(1)}, bf16[320]{0:T(512)(128)(2,1)S(1)}) fusion(s32[320]{0:T(512)} %param.7), kind=kLoop, calls=%fused_computation.26 | loop fusion | flops 14080 | bytes 4480 | tf_op jit(solution)/shard_map/convert.7
  7.1 0.1 select_select_fusion.refs_0_
  7.2 0.1 pad_maximum_fusion.1
  7.3 5.6 %shard_map.68 = (f32[320,1024]{1,0:T(8,128)}, f32[640,1024]{1,0:T(8,128)}) custom-call(f32[8,128]{1,0:T(8,128)S(1)} %select_select_fusion.refs_0_, f32[1,640]{1,0:T(1,128)S(1)} %get-tuple-element.53.refs_1_, bf16[320,1024]{1,0:T(8,128)(2,1)} %refs_3_.1, bf16[320,1024]{1,0:T(8,128)(2,1)S(1)} %collective-permute-done.1.refs_3_.refs_4_, bf16[320,1024]{1,0:T(8,128)(2,1)} %refs_4_.4), custom_call_target="tpu_custom_call" | custom-call | flops 1024 | bytes 1024 | tf_op jit(solution)/shard_map/pallas_call | solution.py:310
  12.9 5.8 %collective-permute-done.3.refs_4_.refs_5_ = bf16[320,1024]{1,0:T(8,128)(2,1)S(1)} collective-permute-done((bf16[320,1024]{1,0:T(8,128)(2,1)}, bf16[320,1024]{1,0:T(8,128)(2,1)S(1)}, u32[]{:S(2)}, u32[]{:S(2)}) %collective-permute-start.3) | collective-permute-done | bytes 655392 | tf_op jit(solution)/shard_map/ppermute | solution.py:434
  18.7 0.8 %copy-done.1 = bf16[320,1024]{1,0:T(8,128)(2,1)} copy-done((bf16[320,1024]{1,0:T(8,128)(2,1)}, bf16[320,1024]{1,0:T(8,128)(2,1)S(1)}, u32[]{:S(2)}) %copy-start.1) | copy-done | bytes 655384
  19.5 1.2 %shard_map.69 = bf16[336,1024]{1,0:T(8,128)(2,1)S(1)} custom-call(s32[1]{0:T(128)} %bitcast.3.flag, bf16[320,1024]{1,0:T(8,128)(2,1)} %refs_3_.1, bf16[320,1024]{1,0:T(8,128)(2,1)S(1)} %collective-permute-done.2.if_false.refs_5_, bf16[16,1024]{1,0:T(8,128)(2,1)S(1)} %fusion.8.tail), custom_call_target="tpu_custom_call" | custom-call | flops 1024 | bytes 1024 | tf_op jit(solution)/shard_map/pallas_call | solution.py:345
  20.7 1.2 %collective-permute-start.4 = (bf16[336,1024]{1,0:T(8,128)(2,1)S(1)}, bf16[336,1024]{1,0:T(8,128)(2,1)S(1)}, u32[]{:S(2)}, u32[]{:S(2)}) collective-permute-start(bf16[336,1024]{1,0:T(8,128)(2,1)S(1)} %shard_map.69), channel_id=1, source_target_pairs={{0,4},{4,0},{8,12},{12,8},{1,5},{5,1},{9,13},{13,9},{2,6},{6,2},{1... | collective-permute-start | bytes 2064392 | tf_op jit(solution)/shard_map/ppermute | solution.py:434
  21.9 8.1 %shard_map.70 = (f32[320,1024]{1,0:T(8,128)}, f32[320,1024]{1,0:T(8,128)}, f32[640,1024]{1,0:T(8,128)}) custom-call(f32[8,128]{1,0:T(8,128)S(1)} %select_select_fusion.refs_0_, f32[1,640]{1,0:T(1,128)S(1)} %get-tuple-element.53.refs_1_, bf16[320,1024]{1,0:T(8,128)(2,1)} %refs_3_.1, bf16[320,1024]{1,0:T(8,128)(2,1)S(1)} %collective-permute-done.1.refs_3_.refs_4_, ...), custom_call_target="tpu_custom_call" | custom-call | flops 1024 | bytes 1024 | tf_op jit(solution)/shard_map/pallas_call | solution.py:310
  30.0 7.4 %collective-permute-done.4.refs_2_.refs_6_ = bf16[336,1024]{1,0:T(8,128)(2,1)S(1)} collective-permute-done((bf16[336,1024]{1,0:T(8,128)(2,1)S(1)}, bf16[336,1024]{1,0:T(8,128)(2,1)S(1)}, u32[]{:S(2)}, u32[]{:S(2)}) %collective-permute-start.4) | collective-permute-done | bytes 688160 | tf_op jit(solution)/shard_map/ppermute | solution.py:434
  37.4 1.9 %collective-permute-start.9 = (bf16[320,1024]{1,0:T(8,128)(2,1)S(1)}, bf16[320,1024]{1,0:T(8,128)(2,1)}, u32[]{:S(2)}, u32[]{:S(2)}) collective-permute-start(bf16[320,1024]{1,0:T(8,128)(2,1)S(1)} %collective-permute-done.5.refs_5_.refs_3_.refs_4_), channel_id=1, source_target_pairs={{0,4},{4,0},{8,12},{12,8},{1,5},{5,1},{9,13},{13,9},{2,6},{6,2},{1... | collective-permute-start | bytes 1966088 | tf_op jit(solution)/shard_map/ppermute | solution.py:434
  39.2 2.9 %shard_map.71.refs_4_.refs_6_ = f32[320,1024]{1,0:T(8,128)S(1)} custom-call(f32[8,128]{1,0:T(8,128)S(1)} %select_select_fusion.refs_0_, f32[1,640]{1,0:T(1,128)S(1)} %get-tuple-element.52.refs_1_, bf16[336,1024]{1,0:T(8,128)(2,1)S(1)} %collective-permute-done.4.refs_2_.refs_6_, bf16[320,1024]{1,0:T(8,128)(2,1)S(1)} %collective-permute-done.1.refs_3_.refs_4_, ...), custom_call_target="tpu_custom_call" | custom-call | flops 1024 | bytes 1024 | tf_op jit(solution)/shard_map/pallas_call | solution.py:310
  42.2 0.9 %shard_map.72 = bf16[176,1024]{1,0:T(8,128)(2,1)S(1)} custom-call(f32[8,128]{1,0:T(8,128)S(1)} %select_select_fusion.refs_0_, f32[1,640]{1,0:T(1,128)S(1)} %get-tuple-element.53.refs_1_, bf16[336,1024]{1,0:T(8,128)(2,1)S(1)} %collective-permute-done.6.refs_2_.refs_3_, bf16[320,1024]{1,0:T(8,128)(2,1)S(1)} %collective-permute-done.5.refs_5_.refs_3_.refs_4_, ...), custom_call_target="tpu_custom_call" | custom-call | flops 1024 | bytes 1024 | tf_op jit(solution)/shard_map/pallas_call | solution.py:310
  43.1 0.3 collective-permute-start.8
  43.4 3.6 %shard_map.73 = (bf16[144,1024]{1,0:T(8,128)(2,1)}, bf16[320,1024]{1,0:T(8,128)(2,1)}) custom-call(f32[8,128]{1,0:T(8,128)S(1)} %select_select_fusion.refs_0_, f32[1,640]{1,0:T(1,128)S(1)} %get-tuple-element.53.refs_1_, bf16[336,1024]{1,0:T(8,128)(2,1)S(1)} %collective-permute-done.4.refs_2_.refs_6_, ...), custom_call_target="tpu_custom_call" | custom-call | flops 1024 | bytes 1024 | tf_op jit(solution)/shard_map/pallas_call | solution.py:310
  47.0 0.3 collective-permute-start.7
  47.3 4.1 %shard_map.74 = (f32[176,1024]{1,0:T(8,128)S(1)}, f32[144,1024]{1,0:T(8,128)}) custom-call(f32[8,128]{1,0:T(8,128)S(1)} %select_select_fusion.refs_0_, f32[1,640]{1,0:T(1,128)S(1)} %get-tuple-element.53.refs_1_, bf16[336,1024]{1,0:T(8,128)(2,1)S(1)} %collective-permute-done.4.refs_2_.refs_6_, bf16[336,1024]{1,0:T(8,128)(2,1)S(1)} %collective-permute-done.6.refs_2_.refs_3_, ...), custom_call_target="tpu_custom_call" | custom-call | flops 1024 | bytes 1024 | tf_op jit(solution)/shard_map/pallas_call | solution.py:310
  51.4 0.1 shard_map.75
  51.5 0.7 copy-done
  52.3 0.2 collective-permute-start.15
  52.5 5.4 %collective-permute-start.12 = (bf16[176,1024]{1,0:T(8,128)(2,1)}, bf16[176,1024]{1,0:T(8,128)(2,1)S(1)}, u32[]{:S(2)}, u32[]{:S(2)}) collective-permute-start(bf16[176,1024]{1,0:T(8,128)(2,1)} %copy-done), channel_id=1, source_target_pairs={{0,4},{4,0},{8,12},{12,8},{1,5},{5,1},{9,13},{13,9},{2,6},{6,2},{1... | collective-permute-start | bytes 1081352 | tf_op jit(solution)/shard_map/ppermute | solution.py:434
  58.0 2.1 %shard_map.76 = bf16[144,1024]{1,0:T(8,128)(2,1)S(1)} custom-call(f32[144,1024]{1,0:T(8,128)} %get-tuple-element.38.total, bf16[144,1024]{1,0:T(8,128)(2,1)} %collective-permute-done.7.arrived), custom_call_target="tpu_custom_call" | custom-call | flops 1024 | bytes 1024 | tf_op jit(solution)/shard_map/pallas_call | solution.py:369
  60.1 3.5 %collective-permute-start.11 = (bf16[144,1024]{1,0:T(8,128)(2,1)S(1)}, bf16[144,1024]{1,0:T(8,128)(2,1)S(1)}, u32[]{:S(2)}, u32[]{:S(2)}) collective-permute-start(bf16[144,1024]{1,0:T(8,128)(2,1)S(1)} %shard_map.76), channel_id=1, source_target_pairs={{0,4},{4,0},{8,12},{12,8},{1,5},{5,1},{9,13},{13,9},{2,6},{6,2},{1... | collective-permute-start | bytes 884744 | tf_op jit(solution)/shard_map/ppermute | solution.py:434
  63.6 7.5 %shard_map.77 = (f32[320,1024]{1,0:T(8,128)S(1)}, bf16[320,1024]{1,0:T(8,128)(2,1)S(1)}) custom-call(f32[8,128]{1,0:T(8,128)S(1)} %select_select_fusion.refs_0_, f32[1,640]{1,0:T(1,128)S(1)} %get-tuple-element.53.refs_1_, s32[3]{0:T(128)S(1)} %pad_add_fusion.refs_2_, bf16[320,1024]{1,0:T(8,128)(2,1)} %refs_3_.1, ...), custom_call_target="tpu_custom_call" | custom-call | flops 1024 | bytes 1024 | tf_op jit(solution)/shard_map/pallas_call | solution.py:310
  71.2 0.5 collective-permute-start.13
  71.8 0.1 collective-permute-start.14
  71.9 2.8 %shard_map.78.here_total = f32[320,1024]{1,0:T(8,128)S(1)} custom-call(f32[8,128]{1,0:T(8,128)S(1)} %select_select_fusion.refs_0_, f32[1,640]{1,0:T(1,128)S(1)} %get-tuple-element.53.refs_1_, bf16[336,1024]{1,0:T(8,128)(2,1)S(1)} %collective-permute-done.4.refs_2_.refs_6_, bf16[336,1024]{1,0:T(8,128)(2,1)S(1)} %collective-permute-done.6.refs_2_.refs_3_, ...), custom_call_target="tpu_custom_call" | custom-call | flops 838860800 | bytes 2621440 | tf_op jit(solution)/shard_map/pallas_call | solution.py:310
  74.8 0.9 %shard_map.79 = bf16[320,1024]{1,0:T(8,128)(2,1)} custom-call(f32[320,1024]{1,0:T(8,128)S(1)} %get-tuple-element.42.mine_s, bf16[112,1024]{1,0:T(8,128)(2,1)S(1)} %collective-permute-done.10.rest_0_, bf16[112,1024]{1,0:T(8,128)(2,1)S(1)} %collective-permute-done.13.rest_1_, bf16[96,1024]{1,0:T(8,128)(2,1)S(1)} %collective-permute-done.14.rest_2_), custom_call_target="tpu_custom_call" | custom-call | flops 1024 | bytes 1024 | tf_op jit(solution)/shard_map/pallas_call | solution.py:390
  75.7 0.9 %shard_map.80 = bf16[320,1024]{1,0:T(8,128)(2,1)} custom-call(s32[1]{0:T(128)} %bitcast.3.flag, f32[320,1024]{1,0:T(8,128)S(1)} %shard_map.78.here_total, bf16[320,1024]{1,0:T(8,128)(2,1)S(1)} %collective-permute-done.15.across_back, bf16[176,1024]{1,0:T(8,128)(2,1)S(1)} %collective-permute-done.12.inside_a, ...), custom_call_target="tpu_custom_call" | custom-call | flops 1024 | bytes 1024 | tf_op jit(solution)/shard_map/pallas_call | solution.py:414
  (36 shorter events, 0.3 us)
Async XLA Ops:
  0.6 18.0 %collective-permute-start.3 = (bf16[320,1024]{1,0:T(8,128)(2,1)}, bf16[320,1024]{1,0:T(8,128)(2,1)S(1)}, u32[]{:S(2)}, u32[]{:S(2)}) collective-permute-start(bf16[320,1024]{1,0:T(8,128)(2,1)} %refs_4_.4), channel_id=1, source_target_pairs={{0,4},{4,0},{8,12},{12,8},{1,5},{5,1},{9,13},{13,9},{2,6},{6,2},{1... | collective-permute-start | bytes 1966088 | tf_op jit(solution)/shard_map/ppermute | solution.py:434
  3.7 14.9 %collective-permute-start.2 = (bf16[320,1024]{1,0:T(8,128)(2,1)}, bf16[320,1024]{1,0:T(8,128)(2,1)S(1)}, u32[]{:S(2)}, u32[]{:S(2)}) collective-permute-start(bf16[320,1024]{1,0:T(8,128)(2,1)} %refs_4_.4), channel_id=1, source_target_pairs={{4,8},{8,4},{0,1},{12,13},{5,9},{9,5},{1,0},{13,12},{6,10},{10,6},... | collective-permute-start | bytes 1966088 | tf_op jit(solution)/shard_map/ppermute | solution.py:434
  4.4 2.8 %collective-permute-start = (s32[1,320]{1,0:T(1,128)S(1)}, s32[1,320]{1,0:T(1,128)S(1)}, u32[]{:S(2)}, u32[]{:S(2)}) collective-permute-start(s32[1,320]{1,0:T(1,128)S(1)} %reshape.10), channel_id=1, source_target_pairs={{1,0},{0,1},{3,2},{2,3},{5,4},{4,5},{7,6},{6,7},{9,8},{8,9},{11,10... | collective-permute-start | bytes 3848 | tf_op jit(solution)/shard_map/ppermute | solution.py:21
  4.9 2.4 %collective-permute-start.1 = (bf16[320,1024]{1,0:T(8,128)(2,1)}, bf16[320,1024]{1,0:T(8,128)(2,1)S(1)}, u32[]{:S(2)}, u32[]{:S(2)}) collective-permute-start(bf16[320,1024]{1,0:T(8,128)(2,1)} %refs_3_.1), channel_id=1, source_target_pairs={{1,0},{0,1},{3,2},{2,3},{5,4},{4,5},{7,6},{6,7},{9,8},{8,9},{11,10... | collective-permute-start | bytes 1966088 | tf_op jit(solution)/shard_map/ppermute | solution.py:21
  18.7 0.8 %copy-start.1 = (bf16[320,1024]{1,0:T(8,128)(2,1)}, bf16[320,1024]{1,0:T(8,128)(2,1)S(1)}, u32[]{:S(2)}) copy-start(bf16[320,1024]{1,0:T(8,128)(2,1)S(1)} %collective-permute-done.3.refs_4_.refs_5_) | copy-start | bytes 1966084
  19.5 2.4 %copy-start.2 = (bf16[320,1024]{1,0:T(8,128)(2,1)S(1)}, bf16[320,1024]{1,0:T(8,128)(2,1)}, u32[]{:S(2)}) copy-start(bf16[320,1024]{1,0:T(8,128)(2,1)} %copy-done.1) | copy-start | bytes 1966084
  20.7 16.7 %collective-permute-start.4 = (bf16[336,1024]{1,0:T(8,128)(2,1)S(1)}, bf16[336,1024]{1,0:T(8,128)(2,1)S(1)}, u32[]{:S(2)}, u32[]{:S(2)}) collective-permute-start(bf16[336,1024]{1,0:T(8,128)(2,1)S(1)} %shard_map.69), channel_id=1, source_target_pairs={{0,4},{4,0},{8,12},{12,8},{1,5},{5,1},{9,13},{13,9},{2,6},{6,2},{1... | collective-permute-start | bytes 2064392 | tf_op jit(solution)/shard_map/ppermute | solution.py:434
  21.9 8.1 %collective-permute-start.5 = (bf16[320,1024]{1,0:T(8,128)(2,1)S(1)}, bf16[320,1024]{1,0:T(8,128)(2,1)S(1)}, u32[]{:S(2)}, u32[]{:S(2)}) collective-permute-start(bf16[320,1024]{1,0:T(8,128)(2,1)S(1)} %copy-done.2), channel_id=1, source_target_pairs={{4,8},{8,4},{0,1},{12,13},{5,9},{9,5},{1,0},{13,12},{6,10},{10,6},... | collective-permute-start | bytes 1966088 | tf_op jit(solution)/shard_map/ppermute | solution.py:434
  37.4 4.8 %collective-permute-start.6 = (bf16[336,1024]{1,0:T(8,128)(2,1)S(1)}, bf16[336,1024]{1,0:T(8,128)(2,1)S(1)}, u32[]{:S(2)}, u32[]{:S(2)}) collective-permute-start(bf16[336,1024]{1,0:T(8,128)(2,1)S(1)} %collective-permute-done.4.refs_2_.refs_6_), channel_id=1, source_target_pairs={{1,0},{0,1},{3,2},{2,3},{5,4},{4,5},{7,6},{6,7},{9,8},{8,9},{11,10... | collective-permute-start | bytes 2064392 | tf_op jit(solution)/shard_map/ppermute | solution.py:21
  37.4 26.3 %collective-permute-start.9 = (bf16[320,1024]{1,0:T(8,128)(2,1)S(1)}, bf16[320,1024]{1,0:T(8,128)(2,1)}, u32[]{:S(2)}, u32[]{:S(2)}) collective-permute-start(bf16[320,1024]{1,0:T(8,128)(2,1)S(1)} %collective-permute-done.5.refs_5_.refs_3_.refs_4_), channel_id=1, source_target_pairs={{0,4},{4,0},{8,12},{12,8},{1,5},{5,1},{9,13},{13,9},{2,6},{6,2},{1... | collective-permute-start | bytes 1966088 | tf_op jit(solution)/shard_map/ppermute | solution.py:434
  43.1 8.4 %collective-permute-start.8 = (bf16[176,1024]{1,0:T(8,128)(2,1)S(1)}, bf16[176,1024]{1,0:T(8,128)(2,1)S(1)}, u32[]{:S(2)}, u32[]{:S(2)}) collective-permute-start(bf16[176,1024]{1,0:T(8,128)(2,1)S(1)} %shard_map.72), channel_id=1, source_target_pairs={{4,8},{8,4},{0,1},{12,13},{5,9},{9,5},{1,0},{13,12},{6,10},{10,6},... | collective-permute-start | bytes 1081352 | tf_op jit(solution)/shard_map/ppermute | solution.py:434
  47.0 11.0 %collective-permute-start.7 = (bf16[144,1024]{1,0:T(8,128)(2,1)}, bf16[144,1024]{1,0:T(8,128)(2,1)}, u32[]{:S(2)}, u32[]{:S(2)}) collective-permute-start(bf16[144,1024]{1,0:T(8,128)(2,1)} %get-tuple-element.35), channel_id=1, source_target_pairs={{4,8},{8,4},{0,1},{12,13},{5,9},{9,5},{1,0},{13,12},{6,10},{10,6},... | collective-permute-start | bytes 884744 | tf_op jit(solution)/shard_map/ppermute | solution.py:434
  51.5 0.7 copy-start
  52.3 23.5 %collective-permute-start.15 = (bf16[320,1024]{1,0:T(8,128)(2,1)}, bf16[320,1024]{1,0:T(8,128)(2,1)S(1)}, u32[]{:S(2)}, u32[]{:S(2)}) collective-permute-start(bf16[320,1024]{1,0:T(8,128)(2,1)} %get-tuple-element.47), channel_id=1, source_target_pairs={{4,8},{8,4},{0,1},{12,13},{5,9},{9,5},{1,0},{13,12},{6,10},{10,6},... | collective-permute-start | bytes 1966088 | tf_op jit(solution)/shard_map/ppermute | solution.py:434
  52.5 19.3 %collective-permute-start.12 = (bf16[176,1024]{1,0:T(8,128)(2,1)}, bf16[176,1024]{1,0:T(8,128)(2,1)S(1)}, u32[]{:S(2)}, u32[]{:S(2)}) collective-permute-start(bf16[176,1024]{1,0:T(8,128)(2,1)} %copy-done), channel_id=1, source_target_pairs={{0,4},{4,0},{8,12},{12,8},{1,5},{5,1},{9,13},{13,9},{2,6},{6,2},{1... | collective-permute-start | bytes 1081352 | tf_op jit(solution)/shard_map/ppermute | solution.py:434
  60.1 14.7 %collective-permute-start.11 = (bf16[144,1024]{1,0:T(8,128)(2,1)S(1)}, bf16[144,1024]{1,0:T(8,128)(2,1)S(1)}, u32[]{:S(2)}, u32[]{:S(2)}) collective-permute-start(bf16[144,1024]{1,0:T(8,128)(2,1)S(1)} %shard_map.76), channel_id=1, source_target_pairs={{0,4},{4,0},{8,12},{12,8},{1,5},{5,1},{9,13},{13,9},{2,6},{6,2},{1... | collective-permute-start | bytes 884744 | tf_op jit(solution)/shard_map/ppermute | solution.py:434
  71.1 3.6 %collective-permute-start.10 = (bf16[112,1024]{1,0:T(8,128)(2,1)S(1)}, bf16[112,1024]{1,0:T(8,128)(2,1)S(1)}, u32[]{:S(2)}, u32[]{:S(2)}) collective-permute-start(bf16[112,1024]{1,0:T(8,128)(2,1)S(1)} %get-tuple-element.51), channel_id=1, source_target_pairs={{1,0},{0,1},{3,2},{2,3},{5,4},{4,5},{7,6},{6,7},{9,8},{8,9},{11,10... | collective-permute-start | bytes 688136 | tf_op jit(solution)/shard_map/ppermute | solution.py:21
  71.2 3.6 %collective-permute-start.13 = (bf16[112,1024]{1,0:T(8,128)(2,1)S(1)}, bf16[112,1024]{1,0:T(8,128)(2,1)S(1)}, u32[]{:S(2)}, u32[]{:S(2)}) collective-permute-start(bf16[112,1024]{1,0:T(8,128)(2,1)S(1)} %get-tuple-element.50), channel_id=1, source_target_pairs={{1,0},{0,1},{3,2},{2,3},{5,4},{4,5},{7,6},{6,7},{9,8},{8,9},{11,10... | collective-permute-start | bytes 688136 | tf_op jit(solution)/shard_map/ppermute | solution.py:21
  71.8 3.0 %collective-permute-start.14 = (bf16[96,1024]{1,0:T(8,128)(2,1)S(1)}, bf16[96,1024]{1,0:T(8,128)(2,1)S(1)}, u32[]{:S(2)}, u32[]{:S(2)}) collective-permute-start(bf16[96,1024]{1,0:T(8,128)(2,1)S(1)} %slice.11), channel_id=1, source_target_pairs={{1,0},{0,1},{3,2},{2,3},{5,4},{4,5},{7,6},{6,7},{9,8},{8,9},{11,10... | collective-permute-start | bytes 589832 | tf_op jit(solution)/shard_map/ppermute | solution.py:21

commit v6 on v5

v6 whole, which is shorter than its diff:
```python
import dataclasses
import functools

import jax
import jax.numpy as jnp
from jax import lax
from jax.experimental import pallas as pl
from jax.experimental.pallas import tpu as pltpu
from jax.sharding import PartitionSpec as P

STEPS = 4
LINE = 4
LABEL_ROWS = 16
KEEP_ROW = 6
VMEM_BYTES = 20 * 1024 * 1024


def from_behind(block, axis, distance):
    devices = range(lax.axis_size(axis))
    route = [((i - distance) % len(devices), i) for i in devices]
    return lax.ppermute(block, axis, route)


def swap_inner(block):
    return from_behind(block, "inner", 1)


def after(value, *earlier):
    return lax.optimization_barrier((value,) + earlier)[0]


def coefficients(spectra, glycans, labels, first_target, scale, shift):
    logits = (
        scale
        * lax.dot_general(
            spectra, glycans, (((1,), (1,)), ((), ())), preferred_element_type=jnp.float32
        )
        + shift
    )
    targets = first_target + jnp.arange(glycans.shape[0], dtype=jnp.int32)
    positive = (labels[:, None] == targets[None, :]).astype(jnp.float32)
    return (jax.nn.sigmoid(logits) - positive).astype(jnp.bfloat16)


def around_ring(spectra, glycans, labels, scale, shift):
    rows_here = spectra.shape[0]
    node_rows = rows_here * lax.axis_size("inner")
    loop_count = lax.axis_size("blk")
    position = lax.axis_index("blk")
    core_first = lax.axis_index("sub") * node_rows + lax.axis_index("inner") * rows_here
    lane_rows = lax.axis_size("sub") * node_rows
    node_spectra = jnp.concatenate([spectra, swap_inner(spectra)])
    node_labels = jnp.concatenate([labels, swap_inner(labels)])
    spectrum_total = 0.0
    glycan_total = 0.0
    held = glycans
    for step in range(STEPS):
        if step > 0:
            held = from_behind(held, "blk", 1)
        first_target = (position - step) % loop_count * lane_rows + core_first
        coef = coefficients(node_spectra, held, node_labels, first_target, scale, shift)
        spectrum_total += jnp.dot(coef, held, preferred_element_type=jnp.float32)
        partial_value = scale * lax.dot_general(
            coef, node_spectra, (((0,), (0,)), ((), ())), preferred_element_type=jnp.float32
        )
        if step > 0:
            back = from_behind(partial_value.astype(jnp.bfloat16), "blk", -step)
            partial_value = back.astype(jnp.float32)
        glycan_total += partial_value
    other = swap_inner((scale * spectrum_total[rows_here:]).astype(jnp.bfloat16))
    spectrum_total = scale * spectrum_total[:rows_here] + other.astype(jnp.float32)
    return spectrum_total.astype(jnp.bfloat16), glycan_total.astype(jnp.bfloat16)


@dataclasses.dataclass(frozen=True)
class Away:
    array: jax.Array


@dataclasses.dataclass(frozen=True)
class Block:
    target: int
    uses: tuple
    out: str
    start: int = 0
    count: int = 0
    prior: str = ""
    optional: str = ""


@dataclasses.dataclass(frozen=True)
class Plan:
    blocks: tuple
    pieces: tuple
    node: bool
    ends: tuple
    gradient: str
    prior_s: bool
    rows: int


def pair_body(plan, *refs):
    refs = list(refs)
    blocks, rows = plan.blocks, plan.rows
    half = rows // 2

    def take(count):
        taken = refs[:count]
        del refs[:count]
        return taken

    def take_if(condition):
        return take(1)[0] if condition else None

    (consts,) = take(1)
    labels = take_if(plan.node)
    flags = take_if(any(b.optional == "all" for b in blocks))
    node_in = take(2) if plan.node else []
    ends_in = take(len(plan.ends))
    held_in = [take(len(p)) for p in plan.pieces]
    priors = [take_if(b.prior) for b in blocks]
    prior_s = take_if(plan.prior_s)
    outs = [take((b.out != "") + (b.out == "split")) for b in blocks]
    if plan.gradient == "final":
        mine_out, other_out = take(2)
    elif plan.gradient:
        (s_out,) = take(1)
    spectra = take_if(plan.node)
    ends = take_if(plan.ends)
    held = take(len(blocks))
    prior_held = [take_if(b.prior == "kept") for b in blocks]
    out_held = [take_if(b.out in ("kept", "split")) for b in blocks]
    s_held = take_if(plan.gradient)
    (sems,) = take(1)
    used = 0

    def move(source, target):
        nonlocal used
        copy = pltpu.make_async_copy(source, target, sems.at[used])
        copy.start()
        used += 1
        return copy

    moving_node = [move(ref, spectra.at[pl.ds(i * rows, rows)]) for i, ref in enumerate(node_in)]
    moving = []
    for i, block in enumerate(blocks):
        moves = []
        at = 0
        for ref, (count, away) in zip(held_in[i], plan.pieces[i]):
            if away:
                part = ref.at[pl.ds(block.start, count)]
                moves.append(move(part, held[i].at[pl.ds(at, count)]))
            at += count
        moving.append(moves)
    moving_prior = [
        move(priors[i], prior_held[i]) if b.prior == "kept" else None for i, b in enumerate(blocks)
    ]
    moving_s = move(prior_s, s_held) if plan.prior_s else None
    leaving = []

    def const(row):
        return consts[pl.ds(row, 1), pl.ds(0, 1)]

    scale, shift = const(0), const(1)
    if plan.ends:
        width = 2 * rows
        at = 0
        coded = []
        for ref, count in zip(ends_in, plan.ends):
            ending = at % rows + count > rows
            keep = count - LABEL_ROWS if ending else count
            ends[pl.ds(at, keep)] = ref[pl.ds(0, keep)]
            at += keep
            if ending:
                digits = ref[pl.ds(keep, LABEL_ROWS), pl.ds(0, width)].astype(jnp.float32)
                coded.append(digits[0:1] * 16384.0 + digits[1:2] * 128.0 + digits[2:3])
        lane = lax.broadcasted_iota(jnp.int32, (1, width), 1)
        end_labels = jnp.where(lane >= rows, coded[1], coded[0])

    def source(use):
        if use == "node":
            while moving_node:
                moving_node.pop(0).wait()
            return spectra[...], labels[...]
        return ends[...], end_labels

    if plan.gradient == "final":
        for copy in moving_node + [c for moves in moving for c in moves] + [moving_s]:
            copy.wait()
        moving_node, moving, moving_s = [], [[] for _ in blocks], None
    for i, block in enumerate(blocks):

        def work(i=i, block=block):
            nonlocal moving_s
            at = 0
            for ref, (count, away) in zip(held_in[i], plan.pieces[i]):
                if not away:
                    held[i][pl.ds(at, count)] = ref[pl.ds(block.start, count)]
                at += count
            for copy in moving[i]:
                copy.wait()
            glycans = held[i][...]
            targets = lax.broadcasted_iota(jnp.int32, (glycans.shape[0], 1), 0)
            targets = targets.astype(jnp.float32) + (const(block.target) + float(block.start))
            total = None
            for use in block.uses:
                here, row_labels = source(use)
                logits = lax.dot_general(
                    glycans, here, (((1,), (1,)), ((), ())), preferred_element_type=jnp.float32
                )
                logits = scale * logits + shift
                positive = jnp.where(targets == row_labels, 1.0, 0.0)
                coef = jax.nn.sigmoid(logits) - positive
                masked = coef * const(KEEP_ROW) if block.optional == "spectra" else coef
                coef = coef.astype(jnp.bfloat16)
                if block.out:
                    part = jnp.dot(coef, here, preferred_element_type=jnp.float32)
                    total = part if total is None else total + part
                if plan.gradient:
                    part = lax.dot_general(
                        masked.astype(jnp.bfloat16),
                        glycans,
                        (((0,), (0,)), ((), ())),
                        preferred_element_type=jnp.float32,
                    )
                    if moving_s is not None:
                        moving_s.wait()
                        moving_s = None
                    if i > 0 or plan.prior_s:
                        s_held[...] += part
                    else:
                        s_held[...] = part
            if block.prior == "kept":
                moving_prior[i].wait()
                total = total + prior_held[i][...]
            elif block.prior:
                total = total + priors[i][...]
            if block.out == "kept":
                out_held[i][...] = total
                leaving.append(move(out_held[i], outs[i][0]))
            elif block.out == "split":
                outs[i][0][...] = scale * total[:half]
                out_held[i][...] = scale * total[half:]
                leaving.append(move(out_held[i], outs[i][1]))
            elif block.out == "total":
                outs[i][0][...] = total
            elif block.out == "scaled":
                outs[i][0][...] = scale * total
            elif block.out:
                outs[i][0][...] = (scale * total).astype(jnp.bfloat16)

        if block.optional == "all":
            if block.prior == "kept":
                moving_prior[i].wait()
                moving_prior[i] = Waited()
                for copy in moving[i]:
                    copy.wait()
                moving[i] = []
            pl.when(flags[i] != 0)(work)
        else:
            work()
    if plan.gradient == "final":
        mine_out[...] = scale * s_held[pl.ds(0, rows)]
        other_out[...] = (scale * s_held[pl.ds(rows, rows)]).astype(jnp.bfloat16)
    elif plan.gradient:
        leaving.append(move(s_held, s_out))
    for copy in leaving:
        copy.wait()


class Waited:
    def wait(self):
        pass


def in_vmem(array):
    return pltpu.with_memory_space_constraint(array, pltpu.VMEM)


def in_hbm(array):
    return pltpu.with_memory_space_constraint(array, pltpu.HBM)


def vmem_out(shape, kind):
    return pltpu.VMEM(shape, kind)


def hbm_out(shape, kind):
    return pltpu.HBM(shape, kind)


VMEM_SPEC = pl.BlockSpec(memory_space=pltpu.VMEM)
SMEM_SPEC = pl.BlockSpec(memory_space=pltpu.SMEM)
HBM_SPEC = pl.BlockSpec(memory_space=pltpu.HBM)
SMALL_COST = pl.CostEstimate(flops=1024, bytes_accessed=1024, transcendentals=0)


def params():
    return pltpu.CompilerParams(vmem_limit_bytes=VMEM_BYTES)


def pair_work(consts, blocks, rows, labels=None, node=None, ends=None, gradient="", prior_s=None, cost=SMALL_COST):
    half = rows // 2
    shapes = tuple(b[0] for b in blocks)
    pieces = []
    arrays = []
    for shape, array, _, _ in blocks:
        parts = array if isinstance(array, tuple) else (array,)
        away = [isinstance(x, Away) for x in parts]
        parts = [x.array if flag else x for x, flag in zip(parts, away)]
        pieces.append(tuple((shape.count or x.shape[0], flag) for x, flag in zip(parts, away)))
        arrays += list(zip(parts, away))
    width = arrays[0][0].shape[1]
    ends = ends or ()
    end_rows = tuple(x.shape[0] for x in ends)
    plan = Plan(shapes, tuple(pieces), node is not None, end_rows, gradient, prior_s is not None, rows)

    operands = [in_vmem(consts)]
    in_specs = [VMEM_SPEC]

    def give(array, away):
        operands.append(in_hbm(array) if away else in_vmem(array))
        in_specs.append(HBM_SPEC if away else VMEM_SPEC)

    if node is not None:
        give(labels, False)
    if any(b.optional == "all" for b in shapes):
        operands.append(jnp.stack([jnp.int32(b[2]) for b in blocks]))
        in_specs.append(SMEM_SPEC)
    for array in node or ():
        give(array, True)
    for array in ends:
        give(array, False)
    for array, away in arrays:
        give(array, away)
    for shape, _, _, prior in blocks:
        if shape.prior:
            give(prior, shape.prior == "kept")
    if prior_s is not None:
        give(prior_s, True)

    counts = [sum(count for count, _ in p) for p in pieces]
    outs = []
    out_specs = []

    def get(shape, kind, away):
        outs.append((hbm_out if away else vmem_out)(shape, kind))
        out_specs.append(HBM_SPEC if away else VMEM_SPEC)

    for shape, count in zip(shapes, counts):
        if shape.out == "split":
            get((half, width), jnp.float32, False)
            get((half, width), jnp.float32, True)
        elif shape.out:
            kind = jnp.bfloat16 if shape.out == "rounded" else jnp.float32
            get((count, width), kind, shape.out == "kept")
    if gradient == "final":
        get((rows, width), jnp.float32, False)
        get((rows, width), jnp.bfloat16, False)
    elif gradient:
        get((2 * rows, width), jnp.float32, True)

    scratch = []
    if node is not None:
        scratch.append(pltpu.VMEM((2 * rows, width), jnp.bfloat16))
    if ends:
        scratch.append(pltpu.VMEM((2 * rows, width), jnp.bfloat16))
    scratch += [pltpu.VMEM((n, width), jnp.bfloat16) for n in counts]
    scratch += [pltpu.VMEM((n, width), jnp.float32) for n, b in zip(counts, shapes) if b.prior == "kept"]
    for n, b in zip(counts, shapes):
        if b.out in ("kept", "split"):
            scratch.append(pltpu.VMEM((n if b.out == "kept" else half, width), jnp.float32))
    if gradient:
        scratch.append(pltpu.VMEM((2 * rows, width), jnp.float32))
    scratch.append(pltpu.SemaphoreType.DMA((len(operands) + len(outs),)))
    return pl.pallas_call(
        functools.partial(pair_body, plan),
        out_shape=outs,
        in_specs=in_specs,
        out_specs=out_specs,
        scratch_shapes=scratch,
        cost_estimate=cost,
        compiler_params=params(),
    )(*operands)


def code_labels(labels, row_count, width):
    digits = jnp.stack([labels // 16384, labels // 128 % 128, labels % 128]).astype(jnp.bfloat16)
    digits = jnp.concatenate([digits, digits, digits], axis=1)
    return jnp.pad(digits, ((0, row_count - 3), (0, width - digits.shape[1])))


def add_body(total, arrived, out, *scratch):
    if scratch:
        near, sem = scratch
        copy = pltpu.make_async_copy(total, near, sem)
        copy.start()
        copy.wait()
        total = near
    out[...] = (total[...] + arrived[...].astype(jnp.float32)).astype(jnp.bfloat16)


def add_rounded(total, arrived):
    away = isinstance(total, Away)
    scratch = [pltpu.VMEM(arrived.shape, jnp.float32), pltpu.SemaphoreType.DMA] if away else []
    return pl.pallas_call(
        add_body,
        out_shape=vmem_out(arrived.shape, jnp.bfloat16),
        in_specs=[HBM_SPEC if away else VMEM_SPEC, VMEM_SPEC],
        out_specs=VMEM_SPEC,
        scratch_shapes=scratch,
        cost_estimate=SMALL_COST,
        compiler_params=params(),
    )(in_hbm(total.array) if away else in_vmem(total), in_vmem(arrived))


def finish_spectra_body(mine_s, *rest):
    others, out = rest[:-1], rest[-1]
    at = 0
    for other in others:
        where = pl.ds(at, other.shape[0])
        out[where] = (mine_s[where] + other[...].astype(jnp.float32)).astype(jnp.bfloat16)
        at += other.shape[0]


def finish_spectra(mine_s, others):
    return pl.pallas_call(
        finish_spectra_body,
        out_shape=jax.ShapeDtypeStruct(mine_s.shape, jnp.bfloat16),
        in_specs=[VMEM_SPEC] * (1 + len(others)),
        out_specs=VMEM_SPEC,
        cost_estimate=SMALL_COST,
        compiler_params=params(),
    )(*[in_vmem(a) for a in [mine_s] + others])


def finish_structures_body(flag, here_total, across_back, inside_a, inside_b, out):
    @pl.when(flag[0] != 0)
    def _():
        out[pl.ds(0, inside_a.shape[0])] = inside_a[...]
        out[pl.ds(inside_a.shape[0], inside_b.shape[0])] = inside_b[...]

    @pl.when(flag[0] == 0)
    def _():
        total = here_total[...] + across_back[...].astype(jnp.float32)
        out[...] = total.astype(jnp.bfloat16)


def finish_structures(flag, here_total, across_back, inside_a, inside_b):
    arrays = [here_total, across_back, inside_a, inside_b]
    return pl.pallas_call(
        finish_structures_body,
        out_shape=jax.ShapeDtypeStruct(here_total.shape, jnp.bfloat16),
        in_specs=[SMEM_SPEC] + [VMEM_SPEC] * len(arrays),
        out_specs=VMEM_SPEC,
        cost_estimate=SMALL_COST,
        compiler_params=params(),
    )(jnp.int32(flag).reshape(1), *[in_vmem(a) for a in arrays])


def along_line(spectra, glycans, labels, scale, shift):
    rows, width = spectra.shape
    half = rows // 2
    node_rows = rows * lax.axis_size("inner")
    position = lax.axis_index("blk")
    outer = (position == 0) | (position == LINE - 1)
    core_first = lax.axis_index("sub") * node_rows + lax.axis_index("inner") * rows
    lane_rows = lax.axis_size("sub") * node_rows

    def permute(block, pairs):
        return lax.ppermute(block, ("blk", "inner"), pairs)

    def first_of(block_position):
        return (block_position * lane_rows + core_first).astype(jnp.float32)

    n_inner = lax.axis_size("inner")
    last = LINE - 1
    sides = []
    middle = []
    inward = []
    for core in range(n_inner):
        inward += [(core, n_inner + core), (last * n_inner + core, (last - 1) * n_inner + core)]
        for at in range(LINE):
            sides.append((at * n_inner + core, (at ^ 1) * n_inner + core))
        for at in range(1, last):
            middle.append((at * n_inner + core, (last - at) * n_inner + core))
        for at in (0, last):
            middle.append((at * n_inner + core, at * n_inner + (core + 1) % n_inner))
    here_at, side_at, across_at, far_at = 2, 3, 4, 5
    rows_of_consts = [
        scale,
        shift,
        first_of(position),
        first_of(position ^ 1),
        first_of(last - position),
        first_of((last - position) ^ 1),
        jnp.where(outer, 0.0, 1.0),
    ]
    index = lax.broadcasted_iota(jnp.int32, (8, 128), 0)
    consts = jnp.zeros((8, 128), jnp.float32)
    for i, value in enumerate(rows_of_consts):
        consts = jnp.where(index == i, value, consts)

    def in_thirds(block):
        piece = -(-block.shape[0] // 48) * 16
        return tuple(swap_inner(block[at : at + piece]) for at in range(0, block.shape[0], piece))

    across = permute(glycans, middle)
    side = permute(glycans, sides)
    end_mine = permute(jnp.concatenate([spectra, code_labels(labels, LABEL_ROWS, width)]), inward)
    partner = swap_inner(spectra)
    own_labels = labels.reshape(1, rows)
    node_labels = jnp.concatenate([own_labels, swap_inner(own_labels)], axis=1)
    node_labels = node_labels.astype(jnp.float32)
    node = dict(node=(spectra, partner), labels=node_labels)
    here_g, own_s = pair_work(
        consts,
        [(Block(here_at, ("node",), "kept"), Away(glycans), 1, None)],
        rows,
        gradient="part",
        **node,
    )

    side = after(side, here_g)
    far = permute(side, middle)
    across = after(across, side)
    next_out = tuple(permute(across[at : at + half], sides) for at in (0, half))
    side_g, across_g, own_s = pair_work(
        consts,
        [
            (Block(side_at, ("node",), "kept"), Away(side), 1, None),
            (Block(across_at, ("node",), "kept", optional="spectra"), across, 1, None),
        ],
        rows,
        gradient="part",
        prior_s=own_s,
        **node,
    )
    end_mine = after(end_mine, own_s)
    ends = (end_mine,) + in_thirds(end_mine)

    far, *next_out = lax.optimization_barrier((far,) + next_out + (own_s,))[:3]
    last_out = permute(far, sides)
    (far_a,) = pair_work(
        consts,
        [(Block(far_at, ("node", "ends"), "rounded", 0, half), far, 1, None)],
        rows,
        ends=ends,
        **node,
    )
    back_a = permute(far_a, middle)
    far_b, across_out = pair_work(
        consts,
        [
            (
                Block(far_at, ("node", "ends"), "rounded", half, half),
                after(far, far_a),
                1,
                None,
            ),
            (Block(across_at, ("ends",), "rounded", prior="kept"), across, 1, across_g),
        ],
        rows,
        ends=ends,
        **node,
    )
    back_b = permute(far_b, middle)
    side_total_a, side_total_b = pair_work(
        consts,
        [
            (
                Block(side_at, ("ends",), "split", prior="kept"),
                Away(after(side, far_b)),
                1,
                side_g,
            )
        ],
        rows,
        ends=ends,
    )
    total_a = add_rounded(side_total_a, back_a)
    inside_a = permute(total_a, sides)
    across_back = permute(after(across_out, total_a), middle)
    total_b = add_rounded(Away(side_total_b), after(back_b, total_a))
    inside_b = permute(total_b, sides)

    def only_s(target):
        return Block(target, ("node",), "", optional="all")

    mine_s, other_s = pair_work(
        consts,
        [
            (only_s(far_at), after(far, total_b), ~outer, None),
            (only_s(far_at), tuple(next_out), outer, None),
            (only_s(across_at), last_out, outer, None),
        ],
        rows,
        gradient="final",
        prior_s=own_s,
        **node,
    )
    others = list(in_thirds(other_s))
    inside_a, late_mine = lax.optimization_barrier((inside_a, glycans))
    flops = 2 * 2 * 2 * rows * rows * width
    (here_total,) = pair_work(
        consts,
        [
            (
                Block(here_at, ("ends",), "scaled", prior="kept", optional="all"),
                Away(late_mine),
                ~outer,
                here_g,
            )
        ],
        rows,
        ends=ends,
        cost=pl.CostEstimate(flops=flops, bytes_accessed=8 * rows * width, transcendentals=0),
    )
    others[0] = after(others[0], inside_b, here_total)
    grad_spectra = finish_spectra(mine_s, others)
    across_back = after(across_back, grad_spectra)
    return grad_spectra, finish_structures(outer, here_total, across_back, inside_a, inside_b)


def local(
    mass_profile_vectors,
    sugar_tree_vectors,
    matching_glycan_rows,
    sharpness_factor,
    offset_shift_term,
):
    work = along_line if lax.axis_size("blk") == STEPS == LINE else around_ring
    return work(
        mass_profile_vectors,
        sugar_tree_vectors,
        matching_glycan_rows,
        sharpness_factor[0],
        offset_shift_term[0],
    )


def solution(mesh):
    placed = (
        P(("groups", "blk", "sub", "inner"), None),
        P(("groups", "blk", "sub", "inner"), None),
        P(("groups", "blk", "sub", "inner")),
        P(),
        P(),
    )
    return jax.shard_map(
        local,
        mesh=mesh,
        in_specs=placed,
        out_specs=(
            P(("groups", "blk", "sub", "inner"), None),
            P(("groups", "blk", "sub", "inner"), None),
        ),
        check_vma=False,
    )
```

time: 77.1 us -> 84 us (1.089)
  starting transfers between devices: 17.2 us -> 23 us
  Pallas kernels: 40.6 us -> 37.5 us
  other arithmetic: 1.05 us -> 3.03 us
  waiting for transfers between devices: 13.2 us -> 14.6 us
    ppermute x10 -> x12, starting transfers between devices: 16 us -> 21.2 us  [permute(): return lax.ppermute(block, ('blk', 'inner'), pairs)]
    concatenate x1 -> x2, other arithmetic: 0.08 us -> 2.08 us  [the longest x1 1.98 us: along_line(): jnp.concatenate([spectra, code_labels(labels, LABEL_ROWS, width)])]
    pallas_call x8 -> x7, Pallas kernels: 35.5 us -> 33.5 us  [pair_work(): pl.pallas_call(functools.partial(pair_body, plan), out_shape=outs, in_spe...]
    ppermute x10 -> x12, waiting for transfers between devices: 13.2 us -> 14.6 us  [permute(): return lax.ppermute(block, ('blk', 'inner'), pairs)]
    pallas_call x1 -> x0, Pallas kernels: 1.16 us -> none  [choose(): pl.pallas_call(choose_body, out_shape=vmem_out((rows + tail.shape[0], wid...]
    unnamed x6 -> x14, local copies, waits for them, and re-layouts: 1.57 us -> 2.31 us
    ppermute x6 -> x8, starting transfers between devices: 1.22 us -> 1.79 us  [from_behind(): return lax.ppermute(block, axis, route)]
  transfers between devices with their start and end apart: 16 -> 20, of which waited for: 2 -> 3; matrix products, arithmetic and copies ran while one was open for 2% -> 5% of each run, Pallas kernels for 50% -> 44%
where the time goes in v6:
time: 84 us; the launch traced here: 83.6 us
  Pallas kernels  37.5 us (45%)
  starting transfers between devices  23 us (27%)
  waiting for transfers between devices  14.6 us (17%)
  local copies, waits for them, and re-layouts  3.14 us (4%)
  other arithmetic  3.03 us (4%)
  between operations  2.25 us (3%)
    pallas_call x7, Pallas kernels, pair_work(): pl.pallas_call(functools.partial(pair_body, plan), out_shape=outs, in_spe...  33.5 us
    ppermute x12, starting transfers between devices, permute(): return lax.ppermute(block, ('blk', 'inner'), pairs)  21.2 us
    ppermute x12, waiting for transfers between devices, permute(): return lax.ppermute(block, ('blk', 'inner'), pairs)  14.6 us
    unnamed x14, local copies, waits for them, and re-layouts  2.31 us
    pallas_call x2, Pallas kernels, add_rounded(): pl.pallas_call(add_body, out_shape=vmem_out(arrived.shape, jnp.bfloat16),...  2.2 us
    concatenate x1, other arithmetic, along_line(): jnp.concatenate([spectra, code_labels(labels, LABEL_ROWS, width)])  1.98 us
    ppermute x8, starting transfers between devices, from_behind(): return lax.ppermute(block, axis, route)  1.79 us
  transfers between devices with their start and end apart: 20, of which 3 were waited for; matrix products, arithmetic and copies ran while one was open for 5% of the time, Pallas kernels for 44%

profile of v6, /device:TPU:0, one launch (start us, length us, event | category | flops | bytes accessed | tf_op | source)
XLA Modules:
  0.0 83.6 jit_solution(1427836488309704314)
XLA Ops:
  0.6 3.1 %collective-permute-start.2 = (bf16[320,1024]{1,0:T(8,128)(2,1)}, bf16[320,1024]{1,0:T(8,128)(2,1)S(1)}, u32[]{:S(2)}, u32[]{:S(2)}) collective-permute-start(bf16[320,1024]{1,0:T(8,128)(2,1)} %refs_6_), channel_id=1, source_target_pairs={{0,4},{4,0},{8,12},{12,8},{1,5},{5,1},{9,13},{13,9},{2,6},{6,2},{1... | collective-permute-start | bytes 1966088 | tf_op jit(solution)/shard_map/ppermute | solution.py:471
  3.7 0.7 concatenate.19
  4.4 0.5 collective-permute-start
  4.9 0.7 fusion.28
  5.6 0.1 fusion.14
  5.7 2.0 %pad_maximum_fusion = bf16[336,1024]{1,0:T(8,128)(2,1)} fusion(bf16[16,1024]{1,0:T(8,128)(2,1)S(1)} %fusion.14, bf16[320,1024]{1,0:T(8,128)(2,1)} %refs_3_.1), kind=kLoop, calls=%fused_computation | loop fusion | flops 1376256 | bytes 1376256 | tf_op jit(solution)/shard_map/concatenate | solution.py:510
  7.7 5.1 %collective-permute-start.7 = (bf16[336,1024]{1,0:T(8,128)(2,1)}, bf16[336,1024]{1,0:T(8,128)(2,1)S(1)}, u32[]{:S(2)}, u32[]{:S(2)}) collective-permute-start(bf16[336,1024]{1,0:T(8,128)(2,1)} %pad_maximum_fusion), channel_id=1, source_target_pairs={{0,4},{12,8},{1,5},{13,9},{2,6},{14,10},{3,7},{15,11},{16,20},{28,... | collective-permute-start | bytes 2064392 | tf_op jit(solution)/shard_map/ppermute | solution.py:471
  14.4 0.8 copy-done.5
  15.2 5.4 %shard_map.68 = (f32[320,1024]{1,0:T(8,128)}, f32[640,1024]{1,0:T(8,128)}) custom-call(f32[8,128]{1,0:T(8,128)S(1)} %select_select_fusion.refs_0_, f32[1,640]{1,0:T(1,128)S(1)} %add_convert_fusion.refs_1_, bf16[320,1024]{1,0:T(8,128)(2,1)} %refs_3_.1, bf16[320,1024]{1,0:T(8,128)(2,1)} %copy-done.5, bf16[320,1024]{1,0:T(8,128)(2,1)} %refs_6_), custom_call_target="tpu_custom_call" | custom-call | flops 1024 | bytes 1024 | tf_op jit(solution)/shard_map/pallas_call | solution.py:376
  20.8 2.5 %collective-permute-start.5 = (bf16[160,1024]{1,0:T(8,128)(2,1)S(1)}, bf16[160,1024]{1,0:T(8,128)(2,1)S(1)}, u32[]{:S(2)}, u32[]{:S(2)}) collective-permute-start(bf16[160,1024]{1,0:T(8,128)(2,1)S(1)} %get-tuple-element.60), channel_id=1, source_target_pairs={{0,4},{4,0},{8,12},{12,8},{1,5},{5,1},{9,13},{13,9},{2,6},{6,2},{1... | collective-permute-start | bytes 983048 | tf_op jit(solution)/shard_map/ppermute | solution.py:471
  23.2 0.1 collective-permute-start.6
  23.3 7.4 %shard_map.69 = (f32[320,1024]{1,0:T(8,128)}, f32[320,1024]{1,0:T(8,128)}, f32[640,1024]{1,0:T(8,128)}) custom-call(f32[8,128]{1,0:T(8,128)S(1)} %select_select_fusion.refs_0_, f32[1,640]{1,0:T(1,128)S(1)} %add_convert_fusion.refs_1_, bf16[320,1024]{1,0:T(8,128)(2,1)} %refs_3_.1, bf16[320,1024]{1,0:T(8,128)(2,1)} %copy-done.5, bf16[320,1024]{1,0:T(8,128)(2,1)} %copy-done.6, ...), custom_call_target="tpu_custom_call" | custom-call | flops 1024 | bytes 1024 | tf_op jit(solution)/shard_map/pallas_call | solution.py:376
  30.8 3.1 %collective-permute-done.7.refs_4_.refs_1_.refs_2_ = bf16[336,1024]{1,0:T(8,128)(2,1)S(1)} collective-permute-done((bf16[336,1024]{1,0:T(8,128)(2,1)}, bf16[336,1024]{1,0:T(8,128)(2,1)S(1)}, u32[]{:S(2)}, u32[]{:S(2)}) %collective-permute-start.7) | collective-permute-done | bytes 688160 | tf_op jit(solution)/shard_map/ppermute | solution.py:471
  34.0 0.5 collective-permute-start.8
  34.5 6.3 %collective-permute-done.5.refs_6_ = bf16[160,1024]{1,0:T(8,128)(2,1)S(1)} collective-permute-done((bf16[160,1024]{1,0:T(8,128)(2,1)S(1)}, bf16[160,1024]{1,0:T(8,128)(2,1)S(1)}, u32[]{:S(2)}, u32[]{:S(2)}) %collective-permute-start.5) | collective-permute-done | bytes 327712 | tf_op jit(solution)/shard_map/ppermute | solution.py:471
  40.8 0.7 copy-done.1
  41.6 5.1 %collective-permute-done.6.refs_7_ = bf16[160,1024]{1,0:T(8,128)(2,1)S(1)} collective-permute-done((bf16[160,1024]{1,0:T(8,128)(2,1)S(1)}, bf16[160,1024]{1,0:T(8,128)(2,1)S(1)}, u32[]{:S(2)}, u32[]{:S(2)}) %collective-permute-start.6) | collective-permute-done | bytes 327712 | tf_op jit(solution)/shard_map/ppermute | solution.py:471
  46.7 2.5 %collective-permute-start.13 = (bf16[320,1024]{1,0:T(8,128)(2,1)S(1)}, bf16[320,1024]{1,0:T(8,128)(2,1)S(1)}, u32[]{:S(2)}, u32[]{:S(2)}) collective-permute-start(bf16[320,1024]{1,0:T(8,128)(2,1)S(1)} %collective-permute-done.3.refs_8_.refs_5_), channel_id=1, source_target_pairs={{0,4},{4,0},{8,12},{12,8},{1,5},{5,1},{9,13},{13,9},{2,6},{6,2},{1... | collective-permute-start | bytes 1966088 | tf_op jit(solution)/shard_map/ppermute | solution.py:471
  49.2 3.0 %shard_map.70 = bf16[160,1024]{1,0:T(8,128)(2,1)S(1)} custom-call(f32[8,128]{1,0:T(8,128)S(1)} %select_select_fusion.refs_0_, f32[1,640]{1,0:T(1,128)S(1)} %add_convert_fusion.refs_1_, bf16[320,1024]{1,0:T(8,128)(2,1)} %refs_3_.1, bf16[320,1024]{1,0:T(8,128)(2,1)} %copy-done.5, bf16[336,1024]{1,0:T(8,128)(2,1)S(1)} %collective-permute-done.7.refs_4_.refs_1_.refs_2_, ...), custom_call_target="tpu_custom_call" | custom-call | flops 1024 | bytes 1024 | tf_op jit(solution)/shard_map/pallas_call | solution.py:376
  52.3 5.6 %shard_map.71 = (bf16[160,1024]{1,0:T(8,128)(2,1)}, bf16[320,1024]{1,0:T(8,128)(2,1)}) custom-call(f32[8,128]{1,0:T(8,128)S(1)} %select_select_fusion.refs_0_, f32[1,640]{1,0:T(1,128)S(1)} %add_convert_fusion.refs_1_, bf16[320,1024]{1,0:T(8,128)(2,1)} %refs_3_.1, bf16[320,1024]{1,0:T(8,128)(2,1)} %copy-done.5, ...), custom_call_target="tpu_custom_call" | custom-call | flops 1024 | bytes 1024 | tf_op jit(solution)/shard_map/pallas_call | solution.py:376
  57.9 0.6 collective-permute-start.11
  58.4 3.9 %shard_map.72 = (f32[160,1024]{1,0:T(8,128)S(1)}, f32[160,1024]{1,0:T(8,128)}) custom-call(f32[8,128]{1,0:T(8,128)S(1)} %select_select_fusion.refs_0_, bf16[336,1024]{1,0:T(8,128)(2,1)S(1)} %collective-permute-done.7.refs_4_.refs_1_.refs_2_, bf16[112,1024]{1,0:T(8,128)(2,1)S(1)} %collective-permute-done.8.refs_5_.refs_2_.refs_3_, ...), custom_call_target="tpu_custom_call" | custom-call | flops 1024 | bytes 1024 | tf_op jit(solution)/shard_map/pallas_call | solution.py:376
  62.4 0.7 copy-done
  63.2 3.2 %collective-permute-start.16 = (bf16[160,1024]{1,0:T(8,128)(2,1)}, bf16[160,1024]{1,0:T(8,128)(2,1)S(1)}, u32[]{:S(2)}, u32[]{:S(2)}) collective-permute-start(bf16[160,1024]{1,0:T(8,128)(2,1)} %copy-done), channel_id=1, source_target_pairs={{0,4},{4,0},{8,12},{12,8},{1,5},{5,1},{9,13},{13,9},{2,6},{6,2},{1... | collective-permute-start | bytes 983048 | tf_op jit(solution)/shard_map/ppermute | solution.py:471
  66.4 2.1 %shard_map.74 = bf16[160,1024]{1,0:T(8,128)(2,1)S(1)} custom-call(f32[160,1024]{1,0:T(8,128)} %get-tuple-element.40.total, bf16[160,1024]{1,0:T(8,128)(2,1)} %collective-permute-done.11.arrived), custom_call_target="tpu_custom_call" | custom-call | flops 1024 | bytes 1024 | tf_op jit(solution)/shard_map/pallas_call | solution.py:406
  68.6 4.1 %collective-permute-start.15 = (bf16[160,1024]{1,0:T(8,128)(2,1)S(1)}, bf16[160,1024]{1,0:T(8,128)(2,1)S(1)}, u32[]{:S(2)}, u32[]{:S(2)}) collective-permute-start(bf16[160,1024]{1,0:T(8,128)(2,1)S(1)} %shard_map.74), channel_id=1, source_target_pairs={{0,4},{4,0},{8,12},{12,8},{1,5},{5,1},{9,13},{13,9},{2,6},{6,2},{1... | collective-permute-start | bytes 983048 | tf_op jit(solution)/shard_map/ppermute | solution.py:471
  72.7 6.6 %shard_map.75 = (f32[320,1024]{1,0:T(8,128)S(1)}, bf16[320,1024]{1,0:T(8,128)(2,1)S(1)}) custom-call(f32[8,128]{1,0:T(8,128)S(1)} %select_select_fusion.refs_0_, f32[1,640]{1,0:T(1,128)S(1)} %add_convert_fusion.refs_1_, s32[3]{0:T(128)S(1)} %pad_add_fusion.refs_2_, bf16[320,1024]{1,0:T(8,128)(2,1)} %refs_3_.1, bf16[320,1024]{1,0:T(8,128)(2,1)} %copy-done.5, ...), custom_call_target="tpu_custom_call" | custom-call | flops 1024 | bytes 1024 | tf_op jit(solution)/shard_map/pallas_call | solution.py:376
  79.4 0.5 collective-permute-start.17
  79.9 0.1 collective-permute-start.18
  80.1 1.6 %shard_map.76.here_total = f32[320,1024]{1,0:T(8,128)S(1)} custom-call(f32[8,128]{1,0:T(8,128)S(1)} %select_select_fusion.refs_0_, s32[1]{0:T(128)} %bitcast.2.refs_1_, bf16[336,1024]{1,0:T(8,128)(2,1)S(1)} %collective-permute-done.7.refs_4_.refs_1_.refs_2_, bf16[112,1024]{1,0:T(8,128)(2,1)S(1)} %collective-permute-done.8.refs_5_.refs_2_.refs_3_, ...), custom_call_target="tpu_custom_call" | custom-call | flops 838860800 | bytes 2621440 | tf_op jit(solution)/shard_map/pallas_call | solution.py:376
  81.7 0.9 %shard_map.77 = bf16[320,1024]{1,0:T(8,128)(2,1)} custom-call(f32[320,1024]{1,0:T(8,128)S(1)} %get-tuple-element.46.mine_s, bf16[112,1024]{1,0:T(8,128)(2,1)S(1)} %collective-permute-done.14.rest_0_, bf16[112,1024]{1,0:T(8,128)(2,1)S(1)} %collective-permute-done.17.rest_1_, bf16[96,1024]{1,0:T(8,128)(2,1)S(1)} %collective-permute-done.18.rest_2_), custom_call_target="tpu_custom_call" | custom-call | flops 1024 | bytes 1024 | tf_op jit(solution)/shard_map/pallas_call | solution.py:427
  82.7 0.9 %shard_map.78 = bf16[320,1024]{1,0:T(8,128)(2,1)} custom-call(s32[1]{0:T(128)} %bitcast.3.flag, f32[320,1024]{1,0:T(8,128)S(1)} %shard_map.76.here_total, bf16[320,1024]{1,0:T(8,128)(2,1)S(1)} %collective-permute-done.19.across_back, bf16[160,1024]{1,0:T(8,128)(2,1)S(1)} %collective-permute-done.16.inside_a, ...), custom_call_target="tpu_custom_call" | custom-call | flops 1024 | bytes 1024 | tf_op jit(solution)/shard_map/pallas_call | solution.py:451
  (51 shorter events, 0.9 us)
Async XLA Ops:
  0.6 20.0 %collective-permute-start.2 = (bf16[320,1024]{1,0:T(8,128)(2,1)}, bf16[320,1024]{1,0:T(8,128)(2,1)S(1)}, u32[]{:S(2)}, u32[]{:S(2)}) collective-permute-start(bf16[320,1024]{1,0:T(8,128)(2,1)} %refs_6_), channel_id=1, source_target_pairs={{0,4},{4,0},{8,12},{12,8},{1,5},{5,1},{9,13},{13,9},{2,6},{6,2},{1... | collective-permute-start | bytes 1966088 | tf_op jit(solution)/shard_map/ppermute | solution.py:471
  3.7 17.0 %collective-permute-start.4 = (bf16[320,1024]{1,0:T(8,128)(2,1)}, bf16[320,1024]{1,0:T(8,128)(2,1)S(1)}, u32[]{:S(2)}, u32[]{:S(2)}) collective-permute-start(bf16[320,1024]{1,0:T(8,128)(2,1)} %refs_6_), channel_id=1, source_target_pairs={{4,8},{8,4},{0,1},{12,13},{5,9},{9,5},{1,0},{13,12},{6,10},{10,6},... | collective-permute-start | bytes 1966088 | tf_op jit(solution)/shard_map/ppermute | solution.py:471
  4.4 9.9 %collective-permute-start = (s32[1,320]{1,0:T(1,128)S(1)}, s32[1,320]{1,0:T(1,128)S(1)}, u32[]{:S(2)}, u32[]{:S(2)}) collective-permute-start(s32[1,320]{1,0:T(1,128)S(1)} %concatenate.19), channel_id=1, source_target_pairs={{1,0},{0,1},{3,2},{2,3},{5,4},{4,5},{7,6},{6,7},{9,8},{8,9},{11,10... | collective-permute-start | bytes 3848 | tf_op jit(solution)/shard_map/ppermute | solution.py:21
  4.9 9.4 %collective-permute-start.1 = (bf16[320,1024]{1,0:T(8,128)(2,1)}, bf16[320,1024]{1,0:T(8,128)(2,1)S(1)}, u32[]{:S(2)}, u32[]{:S(2)}) collective-permute-start(bf16[320,1024]{1,0:T(8,128)(2,1)} %refs_3_.1), channel_id=1, source_target_pairs={{1,0},{0,1},{3,2},{2,3},{5,4},{4,5},{7,6},{6,7},{9,8},{8,9},{11,10... | collective-permute-start | bytes 1966088 | tf_op jit(solution)/shard_map/ppermute | solution.py:21
  7.7 26.2 %collective-permute-start.7 = (bf16[336,1024]{1,0:T(8,128)(2,1)}, bf16[336,1024]{1,0:T(8,128)(2,1)S(1)}, u32[]{:S(2)}, u32[]{:S(2)}) collective-permute-start(bf16[336,1024]{1,0:T(8,128)(2,1)} %pad_maximum_fusion), channel_id=1, source_target_pairs={{0,4},{12,8},{1,5},{13,9},{2,6},{14,10},{3,7},{15,11},{16,20},{28,... | collective-permute-start | bytes 2064392 | tf_op jit(solution)/shard_map/ppermute | solution.py:471
  14.4 0.8 %copy-start.5 = (bf16[320,1024]{1,0:T(8,128)(2,1)}, bf16[320,1024]{1,0:T(8,128)(2,1)S(1)}, u32[]{:S(2)}) copy-start(bf16[320,1024]{1,0:T(8,128)(2,1)S(1)} %collective-permute-done.1.refs_3_.refs_4_) | copy-start | bytes 1966084
  20.6 2.7 %copy-start.6 = (bf16[320,1024]{1,0:T(8,128)(2,1)}, bf16[320,1024]{1,0:T(8,128)(2,1)S(1)}, u32[]{:S(2)}) copy-start(bf16[320,1024]{1,0:T(8,128)(2,1)S(1)} %collective-permute-done.2.refs_4_.refs_5_) | copy-start | bytes 1966084
  20.6 26.1 %collective-permute-start.3 = (bf16[320,1024]{1,0:T(8,128)(2,1)S(1)}, bf16[320,1024]{1,0:T(8,128)(2,1)S(1)}, u32[]{:S(2)}, u32[]{:S(2)}) collective-permute-start(bf16[320,1024]{1,0:T(8,128)(2,1)S(1)} %collective-permute-done.2.refs_4_.refs_5_), channel_id=1, source_target_pairs={{4,8},{8,4},{0,1},{12,13},{5,9},{9,5},{1,0},{13,12},{6,10},{10,6},... | collective-permute-start | bytes 1966088 | tf_op jit(solution)/shard_map/ppermute | solution.py:471
  20.8 20.1 %collective-permute-start.5 = (bf16[160,1024]{1,0:T(8,128)(2,1)S(1)}, bf16[160,1024]{1,0:T(8,128)(2,1)S(1)}, u32[]{:S(2)}, u32[]{:S(2)}) collective-permute-start(bf16[160,1024]{1,0:T(8,128)(2,1)S(1)} %get-tuple-element.60), channel_id=1, source_target_pairs={{0,4},{4,0},{8,12},{12,8},{1,5},{5,1},{9,13},{13,9},{2,6},{6,2},{1... | collective-permute-start | bytes 983048 | tf_op jit(solution)/shard_map/ppermute | solution.py:471
  23.2 23.5 %collective-permute-start.6 = (bf16[160,1024]{1,0:T(8,128)(2,1)S(1)}, bf16[160,1024]{1,0:T(8,128)(2,1)S(1)}, u32[]{:S(2)}, u32[]{:S(2)}) collective-permute-start(bf16[160,1024]{1,0:T(8,128)(2,1)S(1)} %get-tuple-element.59), channel_id=1, source_target_pairs={{0,4},{4,0},{8,12},{12,8},{1,5},{5,1},{9,13},{13,9},{2,6},{6,2},{1... | collective-permute-start | bytes 983048 | tf_op jit(solution)/shard_map/ppermute | solution.py:471
  34.0 15.2 %collective-permute-start.10 = (bf16[112,1024]{1,0:T(8,128)(2,1)S(1)}, bf16[112,1024]{1,0:T(8,128)(2,1)S(1)}, u32[]{:S(2)}, u32[]{:S(2)}) collective-permute-start(bf16[112,1024]{1,0:T(8,128)(2,1)S(1)} %get-tuple-element.54), channel_id=1, source_target_pairs={{1,0},{0,1},{3,2},{2,3},{5,4},{4,5},{7,6},{6,7},{9,8},{8,9},{11,10... | collective-permute-start | bytes 688136 | tf_op jit(solution)/shard_map/ppermute | solution.py:21
  34.0 15.2 %collective-permute-start.8 = (bf16[112,1024]{1,0:T(8,128)(2,1)S(1)}, bf16[112,1024]{1,0:T(8,128)(2,1)S(1)}, u32[]{:S(2)}, u32[]{:S(2)}) collective-permute-start(bf16[112,1024]{1,0:T(8,128)(2,1)S(1)} %get-tuple-element.56), channel_id=1, source_target_pairs={{1,0},{0,1},{3,2},{2,3},{5,4},{4,5},{7,6},{6,7},{9,8},{8,9},{11,10... | collective-permute-start | bytes 688136 | tf_op jit(solution)/shard_map/ppermute | solution.py:21
  40.8 0.7 copy-start.1
  41.6 7.6 %collective-permute-start.9 = (bf16[112,1024]{1,0:T(8,128)(2,1)S(1)}, bf16[112,1024]{1,0:T(8,128)(2,1)S(1)}, u32[]{:S(2)}, u32[]{:S(2)}) collective-permute-start(bf16[112,1024]{1,0:T(8,128)(2,1)S(1)} %get-tuple-element.55), channel_id=1, source_target_pairs={{1,0},{0,1},{3,2},{2,3},{5,4},{4,5},{7,6},{6,7},{9,8},{8,9},{11,10... | collective-permute-start | bytes 688136 | tf_op jit(solution)/shard_map/ppermute | solution.py:21
  46.7 5.5 %copy-start.3 = (bf16[160,1024]{1,0:T(8,128)(2,1)}, bf16[160,1024]{1,0:T(8,128)(2,1)S(1)}, u32[]{:S(2)}) copy-start(bf16[160,1024]{1,0:T(8,128)(2,1)S(1)} %collective-permute-done.6.refs_7_) | copy-start | bytes 983044
  46.7 26.0 %collective-permute-start.13 = (bf16[320,1024]{1,0:T(8,128)(2,1)S(1)}, bf16[320,1024]{1,0:T(8,128)(2,1)S(1)}, u32[]{:S(2)}, u32[]{:S(2)}) collective-permute-start(bf16[320,1024]{1,0:T(8,128)(2,1)S(1)} %collective-permute-done.3.refs_8_.refs_5_), channel_id=1, source_target_pairs={{0,4},{4,0},{8,12},{12,8},{1,5},{5,1},{9,13},{13,9},{2,6},{6,2},{1... | collective-permute-start | bytes 1966088 | tf_op jit(solution)/shard_map/ppermute | solution.py:471
  52.2 10.1 %collective-permute-start.12 = (bf16[160,1024]{1,0:T(8,128)(2,1)S(1)}, bf16[160,1024]{1,0:T(8,128)(2,1)S(1)}, u32[]{:S(2)}, u32[]{:S(2)}) collective-permute-start(bf16[160,1024]{1,0:T(8,128)(2,1)S(1)} %shard_map.70), channel_id=1, source_target_pairs={{4,8},{8,4},{0,1},{12,13},{5,9},{9,5},{1,0},{13,12},{6,10},{10,6},... | collective-permute-start | bytes 983048 | tf_op jit(solution)/shard_map/ppermute | solution.py:471
  57.9 8.6 %collective-permute-start.11 = (bf16[160,1024]{1,0:T(8,128)(2,1)}, bf16[160,1024]{1,0:T(8,128)(2,1)}, u32[]{:S(2)}, u32[]{:S(2)}) collective-permute-start(bf16[160,1024]{1,0:T(8,128)(2,1)} %get-tuple-element.37), channel_id=1, source_target_pairs={{4,8},{8,4},{0,1},{12,13},{5,9},{9,5},{1,0},{13,12},{6,10},{10,6},... | collective-permute-start | bytes 983048 | tf_op jit(solution)/shard_map/ppermute | solution.py:471
  62.4 0.7 copy-start
  63.1 19.5 %collective-permute-start.19 = (bf16[320,1024]{1,0:T(8,128)(2,1)}, bf16[320,1024]{1,0:T(8,128)(2,1)S(1)}, u32[]{:S(2)}, u32[]{:S(2)}) collective-permute-start(bf16[320,1024]{1,0:T(8,128)(2,1)} %get-tuple-element.51), channel_id=1, source_target_pairs={{4,8},{8,4},{0,1},{12,13},{5,9},{9,5},{1,0},{13,12},{6,10},{10,6},... | collective-permute-start | bytes 1966088 | tf_op jit(solution)/shard_map/ppermute | solution.py:471
  63.2 9.5 %copy-start.2 = (bf16[160,1024]{1,0:T(8,128)(2,1)S(1)}, bf16[160,1024]{1,0:T(8,128)(2,1)}, u32[]{:S(2)}) copy-start(bf16[160,1024]{1,0:T(8,128)(2,1)} %copy-done.1) | copy-start | bytes 983044
  63.2 9.5 %copy-start.4 = (bf16[160,1024]{1,0:T(8,128)(2,1)S(1)}, bf16[160,1024]{1,0:T(8,128)(2,1)}, u32[]{:S(2)}) copy-start(bf16[160,1024]{1,0:T(8,128)(2,1)} %copy-done.3) | copy-start | bytes 983044
  63.2 16.8 %collective-permute-start.16 = (bf16[160,1024]{1,0:T(8,128)(2,1)}, bf16[160,1024]{1,0:T(8,128)(2,1)S(1)}, u32[]{:S(2)}, u32[]{:S(2)}) collective-permute-start(bf16[160,1024]{1,0:T(8,128)(2,1)} %copy-done), channel_id=1, source_target_pairs={{0,4},{4,0},{8,12},{12,8},{1,5},{5,1},{9,13},{13,9},{2,6},{6,2},{1... | collective-permute-start | bytes 983048 | tf_op jit(solution)/shard_map/ppermute | solution.py:471
  68.6 13.1 %collective-permute-start.15 = (bf16[160,1024]{1,0:T(8,128)(2,1)S(1)}, bf16[160,1024]{1,0:T(8,128)(2,1)S(1)}, u32[]{:S(2)}, u32[]{:S(2)}) collective-permute-start(bf16[160,1024]{1,0:T(8,128)(2,1)S(1)} %shard_map.74), channel_id=1, source_target_pairs={{0,4},{4,0},{8,12},{12,8},{1,5},{5,1},{9,13},{13,9},{2,6},{6,2},{1... | collective-permute-start | bytes 983048 | tf_op jit(solution)/shard_map/ppermute | solution.py:471
  79.3 2.4 %collective-permute-start.14 = (bf16[112,1024]{1,0:T(8,128)(2,1)S(1)}, bf16[112,1024]{1,0:T(8,128)(2,1)S(1)}, u32[]{:S(2)}, u32[]{:S(2)}) collective-permute-start(bf16[112,1024]{1,0:T(8,128)(2,1)S(1)} %get-tuple-element.58), channel_id=1, source_target_pairs={{1,0},{0,1},{3,2},{2,3},{5,4},{4,5},{7,6},{6,7},{9,8},{8,9},{11,10... | collective-permute-start | bytes 688136 | tf_op jit(solution)/shard_map/ppermute | solution.py:21
  79.4 2.3 %collective-permute-start.17 = (bf16[112,1024]{1,0:T(8,128)(2,1)S(1)}, bf16[112,1024]{1,0:T(8,128)(2,1)S(1)}, u32[]{:S(2)}, u32[]{:S(2)}) collective-permute-start(bf16[112,1024]{1,0:T(8,128)(2,1)S(1)} %get-tuple-element.57), channel_id=1, source_target_pairs={{1,0},{0,1},{3,2},{2,3},{5,4},{4,5},{7,6},{6,7},{9,8},{8,9},{11,10... | collective-permute-start | bytes 688136 | tf_op jit(solution)/shard_map/ppermute | solution.py:21
  79.9 1.8 %collective-permute-start.18 = (bf16[96,1024]{1,0:T(8,128)(2,1)S(1)}, bf16[96,1024]{1,0:T(8,128)(2,1)S(1)}, u32[]{:S(2)}, u32[]{:S(2)}) collective-permute-start(bf16[96,1024]{1,0:T(8,128)(2,1)S(1)} %slice.31), channel_id=1, source_target_pairs={{1,0},{0,1},{3,2},{2,3},{5,4},{4,5},{7,6},{6,7},{9,8},{8,9},{11,10... | collective-permute-start | bytes 589832 | tf_op jit(solution)/shard_map/ppermute | solution.py:21

commit v7 on v6

--- a/solution.py
+++ b/solution.py
@@ -478,8 +478,10 @@
     sides = []
     middle = []
     inward = []
+    outward = []
     for core in range(n_inner):
         inward += [(core, n_inner + core), (last * n_inner + core, (last - 1) * n_inner + core)]
+        outward += [(n_inner + core, core), ((last - 1) * n_inner + core, last * n_inner + core)]
         for at in range(LINE):
             sides.append((at * n_inner + core, (at ^ 1) * n_inner + core))
         for at in range(1, last):
@@ -524,7 +526,7 @@
     side = after(side, here_g)
     far = permute(side, middle)
     across = after(across, side)
-    next_out = tuple(permute(across[at : at + half], sides) for at in (0, half))
+    next_out = tuple(permute(across[at : at + half], outward) for at in (0, half))
     side_g, across_g, own_s = pair_work(
         consts,
         [

time: 84 us -> 76 us (0.905)
  waiting for transfers between devices: 14.6 us -> 7.37 us
  starting transfers between devices: 23 us -> 22 us
    ppermute x12, waiting for transfers between devices: 14.6 us -> 7.35 us  [permute(): return lax.ppermute(block, ('blk', 'inner'), pairs)]
    ppermute x12, starting transfers between devices: 21.2 us -> 20.1 us  [permute(): return lax.ppermute(block, ('blk', 'inner'), pairs)]
  transfers between devices with their start and end apart: 20 -> 20, of which waited for: 3 -> 2; matrix products, arithmetic and copies ran while one was open for 5% -> 5% of each run, Pallas kernels for 44% -> 49%
where the time goes in v7:
time: 76 us; the launch traced here: 75.4 us
  Pallas kernels  37.6 us (49%)
  starting transfers between devices  22 us (29%)
  waiting for transfers between devices  7.37 us (10%)
  local copies, waits for them, and re-layouts  3.14 us (4%)
  other arithmetic  3.03 us (4%)
  between operations  2.29 us (3%)
    pallas_call x7, Pallas kernels, pair_work(): pl.pallas_call(functools.partial(pair_body, plan), out_shape=outs, in_spe...  33.6 us
    ppermute x12, starting transfers between devices, permute(): return lax.ppermute(block, ('blk', 'inner'), pairs)  20.1 us
    ppermute x12, waiting for transfers between devices, permute(): return lax.ppermute(block, ('blk', 'inner'), pairs)  7.35 us
    unnamed x14, local copies, waits for them, and re-layouts  2.31 us
    pallas_call x2, Pallas kernels, add_rounded(): pl.pallas_call(add_body, out_shape=vmem_out(arrived.shape, jnp.bfloat16),...  2.2 us
    concatenate x1, other arithmetic, along_line(): jnp.concatenate([spectra, code_labels(labels, LABEL_ROWS, width)])  1.98 us
    ppermute x8, starting transfers between devices, from_behind(): return lax.ppermute(block, axis, route)  1.87 us
  transfers between devices with their start and end apart: 20, of which 2 were waited for; matrix products, arithmetic and copies ran while one was open for 5% of the time, Pallas kernels for 49%

profile of v7, /device:TPU:0, one launch (start us, length us, event | category | flops | bytes accessed | tf_op | source)
XLA Modules:
  0.0 75.4 jit_solution(8948730671163382044)
XLA Ops:
  0.6 3.1 %collective-permute-start.2 = (bf16[320,1024]{1,0:T(8,128)(2,1)}, bf16[320,1024]{1,0:T(8,128)(2,1)S(1)}, u32[]{:S(2)}, u32[]{:S(2)}) collective-permute-start(bf16[320,1024]{1,0:T(8,128)(2,1)} %refs_6_), channel_id=1, source_target_pairs={{0,4},{4,0},{8,12},{12,8},{1,5},{5,1},{9,13},{13,9},{2,6},{6,2},{1... | collective-permute-start | bytes 1966088 | tf_op jit(solution)/shard_map/ppermute | solution.py:471
  3.7 0.7 concatenate.19
  4.4 0.5 collective-permute-start
  4.9 0.7 fusion.28
  5.6 0.1 fusion.14
  5.7 2.0 %pad_maximum_fusion = bf16[336,1024]{1,0:T(8,128)(2,1)} fusion(bf16[16,1024]{1,0:T(8,128)(2,1)S(1)} %fusion.14, bf16[320,1024]{1,0:T(8,128)(2,1)} %refs_3_.1), kind=kLoop, calls=%fused_computation | loop fusion | flops 1376256 | bytes 1376256 | tf_op jit(solution)/shard_map/concatenate | solution.py:512
  7.7 5.1 %collective-permute-start.7 = (bf16[336,1024]{1,0:T(8,128)(2,1)}, bf16[336,1024]{1,0:T(8,128)(2,1)S(1)}, u32[]{:S(2)}, u32[]{:S(2)}) collective-permute-start(bf16[336,1024]{1,0:T(8,128)(2,1)} %pad_maximum_fusion), channel_id=1, source_target_pairs={{0,4},{12,8},{1,5},{13,9},{2,6},{14,10},{3,7},{15,11},{16,20},{28,... | collective-permute-start | bytes 2064392 | tf_op jit(solution)/shard_map/ppermute | solution.py:471
  14.2 0.1 select_select_fusion.refs_0_
  14.4 0.8 %copy-done.5 = bf16[320,1024]{1,0:T(8,128)(2,1)} copy-done((bf16[320,1024]{1,0:T(8,128)(2,1)}, bf16[320,1024]{1,0:T(8,128)(2,1)S(1)}, u32[]{:S(2)}) %copy-start.5) | copy-done | bytes 655384
  15.2 5.4 %shard_map.68 = (f32[320,1024]{1,0:T(8,128)}, f32[640,1024]{1,0:T(8,128)}) custom-call(f32[8,128]{1,0:T(8,128)S(1)} %select_select_fusion.refs_0_, f32[1,640]{1,0:T(1,128)S(1)} %add_convert_fusion.refs_1_, bf16[320,1024]{1,0:T(8,128)(2,1)} %refs_3_.1, bf16[320,1024]{1,0:T(8,128)(2,1)} %copy-done.5, bf16[320,1024]{1,0:T(8,128)(2,1)} %refs_6_), custom_call_target="tpu_custom_call" | custom-call | flops 1024 | bytes 1024 | tf_op jit(solution)/shard_map/pallas_call | solution.py:376
  20.8 1.3 %collective-permute-start.5 = (bf16[160,1024]{1,0:T(8,128)(2,1)S(1)}, bf16[160,1024]{1,0:T(8,128)(2,1)S(1)}, u32[]{:S(2)}, u32[]{:S(2)}) collective-permute-start(bf16[160,1024]{1,0:T(8,128)(2,1)S(1)} %get-tuple-element.60), channel_id=1, source_target_pairs={{4,0},{8,12},{5,1},{9,13},{6,2},{10,14},{7,3},{11,15},{20,16},{24,... | collective-permute-start | bytes 983048 | tf_op jit(solution)/shard_map/ppermute | solution.py:471
  22.1 1.5 %collective-permute-start.6 = (bf16[160,1024]{1,0:T(8,128)(2,1)S(1)}, bf16[160,1024]{1,0:T(8,128)(2,1)S(1)}, u32[]{:S(2)}, u32[]{:S(2)}) collective-permute-start(bf16[160,1024]{1,0:T(8,128)(2,1)S(1)} %get-tuple-element.59), channel_id=1, source_target_pairs={{4,0},{8,12},{5,1},{9,13},{6,2},{10,14},{7,3},{11,15},{20,16},{24,... | collective-permute-start | bytes 983048 | tf_op jit(solution)/shard_map/ppermute | solution.py:471
  23.6 7.5 %shard_map.69 = (f32[320,1024]{1,0:T(8,128)}, f32[320,1024]{1,0:T(8,128)}, f32[640,1024]{1,0:T(8,128)}) custom-call(f32[8,128]{1,0:T(8,128)S(1)} %select_select_fusion.refs_0_, f32[1,640]{1,0:T(1,128)S(1)} %add_convert_fusion.refs_1_, bf16[320,1024]{1,0:T(8,128)(2,1)} %refs_3_.1, bf16[320,1024]{1,0:T(8,128)(2,1)} %copy-done.5, bf16[320,1024]{1,0:T(8,128)(2,1)} %copy-done.6, ...), custom_call_target="tpu_custom_call" | custom-call | flops 1024 | bytes 1024 | tf_op jit(solution)/shard_map/pallas_call | solution.py:376
  31.0 1.7 %collective-permute-done.7.refs_4_.refs_1_.refs_2_ = bf16[336,1024]{1,0:T(8,128)(2,1)S(1)} collective-permute-done((bf16[336,1024]{1,0:T(8,128)(2,1)}, bf16[336,1024]{1,0:T(8,128)(2,1)S(1)}, u32[]{:S(2)}, u32[]{:S(2)}) %collective-permute-start.7) | collective-permute-done | bytes 688160 | tf_op jit(solution)/shard_map/ppermute | solution.py:471
  32.9 0.5 collective-permute-start.8
  33.4 0.7 copy-done.1
  34.1 0.1 collective-permute-start.9
  34.2 5.6 %collective-permute-done.6.refs_7_ = bf16[160,1024]{1,0:T(8,128)(2,1)S(1)} collective-permute-done((bf16[160,1024]{1,0:T(8,128)(2,1)S(1)}, bf16[160,1024]{1,0:T(8,128)(2,1)S(1)}, u32[]{:S(2)}, u32[]{:S(2)}) %collective-permute-start.6) | collective-permute-done | bytes 327712 | tf_op jit(solution)/shard_map/ppermute | solution.py:471
  39.8 3.0 %shard_map.70 = bf16[160,1024]{1,0:T(8,128)(2,1)S(1)} custom-call(f32[8,128]{1,0:T(8,128)S(1)} %select_select_fusion.refs_0_, f32[1,640]{1,0:T(1,128)S(1)} %add_convert_fusion.refs_1_, bf16[320,1024]{1,0:T(8,128)(2,1)} %refs_3_.1, bf16[320,1024]{1,0:T(8,128)(2,1)} %copy-done.5, bf16[336,1024]{1,0:T(8,128)(2,1)S(1)} %collective-permute-done.7.refs_4_.refs_1_.refs_2_, ...), custom_call_target="tpu_custom_call" | custom-call | flops 1024 | bytes 1024 | tf_op jit(solution)/shard_map/pallas_call | solution.py:376
  43.0 5.6 %shard_map.71 = (bf16[160,1024]{1,0:T(8,128)(2,1)}, bf16[320,1024]{1,0:T(8,128)(2,1)}) custom-call(f32[8,128]{1,0:T(8,128)S(1)} %select_select_fusion.refs_0_, f32[1,640]{1,0:T(1,128)S(1)} %add_convert_fusion.refs_1_, bf16[320,1024]{1,0:T(8,128)(2,1)} %refs_3_.1, bf16[320,1024]{1,0:T(8,128)(2,1)} %copy-done.5, ...), custom_call_target="tpu_custom_call" | custom-call | flops 1024 | bytes 1024 | tf_op jit(solution)/shard_map/pallas_call | solution.py:376
  48.6 0.6 collective-permute-start.11
  49.1 3.9 %shard_map.72 = (f32[160,1024]{1,0:T(8,128)S(1)}, f32[160,1024]{1,0:T(8,128)}) custom-call(f32[8,128]{1,0:T(8,128)S(1)} %select_select_fusion.refs_0_, bf16[336,1024]{1,0:T(8,128)(2,1)S(1)} %collective-permute-done.7.refs_4_.refs_1_.refs_2_, bf16[112,1024]{1,0:T(8,128)(2,1)S(1)} %collective-permute-done.8.refs_5_.refs_2_.refs_3_, ...), custom_call_target="tpu_custom_call" | custom-call | flops 1024 | bytes 1024 | tf_op jit(solution)/shard_map/pallas_call | solution.py:376
  53.1 0.7 copy-done
  53.9 4.3 %collective-permute-start.16 = (bf16[160,1024]{1,0:T(8,128)(2,1)}, bf16[160,1024]{1,0:T(8,128)(2,1)S(1)}, u32[]{:S(2)}, u32[]{:S(2)}) collective-permute-start(bf16[160,1024]{1,0:T(8,128)(2,1)} %copy-done), channel_id=1, source_target_pairs={{0,4},{4,0},{8,12},{12,8},{1,5},{5,1},{9,13},{13,9},{2,6},{6,2},{1... | collective-permute-start | bytes 983048 | tf_op jit(solution)/shard_map/ppermute | solution.py:471
  58.2 2.1 %shard_map.74 = bf16[160,1024]{1,0:T(8,128)(2,1)S(1)} custom-call(f32[160,1024]{1,0:T(8,128)} %get-tuple-element.40.total, bf16[160,1024]{1,0:T(8,128)(2,1)} %collective-permute-done.11.arrived), custom_call_target="tpu_custom_call" | custom-call | flops 1024 | bytes 1024 | tf_op jit(solution)/shard_map/pallas_call | solution.py:406
  60.3 4.2 %collective-permute-start.15 = (bf16[160,1024]{1,0:T(8,128)(2,1)S(1)}, bf16[160,1024]{1,0:T(8,128)(2,1)S(1)}, u32[]{:S(2)}, u32[]{:S(2)}) collective-permute-start(bf16[160,1024]{1,0:T(8,128)(2,1)S(1)} %shard_map.74), channel_id=1, source_target_pairs={{0,4},{4,0},{8,12},{12,8},{1,5},{5,1},{9,13},{13,9},{2,6},{6,2},{1... | collective-permute-start | bytes 983048 | tf_op jit(solution)/shard_map/ppermute | solution.py:471
  64.6 6.6 %shard_map.75 = (f32[320,1024]{1,0:T(8,128)S(1)}, bf16[320,1024]{1,0:T(8,128)(2,1)S(1)}) custom-call(f32[8,128]{1,0:T(8,128)S(1)} %select_select_fusion.refs_0_, f32[1,640]{1,0:T(1,128)S(1)} %add_convert_fusion.refs_1_, s32[3]{0:T(128)S(1)} %pad_add_fusion.refs_2_, bf16[320,1024]{1,0:T(8,128)(2,1)} %refs_3_.1, bf16[320,1024]{1,0:T(8,128)(2,1)} %copy-done.5, ...), custom_call_target="tpu_custom_call" | custom-call | flops 1024 | bytes 1024 | tf_op jit(solution)/shard_map/pallas_call | solution.py:376
  71.3 0.5 collective-permute-start.17
  71.8 0.1 collective-permute-start.18
  72.0 1.6 %shard_map.76.here_total = f32[320,1024]{1,0:T(8,128)S(1)} custom-call(f32[8,128]{1,0:T(8,128)S(1)} %select_select_fusion.refs_0_, s32[1]{0:T(128)} %bitcast.2.refs_1_, bf16[336,1024]{1,0:T(8,128)(2,1)S(1)} %collective-permute-done.7.refs_4_.refs_1_.refs_2_, bf16[112,1024]{1,0:T(8,128)(2,1)S(1)} %collective-permute-done.8.refs_5_.refs_2_.refs_3_, ...), custom_call_target="tpu_custom_call" | custom-call | flops 838860800 | bytes 2621440 | tf_op jit(solution)/shard_map/pallas_call | solution.py:376
  73.6 0.9 %shard_map.77 = bf16[320,1024]{1,0:T(8,128)(2,1)} custom-call(f32[320,1024]{1,0:T(8,128)S(1)} %get-tuple-element.46.mine_s, bf16[112,1024]{1,0:T(8,128)(2,1)S(1)} %collective-permute-done.14.rest_0_, bf16[112,1024]{1,0:T(8,128)(2,1)S(1)} %collective-permute-done.17.rest_1_, bf16[96,1024]{1,0:T(8,128)(2,1)S(1)} %collective-permute-done.18.rest_2_), custom_call_target="tpu_custom_call" | custom-call | flops 1024 | bytes 1024 | tf_op jit(solution)/shard_map/pallas_call | solution.py:427
  74.6 0.9 %shard_map.78 = bf16[320,1024]{1,0:T(8,128)(2,1)} custom-call(s32[1]{0:T(128)} %bitcast.3.flag, f32[320,1024]{1,0:T(8,128)S(1)} %shard_map.76.here_total, bf16[320,1024]{1,0:T(8,128)(2,1)S(1)} %collective-permute-done.19.across_back, bf16[160,1024]{1,0:T(8,128)(2,1)S(1)} %collective-permute-done.16.inside_a, ...), custom_call_target="tpu_custom_call" | custom-call | flops 1024 | bytes 1024 | tf_op jit(solution)/shard_map/pallas_call | solution.py:451
  (51 shorter events, 0.8 us)
Async XLA Ops:
  0.6 20.0 %collective-permute-start.2 = (bf16[320,1024]{1,0:T(8,128)(2,1)}, bf16[320,1024]{1,0:T(8,128)(2,1)S(1)}, u32[]{:S(2)}, u32[]{:S(2)}) collective-permute-start(bf16[320,1024]{1,0:T(8,128)(2,1)} %refs_6_), channel_id=1, source_target_pairs={{0,4},{4,0},{8,12},{12,8},{1,5},{5,1},{9,13},{13,9},{2,6},{6,2},{1... | collective-permute-start | bytes 1966088 | tf_op jit(solution)/shard_map/ppermute | solution.py:471
  3.7 17.0 %collective-permute-start.4 = (bf16[320,1024]{1,0:T(8,128)(2,1)}, bf16[320,1024]{1,0:T(8,128)(2,1)S(1)}, u32[]{:S(2)}, u32[]{:S(2)}) collective-permute-start(bf16[320,1024]{1,0:T(8,128)(2,1)} %refs_6_), channel_id=1, source_target_pairs={{4,8},{8,4},{0,1},{12,13},{5,9},{9,5},{1,0},{13,12},{6,10},{10,6},... | collective-permute-start | bytes 1966088 | tf_op jit(solution)/shard_map/ppermute | solution.py:471
  4.4 9.9 %collective-permute-start = (s32[1,320]{1,0:T(1,128)S(1)}, s32[1,320]{1,0:T(1,128)S(1)}, u32[]{:S(2)}, u32[]{:S(2)}) collective-permute-start(s32[1,320]{1,0:T(1,128)S(1)} %concatenate.19), channel_id=1, source_target_pairs={{1,0},{0,1},{3,2},{2,3},{5,4},{4,5},{7,6},{6,7},{9,8},{8,9},{11,10... | collective-permute-start | bytes 3848 | tf_op jit(solution)/shard_map/ppermute | solution.py:21
  4.9 9.4 %collective-permute-start.1 = (bf16[320,1024]{1,0:T(8,128)(2,1)}, bf16[320,1024]{1,0:T(8,128)(2,1)S(1)}, u32[]{:S(2)}, u32[]{:S(2)}) collective-permute-start(bf16[320,1024]{1,0:T(8,128)(2,1)} %refs_3_.1), channel_id=1, source_target_pairs={{1,0},{0,1},{3,2},{2,3},{5,4},{4,5},{7,6},{6,7},{9,8},{8,9},{11,10... | collective-permute-start | bytes 1966088 | tf_op jit(solution)/shard_map/ppermute | solution.py:21
  7.7 25.0 %collective-permute-start.7 = (bf16[336,1024]{1,0:T(8,128)(2,1)}, bf16[336,1024]{1,0:T(8,128)(2,1)S(1)}, u32[]{:S(2)}, u32[]{:S(2)}) collective-permute-start(bf16[336,1024]{1,0:T(8,128)(2,1)} %pad_maximum_fusion), channel_id=1, source_target_pairs={{0,4},{12,8},{1,5},{13,9},{2,6},{14,10},{3,7},{15,11},{16,20},{28,... | collective-permute-start | bytes 2064392 | tf_op jit(solution)/shard_map/ppermute | solution.py:471
  14.4 0.8 %copy-start.5 = (bf16[320,1024]{1,0:T(8,128)(2,1)}, bf16[320,1024]{1,0:T(8,128)(2,1)S(1)}, u32[]{:S(2)}) copy-start(bf16[320,1024]{1,0:T(8,128)(2,1)S(1)} %collective-permute-done.1.refs_3_.refs_4_) | copy-start | bytes 1966084
  20.6 2.9 %copy-start.6 = (bf16[320,1024]{1,0:T(8,128)(2,1)}, bf16[320,1024]{1,0:T(8,128)(2,1)S(1)}, u32[]{:S(2)}) copy-start(bf16[320,1024]{1,0:T(8,128)(2,1)S(1)} %collective-permute-done.2.refs_4_.refs_5_) | copy-start | bytes 1966084
  20.6 19.2 %collective-permute-start.3 = (bf16[320,1024]{1,0:T(8,128)(2,1)S(1)}, bf16[320,1024]{1,0:T(8,128)(2,1)S(1)}, u32[]{:S(2)}, u32[]{:S(2)}) collective-permute-start(bf16[320,1024]{1,0:T(8,128)(2,1)S(1)} %collective-permute-done.2.refs_4_.refs_5_), channel_id=1, source_target_pairs={{4,8},{8,4},{0,1},{12,13},{5,9},{9,5},{1,0},{13,12},{6,10},{10,6},... | collective-permute-start | bytes 1966088 | tf_op jit(solution)/shard_map/ppermute | solution.py:471
  20.8 12.6 %collective-permute-start.5 = (bf16[160,1024]{1,0:T(8,128)(2,1)S(1)}, bf16[160,1024]{1,0:T(8,128)(2,1)S(1)}, u32[]{:S(2)}, u32[]{:S(2)}) collective-permute-start(bf16[160,1024]{1,0:T(8,128)(2,1)S(1)} %get-tuple-element.60), channel_id=1, source_target_pairs={{4,0},{8,12},{5,1},{9,13},{6,2},{10,14},{7,3},{11,15},{20,16},{24,... | collective-permute-start | bytes 983048 | tf_op jit(solution)/shard_map/ppermute | solution.py:471
  22.1 17.7 %collective-permute-start.6 = (bf16[160,1024]{1,0:T(8,128)(2,1)S(1)}, bf16[160,1024]{1,0:T(8,128)(2,1)S(1)}, u32[]{:S(2)}, u32[]{:S(2)}) collective-permute-start(bf16[160,1024]{1,0:T(8,128)(2,1)S(1)} %get-tuple-element.59), channel_id=1, source_target_pairs={{4,0},{8,12},{5,1},{9,13},{6,2},{10,14},{7,3},{11,15},{20,16},{24,... | collective-permute-start | bytes 983048 | tf_op jit(solution)/shard_map/ppermute | solution.py:471
  32.8 7.0 %collective-permute-start.10 = (bf16[112,1024]{1,0:T(8,128)(2,1)S(1)}, bf16[112,1024]{1,0:T(8,128)(2,1)S(1)}, u32[]{:S(2)}, u32[]{:S(2)}) collective-permute-start(bf16[112,1024]{1,0:T(8,128)(2,1)S(1)} %get-tuple-element.54), channel_id=1, source_target_pairs={{1,0},{0,1},{3,2},{2,3},{5,4},{4,5},{7,6},{6,7},{9,8},{8,9},{11,10... | collective-permute-start | bytes 688136 | tf_op jit(solution)/shard_map/ppermute | solution.py:21
  32.9 6.9 %collective-permute-start.8 = (bf16[112,1024]{1,0:T(8,128)(2,1)S(1)}, bf16[112,1024]{1,0:T(8,128)(2,1)S(1)}, u32[]{:S(2)}, u32[]{:S(2)}) collective-permute-start(bf16[112,1024]{1,0:T(8,128)(2,1)S(1)} %get-tuple-element.56), channel_id=1, source_target_pairs={{1,0},{0,1},{3,2},{2,3},{5,4},{4,5},{7,6},{6,7},{9,8},{8,9},{11,10... | collective-permute-start | bytes 688136 | tf_op jit(solution)/shard_map/ppermute | solution.py:21
  33.4 0.7 copy-start.1
  34.1 5.7 %collective-permute-start.9 = (bf16[112,1024]{1,0:T(8,128)(2,1)S(1)}, bf16[112,1024]{1,0:T(8,128)(2,1)S(1)}, u32[]{:S(2)}, u32[]{:S(2)}) collective-permute-start(bf16[112,1024]{1,0:T(8,128)(2,1)S(1)} %get-tuple-element.55), channel_id=1, source_target_pairs={{1,0},{0,1},{3,2},{2,3},{5,4},{4,5},{7,6},{6,7},{9,8},{8,9},{11,10... | collective-permute-start | bytes 688136 | tf_op jit(solution)/shard_map/ppermute | solution.py:21
  39.8 3.1 %copy-start.3 = (bf16[160,1024]{1,0:T(8,128)(2,1)}, bf16[160,1024]{1,0:T(8,128)(2,1)S(1)}, u32[]{:S(2)}) copy-start(bf16[160,1024]{1,0:T(8,128)(2,1)S(1)} %collective-permute-done.6.refs_7_) | copy-start | bytes 983044
  39.8 24.7 %collective-permute-start.13 = (bf16[320,1024]{1,0:T(8,128)(2,1)S(1)}, bf16[320,1024]{1,0:T(8,128)(2,1)S(1)}, u32[]{:S(2)}, u32[]{:S(2)}) collective-permute-start(bf16[320,1024]{1,0:T(8,128)(2,1)S(1)} %collective-permute-done.3.refs_8_.refs_5_), channel_id=1, source_target_pairs={{0,4},{4,0},{8,12},{12,8},{1,5},{5,1},{9,13},{13,9},{2,6},{6,2},{1... | collective-permute-start | bytes 1966088 | tf_op jit(solution)/shard_map/ppermute | solution.py:471
  42.9 10.1 %collective-permute-start.12 = (bf16[160,1024]{1,0:T(8,128)(2,1)S(1)}, bf16[160,1024]{1,0:T(8,128)(2,1)S(1)}, u32[]{:S(2)}, u32[]{:S(2)}) collective-permute-start(bf16[160,1024]{1,0:T(8,128)(2,1)S(1)} %shard_map.70), channel_id=1, source_target_pairs={{4,8},{8,4},{0,1},{12,13},{5,9},{9,5},{1,0},{13,12},{6,10},{10,6},... | collective-permute-start | bytes 983048 | tf_op jit(solution)/shard_map/ppermute | solution.py:471
  48.6 9.6 %collective-permute-start.11 = (bf16[160,1024]{1,0:T(8,128)(2,1)}, bf16[160,1024]{1,0:T(8,128)(2,1)}, u32[]{:S(2)}, u32[]{:S(2)}) collective-permute-start(bf16[160,1024]{1,0:T(8,128)(2,1)} %get-tuple-element.37), channel_id=1, source_target_pairs={{4,8},{8,4},{0,1},{12,13},{5,9},{9,5},{1,0},{13,12},{6,10},{10,6},... | collective-permute-start | bytes 983048 | tf_op jit(solution)/shard_map/ppermute | solution.py:471
  53.1 0.7 copy-start
  53.9 20.7 %collective-permute-start.19 = (bf16[320,1024]{1,0:T(8,128)(2,1)}, bf16[320,1024]{1,0:T(8,128)(2,1)S(1)}, u32[]{:S(2)}, u32[]{:S(2)}) collective-permute-start(bf16[320,1024]{1,0:T(8,128)(2,1)} %get-tuple-element.51), channel_id=1, source_target_pairs={{4,8},{8,4},{0,1},{12,13},{5,9},{9,5},{1,0},{13,12},{6,10},{10,6},... | collective-permute-start | bytes 1966088 | tf_op jit(solution)/shard_map/ppermute | solution.py:471
  53.9 10.7 %copy-start.2 = (bf16[160,1024]{1,0:T(8,128)(2,1)S(1)}, bf16[160,1024]{1,0:T(8,128)(2,1)}, u32[]{:S(2)}) copy-start(bf16[160,1024]{1,0:T(8,128)(2,1)} %copy-done.1) | copy-start | bytes 983044
  53.9 10.7 %copy-start.4 = (bf16[160,1024]{1,0:T(8,128)(2,1)S(1)}, bf16[160,1024]{1,0:T(8,128)(2,1)}, u32[]{:S(2)}) copy-start(bf16[160,1024]{1,0:T(8,128)(2,1)} %copy-done.3) | copy-start | bytes 983044
  53.9 17.9 %collective-permute-start.16 = (bf16[160,1024]{1,0:T(8,128)(2,1)}, bf16[160,1024]{1,0:T(8,128)(2,1)S(1)}, u32[]{:S(2)}, u32[]{:S(2)}) collective-permute-start(bf16[160,1024]{1,0:T(8,128)(2,1)} %copy-done), channel_id=1, source_target_pairs={{0,4},{4,0},{8,12},{12,8},{1,5},{5,1},{9,13},{13,9},{2,6},{6,2},{1... | collective-permute-start | bytes 983048 | tf_op jit(solution)/shard_map/ppermute | solution.py:471
  60.3 13.2 %collective-permute-start.15 = (bf16[160,1024]{1,0:T(8,128)(2,1)S(1)}, bf16[160,1024]{1,0:T(8,128)(2,1)S(1)}, u32[]{:S(2)}, u32[]{:S(2)}) collective-permute-start(bf16[160,1024]{1,0:T(8,128)(2,1)S(1)} %shard_map.74), channel_id=1, source_target_pairs={{0,4},{4,0},{8,12},{12,8},{1,5},{5,1},{9,13},{13,9},{2,6},{6,2},{1... | collective-permute-start | bytes 983048 | tf_op jit(solution)/shard_map/ppermute | solution.py:471
  71.2 2.4 %collective-permute-start.14 = (bf16[112,1024]{1,0:T(8,128)(2,1)S(1)}, bf16[112,1024]{1,0:T(8,128)(2,1)S(1)}, u32[]{:S(2)}, u32[]{:S(2)}) collective-permute-start(bf16[112,1024]{1,0:T(8,128)(2,1)S(1)} %get-tuple-element.58), channel_id=1, source_target_pairs={{1,0},{0,1},{3,2},{2,3},{5,4},{4,5},{7,6},{6,7},{9,8},{8,9},{11,10... | collective-permute-start | bytes 688136 | tf_op jit(solution)/shard_map/ppermute | solution.py:21
  71.3 2.3 %collective-permute-start.17 = (bf16[112,1024]{1,0:T(8,128)(2,1)S(1)}, bf16[112,1024]{1,0:T(8,128)(2,1)S(1)}, u32[]{:S(2)}, u32[]{:S(2)}) collective-permute-start(bf16[112,1024]{1,0:T(8,128)(2,1)S(1)} %get-tuple-element.57), channel_id=1, source_target_pairs={{1,0},{0,1},{3,2},{2,3},{5,4},{4,5},{7,6},{6,7},{9,8},{8,9},{11,10... | collective-permute-start | bytes 688136 | tf_op jit(solution)/shard_map/ppermute | solution.py:21
  71.8 1.8 %collective-permute-start.18 = (bf16[96,1024]{1,0:T(8,128)(2,1)S(1)}, bf16[96,1024]{1,0:T(8,128)(2,1)S(1)}, u32[]{:S(2)}, u32[]{:S(2)}) collective-permute-start(bf16[96,1024]{1,0:T(8,128)(2,1)S(1)} %slice.31), channel_id=1, source_target_pairs={{1,0},{0,1},{3,2},{2,3},{5,4},{4,5},{7,6},{6,7},{9,8},{8,9},{11,10... | collective-permute-start | bytes 589832 | tf_op jit(solution)/shard_map/ppermute | solution.py:21

commit v8 on v7

--- a/solution.py
+++ b/solution.py
@@ -96,10 +96,18 @@
     ends: tuple
     gradient: str
     prior_s: bool
+    skips: bool
     rows: int
 
 
 def pair_body(plan, *refs):
+    if plan.skips:
+        pl.when(refs[0][0] != 0)(functools.partial(pair_steps, plan, *refs[1:]))
+    else:
+        pair_steps(plan, *refs)
+
+
+def pair_steps(plan, *refs):
     refs = list(refs)
     blocks, rows = plan.blocks, plan.rows
     half = rows // 2
@@ -250,12 +258,6 @@
                 outs[i][0][...] = (scale * total).astype(jnp.bfloat16)
 
         if block.optional == "all":
-            if block.prior == "kept":
-                moving_prior[i].wait()
-                moving_prior[i] = Waited()
-                for copy in moving[i]:
-                    copy.wait()
-                moving[i] = []
             pl.when(flags[i] != 0)(work)
         else:
             work()
@@ -268,11 +270,6 @@
         copy.wait()
 
 
-class Waited:
-    def wait(self):
-        pass
-
-
 def in_vmem(array):
     return pltpu.with_memory_space_constraint(array, pltpu.VMEM)
 
@@ -299,7 +296,7 @@
     return pltpu.CompilerParams(vmem_limit_bytes=VMEM_BYTES)
 
 
-def pair_work(consts, blocks, rows, labels=None, node=None, ends=None, gradient="", prior_s=None, cost=SMALL_COST):
+def pair_work(consts, blocks, rows, labels=None, node=None, ends=None, gradient="", prior_s=None, wanted=None, cost=SMALL_COST):
     half = rows // 2
     shapes = tuple(b[0] for b in blocks)
     pieces = []
@@ -313,15 +310,28 @@
     width = arrays[0][0].shape[1]
     ends = ends or ()
     end_rows = tuple(x.shape[0] for x in ends)
-    plan = Plan(shapes, tuple(pieces), node is not None, end_rows, gradient, prior_s is not None, rows)
-
-    operands = [in_vmem(consts)]
-    in_specs = [VMEM_SPEC]
+    plan = Plan(
+        shapes,
+        tuple(pieces),
+        node is not None,
+        end_rows,
+        gradient,
+        prior_s is not None,
+        wanted is not None,
+        rows,
+    )
+
+    operands = []
+    in_specs = []
+    if wanted is not None:
+        operands.append(jnp.int32(wanted).reshape(1))
+        in_specs.append(SMEM_SPEC)
 
     def give(array, away):
         operands.append(in_hbm(array) if away else in_vmem(array))
         in_specs.append(HBM_SPEC if away else VMEM_SPEC)
 
+    give(consts, False)
     if node is not None:
         give(labels, False)
     if any(b.optional == "all" for b in shapes):
@@ -542,15 +552,16 @@
     ends = (end_mine,) + in_thirds(end_mine)
 
     far, *next_out = lax.optimization_barrier((far,) + next_out + (own_s,))[:3]
-    last_out = permute(far, sides)
     (far_a,) = pair_work(
         consts,
         [(Block(far_at, ("node", "ends"), "rounded", 0, half), far, 1, None)],
         rows,
+        wanted=~outer,
         ends=ends,
         **node,
     )
     back_a = permute(far_a, middle)
+    last_out = permute(after(far, far_a), sides)
     far_b, across_out = pair_work(
         consts,
         [
@@ -563,6 +574,7 @@
             (Block(across_at, ("ends",), "rounded", prior="kept"), across, 1, across_g),
         ],
         rows,
+        wanted=~outer,
         ends=ends,
         **node,
     )
@@ -578,6 +590,7 @@
             )
         ],
         rows,
+        wanted=~outer,
         ends=ends,
     )
     total_a = add_rounded(side_total_a, back_a)
@@ -608,13 +621,14 @@
         consts,
         [
             (
-                Block(here_at, ("ends",), "scaled", prior="kept", optional="all"),
+                Block(here_at, ("ends",), "scaled", prior="kept"),
                 Away(late_mine),
-                ~outer,
+                1,
                 here_g,
             )
         ],
         rows,
+        wanted=~outer,
         ends=ends,
         cost=pl.CostEstimate(flops=flops, bytes_accessed=8 * rows * width, transcendentals=0),
     )

time: 76 us -> 74.2 us (0.976)
  Pallas kernels: 37.6 us -> 24.9 us
  starting transfers between devices: 22 us -> 30.8 us
  local copies, waits for them, and re-layouts: 3.14 us -> 4.67 us
  waiting for transfers between devices: 7.37 us -> 8.2 us
    pallas_call x7, Pallas kernels: 33.6 us -> 20.8 us  [pair_work(): pl.pallas_call(functools.partial(pair_body, plan), out_shape=outs, in_spe...]
    ppermute x12, starting transfers between devices: 20.1 us -> 29 us  [permute(): return lax.ppermute(block, ('blk', 'inner'), pairs)]
    slice x3, local copies, waits for them, and re-layouts: 0.09 us -> 0.92 us  [in_thirds(): block[at:at + piece]]
    unnamed x14 -> x12, local copies, waits for them, and re-layouts: 2.31 us -> 3.01 us
  transfers between devices with their start and end apart: 20 -> 20, of which waited for: 2 -> 4; matrix products, arithmetic and copies ran while one was open for 5% -> 6% of each run, Pallas kernels for 49% -> 32%
where the time goes in v8:
time: 74.2 us; the launch traced here: 73.7 us
  starting transfers between devices  30.8 us (42%)
  Pallas kernels  24.9 us (34%)
  waiting for transfers between devices  8.2 us (11%)
  local copies, waits for them, and re-layouts  4.67 us (6%)
  other arithmetic  3.03 us (4%)
  between operations  2.21 us (3%)
    ppermute x12, starting transfers between devices, permute(): return lax.ppermute(block, ('blk', 'inner'), pairs)  29 us
    pallas_call x7, Pallas kernels, pair_work(): pl.pallas_call(functools.partial(pair_body, plan), out_shape=outs, in_spe...  20.8 us
    ppermute x12, waiting for transfers between devices, permute(): return lax.ppermute(block, ('blk', 'inner'), pairs)  8.08 us
    unnamed x12, local copies, waits for them, and re-layouts  3.01 us
    pallas_call x2, Pallas kernels, add_rounded(): pl.pallas_call(add_body, out_shape=vmem_out(arrived.shape, jnp.bfloat16),...  2.2 us
    concatenate x1, other arithmetic, along_line(): jnp.concatenate([spectra, code_labels(labels, LABEL_ROWS, width)])  1.98 us
    ppermute x8, starting transfers between devices, from_behind(): return lax.ppermute(block, axis, route)  1.73 us
  transfers between devices with their start and end apart: 20, of which 4 were waited for; matrix products, arithmetic and copies ran while one was open for 6% of the time, Pallas kernels for 32%

profile of v8, /device:TPU:0, one launch (start us, length us, event | category | flops | bytes accessed | tf_op | source)
XLA Modules:
  0.0 73.7 jit_solution(4508369857089876295)
XLA Ops:
  0.6 3.1 %collective-permute-start.2 = (bf16[320,1024]{1,0:T(8,128)(2,1)}, bf16[320,1024]{1,0:T(8,128)(2,1)}, u32[]{:S(2)}, u32[]{:S(2)}) collective-permute-start(bf16[320,1024]{1,0:T(8,128)(2,1)} %refs_6_), channel_id=1, source_target_pairs={{0,4},{4,0},{8,12},{12,8},{1,5},{5,1},{9,13},{13,9},{2,6},{6,2},{1... | collective-permute-start | bytes 1966088 | tf_op jit(solution)/shard_map/ppermute | solution.py:481
  3.7 0.7 concatenate.19
  4.4 0.5 collective-permute-start
  4.9 0.7 fusion.28
  5.7 2.0 %pad_maximum_fusion = bf16[336,1024]{1,0:T(8,128)(2,1)} fusion(bf16[16,1024]{1,0:T(8,128)(2,1)S(1)} %fusion.14, bf16[320,1024]{1,0:T(8,128)(2,1)} %refs_3_.5), kind=kLoop, calls=%fused_computation | loop fusion | flops 1376256 | bytes 1376256 | tf_op jit(solution)/shard_map/concatenate | solution.py:522
  7.7 5.1 %collective-permute-start.7 = (bf16[336,1024]{1,0:T(8,128)(2,1)}, bf16[336,1024]{1,0:T(8,128)(2,1)S(1)}, u32[]{:S(2)}, u32[]{:S(2)}) collective-permute-start(bf16[336,1024]{1,0:T(8,128)(2,1)} %pad_maximum_fusion), channel_id=1, source_target_pairs={{0,4},{12,8},{1,5},{13,9},{2,6},{14,10},{3,7},{15,11},{16,20},{28,... | collective-permute-start | bytes 2064392 | tf_op jit(solution)/shard_map/ppermute | solution.py:481
  14.4 0.8 %copy-done.5 = bf16[320,1024]{1,0:T(8,128)(2,1)} copy-done((bf16[320,1024]{1,0:T(8,128)(2,1)}, bf16[320,1024]{1,0:T(8,128)(2,1)S(1)}, u32[]{:S(2)}) %copy-start.5) | copy-done | bytes 655384
  15.2 5.4 %shard_map.68 = (f32[320,1024]{1,0:T(8,128)}, f32[640,1024]{1,0:T(8,128)}) custom-call(f32[8,128]{1,0:T(8,128)S(1)} %select_select_fusion.refs_0_.refs_1_, f32[1,640]{1,0:T(1,128)S(1)} %add_convert_fusion.refs_1_.refs_2_, bf16[320,1024]{1,0:T(8,128)(2,1)} %refs_3_.5, bf16[320,1024]{1,0:T(8,128)(2,1)} %copy-done.5, bf16[320,1024]{1,0:T(8,128)(2,1)} %refs_6_), custom_call_target="tpu_custom_call" | custom-call | flops 1024 | bytes 1024 | tf_op jit(solution)/shard_map/pallas_call | solution.py:386
  20.8 1.3 %collective-permute-start.5 = (bf16[160,1024]{1,0:T(8,128)(2,1)S(1)}, bf16[160,1024]{1,0:T(8,128)(2,1)S(1)}, u32[]{:S(2)}, u32[]{:S(2)}) collective-permute-start(bf16[160,1024]{1,0:T(8,128)(2,1)S(1)} %get-tuple-element.60), channel_id=1, source_target_pairs={{4,0},{8,12},{5,1},{9,13},{6,2},{10,14},{7,3},{11,15},{20,16},{24,... | collective-permute-start | bytes 983048 | tf_op jit(solution)/shard_map/ppermute | solution.py:481
  22.1 1.3 %collective-permute-start.6 = (bf16[160,1024]{1,0:T(8,128)(2,1)S(1)}, bf16[160,1024]{1,0:T(8,128)(2,1)S(1)}, u32[]{:S(2)}, u32[]{:S(2)}) collective-permute-start(bf16[160,1024]{1,0:T(8,128)(2,1)S(1)} %get-tuple-element.59), channel_id=1, source_target_pairs={{4,0},{8,12},{5,1},{9,13},{6,2},{10,14},{7,3},{11,15},{20,16},{24,... | collective-permute-start | bytes 983048 | tf_op jit(solution)/shard_map/ppermute | solution.py:481
  23.4 7.5 %shard_map.69 = (f32[320,1024]{1,0:T(8,128)}, f32[320,1024]{1,0:T(8,128)}, f32[640,1024]{1,0:T(8,128)}) custom-call(f32[8,128]{1,0:T(8,128)S(1)} %select_select_fusion.refs_0_.refs_1_, f32[1,640]{1,0:T(1,128)S(1)} %add_convert_fusion.refs_1_.refs_2_, bf16[320,1024]{1,0:T(8,128)(2,1)} %refs_3_.5, bf16[320,1024]{1,0:T(8,128)(2,1)} %copy-done.5, ...), custom_call_target="tpu_custom_call" | custom-call | flops 1024 | bytes 1024 | tf_op jit(solution)/shard_map/pallas_call | solution.py:386
  30.8 1.9 %collective-permute-done.7.refs_5_.refs_2_ = bf16[336,1024]{1,0:T(8,128)(2,1)S(1)} collective-permute-done((bf16[336,1024]{1,0:T(8,128)(2,1)}, bf16[336,1024]{1,0:T(8,128)(2,1)S(1)}, u32[]{:S(2)}, u32[]{:S(2)}) %collective-permute-start.7) | collective-permute-done | bytes 688160 | tf_op jit(solution)/shard_map/ppermute | solution.py:481
  32.8 0.9 %fusion.32 = (bf16[112,1024]{1,0:T(8,128)(2,1)}, bf16[112,1024]{1,0:T(8,128)(2,1)}, bf16[112,1024]{1,0:T(8,128)(2,1)}) fusion(bf16[336,1024]{1,0:T(8,128)(2,1)S(1)} %collective-permute-done.7.refs_5_.refs_2_), kind=kLoop, calls=%fused_computation.58 | loop fusion | bytes 1376256 | tf_op jit(solution)/shard_map/slice | solution.py:518
  33.6 0.5 collective-permute-start.8
  34.2 0.7 copy-done.1
  34.9 4.9 %collective-permute-done.6.refs_7_ = bf16[160,1024]{1,0:T(8,128)(2,1)S(1)} collective-permute-done((bf16[160,1024]{1,0:T(8,128)(2,1)S(1)}, bf16[160,1024]{1,0:T(8,128)(2,1)S(1)}, u32[]{:S(2)}, u32[]{:S(2)}) %collective-permute-start.6) | collective-permute-done | bytes 327712 | tf_op jit(solution)/shard_map/ppermute | solution.py:481
  39.8 0.7 copy-done.3
  40.5 0.1 shard_map.70
  40.7 2.5 %collective-permute-start.13 = (bf16[320,1024]{1,0:T(8,128)(2,1)S(1)}, bf16[320,1024]{1,0:T(8,128)(2,1)S(1)}, u32[]{:S(2)}, u32[]{:S(2)}) collective-permute-start(bf16[320,1024]{1,0:T(8,128)(2,1)S(1)} %collective-permute-done.3.refs_9_.refs_5_), channel_id=1, source_target_pairs={{0,4},{4,0},{8,12},{12,8},{1,5},{5,1},{9,13},{13,9},{2,6},{6,2},{1... | collective-permute-start | bytes 1966088 | tf_op jit(solution)/shard_map/ppermute | solution.py:481
  43.2 1.1 %shard_map.71 = (bf16[160,1024]{1,0:T(8,128)(2,1)}, bf16[320,1024]{1,0:T(8,128)(2,1)}) custom-call(s32[1]{0:T(128)} %bitcast.2.refs_0_, f32[8,128]{1,0:T(8,128)S(1)} %select_select_fusion.refs_0_.refs_1_, f32[1,640]{1,0:T(1,128)S(1)} %add_convert_fusion.refs_1_.refs_2_, bf16[320,1024]{1,0:T(8,128)(2,1)} %refs_3_.5, bf16[320,1024]{1,0:T(8,128)(2,1)} %copy-done.5, ...), custom_call_target="tpu_custom_call" | custom-call | flops 1024 | bytes 1024 | tf_op jit(solution)/shard_map/pallas_call | solution.py:386
  44.2 0.6 collective-permute-start.11
  45.0 0.7 copy-done
  45.7 0.2 collective-permute-start.19
  45.9 10.7 %collective-permute-start.16 = (bf16[160,1024]{1,0:T(8,128)(2,1)}, bf16[160,1024]{1,0:T(8,128)(2,1)S(1)}, u32[]{:S(2)}, u32[]{:S(2)}) collective-permute-start(bf16[160,1024]{1,0:T(8,128)(2,1)} %copy-done), channel_id=1, source_target_pairs={{0,4},{4,0},{8,12},{12,8},{1,5},{5,1},{9,13},{13,9},{2,6},{6,2},{1... | collective-permute-start | bytes 983048 | tf_op jit(solution)/shard_map/ppermute | solution.py:481
  56.7 2.1 %shard_map.74 = bf16[160,1024]{1,0:T(8,128)(2,1)S(1)} custom-call(f32[160,1024]{1,0:T(8,128)} %get-tuple-element.40.total, bf16[160,1024]{1,0:T(8,128)(2,1)} %collective-permute-done.11.arrived), custom_call_target="tpu_custom_call" | custom-call | flops 1024 | bytes 1024 | tf_op jit(solution)/shard_map/pallas_call | solution.py:416
  58.9 4.2 %collective-permute-start.15 = (bf16[160,1024]{1,0:T(8,128)(2,1)S(1)}, bf16[160,1024]{1,0:T(8,128)(2,1)S(1)}, u32[]{:S(2)}, u32[]{:S(2)}) collective-permute-start(bf16[160,1024]{1,0:T(8,128)(2,1)S(1)} %shard_map.74), channel_id=1, source_target_pairs={{0,4},{4,0},{8,12},{12,8},{1,5},{5,1},{9,13},{13,9},{2,6},{6,2},{1... | collective-permute-start | bytes 983048 | tf_op jit(solution)/shard_map/ppermute | solution.py:481
  63.1 6.6 %shard_map.75 = (f32[320,1024]{1,0:T(8,128)S(1)}, bf16[320,1024]{1,0:T(8,128)(2,1)S(1)}) custom-call(f32[8,128]{1,0:T(8,128)S(1)} %select_select_fusion.refs_0_.refs_1_, f32[1,640]{1,0:T(1,128)S(1)} %add_convert_fusion.refs_1_.refs_2_, s32[3]{0:T(128)S(1)} %pad_add_fusion.refs_2_, bf16[320,1024]{1,0:T(8,128)(2,1)} %refs_3_.5, bf16[320,1024]{1,0:T(8,128)(2,1)} %copy-done.5, ...), custom_call_target="tpu_custom_call" | custom-call | flops 1024 | bytes 1024 | tf_op jit(solution)/shard_map/pallas_call | solution.py:386
  69.8 0.5 collective-permute-start.17
  70.3 0.1 collective-permute-start.18
  70.6 1.2 %collective-permute-done.15.inside_b = bf16[160,1024]{1,0:T(8,128)(2,1)S(1)} collective-permute-done((bf16[160,1024]{1,0:T(8,128)(2,1)S(1)}, bf16[160,1024]{1,0:T(8,128)(2,1)S(1)}, u32[]{:S(2)}, u32[]{:S(2)}) %collective-permute-start.15) | collective-permute-done | bytes 327712 | tf_op jit(solution)/shard_map/ppermute | solution.py:481
  71.9 0.9 %shard_map.77 = bf16[320,1024]{1,0:T(8,128)(2,1)} custom-call(f32[320,1024]{1,0:T(8,128)S(1)} %get-tuple-element.46.mine_s, bf16[112,1024]{1,0:T(8,128)(2,1)S(1)} %collective-permute-done.14.rest_0_, bf16[112,1024]{1,0:T(8,128)(2,1)S(1)} %collective-permute-done.17.rest_1_, bf16[96,1024]{1,0:T(8,128)(2,1)S(1)} %collective-permute-done.18.rest_2_), custom_call_target="tpu_custom_call" | custom-call | flops 1024 | bytes 1024 | tf_op jit(solution)/shard_map/pallas_call | solution.py:437
  72.8 0.9 %shard_map.78 = bf16[320,1024]{1,0:T(8,128)(2,1)} custom-call(s32[1]{0:T(128)} %bitcast.3.flag, f32[320,1024]{1,0:T(8,128)S(1)} %shard_map.76.here_total, bf16[320,1024]{1,0:T(8,128)(2,1)S(1)} %collective-permute-done.19.across_back, bf16[160,1024]{1,0:T(8,128)(2,1)S(1)} %collective-permute-done.16.inside_a, ...), custom_call_target="tpu_custom_call" | custom-call | flops 1024 | bytes 1024 | tf_op jit(solution)/shard_map/pallas_call | solution.py:461
  (49 shorter events, 1.0 us)
Async XLA Ops:
  0.6 20.0 %collective-permute-start.2 = (bf16[320,1024]{1,0:T(8,128)(2,1)}, bf16[320,1024]{1,0:T(8,128)(2,1)}, u32[]{:S(2)}, u32[]{:S(2)}) collective-permute-start(bf16[320,1024]{1,0:T(8,128)(2,1)} %refs_6_), channel_id=1, source_target_pairs={{0,4},{4,0},{8,12},{12,8},{1,5},{5,1},{9,13},{13,9},{2,6},{6,2},{1... | collective-permute-start | bytes 1966088 | tf_op jit(solution)/shard_map/ppermute | solution.py:481
  3.7 17.0 %collective-permute-start.4 = (bf16[320,1024]{1,0:T(8,128)(2,1)}, bf16[320,1024]{1,0:T(8,128)(2,1)S(1)}, u32[]{:S(2)}, u32[]{:S(2)}) collective-permute-start(bf16[320,1024]{1,0:T(8,128)(2,1)} %refs_6_), channel_id=1, source_target_pairs={{4,8},{8,4},{0,1},{12,13},{5,9},{9,5},{1,0},{13,12},{6,10},{10,6},... | collective-permute-start | bytes 1966088 | tf_op jit(solution)/shard_map/ppermute | solution.py:481
  4.4 9.9 %collective-permute-start = (s32[1,320]{1,0:T(1,128)S(1)}, s32[1,320]{1,0:T(1,128)S(1)}, u32[]{:S(2)}, u32[]{:S(2)}) collective-permute-start(s32[1,320]{1,0:T(1,128)S(1)} %concatenate.19), channel_id=1, source_target_pairs={{1,0},{0,1},{3,2},{2,3},{5,4},{4,5},{7,6},{6,7},{9,8},{8,9},{11,10... | collective-permute-start | bytes 3848 | tf_op jit(solution)/shard_map/ppermute | solution.py:21
  4.9 9.4 %collective-permute-start.1 = (bf16[320,1024]{1,0:T(8,128)(2,1)}, bf16[320,1024]{1,0:T(8,128)(2,1)S(1)}, u32[]{:S(2)}, u32[]{:S(2)}) collective-permute-start(bf16[320,1024]{1,0:T(8,128)(2,1)} %refs_3_.5), channel_id=1, source_target_pairs={{1,0},{0,1},{3,2},{2,3},{5,4},{4,5},{7,6},{6,7},{9,8},{8,9},{11,10... | collective-permute-start | bytes 1966088 | tf_op jit(solution)/shard_map/ppermute | solution.py:21
  7.7 25.0 %collective-permute-start.7 = (bf16[336,1024]{1,0:T(8,128)(2,1)}, bf16[336,1024]{1,0:T(8,128)(2,1)S(1)}, u32[]{:S(2)}, u32[]{:S(2)}) collective-permute-start(bf16[336,1024]{1,0:T(8,128)(2,1)} %pad_maximum_fusion), channel_id=1, source_target_pairs={{0,4},{12,8},{1,5},{13,9},{2,6},{14,10},{3,7},{15,11},{16,20},{28,... | collective-permute-start | bytes 2064392 | tf_op jit(solution)/shard_map/ppermute | solution.py:481
  14.4 0.8 %copy-start.5 = (bf16[320,1024]{1,0:T(8,128)(2,1)}, bf16[320,1024]{1,0:T(8,128)(2,1)S(1)}, u32[]{:S(2)}) copy-start(bf16[320,1024]{1,0:T(8,128)(2,1)S(1)} %collective-permute-done.1.refs_3_.refs_4_) | copy-start | bytes 1966084
  20.6 19.9 %collective-permute-start.3 = (bf16[320,1024]{1,0:T(8,128)(2,1)}, bf16[320,1024]{1,0:T(8,128)(2,1)S(1)}, u32[]{:S(2)}, u32[]{:S(2)}) collective-permute-start(bf16[320,1024]{1,0:T(8,128)(2,1)} %collective-permute-done.2.refs_4_.refs_6_), channel_id=1, source_target_pairs={{4,8},{8,4},{0,1},{12,13},{5,9},{9,5},{1,0},{13,12},{6,10},{10,6},... | collective-permute-start | bytes 1966088 | tf_op jit(solution)/shard_map/ppermute | solution.py:481
  20.8 13.4 %collective-permute-start.5 = (bf16[160,1024]{1,0:T(8,128)(2,1)S(1)}, bf16[160,1024]{1,0:T(8,128)(2,1)S(1)}, u32[]{:S(2)}, u32[]{:S(2)}) collective-permute-start(bf16[160,1024]{1,0:T(8,128)(2,1)S(1)} %get-tuple-element.60), channel_id=1, source_target_pairs={{4,0},{8,12},{5,1},{9,13},{6,2},{10,14},{7,3},{11,15},{20,16},{24,... | collective-permute-start | bytes 983048 | tf_op jit(solution)/shard_map/ppermute | solution.py:481
  22.1 17.7 %collective-permute-start.6 = (bf16[160,1024]{1,0:T(8,128)(2,1)S(1)}, bf16[160,1024]{1,0:T(8,128)(2,1)S(1)}, u32[]{:S(2)}, u32[]{:S(2)}) collective-permute-start(bf16[160,1024]{1,0:T(8,128)(2,1)S(1)} %get-tuple-element.59), channel_id=1, source_target_pairs={{4,0},{8,12},{5,1},{9,13},{6,2},{10,14},{7,3},{11,15},{20,16},{24,... | collective-permute-start | bytes 983048 | tf_op jit(solution)/shard_map/ppermute | solution.py:481
  33.6 6.9 %collective-permute-start.10 = (bf16[112,1024]{1,0:T(8,128)(2,1)}, bf16[112,1024]{1,0:T(8,128)(2,1)S(1)}, u32[]{:S(2)}, u32[]{:S(2)}) collective-permute-start(bf16[112,1024]{1,0:T(8,128)(2,1)} %get-tuple-element.54), channel_id=1, source_target_pairs={{1,0},{0,1},{3,2},{2,3},{5,4},{4,5},{7,6},{6,7},{9,8},{8,9},{11,10... | collective-permute-start | bytes 688136 | tf_op jit(solution)/shard_map/ppermute | solution.py:21
  33.6 6.9 %collective-permute-start.8 = (bf16[112,1024]{1,0:T(8,128)(2,1)}, bf16[112,1024]{1,0:T(8,128)(2,1)S(1)}, u32[]{:S(2)}, u32[]{:S(2)}) collective-permute-start(bf16[112,1024]{1,0:T(8,128)(2,1)} %get-tuple-element.56), channel_id=1, source_target_pairs={{1,0},{0,1},{3,2},{2,3},{5,4},{4,5},{7,6},{6,7},{9,8},{8,9},{11,10... | collective-permute-start | bytes 688136 | tf_op jit(solution)/shard_map/ppermute | solution.py:21
  34.2 0.7 copy-start.1
  34.9 5.7 %collective-permute-start.9 = (bf16[112,1024]{1,0:T(8,128)(2,1)}, bf16[112,1024]{1,0:T(8,128)(2,1)S(1)}, u32[]{:S(2)}, u32[]{:S(2)}) collective-permute-start(bf16[112,1024]{1,0:T(8,128)(2,1)} %get-tuple-element.55), channel_id=1, source_target_pairs={{1,0},{0,1},{3,2},{2,3},{5,4},{4,5},{7,6},{6,7},{9,8},{8,9},{11,10... | collective-permute-start | bytes 688136 | tf_op jit(solution)/shard_map/ppermute | solution.py:21
  39.8 0.7 copy-start.3
  40.7 22.4 %collective-permute-start.13 = (bf16[320,1024]{1,0:T(8,128)(2,1)S(1)}, bf16[320,1024]{1,0:T(8,128)(2,1)S(1)}, u32[]{:S(2)}, u32[]{:S(2)}) collective-permute-start(bf16[320,1024]{1,0:T(8,128)(2,1)S(1)} %collective-permute-done.3.refs_9_.refs_5_), channel_id=1, source_target_pairs={{0,4},{4,0},{8,12},{12,8},{1,5},{5,1},{9,13},{13,9},{2,6},{6,2},{1... | collective-permute-start | bytes 1966088 | tf_op jit(solution)/shard_map/ppermute | solution.py:481
  43.1 1.8 %collective-permute-start.12 = (bf16[160,1024]{1,0:T(8,128)(2,1)S(1)}, bf16[160,1024]{1,0:T(8,128)(2,1)S(1)}, u32[]{:S(2)}, u32[]{:S(2)}) collective-permute-start(bf16[160,1024]{1,0:T(8,128)(2,1)S(1)} %shard_map.70), channel_id=1, source_target_pairs={{4,8},{8,4},{0,1},{12,13},{5,9},{9,5},{1,0},{13,12},{6,10},{10,6},... | collective-permute-start | bytes 983048 | tf_op jit(solution)/shard_map/ppermute | solution.py:481
  44.2 12.5 %collective-permute-start.11 = (bf16[160,1024]{1,0:T(8,128)(2,1)}, bf16[160,1024]{1,0:T(8,128)(2,1)}, u32[]{:S(2)}, u32[]{:S(2)}) collective-permute-start(bf16[160,1024]{1,0:T(8,128)(2,1)} %get-tuple-element.37), channel_id=1, source_target_pairs={{4,8},{8,4},{0,1},{12,13},{5,9},{9,5},{1,0},{13,12},{6,10},{10,6},... | collective-permute-start | bytes 983048 | tf_op jit(solution)/shard_map/ppermute | solution.py:481
  45.0 0.7 copy-start
  45.7 27.1 %collective-permute-start.19 = (bf16[320,1024]{1,0:T(8,128)(2,1)}, bf16[320,1024]{1,0:T(8,128)(2,1)S(1)}, u32[]{:S(2)}, u32[]{:S(2)}) collective-permute-start(bf16[320,1024]{1,0:T(8,128)(2,1)} %get-tuple-element.51), channel_id=1, source_target_pairs={{4,8},{8,4},{0,1},{12,13},{5,9},{9,5},{1,0},{13,12},{6,10},{10,6},... | collective-permute-start | bytes 1966088 | tf_op jit(solution)/shard_map/ppermute | solution.py:481
  45.9 17.2 %copy-start.2 = (bf16[160,1024]{1,0:T(8,128)(2,1)S(1)}, bf16[160,1024]{1,0:T(8,128)(2,1)}, u32[]{:S(2)}) copy-start(bf16[160,1024]{1,0:T(8,128)(2,1)} %copy-done.1) | copy-start | bytes 983044
  45.9 17.2 %copy-start.4 = (bf16[160,1024]{1,0:T(8,128)(2,1)S(1)}, bf16[160,1024]{1,0:T(8,128)(2,1)}, u32[]{:S(2)}) copy-start(bf16[160,1024]{1,0:T(8,128)(2,1)} %copy-done.3) | copy-start | bytes 983044
  45.9 24.4 %collective-permute-start.16 = (bf16[160,1024]{1,0:T(8,128)(2,1)}, bf16[160,1024]{1,0:T(8,128)(2,1)S(1)}, u32[]{:S(2)}, u32[]{:S(2)}) collective-permute-start(bf16[160,1024]{1,0:T(8,128)(2,1)} %copy-done), channel_id=1, source_target_pairs={{0,4},{4,0},{8,12},{12,8},{1,5},{5,1},{9,13},{13,9},{2,6},{6,2},{1... | collective-permute-start | bytes 983048 | tf_op jit(solution)/shard_map/ppermute | solution.py:481
  58.9 12.9 %collective-permute-start.15 = (bf16[160,1024]{1,0:T(8,128)(2,1)S(1)}, bf16[160,1024]{1,0:T(8,128)(2,1)S(1)}, u32[]{:S(2)}, u32[]{:S(2)}) collective-permute-start(bf16[160,1024]{1,0:T(8,128)(2,1)S(1)} %shard_map.74), channel_id=1, source_target_pairs={{0,4},{4,0},{8,12},{12,8},{1,5},{5,1},{9,13},{13,9},{2,6},{6,2},{1... | collective-permute-start | bytes 983048 | tf_op jit(solution)/shard_map/ppermute | solution.py:481
  69.7 2.1 %collective-permute-start.14 = (bf16[112,1024]{1,0:T(8,128)(2,1)S(1)}, bf16[112,1024]{1,0:T(8,128)(2,1)S(1)}, u32[]{:S(2)}, u32[]{:S(2)}) collective-permute-start(bf16[112,1024]{1,0:T(8,128)(2,1)S(1)} %get-tuple-element.58), channel_id=1, source_target_pairs={{1,0},{0,1},{3,2},{2,3},{5,4},{4,5},{7,6},{6,7},{9,8},{8,9},{11,10... | collective-permute-start | bytes 688136 | tf_op jit(solution)/shard_map/ppermute | solution.py:21
  69.8 2.1 %collective-permute-start.17 = (bf16[112,1024]{1,0:T(8,128)(2,1)S(1)}, bf16[112,1024]{1,0:T(8,128)(2,1)S(1)}, u32[]{:S(2)}, u32[]{:S(2)}) collective-permute-start(bf16[112,1024]{1,0:T(8,128)(2,1)S(1)} %get-tuple-element.57), channel_id=1, source_target_pairs={{1,0},{0,1},{3,2},{2,3},{5,4},{4,5},{7,6},{6,7},{9,8},{8,9},{11,10... | collective-permute-start | bytes 688136 | tf_op jit(solution)/shard_map/ppermute | solution.py:21
  70.3 1.6 %collective-permute-start.18 = (bf16[96,1024]{1,0:T(8,128)(2,1)S(1)}, bf16[96,1024]{1,0:T(8,128)(2,1)S(1)}, u32[]{:S(2)}, u32[]{:S(2)}) collective-permute-start(bf16[96,1024]{1,0:T(8,128)(2,1)S(1)} %slice.31), channel_id=1, source_target_pairs={{1,0},{0,1},{3,2},{2,3},{5,4},{4,5},{7,6},{6,7},{9,8},{8,9},{11,10... | collective-permute-start | bytes 589832 | tf_op jit(solution)/shard_map/ppermute | solution.py:21

commit v9 on v8

--- a/solution.py
+++ b/solution.py
@@ -82,8 +82,8 @@
     target: int
     uses: tuple
     out: str
-    start: int = 0
-    count: int = 0
+    offset: int = 0
+    cut: int = 0
     prior: str = ""
     optional: str = ""
 
@@ -156,8 +156,7 @@
         at = 0
         for ref, (count, away) in zip(held_in[i], plan.pieces[i]):
             if away:
-                part = ref.at[pl.ds(block.start, count)]
-                moves.append(move(part, held[i].at[pl.ds(at, count)]))
+                moves.append(move(ref, held[i].at[pl.ds(at, count)]))
             at += count
         moving.append(moves)
     moving_prior = [
@@ -203,13 +202,13 @@
             at = 0
             for ref, (count, away) in zip(held_in[i], plan.pieces[i]):
                 if not away:
-                    held[i][pl.ds(at, count)] = ref[pl.ds(block.start, count)]
+                    held[i][pl.ds(at, count)] = ref[...]
                 at += count
             for copy in moving[i]:
                 copy.wait()
             glycans = held[i][...]
             targets = lax.broadcasted_iota(jnp.int32, (glycans.shape[0], 1), 0)
-            targets = targets.astype(jnp.float32) + (const(block.target) + float(block.start))
+            targets = targets.astype(jnp.float32) + (const(block.target) + float(block.offset))
             total = None
             for use in block.uses:
                 here, row_labels = source(use)
@@ -247,8 +246,9 @@
                 out_held[i][...] = total
                 leaving.append(move(out_held[i], outs[i][0]))
             elif block.out == "split":
-                outs[i][0][...] = scale * total[:half]
-                out_held[i][...] = scale * total[half:]
+                cut = outs[i][0].shape[0]
+                outs[i][0][...] = scale * total[:cut]
+                out_held[i][...] = scale * total[cut:]
                 leaving.append(move(out_held[i], outs[i][1]))
             elif block.out == "total":
                 outs[i][0][...] = total
@@ -305,7 +305,7 @@
         parts = array if isinstance(array, tuple) else (array,)
         away = [isinstance(x, Away) for x in parts]
         parts = [x.array if flag else x for x, flag in zip(parts, away)]
-        pieces.append(tuple((shape.count or x.shape[0], flag) for x, flag in zip(parts, away)))
+        pieces.append(tuple((x.shape[0], flag) for x, flag in zip(parts, away)))
         arrays += list(zip(parts, away))
     width = arrays[0][0].shape[1]
     ends = ends or ()
@@ -359,8 +359,8 @@
 
     for shape, count in zip(shapes, counts):
         if shape.out == "split":
-            get((half, width), jnp.float32, False)
-            get((half, width), jnp.float32, True)
+            get((shape.cut, width), jnp.float32, False)
+            get((count - shape.cut, width), jnp.float32, True)
         elif shape.out:
             kind = jnp.bfloat16 if shape.out == "rounded" else jnp.float32
             get((count, width), kind, shape.out == "kept")
@@ -379,7 +379,7 @@
     scratch += [pltpu.VMEM((n, width), jnp.float32) for n, b in zip(counts, shapes) if b.prior == "kept"]
     for n, b in zip(counts, shapes):
         if b.out in ("kept", "split"):
-            scratch.append(pltpu.VMEM((n if b.out == "kept" else half, width), jnp.float32))
+            scratch.append(pltpu.VMEM((n - b.cut, width), jnp.float32))
     if gradient:
         scratch.append(pltpu.VMEM((2 * rows, width), jnp.float32))
     scratch.append(pltpu.SemaphoreType.DMA((len(operands) + len(outs),)))
@@ -398,6 +398,23 @@
     digits = jnp.stack([labels // 16384, labels // 128 % 128, labels % 128]).astype(jnp.bfloat16)
     digits = jnp.concatenate([digits, digits, digits], axis=1)
     return jnp.pad(digits, ((0, row_count - 3), (0, width - digits.shape[1])))
+
+
+def join_body(first, second, out):
+    out[pl.ds(0, first.shape[0])] = first[...]
+    out[pl.ds(first.shape[0], second.shape[0])] = second[...]
+
+
+def join(first, second):
+    rows = first.shape[0] + second.shape[0]
+    return pl.pallas_call(
+        join_body,
+        out_shape=vmem_out((rows, first.shape[1]), first.dtype),
+        in_specs=[VMEM_SPEC] * 2,
+        out_specs=VMEM_SPEC,
+        cost_estimate=SMALL_COST,
+        compiler_params=params(),
+    )(in_vmem(first), in_vmem(second))
 
 
 def add_body(total, arrived, out, *scratch):
@@ -513,13 +530,14 @@
     for i, value in enumerate(rows_of_consts):
         consts = jnp.where(index == i, value, consts)
 
-    def in_thirds(block):
-        piece = -(-block.shape[0] // 48) * 16
+    def in_pieces(block, piece):
         return tuple(swap_inner(block[at : at + piece]) for at in range(0, block.shape[0], piece))
 
     across = permute(glycans, middle)
+    cut_a = rows // 2 + 16
     side = permute(glycans, sides)
-    end_mine = permute(jnp.concatenate([spectra, code_labels(labels, LABEL_ROWS, width)]), inward)
+    coded = code_labels(labels, LABEL_ROWS, width)
+    end_mine = permute(jnp.concatenate([spectra, coded]), inward)
     partner = swap_inner(spectra)
     own_labels = labels.reshape(1, rows)
     node_labels = jnp.concatenate([own_labels, swap_inner(own_labels)], axis=1)
@@ -534,9 +552,11 @@
     )
 
     side = after(side, here_g)
-    far = permute(side, middle)
+    far_a = permute(side[:cut_a], middle)
+    far_b = permute(side[cut_a:], middle)
     across = after(across, side)
-    next_out = tuple(permute(across[at : at + half], outward) for at in (0, half))
+    cut = rows // 2
+    next_out = (permute(across[:cut], outward), permute(across[cut:], outward))
     side_g, across_g, own_s = pair_work(
         consts,
         [
@@ -548,47 +568,46 @@
         prior_s=own_s,
         **node,
     )
+    far_a = after(far_a, own_s)
+    (far_g,) = pair_work(
+        consts,
+        [(Block(far_at, ("node",), "total"), far_a, 1, None)],
+        rows,
+        wanted=~outer,
+        **node,
+    )
     end_mine = after(end_mine, own_s)
-    ends = (end_mine,) + in_thirds(end_mine)
-
-    far, *next_out = lax.optimization_barrier((far,) + next_out + (own_s,))[:3]
-    (far_a,) = pair_work(
-        consts,
-        [(Block(far_at, ("node", "ends"), "rounded", 0, half), far, 1, None)],
+    piece = -(-rows // 48) * 16
+    ends = (end_mine,) + in_pieces(end_mine, piece)
+
+    far_a, *next_out = lax.optimization_barrier((far_a,) + next_out + (far_g,))[:3]
+    (far_a_out,) = pair_work(
+        consts,
+        [(Block(far_at, ("ends",), "rounded", prior="near"), far_a, 1, far_g)],
+        rows,
+        wanted=~outer,
+        ends=ends,
+    )
+    back_a = permute(far_a_out, middle)
+    far_b = after(far_b, far_a_out)
+    far = join(far_a, far_b)
+    last_out = permute(far, sides)
+    far_b_out, across_out = pair_work(
+        consts,
+        [
+            (Block(far_at, ("node", "ends"), "rounded", cut_a), far_b, 1, None),
+            (Block(across_at, ("ends",), "rounded", prior="kept"), across, 1, across_g),
+        ],
         rows,
         wanted=~outer,
         ends=ends,
         **node,
     )
-    back_a = permute(far_a, middle)
-    last_out = permute(after(far, far_a), sides)
-    far_b, across_out = pair_work(
-        consts,
-        [
-            (
-                Block(far_at, ("node", "ends"), "rounded", half, half),
-                after(far, far_a),
-                1,
-                None,
-            ),
-            (Block(across_at, ("ends",), "rounded", prior="kept"), across, 1, across_g),
-        ],
-        rows,
-        wanted=~outer,
-        ends=ends,
-        **node,
-    )
-    back_b = permute(far_b, middle)
+    back_b = permute(far_b_out, middle)
+    late_side = Away(after(side, far_b_out))
     side_total_a, side_total_b = pair_work(
         consts,
-        [
-            (
-                Block(side_at, ("ends",), "split", prior="kept"),
-                Away(after(side, far_b)),
-                1,
-                side_g,
-            )
-        ],
+        [(Block(side_at, ("ends",), "split", cut=cut_a, prior="kept"), late_side, 1, side_g)],
         rows,
         wanted=~outer,
         ends=ends,
@@ -614,25 +633,18 @@
         prior_s=own_s,
         **node,
     )
-    others = list(in_thirds(other_s))
+    others = list(in_pieces(other_s, piece))
     inside_a, late_mine = lax.optimization_barrier((inside_a, glycans))
     flops = 2 * 2 * 2 * rows * rows * width
     (here_total,) = pair_work(
         consts,
-        [
-            (
-                Block(here_at, ("ends",), "scaled", prior="kept"),
-                Away(late_mine),
-                1,
-                here_g,
-            )
-        ],
+        [(Block(here_at, ("ends",), "scaled", prior="kept"), Away(late_mine), 1, here_g)],
         rows,
         wanted=~outer,
         ends=ends,
         cost=pl.CostEstimate(flops=flops, bytes_accessed=8 * rows * width, transcendentals=0),
     )
-    others[0] = after(others[0], inside_b, here_total)
+    others[0] = after(others[0], here_total)
     grad_spectra = finish_spectra(mine_s, others)
     across_back = after(across_back, grad_spectra)
     return grad_spectra, finish_structures(outer, here_total, across_back, inside_a, inside_b)

time: 74.2 us -> 76.7 us (1.034)
  local copies, waits for them, and re-layouts: 4.67 us -> 7.36 us
  waiting for transfers between devices: 8.2 us -> 6.81 us
    ppermute x12 -> x13, waiting for transfers between devices: 8.08 us -> 5.47 us  [permute(): return lax.ppermute(block, ('blk', 'inner'), pairs)]
    slice x4 -> x6, local copies, waits for them, and re-layouts: 0.96 us -> 2.51 us  [the longest x3 0.89 us: in_pieces(): block[at:at + piece]]
    ppermute x8, waiting for transfers between devices: 0.12 us -> 1.34 us  [from_behind(): return lax.ppermute(block, axis, route)]
    unnamed x12, local copies, waits for them, and re-layouts: 3.01 us -> 4.16 us
    pallas_call x7 -> x8, Pallas kernels: 20.8 us -> 21.4 us  [pair_work(): pl.pallas_call(functools.partial(pair_body, plan), out_shape=outs, in_spe...]
    ppermute x12 -> x13, starting transfers between devices: 29 us -> 29.4 us  [permute(): return lax.ppermute(block, ('blk', 'inner'), pairs)]
  transfers between devices with their start and end apart: 20 -> 21, of which waited for: 4 -> 4; matrix products, arithmetic and copies ran while one was open for 6% -> 8% of each run, Pallas kernels for 32% -> 32%
where the time goes in v9:
time: 76.7 us; the launch traced here: 76.1 us
  starting transfers between devices  31.2 us (41%)
  Pallas kernels  25.5 us (33%)
  local copies, waits for them, and re-layouts  7.36 us (10%)
  waiting for transfers between devices  6.81 us (9%)
  other arithmetic  3.03 us (4%)
  between operations  2.23 us (3%)
    ppermute x13, starting transfers between devices, permute(): return lax.ppermute(block, ('blk', 'inner'), pairs)  29.4 us
    pallas_call x8, Pallas kernels, pair_work(): pl.pallas_call(functools.partial(pair_body, plan), out_shape=outs, in_spe...  21.4 us
    ppermute x13, waiting for transfers between devices, permute(): return lax.ppermute(block, ('blk', 'inner'), pairs)  5.47 us
    unnamed x12, local copies, waits for them, and re-layouts  4.16 us
    pallas_call x2, Pallas kernels, add_rounded(): pl.pallas_call(add_body, out_shape=vmem_out(arrived.shape, jnp.bfloat16),...  2.15 us
    concatenate x1, other arithmetic, along_line(): end_mine = permute(jnp.concatenate([spectra, coded]), inward)  1.98 us
    ppermute x8, starting transfers between devices, from_behind(): return lax.ppermute(block, axis, route)  1.79 us
  transfers between devices with their start and end apart: 21, of which 4 were waited for; matrix products, arithmetic and copies ran while one was open for 8% of the time, Pallas kernels for 32%

profile of v9, /device:TPU:0, one launch (start us, length us, event | category | flops | bytes accessed | tf_op | source)
XLA Modules:
  0.0 76.1 jit_solution(14188924518079006028)
XLA Ops:
  0.6 3.1 %collective-permute-start.2 = (bf16[320,1024]{1,0:T(8,128)(2,1)}, bf16[320,1024]{1,0:T(8,128)(2,1)S(1)}, u32[]{:S(2)}, u32[]{:S(2)}) collective-permute-start(bf16[320,1024]{1,0:T(8,128)(2,1)} %refs_6_), channel_id=1, source_target_pairs={{0,4},{4,0},{8,12},{12,8},{1,5},{5,1},{9,13},{13,9},{2,6},{6,2},{1... | collective-permute-start | bytes 1966088 | tf_op jit(solution)/shard_map/ppermute | solution.py:498
  3.7 0.7 concatenate.19
  4.4 0.5 collective-permute-start
  4.9 0.7 fusion.28
  5.7 2.0 %pad_maximum_fusion = bf16[336,1024]{1,0:T(8,128)(2,1)} fusion(bf16[16,1024]{1,0:T(8,128)(2,1)S(1)} %fusion.14, bf16[320,1024]{1,0:T(8,128)(2,1)} %refs_3_.5), kind=kLoop, calls=%fused_computation | loop fusion | flops 1376256 | bytes 1376256 | tf_op jit(solution)/shard_map/concatenate | solution.py:540
  7.7 5.1 %collective-permute-start.8 = (bf16[336,1024]{1,0:T(8,128)(2,1)}, bf16[336,1024]{1,0:T(8,128)(2,1)S(1)}, u32[]{:S(2)}, u32[]{:S(2)}) collective-permute-start(bf16[336,1024]{1,0:T(8,128)(2,1)} %pad_maximum_fusion), channel_id=1, source_target_pairs={{0,4},{12,8},{1,5},{13,9},{2,6},{14,10},{3,7},{15,11},{16,20},{28,... | collective-permute-start | bytes 2064392 | tf_op jit(solution)/shard_map/ppermute | solution.py:498
  14.4 0.8 %copy-done.4 = bf16[320,1024]{1,0:T(8,128)(2,1)} copy-done((bf16[320,1024]{1,0:T(8,128)(2,1)}, bf16[320,1024]{1,0:T(8,128)(2,1)S(1)}, u32[]{:S(2)}) %copy-start.4) | copy-done | bytes 655384
  15.2 5.4 %shard_map.68 = (f32[320,1024]{1,0:T(8,128)}, f32[640,1024]{1,0:T(8,128)}) custom-call(f32[8,128]{1,0:T(8,128)S(1)} %select_select_fusion.refs_0_.refs_1_, f32[1,640]{1,0:T(1,128)S(1)} %add_convert_fusion.refs_1_.refs_2_, bf16[320,1024]{1,0:T(8,128)(2,1)} %refs_3_.5, bf16[320,1024]{1,0:T(8,128)(2,1)} %copy-done.4, bf16[320,1024]{1,0:T(8,128)(2,1)} %refs_6_), custom_call_target="tpu_custom_call" | custom-call | flops 1024 | bytes 1024 | tf_op jit(solution)/shard_map/pallas_call | solution.py:386
  20.8 0.8 %fusion.34 = (bf16[160,1024]{1,0:T(8,128)(2,1)}, bf16[160,1024]{1,0:T(8,128)(2,1)S(1)}) fusion(bf16[320,1024]{1,0:T(8,128)(2,1)S(1)} %collective-permute-done.4.refs_5_.refs_10_), kind=kLoop, calls=%fused_computation.60 | loop fusion | bytes 1310720 | tf_op jit(solution)/shard_map/slice | solution.py:559
  21.6 1.3 %collective-permute-start.5 = (bf16[160,1024]{1,0:T(8,128)(2,1)S(1)}, bf16[160,1024]{1,0:T(8,128)(2,1)S(1)}, u32[]{:S(2)}, u32[]{:S(2)}) collective-permute-start(bf16[160,1024]{1,0:T(8,128)(2,1)S(1)} %get-tuple-element.62), channel_id=1, source_target_pairs={{4,0},{8,12},{5,1},{9,13},{6,2},{10,14},{7,3},{11,15},{20,16},{24,... | collective-permute-start | bytes 983048 | tf_op jit(solution)/shard_map/ppermute | solution.py:498
  22.9 0.8 slice.33
  23.6 1.3 %collective-permute-start.6 = (bf16[160,1024]{1,0:T(8,128)(2,1)}, bf16[160,1024]{1,0:T(8,128)(2,1)S(1)}, u32[]{:S(2)}, u32[]{:S(2)}) collective-permute-start(bf16[160,1024]{1,0:T(8,128)(2,1)} %get-tuple-element.61), channel_id=1, source_target_pairs={{4,0},{8,12},{5,1},{9,13},{6,2},{10,14},{7,3},{11,15},{20,16},{24,... | collective-permute-start | bytes 983048 | tf_op jit(solution)/shard_map/ppermute | solution.py:498
  24.9 0.5 collective-permute-start.7
  25.5 7.4 %shard_map.69 = (f32[320,1024]{1,0:T(8,128)}, f32[320,1024]{1,0:T(8,128)}, f32[640,1024]{1,0:T(8,128)}) custom-call(f32[8,128]{1,0:T(8,128)S(1)} %select_select_fusion.refs_0_.refs_1_, f32[1,640]{1,0:T(1,128)S(1)} %add_convert_fusion.refs_1_.refs_2_, bf16[320,1024]{1,0:T(8,128)(2,1)} %refs_3_.5, bf16[320,1024]{1,0:T(8,128)(2,1)} %copy-done.4, ...), custom_call_target="tpu_custom_call" | custom-call | flops 1024 | bytes 1024 | tf_op jit(solution)/shard_map/pallas_call | solution.py:386
  32.9 0.8 %fusion.32 = (bf16[112,1024]{1,0:T(8,128)(2,1)}, bf16[112,1024]{1,0:T(8,128)(2,1)}, bf16[112,1024]{1,0:T(8,128)(2,1)S(1)}) fusion(bf16[336,1024]{1,0:T(8,128)(2,1)S(1)} %collective-permute-done.8.refs_2_.refs_5_), kind=kLoop, calls=%fused_computation.58 | loop fusion | bytes 1376256 | tf_op jit(solution)/shard_map/slice | solution.py:534
  34.0 0.7 copy-done
  35.3 5.3 %collective-permute-done.6.refs_7_ = bf16[160,1024]{1,0:T(8,128)(2,1)S(1)} collective-permute-done((bf16[160,1024]{1,0:T(8,128)(2,1)}, bf16[160,1024]{1,0:T(8,128)(2,1)S(1)}, u32[]{:S(2)}, u32[]{:S(2)}) %collective-permute-start.6) | collective-permute-done | bytes 327712 | tf_op jit(solution)/shard_map/ppermute | solution.py:498
  40.7 0.6 copy-done.2
  41.4 0.6 collective-permute-start.14
  42.2 1.1 %shard_map.73 = (bf16[144,1024]{1,0:T(8,128)(2,1)}, bf16[320,1024]{1,0:T(8,128)(2,1)}) custom-call(s32[1]{0:T(128)} %bitcast.2.refs_0_, f32[8,128]{1,0:T(8,128)S(1)} %select_select_fusion.refs_0_.refs_1_, f32[1,640]{1,0:T(1,128)S(1)} %add_convert_fusion.refs_1_.refs_2_, bf16[320,1024]{1,0:T(8,128)(2,1)} %refs_3_.5, bf16[320,1024]{1,0:T(8,128)(2,1)} %copy-done.4, ...), custom_call_target="tpu_custom_call" | custom-call | flops 1024 | bytes 1024 | tf_op jit(solution)/shard_map/pallas_call | solution.py:386
  43.3 0.4 collective-permute-start.12
  44.1 12.0 %collective-permute-start.16 = (bf16[176,1024]{1,0:T(8,128)(2,1)S(1)}, bf16[176,1024]{1,0:T(8,128)(2,1)S(1)}, u32[]{:S(2)}, u32[]{:S(2)}) collective-permute-start(bf16[176,1024]{1,0:T(8,128)(2,1)S(1)} %shard_map.75), channel_id=1, source_target_pairs={{0,4},{4,0},{8,12},{12,8},{1,5},{5,1},{9,13},{13,9},{2,6},{6,2},{1... | collective-permute-start | bytes 1081352 | tf_op jit(solution)/shard_map/ppermute | solution.py:498
  56.2 2.1 %shard_map.76 = bf16[144,1024]{1,0:T(8,128)(2,1)S(1)} custom-call(f32[144,1024]{1,0:T(8,128)} %get-tuple-element.42.total, bf16[144,1024]{1,0:T(8,128)(2,1)} %collective-permute-done.12.arrived), custom_call_target="tpu_custom_call" | custom-call | flops 1024 | bytes 1024 | tf_op jit(solution)/shard_map/pallas_call | solution.py:433
  58.3 4.6 %collective-permute-start.20 = (bf16[144,1024]{1,0:T(8,128)(2,1)S(1)}, bf16[144,1024]{1,0:T(8,128)(2,1)S(1)}, u32[]{:S(2)}, u32[]{:S(2)}) collective-permute-start(bf16[144,1024]{1,0:T(8,128)(2,1)S(1)} %shard_map.76), channel_id=1, source_target_pairs={{0,4},{4,0},{8,12},{12,8},{1,5},{5,1},{9,13},{13,9},{2,6},{6,2},{1... | collective-permute-start | bytes 884744 | tf_op jit(solution)/shard_map/ppermute | solution.py:498
  62.9 1.0 %copy-done.1 = bf16[160,1024]{1,0:T(8,128)(2,1)S(1)} copy-done((bf16[160,1024]{1,0:T(8,128)(2,1)S(1)}, bf16[160,1024]{1,0:T(8,128)(2,1)}, u32[]{:S(2)}) %copy-start.1) | copy-done | bytes 327704
  63.9 1.0 %copy-done.3 = bf16[160,1024]{1,0:T(8,128)(2,1)S(1)} copy-done((bf16[160,1024]{1,0:T(8,128)(2,1)S(1)}, bf16[160,1024]{1,0:T(8,128)(2,1)}, u32[]{:S(2)}) %copy-start.3) | copy-done | bytes 327704
  64.9 7.1 %shard_map.77 = (f32[320,1024]{1,0:T(8,128)S(1)}, bf16[320,1024]{1,0:T(8,128)(2,1)S(1)}) custom-call(f32[8,128]{1,0:T(8,128)S(1)} %select_select_fusion.refs_0_.refs_1_, f32[1,640]{1,0:T(1,128)S(1)} %add_convert_fusion.refs_1_.refs_2_, s32[3]{0:T(128)S(1)} %pad_add_fusion.refs_2_, bf16[320,1024]{1,0:T(8,128)(2,1)} %refs_3_.5, bf16[320,1024]{1,0:T(8,128)(2,1)} %copy-done.4, ...), custom_call_target="tpu_custom_call" | custom-call | flops 1024 | bytes 1024 | tf_op jit(solution)/shard_map/pallas_call | solution.py:386
  72.1 0.5 collective-permute-start.17
  72.9 0.7 collective-permute-done.15.rest_0_
  73.6 0.6 collective-permute-done.18.rest_2_
  74.2 1.0 %shard_map.79 = bf16[320,1024]{1,0:T(8,128)(2,1)} custom-call(f32[320,1024]{1,0:T(8,128)S(1)} %get-tuple-element.48.mine_s, bf16[112,1024]{1,0:T(8,128)(2,1)S(1)} %collective-permute-done.15.rest_0_, bf16[112,1024]{1,0:T(8,128)(2,1)S(1)} %collective-permute-done.17.rest_1_, bf16[96,1024]{1,0:T(8,128)(2,1)S(1)} %collective-permute-done.18.rest_2_), custom_call_target="tpu_custom_call" | custom-call | flops 1024 | bytes 1024 | tf_op jit(solution)/shard_map/pallas_call | solution.py:454
  75.2 0.9 %shard_map.80 = bf16[320,1024]{1,0:T(8,128)(2,1)} custom-call(s32[1]{0:T(128)} %bitcast.3.flag, f32[320,1024]{1,0:T(8,128)S(1)} %shard_map.78.here_total, bf16[320,1024]{1,0:T(8,128)(2,1)S(1)} %collective-permute-done.19.across_back, bf16[176,1024]{1,0:T(8,128)(2,1)S(1)} %collective-permute-done.16.inside_a, ...), custom_call_target="tpu_custom_call" | custom-call | flops 1024 | bytes 1024 | tf_op jit(solution)/shard_map/pallas_call | solution.py:478
  (55 shorter events, 2.5 us)
Async XLA Ops:
  0.6 20.0 %collective-permute-start.2 = (bf16[320,1024]{1,0:T(8,128)(2,1)}, bf16[320,1024]{1,0:T(8,128)(2,1)S(1)}, u32[]{:S(2)}, u32[]{:S(2)}) collective-permute-start(bf16[320,1024]{1,0:T(8,128)(2,1)} %refs_6_), channel_id=1, source_target_pairs={{0,4},{4,0},{8,12},{12,8},{1,5},{5,1},{9,13},{13,9},{2,6},{6,2},{1... | collective-permute-start | bytes 1966088 | tf_op jit(solution)/shard_map/ppermute | solution.py:498
  3.7 17.0 %collective-permute-start.4 = (bf16[320,1024]{1,0:T(8,128)(2,1)}, bf16[320,1024]{1,0:T(8,128)(2,1)S(1)}, u32[]{:S(2)}, u32[]{:S(2)}) collective-permute-start(bf16[320,1024]{1,0:T(8,128)(2,1)} %refs_6_), channel_id=1, source_target_pairs={{4,8},{8,4},{0,1},{12,13},{5,9},{9,5},{1,0},{13,12},{6,10},{10,6},... | collective-permute-start | bytes 1966088 | tf_op jit(solution)/shard_map/ppermute | solution.py:498
  4.4 9.9 %collective-permute-start = (s32[1,320]{1,0:T(1,128)S(1)}, s32[1,320]{1,0:T(1,128)S(1)}, u32[]{:S(2)}, u32[]{:S(2)}) collective-permute-start(s32[1,320]{1,0:T(1,128)S(1)} %concatenate.19), channel_id=1, source_target_pairs={{1,0},{0,1},{3,2},{2,3},{5,4},{4,5},{7,6},{6,7},{9,8},{8,9},{11,10... | collective-permute-start | bytes 3848 | tf_op jit(solution)/shard_map/ppermute | solution.py:21
  4.9 9.4 %collective-permute-start.1 = (bf16[320,1024]{1,0:T(8,128)(2,1)}, bf16[320,1024]{1,0:T(8,128)(2,1)S(1)}, u32[]{:S(2)}, u32[]{:S(2)}) collective-permute-start(bf16[320,1024]{1,0:T(8,128)(2,1)} %refs_3_.5), channel_id=1, source_target_pairs={{1,0},{0,1},{3,2},{2,3},{5,4},{4,5},{7,6},{6,7},{9,8},{8,9},{11,10... | collective-permute-start | bytes 1966088 | tf_op jit(solution)/shard_map/ppermute | solution.py:21
  7.7 25.2 %collective-permute-start.8 = (bf16[336,1024]{1,0:T(8,128)(2,1)}, bf16[336,1024]{1,0:T(8,128)(2,1)S(1)}, u32[]{:S(2)}, u32[]{:S(2)}) collective-permute-start(bf16[336,1024]{1,0:T(8,128)(2,1)} %pad_maximum_fusion), channel_id=1, source_target_pairs={{0,4},{12,8},{1,5},{13,9},{2,6},{14,10},{3,7},{15,11},{16,20},{28,... | collective-permute-start | bytes 2064392 | tf_op jit(solution)/shard_map/ppermute | solution.py:498
  14.4 0.8 %copy-start.4 = (bf16[320,1024]{1,0:T(8,128)(2,1)}, bf16[320,1024]{1,0:T(8,128)(2,1)S(1)}, u32[]{:S(2)}) copy-start(bf16[320,1024]{1,0:T(8,128)(2,1)S(1)} %collective-permute-done.1.refs_3_.refs_4_) | copy-start | bytes 1966084
  20.6 3.0 %copy-start.5 = (bf16[320,1024]{1,0:T(8,128)(2,1)}, bf16[320,1024]{1,0:T(8,128)(2,1)S(1)}, u32[]{:S(2)}) copy-start(bf16[320,1024]{1,0:T(8,128)(2,1)S(1)} %collective-permute-done.2.refs_4_.refs_6_) | copy-start | bytes 1966084
  20.7 14.3 %collective-permute-start.3 = (bf16[176,1024]{1,0:T(8,128)(2,1)S(1)}, bf16[176,1024]{1,0:T(8,128)(2,1)S(1)}, u32[]{:S(2)}, u32[]{:S(2)}) collective-permute-start(bf16[176,1024]{1,0:T(8,128)(2,1)S(1)} %slice.30), channel_id=1, source_target_pairs={{4,8},{8,4},{0,1},{12,13},{5,9},{9,5},{1,0},{13,12},{6,10},{10,6},... | collective-permute-start | bytes 1081352 | tf_op jit(solution)/shard_map/ppermute | solution.py:498
  21.6 12.4 %collective-permute-start.5 = (bf16[160,1024]{1,0:T(8,128)(2,1)S(1)}, bf16[160,1024]{1,0:T(8,128)(2,1)S(1)}, u32[]{:S(2)}, u32[]{:S(2)}) collective-permute-start(bf16[160,1024]{1,0:T(8,128)(2,1)S(1)} %get-tuple-element.62), channel_id=1, source_target_pairs={{4,0},{8,12},{5,1},{9,13},{6,2},{10,14},{7,3},{11,15},{20,16},{24,... | collective-permute-start | bytes 983048 | tf_op jit(solution)/shard_map/ppermute | solution.py:498
  23.6 16.9 %collective-permute-start.6 = (bf16[160,1024]{1,0:T(8,128)(2,1)}, bf16[160,1024]{1,0:T(8,128)(2,1)S(1)}, u32[]{:S(2)}, u32[]{:S(2)}) collective-permute-start(bf16[160,1024]{1,0:T(8,128)(2,1)} %get-tuple-element.61), channel_id=1, source_target_pairs={{4,0},{8,12},{5,1},{9,13},{6,2},{10,14},{7,3},{11,15},{20,16},{24,... | collective-permute-start | bytes 983048 | tf_op jit(solution)/shard_map/ppermute | solution.py:498
  24.9 16.4 %collective-permute-start.7 = (bf16[144,1024]{1,0:T(8,128)(2,1)}, bf16[144,1024]{1,0:T(8,128)(2,1)S(1)}, u32[]{:S(2)}, u32[]{:S(2)}) collective-permute-start(bf16[144,1024]{1,0:T(8,128)(2,1)} %slice.33), channel_id=1, source_target_pairs={{4,8},{8,4},{0,1},{12,13},{5,9},{9,5},{1,0},{13,12},{6,10},{10,6},... | collective-permute-start | bytes 884744 | tf_op jit(solution)/shard_map/ppermute | solution.py:498
  33.8 6.8 %collective-permute-start.10 = (bf16[112,1024]{1,0:T(8,128)(2,1)}, bf16[112,1024]{1,0:T(8,128)(2,1)S(1)}, u32[]{:S(2)}, u32[]{:S(2)}) collective-permute-start(bf16[112,1024]{1,0:T(8,128)(2,1)} %get-tuple-element.57), channel_id=1, source_target_pairs={{1,0},{0,1},{3,2},{2,3},{5,4},{4,5},{7,6},{6,7},{9,8},{8,9},{11,10... | collective-permute-start | bytes 688136 | tf_op jit(solution)/shard_map/ppermute | solution.py:21
  34.0 0.7 copy-start
  34.7 5.9 %collective-permute-start.11 = (bf16[112,1024]{1,0:T(8,128)(2,1)}, bf16[112,1024]{1,0:T(8,128)(2,1)S(1)}, u32[]{:S(2)}, u32[]{:S(2)}) collective-permute-start(bf16[112,1024]{1,0:T(8,128)(2,1)} %get-tuple-element.56), channel_id=1, source_target_pairs={{1,0},{0,1},{3,2},{2,3},{5,4},{4,5},{7,6},{6,7},{9,8},{8,9},{11,10... | collective-permute-start | bytes 688136 | tf_op jit(solution)/shard_map/ppermute | solution.py:21
  35.0 5.6 %collective-permute-start.9 = (bf16[112,1024]{1,0:T(8,128)(2,1)S(1)}, bf16[112,1024]{1,0:T(8,128)(2,1)S(1)}, u32[]{:S(2)}, u32[]{:S(2)}) collective-permute-start(bf16[112,1024]{1,0:T(8,128)(2,1)S(1)} %get-tuple-element.58), channel_id=1, source_target_pairs={{1,0},{0,1},{3,2},{2,3},{5,4},{4,5},{7,6},{6,7},{9,8},{8,9},{11,10... | collective-permute-start | bytes 688136 | tf_op jit(solution)/shard_map/ppermute | solution.py:21
  40.6 0.8 copy-start.2
  41.4 21.5 %collective-permute-start.14 = (bf16[320,1024]{1,0:T(8,128)(2,1)S(1)}, bf16[320,1024]{1,0:T(8,128)(2,1)}, u32[]{:S(2)}, u32[]{:S(2)}) collective-permute-start(bf16[320,1024]{1,0:T(8,128)(2,1)S(1)} %shard_map.72.refs_5_), channel_id=1, source_target_pairs={{0,4},{4,0},{8,12},{12,8},{1,5},{5,1},{9,13},{13,9},{2,6},{6,2},{1... | collective-permute-start | bytes 1966088 | tf_op jit(solution)/shard_map/ppermute | solution.py:498
  42.0 1.8 %collective-permute-start.13 = (bf16[176,1024]{1,0:T(8,128)(2,1)S(1)}, bf16[176,1024]{1,0:T(8,128)(2,1)S(1)}, u32[]{:S(2)}, u32[]{:S(2)}) collective-permute-start(bf16[176,1024]{1,0:T(8,128)(2,1)S(1)} %shard_map.71), channel_id=1, source_target_pairs={{4,8},{8,4},{0,1},{12,13},{5,9},{9,5},{1,0},{13,12},{6,10},{10,6},... | collective-permute-start | bytes 1081352 | tf_op jit(solution)/shard_map/ppermute | solution.py:498
  43.3 12.9 %collective-permute-start.12 = (bf16[144,1024]{1,0:T(8,128)(2,1)}, bf16[144,1024]{1,0:T(8,128)(2,1)}, u32[]{:S(2)}, u32[]{:S(2)}) collective-permute-start(bf16[144,1024]{1,0:T(8,128)(2,1)} %get-tuple-element.39), channel_id=1, source_target_pairs={{4,8},{8,4},{0,1},{12,13},{5,9},{9,5},{1,0},{13,12},{6,10},{10,6},... | collective-permute-start | bytes 884744 | tf_op jit(solution)/shard_map/ppermute | solution.py:498
  43.9 31.4 %collective-permute-start.19 = (bf16[320,1024]{1,0:T(8,128)(2,1)}, bf16[320,1024]{1,0:T(8,128)(2,1)S(1)}, u32[]{:S(2)}, u32[]{:S(2)}) collective-permute-start(bf16[320,1024]{1,0:T(8,128)(2,1)} %get-tuple-element.53), channel_id=1, source_target_pairs={{4,8},{8,4},{0,1},{12,13},{5,9},{9,5},{1,0},{13,12},{6,10},{10,6},... | collective-permute-start | bytes 1966088 | tf_op jit(solution)/shard_map/ppermute | solution.py:498
  44.1 28.5 %collective-permute-start.16 = (bf16[176,1024]{1,0:T(8,128)(2,1)S(1)}, bf16[176,1024]{1,0:T(8,128)(2,1)S(1)}, u32[]{:S(2)}, u32[]{:S(2)}) collective-permute-start(bf16[176,1024]{1,0:T(8,128)(2,1)S(1)} %shard_map.75), channel_id=1, source_target_pairs={{0,4},{4,0},{8,12},{12,8},{1,5},{5,1},{9,13},{13,9},{2,6},{6,2},{1... | collective-permute-start | bytes 1081352 | tf_op jit(solution)/shard_map/ppermute | solution.py:498
  58.3 16.9 %collective-permute-start.20 = (bf16[144,1024]{1,0:T(8,128)(2,1)S(1)}, bf16[144,1024]{1,0:T(8,128)(2,1)S(1)}, u32[]{:S(2)}, u32[]{:S(2)}) collective-permute-start(bf16[144,1024]{1,0:T(8,128)(2,1)S(1)} %shard_map.76), channel_id=1, source_target_pairs={{0,4},{4,0},{8,12},{12,8},{1,5},{5,1},{9,13},{13,9},{2,6},{6,2},{1... | collective-permute-start | bytes 884744 | tf_op jit(solution)/shard_map/ppermute | solution.py:498
  62.9 1.0 %copy-start.1 = (bf16[160,1024]{1,0:T(8,128)(2,1)S(1)}, bf16[160,1024]{1,0:T(8,128)(2,1)}, u32[]{:S(2)}) copy-start(bf16[160,1024]{1,0:T(8,128)(2,1)} %copy-done) | copy-start | bytes 983044
  63.9 1.0 %copy-start.3 = (bf16[160,1024]{1,0:T(8,128)(2,1)S(1)}, bf16[160,1024]{1,0:T(8,128)(2,1)}, u32[]{:S(2)}) copy-start(bf16[160,1024]{1,0:T(8,128)(2,1)} %copy-done.2) | copy-start | bytes 983044
  72.1 1.6 %collective-permute-start.15 = (bf16[112,1024]{1,0:T(8,128)(2,1)S(1)}, bf16[112,1024]{1,0:T(8,128)(2,1)S(1)}, u32[]{:S(2)}, u32[]{:S(2)}) collective-permute-start(bf16[112,1024]{1,0:T(8,128)(2,1)S(1)} %get-tuple-element.60), channel_id=1, source_target_pairs={{1,0},{0,1},{3,2},{2,3},{5,4},{4,5},{7,6},{6,7},{9,8},{8,9},{11,10... | collective-permute-start | bytes 688136 | tf_op jit(solution)/shard_map/ppermute | solution.py:21
  72.1 2.1 %collective-permute-start.17 = (bf16[112,1024]{1,0:T(8,128)(2,1)S(1)}, bf16[112,1024]{1,0:T(8,128)(2,1)S(1)}, u32[]{:S(2)}, u32[]{:S(2)}) collective-permute-start(bf16[112,1024]{1,0:T(8,128)(2,1)S(1)} %get-tuple-element.59), channel_id=1, source_target_pairs={{1,0},{0,1},{3,2},{2,3},{5,4},{4,5},{7,6},{6,7},{9,8},{8,9},{11,10... | collective-permute-start | bytes 688136 | tf_op jit(solution)/shard_map/ppermute | solution.py:21
  72.7 1.6 %collective-permute-start.18 = (bf16[96,1024]{1,0:T(8,128)(2,1)S(1)}, bf16[96,1024]{1,0:T(8,128)(2,1)S(1)}, u32[]{:S(2)}, u32[]{:S(2)}) collective-permute-start(bf16[96,1024]{1,0:T(8,128)(2,1)S(1)} %slice.39), channel_id=1, source_target_pairs={{1,0},{0,1},{3,2},{2,3},{5,4},{4,5},{7,6},{6,7},{9,8},{8,9},{11,10... | collective-permute-start | bytes 589832 | tf_op jit(solution)/shard_map/ppermute | solution.py:21

commit v10 on v9

--- a/solution.py
+++ b/solution.py
@@ -11,7 +11,7 @@
 STEPS = 4
 LINE = 4
 LABEL_ROWS = 16
-KEEP_ROW = 6
+FAR_ROW, KEEP_ROW, LAST_ROW = 5, 6, 7
 VMEM_BYTES = 20 * 1024 * 1024
 
 
@@ -85,7 +85,7 @@
     offset: int = 0
     cut: int = 0
     prior: str = ""
-    optional: str = ""
+    coef: str = ""
 
 
 @dataclasses.dataclass(frozen=True)
@@ -94,8 +94,6 @@
     pieces: tuple
     node: bool
     ends: tuple
-    gradient: str
-    prior_s: bool
     skips: bool
     rows: int
 
@@ -110,7 +108,6 @@
 def pair_steps(plan, *refs):
     refs = list(refs)
     blocks, rows = plan.blocks, plan.rows
-    half = rows // 2
 
     def take(count):
         taken = refs[:count]
@@ -122,23 +119,18 @@
 
     (consts,) = take(1)
     labels = take_if(plan.node)
-    flags = take_if(any(b.optional == "all" for b in blocks))
     node_in = take(2) if plan.node else []
     ends_in = take(len(plan.ends))
     held_in = [take(len(p)) for p in plan.pieces]
     priors = [take_if(b.prior) for b in blocks]
-    prior_s = take_if(plan.prior_s)
     outs = [take((b.out != "") + (b.out == "split")) for b in blocks]
-    if plan.gradient == "final":
-        mine_out, other_out = take(2)
-    elif plan.gradient:
-        (s_out,) = take(1)
+    coef_outs = [take_if(b.coef) for b in blocks]
     spectra = take_if(plan.node)
     ends = take_if(plan.ends)
     held = take(len(blocks))
     prior_held = [take_if(b.prior == "kept") for b in blocks]
-    out_held = [take_if(b.out in ("kept", "split")) for b in blocks]
-    s_held = take_if(plan.gradient)
+    out_held = [take_if(b.out in ("kept", "kept scaled", "split")) for b in blocks]
+    coef_held = [take_if(b.coef) for b in blocks]
     (sems,) = take(1)
     used = 0
 
@@ -162,7 +154,6 @@
     moving_prior = [
         move(priors[i], prior_held[i]) if b.prior == "kept" else None for i, b in enumerate(blocks)
     ]
-    moving_s = move(prior_s, s_held) if plan.prior_s else None
     leaving = []
 
     def const(row):
@@ -191,14 +182,9 @@
             return spectra[...], labels[...]
         return ends[...], end_labels
 
-    if plan.gradient == "final":
-        for copy in moving_node + [c for moves in moving for c in moves] + [moving_s]:
-            copy.wait()
-        moving_node, moving, moving_s = [], [[] for _ in blocks], None
     for i, block in enumerate(blocks):
 
         def work(i=i, block=block):
-            nonlocal moving_s
             at = 0
             for ref, (count, away) in zip(held_in[i], plan.pieces[i]):
                 if not away:
@@ -218,32 +204,21 @@
                 logits = scale * logits + shift
                 positive = jnp.where(targets == row_labels, 1.0, 0.0)
                 coef = jax.nn.sigmoid(logits) - positive
-                masked = coef * const(KEEP_ROW) if block.optional == "spectra" else coef
                 coef = coef.astype(jnp.bfloat16)
                 if block.out:
                     part = jnp.dot(coef, here, preferred_element_type=jnp.float32)
                     total = part if total is None else total + part
-                if plan.gradient:
-                    part = lax.dot_general(
-                        masked.astype(jnp.bfloat16),
-                        glycans,
-                        (((0,), (0,)), ((), ())),
-                        preferred_element_type=jnp.float32,
-                    )
-                    if moving_s is not None:
-                        moving_s.wait()
-                        moving_s = None
-                    if i > 0 or plan.prior_s:
-                        s_held[...] += part
-                    else:
-                        s_held[...] = part
+                if block.coef and use == "node":
+                    kept = coef * const(KEEP_ROW).astype(jnp.bfloat16) if block.coef == "masked" else coef
+                    coef_held[i][...] = kept
+                    leaving.append(move(coef_held[i], coef_outs[i]))
             if block.prior == "kept":
                 moving_prior[i].wait()
                 total = total + prior_held[i][...]
             elif block.prior:
                 total = total + priors[i][...]
-            if block.out == "kept":
-                out_held[i][...] = total
+            if block.out.startswith("kept"):
+                out_held[i][...] = scale * total if block.out == "kept scaled" else total
                 leaving.append(move(out_held[i], outs[i][0]))
             elif block.out == "split":
                 cut = outs[i][0].shape[0]
@@ -252,20 +227,10 @@
                 leaving.append(move(out_held[i], outs[i][1]))
             elif block.out == "total":
                 outs[i][0][...] = total
-            elif block.out == "scaled":
-                outs[i][0][...] = scale * total
             elif block.out:
                 outs[i][0][...] = (scale * total).astype(jnp.bfloat16)
 
-        if block.optional == "all":
-            pl.when(flags[i] != 0)(work)
-        else:
-            work()
-    if plan.gradient == "final":
-        mine_out[...] = scale * s_held[pl.ds(0, rows)]
-        other_out[...] = (scale * s_held[pl.ds(rows, rows)]).astype(jnp.bfloat16)
-    elif plan.gradient:
-        leaving.append(move(s_held, s_out))
+        work()
     for copy in leaving:
         copy.wait()
 
@@ -296,12 +261,11 @@
     return pltpu.CompilerParams(vmem_limit_bytes=VMEM_BYTES)
 
 
-def pair_work(consts, blocks, rows, labels=None, node=None, ends=None, gradient="", prior_s=None, wanted=None, cost=SMALL_COST):
-    half = rows // 2
+def pair_work(consts, blocks, rows, labels=None, node=None, ends=None, wanted=None):
     shapes = tuple(b[0] for b in blocks)
     pieces = []
     arrays = []
-    for shape, array, _, _ in blocks:
+    for shape, array, _ in blocks:
         parts = array if isinstance(array, tuple) else (array,)
         away = [isinstance(x, Away) for x in parts]
         parts = [x.array if flag else x for x, flag in zip(parts, away)]
@@ -315,8 +279,6 @@
         tuple(pieces),
         node is not None,
         end_rows,
-        gradient,
-        prior_s is not None,
         wanted is not None,
         rows,
     )
@@ -334,20 +296,15 @@
     give(consts, False)
     if node is not None:
         give(labels, False)
-    if any(b.optional == "all" for b in shapes):
-        operands.append(jnp.stack([jnp.int32(b[2]) for b in blocks]))
-        in_specs.append(SMEM_SPEC)
     for array in node or ():
         give(array, True)
     for array in ends:
         give(array, False)
     for array, away in arrays:
         give(array, away)
-    for shape, _, _, prior in blocks:
+    for shape, _, prior in blocks:
         if shape.prior:
             give(prior, shape.prior == "kept")
-    if prior_s is not None:
-        give(prior_s, True)
 
     counts = [sum(count for count, _ in p) for p in pieces]
     outs = []
@@ -363,12 +320,10 @@
             get((count - shape.cut, width), jnp.float32, True)
         elif shape.out:
             kind = jnp.bfloat16 if shape.out == "rounded" else jnp.float32
-            get((count, width), kind, shape.out == "kept")
-    if gradient == "final":
-        get((rows, width), jnp.float32, False)
-        get((rows, width), jnp.bfloat16, False)
-    elif gradient:
-        get((2 * rows, width), jnp.float32, True)
+            get((count, width), kind, shape.out.startswith("kept"))
+    for shape, count in zip(shapes, counts):
+        if shape.coef:
+            get((count, 2 * rows), jnp.bfloat16, True)
 
     scratch = []
     if node is not None:
@@ -378,10 +333,9 @@
     scratch += [pltpu.VMEM((n, width), jnp.bfloat16) for n in counts]
     scratch += [pltpu.VMEM((n, width), jnp.float32) for n, b in zip(counts, shapes) if b.prior == "kept"]
     for n, b in zip(counts, shapes):
-        if b.out in ("kept", "split"):
+        if b.out in ("kept", "kept scaled", "split"):
             scratch.append(pltpu.VMEM((n - b.cut, width), jnp.float32))
-    if gradient:
-        scratch.append(pltpu.VMEM((2 * rows, width), jnp.float32))
+    scratch += [pltpu.VMEM((n, 2 * rows), jnp.bfloat16) for n, b in zip(counts, shapes) if b.coef]
     scratch.append(pltpu.SemaphoreType.DMA((len(operands) + len(outs),)))
     return pl.pallas_call(
         functools.partial(pair_body, plan),
@@ -389,7 +343,7 @@
         in_specs=in_specs,
         out_specs=out_specs,
         scratch_shapes=scratch,
-        cost_estimate=cost,
+        cost_estimate=SMALL_COST,
         compiler_params=params(),
     )(*operands)
 
@@ -398,6 +352,115 @@
     digits = jnp.stack([labels // 16384, labels // 128 % 128, labels % 128]).astype(jnp.bfloat16)
     digits = jnp.concatenate([digits, digits, digits], axis=1)
     return jnp.pad(digits, ((0, row_count - 3), (0, width - digits.shape[1])))
+
+
+def spectra_body(plan, outer, consts, labels, s_mine, s_other, coef_here, coef_side, coef_across, here, side, across, *rest):
+    rows, n_next, n_far = plan
+    nexts, rest = rest[:n_next], rest[n_next:]
+    fars, rest = rest[:n_far], rest[n_far:]
+    last, mine_out, other_out, spectra, coefs, held, sems = rest
+    used = 0
+
+    def move(source, target):
+        nonlocal used
+        copy = pltpu.make_async_copy(source, target, sems.at[used])
+        copy.start()
+        used += 1
+        return copy
+
+    def fill(parts, target, at):
+        moves = []
+        for part in parts:
+            moves.append(move(part, target.at[pl.ds(at, part.shape[0])]))
+            at += part.shape[0]
+        return moves
+
+    moves = fill([s_mine, s_other], spectra, 0) + fill([coef_here, coef_side], coefs, 0)
+    moves += fill([here, side], held, 0)
+
+    @pl.when(outer[0] == 0)
+    def _():
+        for copy in fill([across] + list(fars), held, 2 * rows) + fill([coef_across], coefs, 2 * rows):
+            copy.wait()
+
+    @pl.when(outer[0] != 0)
+    def _():
+        for copy in fill(list(nexts) + [last], held, 2 * rows):
+            copy.wait()
+
+    for copy in moves:
+        copy.wait()
+    scale, shift = consts[0:1, 0:1], consts[1:2, 0:1]
+
+    def work_out(first, target_row):
+        logits = lax.dot_general(
+            held[pl.ds(first, rows)],
+            spectra[...],
+            (((1,), (1,)), ((), ())),
+            preferred_element_type=jnp.float32,
+        )
+        logits = scale * logits + shift
+        targets = lax.broadcasted_iota(jnp.int32, (rows, 1), 0).astype(jnp.float32)
+        targets = targets + consts[target_row : target_row + 1, 0:1]
+        positive = jnp.where(targets == labels[...], 1.0, 0.0)
+        coefs[pl.ds(first, rows)] = (jax.nn.sigmoid(logits) - positive).astype(jnp.bfloat16)
+
+    @pl.when(outer[0] != 0)
+    def _():
+        work_out(2 * rows, FAR_ROW)
+
+    work_out(3 * rows, LAST_ROW)
+    for i, out in enumerate((mine_out, other_out)):
+        total = lax.dot_general(
+            coefs[:, i * rows : (i + 1) * rows],
+            held[...],
+            (((0,), (0,)), ((), ())),
+            preferred_element_type=jnp.float32,
+        )
+        out[...] = (scale * total).astype(out.dtype)
+
+
+def spectra_work(outer, consts, labels, node, coefs, here, side, across, nexts, fars, last):
+    rows, width = here.shape
+    arrays = list(node) + list(coefs) + [here, side, across] + list(nexts) + list(fars) + [last]
+    plan = (rows, len(nexts), len(fars))
+    return pl.pallas_call(
+        functools.partial(spectra_body, plan),
+        out_shape=[vmem_out((rows, width), jnp.float32), vmem_out((rows, width), jnp.bfloat16)],
+        in_specs=[SMEM_SPEC, VMEM_SPEC, VMEM_SPEC] + [HBM_SPEC] * len(arrays),
+        out_specs=[VMEM_SPEC] * 2,
+        scratch_shapes=[
+            pltpu.VMEM((2 * rows, width), jnp.bfloat16),
+            pltpu.VMEM((4 * rows, 2 * rows), jnp.bfloat16),
+            pltpu.VMEM((4 * rows, width), jnp.bfloat16),
+            pltpu.SemaphoreType.DMA((len(arrays),)),
+        ],
+        cost_estimate=SMALL_COST,
+        compiler_params=params(),
+    )(
+        jnp.int32(outer).reshape(1),
+        in_vmem(consts),
+        in_vmem(labels),
+        *[in_hbm(a) for a in arrays],
+    )
+
+
+def split_body(whole, *parts):
+    at = 0
+    for part in parts:
+        part[...] = whole[pl.ds(at, part.shape[0])]
+        at += part.shape[0]
+
+
+def split(whole, counts):
+    return pl.pallas_call(
+        split_body,
+        out_shape=[vmem_out((n, whole.shape[1]), whole.dtype) for n in counts],
+        in_specs=[VMEM_SPEC],
+        out_specs=[VMEM_SPEC] * len(counts),
+        cost_estimate=SMALL_COST,
+        compiler_params=params(),
+    )(in_vmem(whole))
 
 
 def join_body(first, second, out):
@@ -441,24 +504,31 @@
     )(in_hbm(total.array) if away else in_vmem(total), in_vmem(arrived))
 
 
-def finish_spectra_body(mine_s, *rest):
-    others, out = rest[:-1], rest[-1]
+def finish_spectra_body(mine_s, away, *rest):
+    others, (out, near, sem) = rest[:-3], rest[-3:]
+    copy = pltpu.make_async_copy(away, near, sem)
+    copy.start()
     at = 0
     for other in others:
         where = pl.ds(at, other.shape[0])
         out[where] = (mine_s[where] + other[...].astype(jnp.float32)).astype(jnp.bfloat16)
         at += other.shape[0]
-
-
-def finish_spectra(mine_s, others):
+    copy.wait()
+
+
+def finish_spectra(mine_s, others, away):
     return pl.pallas_call(
         finish_spectra_body,
-        out_shape=jax.ShapeDtypeStruct(mine_s.shape, jnp.bfloat16),
-        in_specs=[VMEM_SPEC] * (1 + len(others)),
-        out_specs=VMEM_SPEC,
+        out_shape=[
+            jax.ShapeDtypeStruct(mine_s.shape, jnp.bfloat16),
+            vmem_out(away.shape, away.dtype),
+        ],
+        in_specs=[VMEM_SPEC, HBM_SPEC] + [VMEM_SPEC] * len(others),
+        out_specs=[VMEM_SPEC] * 2,
+        scratch_shapes=[pltpu.SemaphoreType.DMA],
         cost_estimate=SMALL_COST,
         compiler_params=params(),
-    )(*[in_vmem(a) for a in [mine_s] + others])
+    )(in_vmem(mine_s), in_hbm(away), *[in_vmem(a) for a in others])
 
 
 def finish_structures_body(flag, here_total, across_back, inside_a, inside_b, out):
@@ -487,7 +557,6 @@
 
 def along_line(spectra, glycans, labels, scale, shift):
     rows, width = spectra.shape
-    half = rows // 2
     node_rows = rows * lax.axis_size("inner")
     position = lax.axis_index("blk")
     outer = (position == 0) | (position == LINE - 1)
@@ -515,7 +584,7 @@
             middle.append((at * n_inner + core, (last - at) * n_inner + core))
         for at in (0, last):
             middle.append((at * n_inner + core, at * n_inner + (core + 1) % n_inner))
-    here_at, side_at, across_at, far_at = 2, 3, 4, 5
+    here_at, side_at, across_at, far_at = 2, 3, 4, FAR_ROW
     rows_of_consts = [
         scale,
         shift,
@@ -524,17 +593,16 @@
         first_of(last - position),
         first_of((last - position) ^ 1),
         jnp.where(outer, 0.0, 1.0),
+        first_of(jnp.where(outer, last - position, (last - position) ^ 1)),
     ]
     index = lax.broadcasted_iota(jnp.int32, (8, 128), 0)
     consts = jnp.zeros((8, 128), jnp.float32)
     for i, value in enumerate(rows_of_consts):
         consts = jnp.where(index == i, value, consts)
 
-    def in_pieces(block, piece):
-        return tuple(swap_inner(block[at : at + piece]) for at in range(0, block.shape[0], piece))
-
+    cut = rows // 2
+    half = rows // 2
     across = permute(glycans, middle)
-    cut_a = rows // 2 + 16
     side = permute(glycans, sides)
     coded = code_labels(labels, LABEL_ROWS, width)
     end_mine = permute(jnp.concatenate([spectra, coded]), inward)
@@ -543,60 +611,47 @@
     node_labels = jnp.concatenate([own_labels, swap_inner(own_labels)], axis=1)
     node_labels = node_labels.astype(jnp.float32)
     node = dict(node=(spectra, partner), labels=node_labels)
-    here_g, own_s = pair_work(
-        consts,
-        [(Block(here_at, ("node",), "kept"), Away(glycans), 1, None)],
-        rows,
-        gradient="part",
-        **node,
+    here_g, here_c = pair_work(
+        consts, [(Block(here_at, ("node",), "kept", coef="all"), Away(glycans), None)], rows, **node
     )
 
     side = after(side, here_g)
-    far_a = permute(side[:cut_a], middle)
-    far_b = permute(side[cut_a:], middle)
-    across = after(across, side)
-    cut = rows // 2
-    next_out = (permute(across[:cut], outward), permute(across[cut:], outward))
-    side_g, across_g, own_s = pair_work(
+    far_a, far_b = [permute(x, middle) for x in split(side, (cut, rows - cut))]
+    across = after(across, here_g)
+    next_out = permute(across, outward)
+    side_g, across_g, side_c, across_c = pair_work(
         consts,
         [
-            (Block(side_at, ("node",), "kept"), Away(side), 1, None),
-            (Block(across_at, ("node",), "kept", optional="spectra"), across, 1, None),
+            (Block(side_at, ("node",), "kept", coef="all"), Away(side), None),
+            (Block(across_at, ("node",), "kept", coef="masked"), across, None),
         ],
         rows,
-        gradient="part",
-        prior_s=own_s,
         **node,
     )
-    far_a = after(far_a, own_s)
+    end_mine = after(end_mine, across_g)
+    piece = -(-rows // 48) * 16
+    ends = (end_mine,) + tuple(swap_inner(x) for x in split(end_mine, (piece,) * 3))
+    far_a = after(far_a, across_g)
     (far_g,) = pair_work(
-        consts,
-        [(Block(far_at, ("node",), "total"), far_a, 1, None)],
-        rows,
-        wanted=~outer,
-        **node,
-    )
-    end_mine = after(end_mine, own_s)
-    piece = -(-rows // 48) * 16
-    ends = (end_mine,) + in_pieces(end_mine, piece)
-
-    far_a, *next_out = lax.optimization_barrier((far_a,) + next_out + (far_g,))[:3]
+        consts, [(Block(far_at, ("node",), "total"), far_a, None)], rows, wanted=~outer, **node
+    )
+
+    far_a, next_out = lax.optimization_barrier((far_a, next_out, far_g))[:2]
     (far_a_out,) = pair_work(
         consts,
-        [(Block(far_at, ("ends",), "rounded", prior="near"), far_a, 1, far_g)],
+        [(Block(far_at, ("ends",), "rounded", prior="near"), far_a, far_g)],
         rows,
         wanted=~outer,
         ends=ends,
     )
     back_a = permute(far_a_out, middle)
+    last_out = permute(join(after(far_a, far_a_out), far_b), sides)
     far_b = after(far_b, far_a_out)
-    far = join(far_a, far_b)
-    last_out = permute(far, sides)
     far_b_out, across_out = pair_work(
         consts,
         [
-            (Block(far_at, ("node", "ends"), "rounded", cut_a), far_b, 1, None),
-            (Block(across_at, ("ends",), "rounded", prior="kept"), across, 1, across_g),
+            (Block(far_at, ("node", "ends"), "rounded", cut), far_b, None),
+            (Block(across_at, ("ends",), "rounded", prior="kept"), across, across_g),
         ],
         rows,
         wanted=~outer,
@@ -607,7 +662,7 @@
     late_side = Away(after(side, far_b_out))
     side_total_a, side_total_b = pair_work(
         consts,
-        [(Block(side_at, ("ends",), "split", cut=cut_a, prior="kept"), late_side, 1, side_g)],
+        [(Block(side_at, ("ends",), "split", cut=cut, prior="kept"), late_side, side_g)],
         rows,
         wanted=~outer,
         ends=ends,
@@ -615,37 +670,32 @@
     total_a = add_rounded(side_total_a, back_a)
     inside_a = permute(total_a, sides)
     across_back = permute(after(across_out, total_a), middle)
-    total_b = add_rounded(Away(side_total_b), after(back_b, total_a))
-    inside_b = permute(total_b, sides)
-
-    def only_s(target):
-        return Block(target, ("node",), "", optional="all")
-
-    mine_s, other_s = pair_work(
-        consts,
-        [
-            (only_s(far_at), after(far, total_b), ~outer, None),
-            (only_s(far_at), tuple(next_out), outer, None),
-            (only_s(across_at), last_out, outer, None),
-        ],
-        rows,
-        gradient="final",
-        prior_s=own_s,
-        **node,
-    )
-    others = list(in_pieces(other_s, piece))
-    inside_a, late_mine = lax.optimization_barrier((inside_a, glycans))
-    flops = 2 * 2 * 2 * rows * rows * width
     (here_total,) = pair_work(
         consts,
-        [(Block(here_at, ("ends",), "scaled", prior="kept"), Away(late_mine), 1, here_g)],
+        [(Block(here_at, ("ends",), "kept scaled", prior="kept"), Away(after(glycans, total_a)), here_g)],
         rows,
         wanted=~outer,
         ends=ends,
-        cost=pl.CostEstimate(flops=flops, bytes_accessed=8 * rows * width, transcendentals=0),
-    )
-    others[0] = after(others[0], here_total)
-    grad_spectra = finish_spectra(mine_s, others)
+    )
+    total_b = add_rounded(Away(side_total_b), after(back_b, here_total))
+    inside_b = permute(total_b, sides)
+
+    mine_s, other_s = spectra_work(
+        outer,
+        consts,
+        node_labels,
+        (spectra, partner),
+        (here_c, side_c, across_c),
+        after(glycans, total_b),
+        side,
+        across,
+        (next_out,),
+        (far_a, far_b),
+        last_out,
+    )
+    others = [swap_inner(x) for x in split(other_s, (piece, piece, rows - 2 * piece))]
+    others[0] = after(others[0], inside_a)
+    grad_spectra, here_total = finish_spectra(mine_s, others, here_total)
     across_back = after(across_back, grad_spectra)
     return grad_spectra, finish_structures(outer, here_total, across_back, inside_a, inside_b)
 

time: 76.7 us -> 74 us (0.965)
  waiting for transfers between devices: 6.81 us -> 12.7 us
  local copies, waits for them, and re-layouts: 7.36 us -> 2.6 us
  Pallas kernels: 25.5 us -> 22.7 us
  starting transfers between devices: 31.2 us -> 30.3 us
    pallas_call x8 -> x7, Pallas kernels: 21.4 us -> 10.7 us  [pair_work(): pl.pallas_call(functools.partial(pair_body, plan), out_shape=outs, in_spe...]
    pallas_call x1 -> x5, Pallas kernels: 1 us -> 8.8 us  [the longest x1 5.66 us: spectra_work(): pl.pallas_call(functools.partial(spectra_body, plan), out_shape=[vmem_out...]
    ppermute x13 -> x12, waiting for transfers between devices: 5.47 us -> 10.2 us  [permute(): return lax.ppermute(block, ('blk', 'inner'), pairs)]
    slice x6 -> x0, local copies, waits for them, and re-layouts: 2.51 us -> none  [the longest x3 0.89 us: in_pieces(): block[at:at + piece]]
    unnamed x12 -> x10, local copies, waits for them, and re-layouts: 4.16 us -> 1.9 us
    ppermute x8, waiting for transfers between devices: 1.34 us -> 2.48 us  [from_behind(): return lax.ppermute(block, axis, route)]
    pallas_call x1, Pallas kernels: 0.89 us -> 1.86 us  [finish_structures(): pl.pallas_call(finish_structures_body, out_shape=jax.ShapeDtypeStruct(her...]
    pallas_call x2, Pallas kernels: 2.15 us -> 1.23 us  [add_rounded(): pl.pallas_call(add_body, out_shape=vmem_out(arrived.shape, jnp.bfloat16),...]
  transfers between devices with their start and end apart: 21 -> 20, of which waited for: 4 -> 9; matrix products, arithmetic and copies ran while one was open for 8% -> 5% of each run, Pallas kernels for 32% -> 28%
where the time goes in v10:
time: 74 us; the launch traced here: 73.5 us
  starting transfers between devices  30.3 us (41%)
  Pallas kernels  22.7 us (31%)
  waiting for transfers between devices  12.7 us (17%)
  other arithmetic  2.98 us (4%)
  local copies, waits for them, and re-layouts  2.6 us (4%)
  between operations  2.24 us (3%)
    ppermute x12, starting transfers between devices, permute(): return lax.ppermute(block, ('blk', 'inner'), pairs)  28.6 us
    pallas_call x7, Pallas kernels, pair_work(): pl.pallas_call(functools.partial(pair_body, plan), out_shape=outs, in_spe...  10.7 us
    ppermute x12, waiting for transfers between devices, permute(): return lax.ppermute(block, ('blk', 'inner'), pairs)  10.2 us
    pallas_call x1, Pallas kernels, spectra_work(): pl.pallas_call(functools.partial(spectra_body, plan), out_shape=[vmem_out...  5.66 us
    ppermute x8, waiting for transfers between devices, from_behind(): return lax.ppermute(block, axis, route)  2.48 us
    pallas_call x1, Pallas kernels, finish_spectra(): pl.pallas_call(finish_spectra_body, out_shape=[jax.ShapeDtypeStruct(mine_...  2.16 us
    concatenate x1, other arithmetic, along_line(): end_mine = permute(jnp.concatenate([spectra, coded]), inward)  2 us
    unnamed x10, local copies, waits for them, and re-layouts  1.9 us
  transfers between devices with their start and end apart: 20, of which 9 were waited for; matrix products, arithmetic and copies ran while one was open for 5% of the time, Pallas kernels for 28%

profile of v10, /device:TPU:0, one launch (start us, length us, event | category | flops | bytes accessed | tf_op | source)
XLA Modules:
  0.0 73.5 jit_solution(7408740745405030194)
XLA Ops:
  0.6 0.5 collective-permute-start.3
  1.1 4.1 %collective-permute-start.2 = (bf16[320,1024]{1,0:T(8,128)(2,1)}, bf16[320,1024]{1,0:T(8,128)(2,1)S(1)}, u32[]{:S(2)}, u32[]{:S(2)}) collective-permute-start(bf16[320,1024]{1,0:T(8,128)(2,1)} %here), channel_id=1, source_target_pairs={{0,4},{4,0},{8,12},{12,8},{1,5},{5,1},{9,13},{13,9},{2,6},{6,2},{1... | collective-permute-start | bytes 1966088 | tf_op jit(solution)/shard_map/ppermute | solution.py:567
  5.3 0.7 concatenate.19
  6.0 0.5 collective-permute-start.1
  6.5 0.7 fusion.28
  7.3 2.0 %pad_maximum_fusion = bf16[336,1024]{1,0:T(8,128)(2,1)} fusion(bf16[16,1024]{1,0:T(8,128)(2,1)S(1)} %fusion.14, bf16[320,1024]{1,0:T(8,128)(2,1)} %s_mine.1), kind=kLoop, calls=%fused_computation | loop fusion | flops 1376256 | bytes 1376256 | tf_op jit(solution)/shard_map/concatenate | solution.py:608
  9.3 1.9 %collective-permute-start.4 = (bf16[336,1024]{1,0:T(8,128)(2,1)}, bf16[336,1024]{1,0:T(8,128)(2,1)S(1)}, u32[]{:S(2)}, u32[]{:S(2)}) collective-permute-start(bf16[336,1024]{1,0:T(8,128)(2,1)} %pad_maximum_fusion), channel_id=1, source_target_pairs={{0,4},{12,8},{1,5},{13,9},{2,6},{14,10},{3,7},{15,11},{16,20},{28,... | collective-permute-start | bytes 2064392 | tf_op jit(solution)/shard_map/ppermute | solution.py:567
  12.8 0.8 %copy-done.4 = bf16[320,1024]{1,0:T(8,128)(2,1)} copy-done((bf16[320,1024]{1,0:T(8,128)(2,1)}, bf16[320,1024]{1,0:T(8,128)(2,1)S(1)}, u32[]{:S(2)}) %copy-start.4) | copy-done | bytes 655384
  13.7 4.3 %shard_map.68 = (f32[320,1024]{1,0:T(8,128)}, bf16[320,640]{1,0:T(8,128)(2,1)}) custom-call(f32[8,128]{1,0:T(8,128)S(1)} %select_select_fusion.refs_0_.refs_1_.consts, f32[1,640]{1,0:T(1,128)S(1)} %add_convert_fusion.refs_1_.refs_2_.labels, bf16[320,1024]{1,0:T(8,128)(2,1)} %s_mine.1, bf16[320,1024]{1,0:T(8,128)(2,1)} %copy-done.4, bf16[320,1024]{1,0:T(8,128)(2,1)} %here), custom_call_target="tpu_custom_call" | custom-call | flops 1024 | bytes 1024 | tf_op jit(solution)/shard_map/pallas_call | solution.py:340
  18.0 1.3 %collective-permute-start.10 = (bf16[320,1024]{1,0:T(8,128)(2,1)S(1)}, bf16[320,1024]{1,0:T(8,128)(2,1)}, u32[]{:S(2)}, u32[]{:S(2)}) collective-permute-start(bf16[320,1024]{1,0:T(8,128)(2,1)S(1)} %collective-permute-done.3.refs_5_.refs_10_.across), channel_id=1, source_target_pairs={{4,0},{8,12},{5,1},{9,13},{6,2},{10,14},{7,3},{11,15},{20,16},{24,... | collective-permute-start | bytes 1966088 | tf_op jit(solution)/shard_map/ppermute | solution.py:567
  19.3 1.5 %collective-permute-done.2.refs_4_.whole.refs_6_.side = bf16[320,1024]{1,0:T(8,128)(2,1)S(1)} collective-permute-done((bf16[320,1024]{1,0:T(8,128)(2,1)}, bf16[320,1024]{1,0:T(8,128)(2,1)S(1)}, u32[]{:S(2)}, u32[]{:S(2)}) %collective-permute-start.2) | collective-permute-done | bytes 655392 | tf_op jit(solution)/shard_map/ppermute | solution.py:567
  20.9 0.5 collective-permute-start.8
  21.6 5.2 %shard_map.69 = (f32[320,1024]{1,0:T(8,128)}, f32[320,1024]{1,0:T(8,128)}, bf16[320,640]{1,0:T(8,128)(2,1)}, bf16[320,640]{1,0:T(8,128)(2,1)}) custom-call(f32[8,128]{1,0:T(8,128)S(1)} %select_select_fusion.refs_0_.refs_1_.consts, f32[1,640]{1,0:T(1,128)S(1)} %add_convert_fusion.refs_1_.refs_2_.labels, bf16[320,1024]{1,0:T(8,128)(2,1)} %s_mine.1, ...), custom_call_target="tpu_custom_call" | custom-call | flops 1024 | bytes 1024 | tf_op jit(solution)/shard_map/pallas_call | solution.py:340
  26.8 7.3 %collective-permute-done.4.whole.refs_2_.refs_5_ = bf16[336,1024]{1,0:T(8,128)(2,1)S(1)} collective-permute-done((bf16[336,1024]{1,0:T(8,128)(2,1)}, bf16[336,1024]{1,0:T(8,128)(2,1)S(1)}, u32[]{:S(2)}, u32[]{:S(2)}) %collective-permute-start.4) | collective-permute-done | bytes 688160 | tf_op jit(solution)/shard_map/ppermute | solution.py:567
  34.1 0.9 %shard_map.70 = (bf16[112,1024]{1,0:T(8,128)(2,1)}, bf16[112,1024]{1,0:T(8,128)(2,1)}, bf16[112,1024]{1,0:T(8,128)(2,1)}) custom-call(bf16[336,1024]{1,0:T(8,128)(2,1)S(1)} %collective-permute-done.4.whole.refs_2_.refs_5_), custom_call_target="tpu_custom_call" | custom-call | flops 1024 | bytes 1024 | tf_op jit(solution)/shard_map/pallas_call | solution.py:456
  35.0 0.5 collective-permute-start.6
  35.6 0.7 collective-permute-done.10.rest_0_
  37.0 0.3 collective-permute-done.7.refs_5_.refs_8_
  37.7 4.9 %collective-permute-start.13 = (bf16[320,1024]{1,0:T(8,128)(2,1)S(1)}, bf16[320,1024]{1,0:T(8,128)(2,1)}, u32[]{:S(2)}, u32[]{:S(2)}) collective-permute-start(bf16[320,1024]{1,0:T(8,128)(2,1)S(1)} %shard_map.79), channel_id=1, source_target_pairs={{0,4},{4,0},{8,12},{12,8},{1,5},{5,1},{9,13},{13,9},{2,6},{6,2},{1... | collective-permute-start | bytes 1966088 | tf_op jit(solution)/shard_map/ppermute | solution.py:567
  42.6 1.0 %shard_map.74 = (bf16[160,1024]{1,0:T(8,128)(2,1)S(1)}, bf16[320,1024]{1,0:T(8,128)(2,1)}) custom-call(s32[1]{0:T(128)} %bitcast.3.refs_0_, f32[8,128]{1,0:T(8,128)S(1)} %select_select_fusion.refs_0_.refs_1_.consts, f32[1,640]{1,0:T(1,128)S(1)} %add_convert_fusion.refs_1_.refs_2_.labels, bf16[320,1024]{1,0:T(8,128)(2,1)} %s_mine.1, ...), custom_call_target="tpu_custom_call" | custom-call | flops 1024 | bytes 1024 | tf_op jit(solution)/shard_map/pallas_call | solution.py:340
  43.6 0.8 %copy-done.1 = bf16[320,1024]{1,0:T(8,128)(2,1)} copy-done((bf16[320,1024]{1,0:T(8,128)(2,1)}, bf16[320,1024]{1,0:T(8,128)(2,1)S(1)}, u32[]{:S(2)}) %copy-start.1) | copy-done | bytes 655384
  44.6 0.6 collective-permute-start.18
  45.2 10.0 %collective-permute-start.15 = (bf16[160,1024]{1,0:T(8,128)(2,1)S(1)}, bf16[160,1024]{1,0:T(8,128)(2,1)}, u32[]{:S(2)}, u32[]{:S(2)}) collective-permute-start(bf16[160,1024]{1,0:T(8,128)(2,1)S(1)} %shard_map.76), channel_id=1, source_target_pairs={{0,4},{4,0},{8,12},{12,8},{1,5},{5,1},{9,13},{13,9},{2,6},{6,2},{1... | collective-permute-start | bytes 983048 | tf_op jit(solution)/shard_map/ppermute | solution.py:567
  55.3 1.2 %shard_map.78 = bf16[160,1024]{1,0:T(8,128)(2,1)S(1)} custom-call(f32[160,1024]{1,0:T(8,128)} %get-tuple-element.58.total, bf16[160,1024]{1,0:T(8,128)(2,1)S(1)} %collective-permute-done.11.arrived), custom_call_target="tpu_custom_call" | custom-call | flops 1024 | bytes 1024 | tf_op jit(solution)/shard_map/pallas_call | solution.py:496
  56.4 4.4 %collective-permute-start.19 = (bf16[160,1024]{1,0:T(8,128)(2,1)S(1)}, bf16[160,1024]{1,0:T(8,128)(2,1)S(1)}, u32[]{:S(2)}, u32[]{:S(2)}) collective-permute-start(bf16[160,1024]{1,0:T(8,128)(2,1)S(1)} %shard_map.78), channel_id=1, source_target_pairs={{0,4},{4,0},{8,12},{12,8},{1,5},{5,1},{9,13},{13,9},{2,6},{6,2},{1... | collective-permute-start | bytes 983048 | tf_op jit(solution)/shard_map/ppermute | solution.py:567
  60.9 5.7 %shard_map.80 = (f32[320,1024]{1,0:T(8,128)S(1)}, bf16[320,1024]{1,0:T(8,128)(2,1)S(1)}) custom-call(s32[1]{0:T(128)} %bitcast.outer.flag, f32[8,128]{1,0:T(8,128)S(1)} %select_select_fusion.refs_0_.refs_1_.consts, f32[1,640]{1,0:T(1,128)S(1)} %add_convert_fusion.refs_1_.refs_2_.labels, bf16[320,1024]{1,0:T(8,128)(2,1)} %s_mine.1, ...), custom_call_target="tpu_custom_call" | custom-call | flops 1024 | bytes 1024 | tf_op jit(solution)/shard_map/pallas_call | solution.py:427
  66.7 0.5 collective-permute-start.16
  67.2 0.9 %collective-permute-done.14.rest_0_ = bf16[112,1024]{1,0:T(8,128)(2,1)S(1)} collective-permute-done((bf16[112,1024]{1,0:T(8,128)(2,1)S(1)}, bf16[112,1024]{1,0:T(8,128)(2,1)S(1)}, u32[]{:S(2)}, u32[]{:S(2)}) %collective-permute-start.14) | collective-permute-done | bytes 229408 | tf_op jit(solution)/shard_map/ppermute | solution.py:21
  68.1 0.6 collective-permute-done.17.rest_2_
  68.8 2.2 %shard_map.82 = (bf16[320,1024]{1,0:T(8,128)(2,1)}, f32[320,1024]{1,0:T(8,128)S(1)}) custom-call(f32[320,1024]{1,0:T(8,128)S(1)} %get-tuple-element.65.mine_s, f32[320,1024]{1,0:T(8,128)} %shard_map.77.away, bf16[112,1024]{1,0:T(8,128)(2,1)S(1)} %collective-permute-done.14.rest_0_, bf16[112,1024]{1,0:T(8,128)(2,1)S(1)} %collective-permute-done.16.rest_1_, ...), custom_call_target="tpu_custom_call" | custom-call | flops 1024 | bytes 1024 | tf_op jit(solution)/shard_map/pallas_call | solution.py:520
  70.9 0.7 collective-permute-done.19.inside_b
  71.6 1.9 %shard_map.83 = bf16[320,1024]{1,0:T(8,128)(2,1)} custom-call(s32[1]{0:T(128)} %bitcast.outer.flag, f32[320,1024]{1,0:T(8,128)S(1)} %get-tuple-element.72.here_total, bf16[320,1024]{1,0:T(8,128)(2,1)S(1)} %collective-permute-done.18.across_back, bf16[160,1024]{1,0:T(8,128)(2,1)} %collective-permute-done.15.inside_a, ...), custom_call_target="tpu_custom_call" | custom-call | flops 1024 | bytes 1024 | tf_op jit(solution)/shard_map/pallas_call | solution.py:548
  (48 shorter events, 2.3 us)
Async XLA Ops:
  0.6 17.3 %collective-permute-start.3 = (bf16[320,1024]{1,0:T(8,128)(2,1)}, bf16[320,1024]{1,0:T(8,128)(2,1)S(1)}, u32[]{:S(2)}, u32[]{:S(2)}) collective-permute-start(bf16[320,1024]{1,0:T(8,128)(2,1)} %here), channel_id=1, source_target_pairs={{4,8},{8,4},{0,1},{12,13},{5,9},{9,5},{1,0},{13,12},{6,10},{10,6},... | collective-permute-start | bytes 1966088 | tf_op jit(solution)/shard_map/ppermute | solution.py:567
  1.1 19.6 %collective-permute-start.2 = (bf16[320,1024]{1,0:T(8,128)(2,1)}, bf16[320,1024]{1,0:T(8,128)(2,1)S(1)}, u32[]{:S(2)}, u32[]{:S(2)}) collective-permute-start(bf16[320,1024]{1,0:T(8,128)(2,1)} %here), channel_id=1, source_target_pairs={{0,4},{4,0},{8,12},{12,8},{1,5},{5,1},{9,13},{13,9},{2,6},{6,2},{1... | collective-permute-start | bytes 1966088 | tf_op jit(solution)/shard_map/ppermute | solution.py:567
  6.0 6.8 %collective-permute-start = (s32[1,320]{1,0:T(1,128)S(1)}, s32[1,320]{1,0:T(1,128)S(1)}, u32[]{:S(2)}, u32[]{:S(2)}) collective-permute-start(s32[1,320]{1,0:T(1,128)S(1)} %concatenate.19), channel_id=1, source_target_pairs={{1,0},{0,1},{3,2},{2,3},{5,4},{4,5},{7,6},{6,7},{9,8},{8,9},{11,10... | collective-permute-start | bytes 3848 | tf_op jit(solution)/shard_map/ppermute | solution.py:21
  6.0 6.9 %collective-permute-start.1 = (bf16[320,1024]{1,0:T(8,128)(2,1)}, bf16[320,1024]{1,0:T(8,128)(2,1)S(1)}, u32[]{:S(2)}, u32[]{:S(2)}) collective-permute-start(bf16[320,1024]{1,0:T(8,128)(2,1)} %s_mine.1), channel_id=1, source_target_pairs={{1,0},{0,1},{3,2},{2,3},{5,4},{4,5},{7,6},{6,7},{9,8},{8,9},{11,10... | collective-permute-start | bytes 1966088 | tf_op jit(solution)/shard_map/ppermute | solution.py:21
  9.3 24.7 %collective-permute-start.4 = (bf16[336,1024]{1,0:T(8,128)(2,1)}, bf16[336,1024]{1,0:T(8,128)(2,1)S(1)}, u32[]{:S(2)}, u32[]{:S(2)}) collective-permute-start(bf16[336,1024]{1,0:T(8,128)(2,1)} %pad_maximum_fusion), channel_id=1, source_target_pairs={{0,4},{12,8},{1,5},{13,9},{2,6},{14,10},{3,7},{15,11},{16,20},{28,... | collective-permute-start | bytes 2064392 | tf_op jit(solution)/shard_map/ppermute | solution.py:567
  12.8 0.8 %copy-start.4 = (bf16[320,1024]{1,0:T(8,128)(2,1)}, bf16[320,1024]{1,0:T(8,128)(2,1)S(1)}, u32[]{:S(2)}) copy-start(bf16[320,1024]{1,0:T(8,128)(2,1)S(1)} %collective-permute-done.1.refs_3_.refs_4_.s_other) | copy-start | bytes 1966084
  18.0 18.4 %collective-permute-start.10 = (bf16[320,1024]{1,0:T(8,128)(2,1)S(1)}, bf16[320,1024]{1,0:T(8,128)(2,1)}, u32[]{:S(2)}, u32[]{:S(2)}) collective-permute-start(bf16[320,1024]{1,0:T(8,128)(2,1)S(1)} %collective-permute-done.3.refs_5_.refs_10_.across), channel_id=1, source_target_pairs={{4,0},{8,12},{5,1},{9,13},{6,2},{10,14},{7,3},{11,15},{20,16},{24,... | collective-permute-start | bytes 1966088 | tf_op jit(solution)/shard_map/ppermute | solution.py:567
  20.8 0.8 %copy-start = (bf16[320,1024]{1,0:T(8,128)(2,1)}, bf16[320,1024]{1,0:T(8,128)(2,1)S(1)}, u32[]{:S(2)}) copy-start(bf16[320,1024]{1,0:T(8,128)(2,1)S(1)} %collective-permute-done.2.refs_4_.whole.refs_6_.side) | copy-start | bytes 1966084
  20.8 14.6 %collective-permute-start.9 = (bf16[160,1024]{1,0:T(8,128)(2,1)S(1)}, bf16[160,1024]{1,0:T(8,128)(2,1)S(1)}, u32[]{:S(2)}, u32[]{:S(2)}) collective-permute-start(bf16[160,1024]{1,0:T(8,128)(2,1)S(1)} %get-tuple-element.51), channel_id=1, source_target_pairs={{4,8},{8,4},{0,1},{12,13},{5,9},{9,5},{1,0},{13,12},{6,10},{10,6},... | collective-permute-start | bytes 983048 | tf_op jit(solution)/shard_map/ppermute | solution.py:567
  20.9 16.7 %collective-permute-start.8 = (bf16[160,1024]{1,0:T(8,128)(2,1)S(1)}, bf16[160,1024]{1,0:T(8,128)(2,1)S(1)}, u32[]{:S(2)}, u32[]{:S(2)}) collective-permute-start(bf16[160,1024]{1,0:T(8,128)(2,1)S(1)} %get-tuple-element.50), channel_id=1, source_target_pairs={{4,8},{8,4},{0,1},{12,13},{5,9},{9,5},{1,0},{13,12},{6,10},{10,6},... | collective-permute-start | bytes 983048 | tf_op jit(solution)/shard_map/ppermute | solution.py:567
  35.0 1.7 %collective-permute-start.5 = (bf16[112,1024]{1,0:T(8,128)(2,1)}, bf16[112,1024]{1,0:T(8,128)(2,1)S(1)}, u32[]{:S(2)}, u32[]{:S(2)}) collective-permute-start(bf16[112,1024]{1,0:T(8,128)(2,1)} %get-tuple-element.47), channel_id=1, source_target_pairs={{1,0},{0,1},{3,2},{2,3},{5,4},{4,5},{7,6},{6,7},{9,8},{8,9},{11,10... | collective-permute-start | bytes 688136 | tf_op jit(solution)/shard_map/ppermute | solution.py:21
  35.0 2.0 %collective-permute-start.6 = (bf16[112,1024]{1,0:T(8,128)(2,1)}, bf16[112,1024]{1,0:T(8,128)(2,1)S(1)}, u32[]{:S(2)}, u32[]{:S(2)}) collective-permute-start(bf16[112,1024]{1,0:T(8,128)(2,1)} %get-tuple-element.48), channel_id=1, source_target_pairs={{1,0},{0,1},{3,2},{2,3},{5,4},{4,5},{7,6},{6,7},{9,8},{8,9},{11,10... | collective-permute-start | bytes 688136 | tf_op jit(solution)/shard_map/ppermute | solution.py:21
  35.5 2.2 %copy-start.2 = (bf16[160,1024]{1,0:T(8,128)(2,1)}, bf16[160,1024]{1,0:T(8,128)(2,1)S(1)}, u32[]{:S(2)}) copy-start(bf16[160,1024]{1,0:T(8,128)(2,1)S(1)} %collective-permute-done.9.refs_5_.refs_6_.first.rest_1_) | copy-start | bytes 983044
  35.5 1.8 %collective-permute-start.7 = (bf16[112,1024]{1,0:T(8,128)(2,1)}, bf16[112,1024]{1,0:T(8,128)(2,1)S(1)}, u32[]{:S(2)}, u32[]{:S(2)}) collective-permute-start(bf16[112,1024]{1,0:T(8,128)(2,1)} %get-tuple-element.49), channel_id=1, source_target_pairs={{1,0},{0,1},{3,2},{2,3},{5,4},{4,5},{7,6},{6,7},{9,8},{8,9},{11,10... | collective-permute-start | bytes 688136 | tf_op jit(solution)/shard_map/ppermute | solution.py:21
  37.4 7.1 %collective-permute-start.12 = (bf16[160,1024]{1,0:T(8,128)(2,1)S(1)}, bf16[160,1024]{1,0:T(8,128)(2,1)S(1)}, u32[]{:S(2)}, u32[]{:S(2)}) collective-permute-start(bf16[160,1024]{1,0:T(8,128)(2,1)S(1)} %shard_map.73), channel_id=1, source_target_pairs={{4,8},{8,4},{0,1},{12,13},{5,9},{9,5},{1,0},{13,12},{6,10},{10,6},... | collective-permute-start | bytes 983048 | tf_op jit(solution)/shard_map/ppermute | solution.py:567
  37.7 5.9 %copy-start.3 = (bf16[160,1024]{1,0:T(8,128)(2,1)}, bf16[160,1024]{1,0:T(8,128)(2,1)S(1)}, u32[]{:S(2)}) copy-start(bf16[160,1024]{1,0:T(8,128)(2,1)S(1)} %collective-permute-done.8.refs_9_.second.rest_2_) | copy-start | bytes 983044
  37.7 23.2 %collective-permute-start.13 = (bf16[320,1024]{1,0:T(8,128)(2,1)S(1)}, bf16[320,1024]{1,0:T(8,128)(2,1)}, u32[]{:S(2)}, u32[]{:S(2)}) collective-permute-start(bf16[320,1024]{1,0:T(8,128)(2,1)S(1)} %shard_map.79), channel_id=1, source_target_pairs={{0,4},{4,0},{8,12},{12,8},{1,5},{5,1},{9,13},{13,9},{2,6},{6,2},{1... | collective-permute-start | bytes 1966088 | tf_op jit(solution)/shard_map/ppermute | solution.py:567
  43.6 0.9 %copy-start.1 = (bf16[320,1024]{1,0:T(8,128)(2,1)}, bf16[320,1024]{1,0:T(8,128)(2,1)S(1)}, u32[]{:S(2)}) copy-start(bf16[320,1024]{1,0:T(8,128)(2,1)S(1)} %collective-permute-done.3.refs_5_.refs_10_.across) | copy-start | bytes 1966084
  44.4 10.8 %collective-permute-start.11 = (bf16[160,1024]{1,0:T(8,128)(2,1)S(1)}, bf16[160,1024]{1,0:T(8,128)(2,1)S(1)}, u32[]{:S(2)}, u32[]{:S(2)}) collective-permute-start(bf16[160,1024]{1,0:T(8,128)(2,1)S(1)} %get-tuple-element.55), channel_id=1, source_target_pairs={{4,8},{8,4},{0,1},{12,13},{5,9},{9,5},{1,0},{13,12},{6,10},{10,6},... | collective-permute-start | bytes 983048 | tf_op jit(solution)/shard_map/ppermute | solution.py:567
  44.6 26.3 %collective-permute-start.18 = (bf16[320,1024]{1,0:T(8,128)(2,1)}, bf16[320,1024]{1,0:T(8,128)(2,1)S(1)}, u32[]{:S(2)}, u32[]{:S(2)}) collective-permute-start(bf16[320,1024]{1,0:T(8,128)(2,1)} %get-tuple-element.74), channel_id=1, source_target_pairs={{4,8},{8,4},{0,1},{12,13},{5,9},{9,5},{1,0},{13,12},{6,10},{10,6},... | collective-permute-start | bytes 1966088 | tf_op jit(solution)/shard_map/ppermute | solution.py:567
  45.2 22.0 %collective-permute-start.15 = (bf16[160,1024]{1,0:T(8,128)(2,1)S(1)}, bf16[160,1024]{1,0:T(8,128)(2,1)}, u32[]{:S(2)}, u32[]{:S(2)}) collective-permute-start(bf16[160,1024]{1,0:T(8,128)(2,1)S(1)} %shard_map.76), channel_id=1, source_target_pairs={{0,4},{4,0},{8,12},{12,8},{1,5},{5,1},{9,13},{13,9},{2,6},{6,2},{1... | collective-permute-start | bytes 983048 | tf_op jit(solution)/shard_map/ppermute | solution.py:567
  56.4 15.2 %collective-permute-start.19 = (bf16[160,1024]{1,0:T(8,128)(2,1)S(1)}, bf16[160,1024]{1,0:T(8,128)(2,1)S(1)}, u32[]{:S(2)}, u32[]{:S(2)}) collective-permute-start(bf16[160,1024]{1,0:T(8,128)(2,1)S(1)} %shard_map.78), channel_id=1, source_target_pairs={{0,4},{4,0},{8,12},{12,8},{1,5},{5,1},{9,13},{13,9},{2,6},{6,2},{1... | collective-permute-start | bytes 983048 | tf_op jit(solution)/shard_map/ppermute | solution.py:567
  66.6 1.6 %collective-permute-start.14 = (bf16[112,1024]{1,0:T(8,128)(2,1)S(1)}, bf16[112,1024]{1,0:T(8,128)(2,1)S(1)}, u32[]{:S(2)}, u32[]{:S(2)}) collective-permute-start(bf16[112,1024]{1,0:T(8,128)(2,1)S(1)} %get-tuple-element.67), channel_id=1, source_target_pairs={{1,0},{0,1},{3,2},{2,3},{5,4},{4,5},{7,6},{6,7},{9,8},{8,9},{11,10... | collective-permute-start | bytes 688136 | tf_op jit(solution)/shard_map/ppermute | solution.py:21
  66.7 2.1 %collective-permute-start.16 = (bf16[112,1024]{1,0:T(8,128)(2,1)S(1)}, bf16[112,1024]{1,0:T(8,128)(2,1)S(1)}, u32[]{:S(2)}, u32[]{:S(2)}) collective-permute-start(bf16[112,1024]{1,0:T(8,128)(2,1)S(1)} %get-tuple-element.69), channel_id=1, source_target_pairs={{1,0},{0,1},{3,2},{2,3},{5,4},{4,5},{7,6},{6,7},{9,8},{8,9},{11,10... | collective-permute-start | bytes 688136 | tf_op jit(solution)/shard_map/ppermute | solution.py:21
  67.2 1.6 %collective-permute-start.17 = (bf16[96,1024]{1,0:T(8,128)(2,1)S(1)}, bf16[96,1024]{1,0:T(8,128)(2,1)S(1)}, u32[]{:S(2)}, u32[]{:S(2)}) collective-permute-start(bf16[96,1024]{1,0:T(8,128)(2,1)S(1)} %get-tuple-element.70), channel_id=1, source_target_pairs={{1,0},{0,1},{3,2},{2,3},{5,4},{4,5},{7,6},{6,7},{9,8},{8,9},{11,10... | collective-permute-start | bytes 589832 | tf_op jit(solution)/shard_map/ppermute | solution.py:21

commit v11 on v10

--- a/solution.py
+++ b/solution.py
@@ -504,8 +504,8 @@
     )(in_hbm(total.array) if away else in_vmem(total), in_vmem(arrived))
 
 
-def finish_spectra_body(mine_s, away, *rest):
-    others, (out, near, sem) = rest[:-3], rest[-3:]
+def finish_spectra_body(mine_s, away, inside, *rest):
+    others, (out, near, inside_near, sem) = rest[:-4], rest[-4:]
     copy = pltpu.make_async_copy(away, near, sem)
     copy.start()
     at = 0
@@ -513,22 +513,24 @@
         where = pl.ds(at, other.shape[0])
         out[where] = (mine_s[where] + other[...].astype(jnp.float32)).astype(jnp.bfloat16)
         at += other.shape[0]
+    inside_near[...] = inside[...]
     copy.wait()
 
 
-def finish_spectra(mine_s, others, away):
+def finish_spectra(mine_s, others, away, inside):
     return pl.pallas_call(
         finish_spectra_body,
         out_shape=[
             jax.ShapeDtypeStruct(mine_s.shape, jnp.bfloat16),
             vmem_out(away.shape, away.dtype),
+            vmem_out(inside.shape, inside.dtype),
         ],
-        in_specs=[VMEM_SPEC, HBM_SPEC] + [VMEM_SPEC] * len(others),
-        out_specs=[VMEM_SPEC] * 2,
+        in_specs=[VMEM_SPEC, HBM_SPEC] + [VMEM_SPEC] * (1 + len(others)),
+        out_specs=[VMEM_SPEC] * 3,
         scratch_shapes=[pltpu.SemaphoreType.DMA],
         cost_estimate=SMALL_COST,
         compiler_params=params(),
-    )(in_vmem(mine_s), in_hbm(away), *[in_vmem(a) for a in others])
+    )(in_vmem(mine_s), in_hbm(away), *[in_vmem(a) for a in [inside] + others])
 
 
 def finish_structures_body(flag, here_total, across_back, inside_a, inside_b, out):
@@ -623,18 +625,18 @@
         consts,
         [
             (Block(side_at, ("node",), "kept", coef="all"), Away(side), None),
-            (Block(across_at, ("node",), "kept", coef="masked"), across, None),
+            (Block(across_at, ("node",), "kept", coef="masked"), Away(across), None),
         ],
         rows,
         **node,
     )
-    end_mine = after(end_mine, across_g)
-    piece = -(-rows // 48) * 16
-    ends = (end_mine,) + tuple(swap_inner(x) for x in split(end_mine, (piece,) * 3))
     far_a = after(far_a, across_g)
     (far_g,) = pair_work(
         consts, [(Block(far_at, ("node",), "total"), far_a, None)], rows, wanted=~outer, **node
     )
+    end_mine = after(end_mine, far_g)
+    piece = -(-rows // 48) * 16
+    ends = (end_mine,) + tuple(swap_inner(x) for x in split(end_mine, (piece,) * 3))
 
     far_a, next_out = lax.optimization_barrier((far_a, next_out, far_g))[:2]
     (far_a_out,) = pair_work(
@@ -651,7 +653,7 @@
         consts,
         [
             (Block(far_at, ("node", "ends"), "rounded", cut), far_b, None),
-            (Block(across_at, ("ends",), "rounded", prior="kept"), across, across_g),
+            (Block(across_at, ("ends",), "rounded", prior="kept"), Away(across), across_g),
         ],
         rows,
         wanted=~outer,
@@ -694,8 +696,7 @@
         last_out,
     )
     others = [swap_inner(x) for x in split(other_s, (piece, piece, rows - 2 * piece))]
-    others[0] = after(others[0], inside_a)
-    grad_spectra, here_total = finish_spectra(mine_s, others, here_total)
+    grad_spectra, here_total, inside_a = finish_spectra(mine_s, others, here_total, inside_a)
     across_back = after(across_back, grad_spectra)
     return grad_spectra, finish_structures(outer, here_total, across_back, inside_a, inside_b)
 

time: 74 us -> 71 us (0.959)
  Pallas kernels: 22.7 us -> 21.4 us
  starting transfers between devices: 30.3 us -> 29 us
    ppermute x12, starting transfers between devices: 28.6 us -> 27.2 us  [permute(): return lax.ppermute(block, ('blk', 'inner'), pairs)]
    pallas_call x1, Pallas kernels: 1.86 us -> 0.88 us  [finish_structures(): pl.pallas_call(finish_structures_body, out_shape=jax.ShapeDtypeStruct(her...]
    ppermute x8, waiting for transfers between devices: 2.48 us -> 1.52 us  [from_behind(): return lax.ppermute(block, axis, route)]
    pallas_call x3, Pallas kernels: 0.98 us -> 0.13 us  [split(): pl.pallas_call(split_body, out_shape=[vmem_out((n, whole.shape[1]), whole...]
  transfers between devices with their start and end apart: 20 -> 20, of which waited for: 9 -> 5; matrix products, arithmetic and copies ran while one was open for 5% -> 5% of each run, Pallas kernels for 28% -> 29%
where the time goes in v11:
time: 71 us; the launch traced here: 70.6 us
  starting transfers between devices  29 us (41%)
  Pallas kernels  21.4 us (30%)
  waiting for transfers between devices  12.4 us (17%)
  other arithmetic  2.98 us (4%)
  local copies, waits for them, and re-layouts  2.48 us (3%)
  between operations  2.29 us (3%)
    ppermute x12, starting transfers between devices, permute(): return lax.ppermute(block, ('blk', 'inner'), pairs)  27.2 us
    pallas_call x7, Pallas kernels, pair_work(): pl.pallas_call(functools.partial(pair_body, plan), out_shape=outs, in_spe...  11.2 us
    ppermute x12, waiting for transfers between devices, permute(): return lax.ppermute(block, ('blk', 'inner'), pairs)  10.9 us
    pallas_call x1, Pallas kernels, spectra_work(): pl.pallas_call(functools.partial(spectra_body, plan), out_shape=[vmem_out...  5.66 us
    pallas_call x1, Pallas kernels, finish_spectra(): pl.pallas_call(finish_spectra_body, out_shape=[jax.ShapeDtypeStruct(mine_...  2.16 us
    concatenate x1, other arithmetic, along_line(): end_mine = permute(jnp.concatenate([spectra, coded]), inward)  2 us
    ppermute x8, starting transfers between devices, from_behind(): return lax.ppermute(block, axis, route)  1.8 us
    unnamed x10, local copies, waits for them, and re-layouts  1.79 us
  transfers between devices with their start and end apart: 20, of which 5 were waited for; matrix products, arithmetic and copies ran while one was open for 5% of the time, Pallas kernels for 29%

profile of v11, /device:TPU:0, one launch (start us, length us, event | category | flops | bytes accessed | tf_op | source)
XLA Modules:
  0.0 70.6 jit_solution(434165234266633119)
XLA Ops:
  0.6 0.5 collective-permute-start.3
  1.1 4.1 %collective-permute-start.2 = (bf16[320,1024]{1,0:T(8,128)(2,1)}, bf16[320,1024]{1,0:T(8,128)(2,1)S(1)}, u32[]{:S(2)}, u32[]{:S(2)}) collective-permute-start(bf16[320,1024]{1,0:T(8,128)(2,1)} %here), channel_id=1, source_target_pairs={{0,4},{4,0},{8,12},{12,8},{1,5},{5,1},{9,13},{13,9},{2,6},{6,2},{1... | collective-permute-start | bytes 1966088 | tf_op jit(solution)/shard_map/ppermute | solution.py:569
  5.3 0.7 concatenate.19
  6.0 0.5 collective-permute-start.1
  6.5 0.7 fusion.28
  7.2 0.1 fusion.14
  7.3 2.0 %pad_maximum_fusion = bf16[336,1024]{1,0:T(8,128)(2,1)} fusion(bf16[16,1024]{1,0:T(8,128)(2,1)S(1)} %fusion.14, bf16[320,1024]{1,0:T(8,128)(2,1)} %s_mine.1), kind=kLoop, calls=%fused_computation | loop fusion | flops 1376256 | bytes 1376256 | tf_op jit(solution)/shard_map/concatenate | solution.py:610
  9.3 1.9 %collective-permute-start.4 = (bf16[336,1024]{1,0:T(8,128)(2,1)}, bf16[336,1024]{1,0:T(8,128)(2,1)S(1)}, u32[]{:S(2)}, u32[]{:S(2)}) collective-permute-start(bf16[336,1024]{1,0:T(8,128)(2,1)} %pad_maximum_fusion), channel_id=1, source_target_pairs={{0,4},{12,8},{1,5},{13,9},{2,6},{14,10},{3,7},{15,11},{16,20},{28,... | collective-permute-start | bytes 2064392 | tf_op jit(solution)/shard_map/ppermute | solution.py:569
  12.8 0.8 %copy-done.3 = bf16[320,1024]{1,0:T(8,128)(2,1)} copy-done((bf16[320,1024]{1,0:T(8,128)(2,1)}, bf16[320,1024]{1,0:T(8,128)(2,1)S(1)}, u32[]{:S(2)}) %copy-start.3) | copy-done | bytes 655384
  13.7 4.3 %shard_map.68 = (f32[320,1024]{1,0:T(8,128)}, bf16[320,640]{1,0:T(8,128)(2,1)}) custom-call(f32[8,128]{1,0:T(8,128)S(1)} %select_select_fusion.refs_0_.refs_1_.consts, f32[1,640]{1,0:T(1,128)S(1)} %add_convert_fusion.refs_1_.refs_2_.labels, bf16[320,1024]{1,0:T(8,128)(2,1)} %s_mine.1, bf16[320,1024]{1,0:T(8,128)(2,1)} %copy-done.3, bf16[320,1024]{1,0:T(8,128)(2,1)} %here), custom_call_target="tpu_custom_call" | custom-call | flops 1024 | bytes 1024 | tf_op jit(solution)/shard_map/pallas_call | solution.py:340
  18.0 1.3 %collective-permute-start.10 = (bf16[320,1024]{1,0:T(8,128)(2,1)}, bf16[320,1024]{1,0:T(8,128)(2,1)S(1)}, u32[]{:S(2)}, u32[]{:S(2)}) collective-permute-start(bf16[320,1024]{1,0:T(8,128)(2,1)} %collective-permute-done.3.refs_5_.refs_10_.across), channel_id=1, source_target_pairs={{4,0},{8,12},{5,1},{9,13},{6,2},{10,14},{7,3},{11,15},{20,16},{24,... | collective-permute-start | bytes 1966088 | tf_op jit(solution)/shard_map/ppermute | solution.py:569
  19.3 1.5 %collective-permute-done.2.refs_4_.whole.refs_6_.side = bf16[320,1024]{1,0:T(8,128)(2,1)S(1)} collective-permute-done((bf16[320,1024]{1,0:T(8,128)(2,1)}, bf16[320,1024]{1,0:T(8,128)(2,1)S(1)}, u32[]{:S(2)}, u32[]{:S(2)}) %collective-permute-start.2) | collective-permute-done | bytes 655392 | tf_op jit(solution)/shard_map/ppermute | solution.py:569
  20.9 0.5 collective-permute-start.9
  21.4 0.2 copy-done
  21.6 5.7 %shard_map.69 = (f32[320,1024]{1,0:T(8,128)}, f32[320,1024]{1,0:T(8,128)}, bf16[320,640]{1,0:T(8,128)(2,1)}, bf16[320,640]{1,0:T(8,128)(2,1)}) custom-call(f32[8,128]{1,0:T(8,128)S(1)} %select_select_fusion.refs_0_.refs_1_.consts, f32[1,640]{1,0:T(1,128)S(1)} %add_convert_fusion.refs_1_.refs_2_.labels, bf16[320,1024]{1,0:T(8,128)(2,1)} %s_mine.1, ...), custom_call_target="tpu_custom_call" | custom-call | flops 1024 | bytes 1024 | tf_op jit(solution)/shard_map/pallas_call | solution.py:340
  27.4 6.7 %collective-permute-done.4.whole.refs_2_.refs_5_ = bf16[336,1024]{1,0:T(8,128)(2,1)S(1)} collective-permute-done((bf16[336,1024]{1,0:T(8,128)(2,1)}, bf16[336,1024]{1,0:T(8,128)(2,1)S(1)}, u32[]{:S(2)}, u32[]{:S(2)}) %collective-permute-start.4) | collective-permute-done | bytes 688160 | tf_op jit(solution)/shard_map/ppermute | solution.py:569
  34.2 0.5 collective-permute-start.7
  34.8 1.7 %collective-permute-done.10.rest_0_ = bf16[320,1024]{1,0:T(8,128)(2,1)S(1)} collective-permute-done((bf16[320,1024]{1,0:T(8,128)(2,1)}, bf16[320,1024]{1,0:T(8,128)(2,1)S(1)}, u32[]{:S(2)}, u32[]{:S(2)}) %collective-permute-start.10) | collective-permute-done | bytes 655392 | tf_op jit(solution)/shard_map/ppermute | solution.py:569
  36.6 0.7 %copy-done.4 = bf16[320,1024]{1,0:T(8,128)(2,1)} copy-done((bf16[320,1024]{1,0:T(8,128)(2,1)}, bf16[320,1024]{1,0:T(8,128)(2,1)S(1)}, u32[]{:S(2)}) %copy-start.4) | copy-done | bytes 655384
  37.4 3.5 %collective-permute-start.13 = (bf16[320,1024]{1,0:T(8,128)(2,1)S(1)}, bf16[320,1024]{1,0:T(8,128)(2,1)}, u32[]{:S(2)}, u32[]{:S(2)}) collective-permute-start(bf16[320,1024]{1,0:T(8,128)(2,1)S(1)} %shard_map.79), channel_id=1, source_target_pairs={{0,4},{4,0},{8,12},{12,8},{1,5},{5,1},{9,13},{13,9},{2,6},{6,2},{1... | collective-permute-start | bytes 1966088 | tf_op jit(solution)/shard_map/ppermute | solution.py:569
  40.8 1.0 %shard_map.74 = (bf16[160,1024]{1,0:T(8,128)(2,1)S(1)}, bf16[320,1024]{1,0:T(8,128)(2,1)}) custom-call(s32[1]{0:T(128)} %bitcast.3.refs_0_, f32[8,128]{1,0:T(8,128)S(1)} %select_select_fusion.refs_0_.refs_1_.consts, f32[1,640]{1,0:T(1,128)S(1)} %add_convert_fusion.refs_1_.refs_2_.labels, bf16[320,1024]{1,0:T(8,128)(2,1)} %s_mine.1, ...), custom_call_target="tpu_custom_call" | custom-call | flops 1024 | bytes 1024 | tf_op jit(solution)/shard_map/pallas_call | solution.py:340
  41.9 0.1 shard_map.75
  42.1 0.6 collective-permute-start.18
  42.7 10.1 %collective-permute-start.14 = (bf16[160,1024]{1,0:T(8,128)(2,1)S(1)}, bf16[160,1024]{1,0:T(8,128)(2,1)S(1)}, u32[]{:S(2)}, u32[]{:S(2)}) collective-permute-start(bf16[160,1024]{1,0:T(8,128)(2,1)S(1)} %shard_map.76), channel_id=1, source_target_pairs={{0,4},{4,0},{8,12},{12,8},{1,5},{5,1},{9,13},{13,9},{2,6},{6,2},{1... | collective-permute-start | bytes 983048 | tf_op jit(solution)/shard_map/ppermute | solution.py:569
  52.9 1.2 %shard_map.78 = bf16[160,1024]{1,0:T(8,128)(2,1)S(1)} custom-call(f32[160,1024]{1,0:T(8,128)} %get-tuple-element.58.total, bf16[160,1024]{1,0:T(8,128)(2,1)S(1)} %collective-permute-done.11.arrived), custom_call_target="tpu_custom_call" | custom-call | flops 1024 | bytes 1024 | tf_op jit(solution)/shard_map/pallas_call | solution.py:496
  54.1 4.5 %collective-permute-start.19 = (bf16[160,1024]{1,0:T(8,128)(2,1)S(1)}, bf16[160,1024]{1,0:T(8,128)(2,1)S(1)}, u32[]{:S(2)}, u32[]{:S(2)}) collective-permute-start(bf16[160,1024]{1,0:T(8,128)(2,1)S(1)} %shard_map.78), channel_id=1, source_target_pairs={{0,4},{4,0},{8,12},{12,8},{1,5},{5,1},{9,13},{13,9},{2,6},{6,2},{1... | collective-permute-start | bytes 983048 | tf_op jit(solution)/shard_map/ppermute | solution.py:569
  58.6 5.7 %shard_map.80 = (f32[320,1024]{1,0:T(8,128)S(1)}, bf16[320,1024]{1,0:T(8,128)(2,1)S(1)}) custom-call(s32[1]{0:T(128)} %bitcast.outer.flag, f32[8,128]{1,0:T(8,128)S(1)} %select_select_fusion.refs_0_.refs_1_.consts, f32[1,640]{1,0:T(1,128)S(1)} %add_convert_fusion.refs_1_.refs_2_.labels, bf16[320,1024]{1,0:T(8,128)(2,1)} %s_mine.1, ...), custom_call_target="tpu_custom_call" | custom-call | flops 1024 | bytes 1024 | tf_op jit(solution)/shard_map/pallas_call | solution.py:427
  64.4 0.5 collective-permute-start.16
  64.9 1.5 %collective-permute-done.17.rest_2_ = bf16[96,1024]{1,0:T(8,128)(2,1)S(1)} collective-permute-done((bf16[96,1024]{1,0:T(8,128)(2,1)S(1)}, bf16[96,1024]{1,0:T(8,128)(2,1)S(1)}, u32[]{:S(2)}, u32[]{:S(2)}) %collective-permute-start.17) | collective-permute-done | bytes 196640 | tf_op jit(solution)/shard_map/ppermute | solution.py:21
  66.4 2.2 %shard_map.82 = (bf16[320,1024]{1,0:T(8,128)(2,1)}, f32[320,1024]{1,0:T(8,128)S(1)}, bf16[160,1024]{1,0:T(8,128)(2,1)S(1)}) custom-call(f32[320,1024]{1,0:T(8,128)S(1)} %get-tuple-element.65.mine_s, f32[320,1024]{1,0:T(8,128)} %shard_map.77.away, bf16[160,1024]{1,0:T(8,128)(2,1)S(1)} %collective-permute-done.14.inside, ...), custom_call_target="tpu_custom_call" | custom-call | flops 1024 | bytes 1024 | tf_op jit(solution)/shard_map/pallas_call | solution.py:521
  68.6 1.1 %collective-permute-done.19.inside_b = bf16[160,1024]{1,0:T(8,128)(2,1)S(1)} collective-permute-done((bf16[160,1024]{1,0:T(8,128)(2,1)S(1)}, bf16[160,1024]{1,0:T(8,128)(2,1)S(1)}, u32[]{:S(2)}, u32[]{:S(2)}) %collective-permute-start.19) | collective-permute-done | bytes 327712 | tf_op jit(solution)/shard_map/ppermute | solution.py:569
  69.7 0.9 %shard_map.83 = bf16[320,1024]{1,0:T(8,128)(2,1)} custom-call(s32[1]{0:T(128)} %bitcast.outer.flag, f32[320,1024]{1,0:T(8,128)S(1)} %get-tuple-element.71.here_total, bf16[320,1024]{1,0:T(8,128)(2,1)S(1)} %collective-permute-done.18.across_back, bf16[160,1024]{1,0:T(8,128)(2,1)S(1)} %get-tuple-element.75.inside_a, ...), custom_call_target="tpu_custom_call" | custom-call | flops 1024 | bytes 1024 | tf_op jit(solution)/shard_map/pallas_call | solution.py:550
  (48 shorter events, 1.2 us)
Async XLA Ops:
  0.6 17.3 %collective-permute-start.3 = (bf16[320,1024]{1,0:T(8,128)(2,1)}, bf16[320,1024]{1,0:T(8,128)(2,1)}, u32[]{:S(2)}, u32[]{:S(2)}) collective-permute-start(bf16[320,1024]{1,0:T(8,128)(2,1)} %here), channel_id=1, source_target_pairs={{4,8},{8,4},{0,1},{12,13},{5,9},{9,5},{1,0},{13,12},{6,10},{10,6},... | collective-permute-start | bytes 1966088 | tf_op jit(solution)/shard_map/ppermute | solution.py:569
  1.1 19.6 %collective-permute-start.2 = (bf16[320,1024]{1,0:T(8,128)(2,1)}, bf16[320,1024]{1,0:T(8,128)(2,1)S(1)}, u32[]{:S(2)}, u32[]{:S(2)}) collective-permute-start(bf16[320,1024]{1,0:T(8,128)(2,1)} %here), channel_id=1, source_target_pairs={{0,4},{4,0},{8,12},{12,8},{1,5},{5,1},{9,13},{13,9},{2,6},{6,2},{1... | collective-permute-start | bytes 1966088 | tf_op jit(solution)/shard_map/ppermute | solution.py:569
  6.0 6.8 %collective-permute-start = (s32[1,320]{1,0:T(1,128)S(1)}, s32[1,320]{1,0:T(1,128)S(1)}, u32[]{:S(2)}, u32[]{:S(2)}) collective-permute-start(s32[1,320]{1,0:T(1,128)S(1)} %concatenate.19), channel_id=1, source_target_pairs={{1,0},{0,1},{3,2},{2,3},{5,4},{4,5},{7,6},{6,7},{9,8},{8,9},{11,10... | collective-permute-start | bytes 3848 | tf_op jit(solution)/shard_map/ppermute | solution.py:21
  6.0 6.9 %collective-permute-start.1 = (bf16[320,1024]{1,0:T(8,128)(2,1)}, bf16[320,1024]{1,0:T(8,128)(2,1)S(1)}, u32[]{:S(2)}, u32[]{:S(2)}) collective-permute-start(bf16[320,1024]{1,0:T(8,128)(2,1)} %s_mine.1), channel_id=1, source_target_pairs={{1,0},{0,1},{3,2},{2,3},{5,4},{4,5},{7,6},{6,7},{9,8},{8,9},{11,10... | collective-permute-start | bytes 1966088 | tf_op jit(solution)/shard_map/ppermute | solution.py:21
  9.3 24.7 %collective-permute-start.4 = (bf16[336,1024]{1,0:T(8,128)(2,1)}, bf16[336,1024]{1,0:T(8,128)(2,1)S(1)}, u32[]{:S(2)}, u32[]{:S(2)}) collective-permute-start(bf16[336,1024]{1,0:T(8,128)(2,1)} %pad_maximum_fusion), channel_id=1, source_target_pairs={{0,4},{12,8},{1,5},{13,9},{2,6},{14,10},{3,7},{15,11},{16,20},{28,... | collective-permute-start | bytes 2064392 | tf_op jit(solution)/shard_map/ppermute | solution.py:569
  12.8 0.8 %copy-start.3 = (bf16[320,1024]{1,0:T(8,128)(2,1)}, bf16[320,1024]{1,0:T(8,128)(2,1)S(1)}, u32[]{:S(2)}) copy-start(bf16[320,1024]{1,0:T(8,128)(2,1)S(1)} %collective-permute-done.1.refs_3_.refs_4_.s_other) | copy-start | bytes 1966084
  18.0 18.5 %collective-permute-start.10 = (bf16[320,1024]{1,0:T(8,128)(2,1)}, bf16[320,1024]{1,0:T(8,128)(2,1)S(1)}, u32[]{:S(2)}, u32[]{:S(2)}) collective-permute-start(bf16[320,1024]{1,0:T(8,128)(2,1)} %collective-permute-done.3.refs_5_.refs_10_.across), channel_id=1, source_target_pairs={{4,0},{8,12},{5,1},{9,13},{6,2},{10,14},{7,3},{11,15},{20,16},{24,... | collective-permute-start | bytes 1966088 | tf_op jit(solution)/shard_map/ppermute | solution.py:569
  20.8 0.8 %copy-start = (bf16[320,1024]{1,0:T(8,128)(2,1)}, bf16[320,1024]{1,0:T(8,128)(2,1)S(1)}, u32[]{:S(2)}) copy-start(bf16[320,1024]{1,0:T(8,128)(2,1)S(1)} %collective-permute-done.2.refs_4_.whole.refs_6_.side) | copy-start | bytes 1966084
  20.8 6.5 %collective-permute-start.5 = (bf16[160,1024]{1,0:T(8,128)(2,1)S(1)}, bf16[160,1024]{1,0:T(8,128)(2,1)S(1)}, u32[]{:S(2)}, u32[]{:S(2)}) collective-permute-start(bf16[160,1024]{1,0:T(8,128)(2,1)S(1)} %get-tuple-element.45), channel_id=1, source_target_pairs={{4,8},{8,4},{0,1},{12,13},{5,9},{9,5},{1,0},{13,12},{6,10},{10,6},... | collective-permute-start | bytes 983048 | tf_op jit(solution)/shard_map/ppermute | solution.py:569
  20.9 16.4 %collective-permute-start.9 = (bf16[160,1024]{1,0:T(8,128)(2,1)S(1)}, bf16[160,1024]{1,0:T(8,128)(2,1)S(1)}, u32[]{:S(2)}, u32[]{:S(2)}) collective-permute-start(bf16[160,1024]{1,0:T(8,128)(2,1)S(1)} %get-tuple-element.52), channel_id=1, source_target_pairs={{4,8},{8,4},{0,1},{12,13},{5,9},{9,5},{1,0},{13,12},{6,10},{10,6},... | collective-permute-start | bytes 983048 | tf_op jit(solution)/shard_map/ppermute | solution.py:569
  27.3 10.0 %copy-start.1 = (bf16[160,1024]{1,0:T(8,128)(2,1)}, bf16[160,1024]{1,0:T(8,128)(2,1)S(1)}, u32[]{:S(2)}) copy-start(bf16[160,1024]{1,0:T(8,128)(2,1)S(1)} %collective-permute-done.5.refs_5_.refs_6_.first.rest_1_) | copy-start | bytes 983044
  34.1 2.3 %collective-permute-start.6 = (bf16[112,1024]{1,0:T(8,128)(2,1)S(1)}, bf16[112,1024]{1,0:T(8,128)(2,1)S(1)}, u32[]{:S(2)}, u32[]{:S(2)}) collective-permute-start(bf16[112,1024]{1,0:T(8,128)(2,1)S(1)} %get-tuple-element.49), channel_id=1, source_target_pairs={{1,0},{0,1},{3,2},{2,3},{5,4},{4,5},{7,6},{6,7},{9,8},{8,9},{11,10... | collective-permute-start | bytes 688136 | tf_op jit(solution)/shard_map/ppermute | solution.py:21
  34.2 2.2 %collective-permute-start.7 = (bf16[112,1024]{1,0:T(8,128)(2,1)S(1)}, bf16[112,1024]{1,0:T(8,128)(2,1)S(1)}, u32[]{:S(2)}, u32[]{:S(2)}) collective-permute-start(bf16[112,1024]{1,0:T(8,128)(2,1)S(1)} %get-tuple-element.50), channel_id=1, source_target_pairs={{1,0},{0,1},{3,2},{2,3},{5,4},{4,5},{7,6},{6,7},{9,8},{8,9},{11,10... | collective-permute-start | bytes 688136 | tf_op jit(solution)/shard_map/ppermute | solution.py:21
  34.7 1.8 %collective-permute-start.8 = (bf16[112,1024]{1,0:T(8,128)(2,1)S(1)}, bf16[112,1024]{1,0:T(8,128)(2,1)S(1)}, u32[]{:S(2)}, u32[]{:S(2)}) collective-permute-start(bf16[112,1024]{1,0:T(8,128)(2,1)S(1)} %get-tuple-element.51), channel_id=1, source_target_pairs={{1,0},{0,1},{3,2},{2,3},{5,4},{4,5},{7,6},{6,7},{9,8},{8,9},{11,10... | collective-permute-start | bytes 688136 | tf_op jit(solution)/shard_map/ppermute | solution.py:21
  36.4 0.8 %copy-start.4 = (bf16[320,1024]{1,0:T(8,128)(2,1)}, bf16[320,1024]{1,0:T(8,128)(2,1)S(1)}, u32[]{:S(2)}) copy-start(bf16[320,1024]{1,0:T(8,128)(2,1)S(1)} %collective-permute-done.10.rest_0_) | copy-start | bytes 1966084
  37.3 4.7 %collective-permute-start.12 = (bf16[160,1024]{1,0:T(8,128)(2,1)S(1)}, bf16[160,1024]{1,0:T(8,128)(2,1)S(1)}, u32[]{:S(2)}, u32[]{:S(2)}) collective-permute-start(bf16[160,1024]{1,0:T(8,128)(2,1)S(1)} %shard_map.73), channel_id=1, source_target_pairs={{4,8},{8,4},{0,1},{12,13},{5,9},{9,5},{1,0},{13,12},{6,10},{10,6},... | collective-permute-start | bytes 983048 | tf_op jit(solution)/shard_map/ppermute | solution.py:569
  37.3 4.5 %copy-start.2 = (bf16[160,1024]{1,0:T(8,128)(2,1)}, bf16[160,1024]{1,0:T(8,128)(2,1)S(1)}, u32[]{:S(2)}) copy-start(bf16[160,1024]{1,0:T(8,128)(2,1)S(1)} %collective-permute-done.9.refs_9_.second.rest_2_) | copy-start | bytes 983044
  37.4 21.2 %collective-permute-start.13 = (bf16[320,1024]{1,0:T(8,128)(2,1)S(1)}, bf16[320,1024]{1,0:T(8,128)(2,1)}, u32[]{:S(2)}, u32[]{:S(2)}) collective-permute-start(bf16[320,1024]{1,0:T(8,128)(2,1)S(1)} %shard_map.79), channel_id=1, source_target_pairs={{0,4},{4,0},{8,12},{12,8},{1,5},{5,1},{9,13},{13,9},{2,6},{6,2},{1... | collective-permute-start | bytes 1966088 | tf_op jit(solution)/shard_map/ppermute | solution.py:569
  41.8 11.1 %collective-permute-start.11 = (bf16[160,1024]{1,0:T(8,128)(2,1)S(1)}, bf16[160,1024]{1,0:T(8,128)(2,1)S(1)}, u32[]{:S(2)}, u32[]{:S(2)}) collective-permute-start(bf16[160,1024]{1,0:T(8,128)(2,1)S(1)} %get-tuple-element.55), channel_id=1, source_target_pairs={{4,8},{8,4},{0,1},{12,13},{5,9},{9,5},{1,0},{13,12},{6,10},{10,6},... | collective-permute-start | bytes 983048 | tf_op jit(solution)/shard_map/ppermute | solution.py:569
  42.1 26.5 %collective-permute-start.18 = (bf16[320,1024]{1,0:T(8,128)(2,1)}, bf16[320,1024]{1,0:T(8,128)(2,1)S(1)}, u32[]{:S(2)}, u32[]{:S(2)}) collective-permute-start(bf16[320,1024]{1,0:T(8,128)(2,1)} %get-tuple-element.73), channel_id=1, source_target_pairs={{4,8},{8,4},{0,1},{12,13},{5,9},{9,5},{1,0},{13,12},{6,10},{10,6},... | collective-permute-start | bytes 1966088 | tf_op jit(solution)/shard_map/ppermute | solution.py:569
  42.7 22.2 %collective-permute-start.14 = (bf16[160,1024]{1,0:T(8,128)(2,1)S(1)}, bf16[160,1024]{1,0:T(8,128)(2,1)S(1)}, u32[]{:S(2)}, u32[]{:S(2)}) collective-permute-start(bf16[160,1024]{1,0:T(8,128)(2,1)S(1)} %shard_map.76), channel_id=1, source_target_pairs={{0,4},{4,0},{8,12},{12,8},{1,5},{5,1},{9,13},{13,9},{2,6},{6,2},{1... | collective-permute-start | bytes 983048 | tf_op jit(solution)/shard_map/ppermute | solution.py:569
  54.1 15.6 %collective-permute-start.19 = (bf16[160,1024]{1,0:T(8,128)(2,1)S(1)}, bf16[160,1024]{1,0:T(8,128)(2,1)S(1)}, u32[]{:S(2)}, u32[]{:S(2)}) collective-permute-start(bf16[160,1024]{1,0:T(8,128)(2,1)S(1)} %shard_map.78), channel_id=1, source_target_pairs={{0,4},{4,0},{8,12},{12,8},{1,5},{5,1},{9,13},{13,9},{2,6},{6,2},{1... | collective-permute-start | bytes 983048 | tf_op jit(solution)/shard_map/ppermute | solution.py:569
  64.3 2.2 %collective-permute-start.15 = (bf16[112,1024]{1,0:T(8,128)(2,1)S(1)}, bf16[112,1024]{1,0:T(8,128)(2,1)S(1)}, u32[]{:S(2)}, u32[]{:S(2)}) collective-permute-start(bf16[112,1024]{1,0:T(8,128)(2,1)S(1)} %get-tuple-element.67), channel_id=1, source_target_pairs={{1,0},{0,1},{3,2},{2,3},{5,4},{4,5},{7,6},{6,7},{9,8},{8,9},{11,10... | collective-permute-start | bytes 688136 | tf_op jit(solution)/shard_map/ppermute | solution.py:21
  64.4 2.1 %collective-permute-start.16 = (bf16[112,1024]{1,0:T(8,128)(2,1)S(1)}, bf16[112,1024]{1,0:T(8,128)(2,1)S(1)}, u32[]{:S(2)}, u32[]{:S(2)}) collective-permute-start(bf16[112,1024]{1,0:T(8,128)(2,1)S(1)} %get-tuple-element.68), channel_id=1, source_target_pairs={{1,0},{0,1},{3,2},{2,3},{5,4},{4,5},{7,6},{6,7},{9,8},{8,9},{11,10... | collective-permute-start | bytes 688136 | tf_op jit(solution)/shard_map/ppermute | solution.py:21
  64.9 1.6 %collective-permute-start.17 = (bf16[96,1024]{1,0:T(8,128)(2,1)S(1)}, bf16[96,1024]{1,0:T(8,128)(2,1)S(1)}, u32[]{:S(2)}, u32[]{:S(2)}) collective-permute-start(bf16[96,1024]{1,0:T(8,128)(2,1)S(1)} %get-tuple-element.69), channel_id=1, source_target_pairs={{1,0},{0,1},{3,2},{2,3},{5,4},{4,5},{7,6},{6,7},{9,8},{8,9},{11,10... | collective-permute-start | bytes 589832 | tf_op jit(solution)/shard_map/ppermute | solution.py:21

commit v12 on v11

--- a/solution.py
+++ b/solution.py
@@ -355,10 +355,11 @@
 
 
 def spectra_body(plan, outer, consts, labels, s_mine, s_other, coef_here, coef_side, coef_across, here, side, across, *rest):
-    rows, n_next, n_far = plan
+    rows, n_next, n_far, n_last = plan
     nexts, rest = rest[:n_next], rest[n_next:]
     fars, rest = rest[:n_far], rest[n_far:]
-    last, mine_out, other_out, spectra, coefs, held, sems = rest
+    lasts, rest = rest[:n_last], rest[n_last:]
+    mine_out, other_out, spectra, coefs, held, sems = rest
     used = 0
 
     def move(source, target):
@@ -385,7 +386,7 @@
 
     @pl.when(outer[0] != 0)
     def _():
-        for copy in fill(list(nexts) + [last], held, 2 * rows):
+        for copy in fill(list(nexts) + list(lasts), held, 2 * rows):
             copy.wait()
 
     for copy in moves:
@@ -420,10 +421,10 @@
         out[...] = (scale * total).astype(out.dtype)
 
 
-def spectra_work(outer, consts, labels, node, coefs, here, side, across, nexts, fars, last):
+def spectra_work(outer, consts, labels, node, coefs, here, side, across, nexts, fars, lasts):
     rows, width = here.shape
-    arrays = list(node) + list(coefs) + [here, side, across] + list(nexts) + list(fars) + [last]
-    plan = (rows, len(nexts), len(fars))
+    arrays = list(node) + list(coefs) + [here, side, across] + list(nexts) + list(fars) + list(lasts)
+    plan = (rows, len(nexts), len(fars), len(lasts))
     return pl.pallas_call(
         functools.partial(spectra_body, plan),
         out_shape=[vmem_out((rows, width), jnp.float32), vmem_out((rows, width), jnp.bfloat16)],
@@ -461,23 +462,6 @@
         cost_estimate=SMALL_COST,
         compiler_params=params(),
     )(in_vmem(whole))
-
-
-def join_body(first, second, out):
-    out[pl.ds(0, first.shape[0])] = first[...]
-    out[pl.ds(first.shape[0], second.shape[0])] = second[...]
-
-
-def join(first, second):
-    rows = first.shape[0] + second.shape[0]
-    return pl.pallas_call(
-        join_body,
-        out_shape=vmem_out((rows, first.shape[1]), first.dtype),
-        in_specs=[VMEM_SPEC] * 2,
-        out_specs=VMEM_SPEC,
-        cost_estimate=SMALL_COST,
-        compiler_params=params(),
-    )(in_vmem(first), in_vmem(second))
 
 
 def add_body(total, arrived, out, *scratch):
@@ -602,7 +586,7 @@
     for i, value in enumerate(rows_of_consts):
         consts = jnp.where(index == i, value, consts)
 
-    cut = rows // 2
+    cut = 2 * rows // 5
     half = rows // 2
     across = permute(glycans, middle)
     side = permute(glycans, sides)
@@ -631,14 +615,16 @@
         **node,
     )
     far_a = after(far_a, across_g)
+    last_a = permute(far_a, sides)
     (far_g,) = pair_work(
         consts, [(Block(far_at, ("node",), "total"), far_a, None)], rows, wanted=~outer, **node
     )
     end_mine = after(end_mine, far_g)
     piece = -(-rows // 48) * 16
-    ends = (end_mine,) + tuple(swap_inner(x) for x in split(end_mine, (piece,) * 3))
-
-    far_a, next_out = lax.optimization_barrier((far_a, next_out, far_g))[:2]
+    two = (half + LABEL_ROWS, half)
+    ends = (end_mine,) + tuple(swap_inner(x) for x in split(end_mine, two))
+
+    far_a, far_b, next_out = lax.optimization_barrier((far_a, far_b, next_out, far_g))[:3]
     (far_a_out,) = pair_work(
         consts,
         [(Block(far_at, ("ends",), "rounded", prior="near"), far_a, far_g)],
@@ -647,21 +633,32 @@
         ends=ends,
     )
     back_a = permute(far_a_out, middle)
-    last_out = permute(join(after(far_a, far_a_out), far_b), sides)
     far_b = after(far_b, far_a_out)
-    far_b_out, across_out = pair_work(
+    last_b = permute(far_b, sides)
+    (far_b_out,) = pair_work(
+        consts,
+        [(Block(far_at, ("node", "ends"), "rounded", cut), far_b, None)],
+        rows,
+        wanted=~outer,
+        ends=ends,
+        **node,
+    )
+    back_b = permute(far_b_out, middle)
+    (across_out,) = pair_work(
         consts,
         [
-            (Block(far_at, ("node", "ends"), "rounded", cut), far_b, None),
-            (Block(across_at, ("ends",), "rounded", prior="kept"), Away(across), across_g),
+            (
+                Block(across_at, ("ends",), "rounded", prior="kept"),
+                Away(after(across, far_b_out)),
+                across_g,
+            )
         ],
         rows,
         wanted=~outer,
         ends=ends,
-        **node,
-    )
-    back_b = permute(far_b_out, middle)
-    late_side = Away(after(side, far_b_out))
+    )
+    late_side, last_a = lax.optimization_barrier((side, last_a, across_out))[:2]
+    late_side = Away(late_side)
     side_total_a, side_total_b = pair_work(
         consts,
         [(Block(side_at, ("ends",), "split", cut=cut, prior="kept"), late_side, side_g)],
@@ -679,7 +676,8 @@
         wanted=~outer,
         ends=ends,
     )
-    total_b = add_rounded(Away(side_total_b), after(back_b, here_total))
+    back_b, last_b = lax.optimization_barrier((back_b, last_b, here_total))[:2]
+    total_b = add_rounded(Away(side_total_b), back_b)
     inside_b = permute(total_b, sides)
 
     mine_s, other_s = spectra_work(
@@ -693,7 +691,7 @@
         across,
         (next_out,),
         (far_a, far_b),
-        last_out,
+        (last_a, last_b),
     )
     others = [swap_inner(x) for x in split(other_s, (piece, piece, rows - 2 * piece))]
     grad_spectra, here_total, inside_a = finish_spectra(mine_s, others, here_total, inside_a)

time: 71 us -> 71.4 us (level)
  starting transfers between devices: 29 us -> 32.9 us
  waiting for transfers between devices: 12.4 us -> 9.83 us
  Pallas kernels: 21.4 us -> 20.6 us
    ppermute x12 -> x13, starting transfers between devices: 27.2 us -> 31.2 us  [permute(): return lax.ppermute(block, ('blk', 'inner'), pairs)]
    ppermute x12 -> x13, waiting for transfers between devices: 10.9 us -> 8.31 us  [permute(): return lax.ppermute(block, ('blk', 'inner'), pairs)]
    pallas_call x7 -> x8, Pallas kernels: 11.2 us -> 10.3 us  [pair_work(): pl.pallas_call(functools.partial(pair_body, plan), out_shape=outs, in_spe...]
    unnamed x10 -> x12, local copies, waits for them, and re-layouts: 1.79 us -> 1.67 us
    ppermute x8 -> x7, starting transfers between devices: 1.8 us -> 1.72 us  [from_behind(): return lax.ppermute(block, axis, route)]
    ppermute x8 -> x7, waiting for transfers between devices: 1.52 us -> 1.52 us  [from_behind(): return lax.ppermute(block, axis, route)]
  transfers between devices with their start and end apart: 20 -> 20, of which waited for: 5 -> 3; matrix products, arithmetic and copies ran while one was open for 5% -> 5% of each run, Pallas kernels for 29% -> 28%
where the time goes in v12:
time: 71.4 us; the launch traced here: 70.9 us
  starting transfers between devices  32.9 us (46%)
  Pallas kernels  20.6 us (29%)
  waiting for transfers between devices  9.83 us (14%)
  other arithmetic  2.98 us (4%)
  local copies, waits for them, and re-layouts  2.36 us (3%)
  between operations  2.33 us (3%)
    ppermute x13, starting transfers between devices, permute(): return lax.ppermute(block, ('blk', 'inner'), pairs)  31.2 us
    pallas_call x8, Pallas kernels, pair_work(): pl.pallas_call(functools.partial(pair_body, plan), out_shape=outs, in_spe...  10.3 us
    ppermute x13, waiting for transfers between devices, permute(): return lax.ppermute(block, ('blk', 'inner'), pairs)  8.31 us
    pallas_call x1, Pallas kernels, spectra_work(): pl.pallas_call(functools.partial(spectra_body, plan), out_shape=[vmem_out...  5.64 us
    pallas_call x1, Pallas kernels, finish_spectra(): pl.pallas_call(finish_spectra_body, out_shape=[jax.ShapeDtypeStruct(mine_...  2.16 us
    concatenate x1, other arithmetic, along_line(): end_mine = permute(jnp.concatenate([spectra, coded]), inward)  2 us
    ppermute x7, starting transfers between devices, from_behind(): return lax.ppermute(block, axis, route)  1.72 us
    unnamed x12, local copies, waits for them, and re-layouts  1.67 us
  transfers between devices with their start and end apart: 20, of which 3 were waited for; matrix products, arithmetic and copies ran while one was open for 5% of the time, Pallas kernels for 28%

profile of v12, /device:TPU:0, one launch (start us, length us, event | category | flops | bytes accessed | tf_op | source)
XLA Modules:
  0.0 70.9 jit_solution(17702421584023710157)
XLA Ops:
  0.6 0.5 collective-permute-start.3
  1.1 4.1 %collective-permute-start.2 = (bf16[320,1024]{1,0:T(8,128)(2,1)}, bf16[320,1024]{1,0:T(8,128)(2,1)S(1)}, u32[]{:S(2)}, u32[]{:S(2)}) collective-permute-start(bf16[320,1024]{1,0:T(8,128)(2,1)} %here), channel_id=1, source_target_pairs={{0,4},{4,0},{8,12},{12,8},{1,5},{5,1},{9,13},{13,9},{2,6},{6,2},{1... | collective-permute-start | bytes 1966088 | tf_op jit(solution)/shard_map/ppermute | solution.py:553
  5.3 0.7 concatenate.19
  6.0 0.5 collective-permute-start.1
  6.5 0.7 fusion.28
  7.2 0.1 fusion.14
  7.3 2.0 %pad_maximum_fusion = bf16[336,1024]{1,0:T(8,128)(2,1)} fusion(bf16[16,1024]{1,0:T(8,128)(2,1)S(1)} %fusion.14, bf16[320,1024]{1,0:T(8,128)(2,1)} %s_mine.1), kind=kLoop, calls=%fused_computation | loop fusion | flops 1376256 | bytes 1376256 | tf_op jit(solution)/shard_map/concatenate | solution.py:594
  9.3 1.9 %collective-permute-start.4 = (bf16[336,1024]{1,0:T(8,128)(2,1)}, bf16[336,1024]{1,0:T(8,128)(2,1)S(1)}, u32[]{:S(2)}, u32[]{:S(2)}) collective-permute-start(bf16[336,1024]{1,0:T(8,128)(2,1)} %pad_maximum_fusion), channel_id=1, source_target_pairs={{0,4},{12,8},{1,5},{13,9},{2,6},{14,10},{3,7},{15,11},{16,20},{28,... | collective-permute-start | bytes 2064392 | tf_op jit(solution)/shard_map/ppermute | solution.py:553
  12.7 0.1 select_select_fusion.refs_0_.refs_1_.consts
  12.8 0.8 %copy-done.3 = bf16[320,1024]{1,0:T(8,128)(2,1)} copy-done((bf16[320,1024]{1,0:T(8,128)(2,1)}, bf16[320,1024]{1,0:T(8,128)(2,1)S(1)}, u32[]{:S(2)}) %copy-start.3) | copy-done | bytes 655384
  13.7 4.3 %shard_map.68 = (f32[320,1024]{1,0:T(8,128)}, bf16[320,640]{1,0:T(8,128)(2,1)}) custom-call(f32[8,128]{1,0:T(8,128)S(1)} %select_select_fusion.refs_0_.refs_1_.consts, f32[1,640]{1,0:T(1,128)S(1)} %add_convert_fusion.refs_1_.refs_2_.labels, bf16[320,1024]{1,0:T(8,128)(2,1)} %s_mine.1, bf16[320,1024]{1,0:T(8,128)(2,1)} %copy-done.3, bf16[320,1024]{1,0:T(8,128)(2,1)} %here), custom_call_target="tpu_custom_call" | custom-call | flops 1024 | bytes 1024 | tf_op jit(solution)/shard_map/pallas_call | solution.py:340
  18.0 1.3 %collective-permute-start.10 = (bf16[320,1024]{1,0:T(8,128)(2,1)}, bf16[320,1024]{1,0:T(8,128)(2,1)}, u32[]{:S(2)}, u32[]{:S(2)}) collective-permute-start(bf16[320,1024]{1,0:T(8,128)(2,1)} %collective-permute-done.3.refs_5_.across), channel_id=1, source_target_pairs={{4,0},{8,12},{5,1},{9,13},{6,2},{10,14},{7,3},{11,15},{20,16},{24,... | collective-permute-start | bytes 1966088 | tf_op jit(solution)/shard_map/ppermute | solution.py:553
  19.3 1.5 %collective-permute-done.2.refs_4_.whole.refs_5_.side = bf16[320,1024]{1,0:T(8,128)(2,1)S(1)} collective-permute-done((bf16[320,1024]{1,0:T(8,128)(2,1)}, bf16[320,1024]{1,0:T(8,128)(2,1)S(1)}, u32[]{:S(2)}, u32[]{:S(2)}) %collective-permute-start.2) | collective-permute-done | bytes 655392 | tf_op jit(solution)/shard_map/ppermute | solution.py:553
  20.9 0.5 collective-permute-start.9
  21.4 0.2 copy-done
  21.6 5.6 %shard_map.69 = (f32[320,1024]{1,0:T(8,128)}, f32[320,1024]{1,0:T(8,128)}, bf16[320,640]{1,0:T(8,128)(2,1)}, bf16[320,640]{1,0:T(8,128)(2,1)}) custom-call(f32[8,128]{1,0:T(8,128)S(1)} %select_select_fusion.refs_0_.refs_1_.consts, f32[1,640]{1,0:T(1,128)S(1)} %add_convert_fusion.refs_1_.refs_2_.labels, bf16[320,1024]{1,0:T(8,128)(2,1)} %s_mine.1, ...), custom_call_target="tpu_custom_call" | custom-call | flops 1024 | bytes 1024 | tf_op jit(solution)/shard_map/pallas_call | solution.py:340
  27.3 6.8 %collective-permute-done.4.whole.refs_2_.refs_5_ = bf16[336,1024]{1,0:T(8,128)(2,1)S(1)} collective-permute-done((bf16[336,1024]{1,0:T(8,128)(2,1)}, bf16[336,1024]{1,0:T(8,128)(2,1)S(1)}, u32[]{:S(2)}, u32[]{:S(2)}) %collective-permute-start.4) | collective-permute-done | bytes 688160 | tf_op jit(solution)/shard_map/ppermute | solution.py:553
  34.2 0.5 collective-permute-start.7
  34.7 2.4 %collective-permute-start.8 = (bf16[128,1024]{1,0:T(8,128)(2,1)S(1)}, bf16[128,1024]{1,0:T(8,128)(2,1)S(1)}, u32[]{:S(2)}, u32[]{:S(2)}) collective-permute-start(bf16[128,1024]{1,0:T(8,128)(2,1)S(1)} %collective-permute-done.5.refs_5_.rest_1_), channel_id=1, source_target_pairs={{0,4},{4,0},{8,12},{12,8},{1,5},{5,1},{9,13},{13,9},{2,6},{6,2},{1... | collective-permute-start | bytes 786440 | tf_op jit(solution)/shard_map/ppermute | solution.py:553
  37.3 0.1 shard_map.74
  37.4 0.6 collective-permute-start.11
  37.9 7.4 %collective-permute-start.12 = (bf16[192,1024]{1,0:T(8,128)(2,1)S(1)}, bf16[192,1024]{1,0:T(8,128)(2,1)S(1)}, u32[]{:S(2)}, u32[]{:S(2)}) collective-permute-start(bf16[192,1024]{1,0:T(8,128)(2,1)S(1)} %collective-permute-done.9.refs_8_.rest_2_), channel_id=1, source_target_pairs={{0,4},{4,0},{8,12},{12,8},{1,5},{5,1},{9,13},{13,9},{2,6},{6,2},{1... | collective-permute-start | bytes 1179656 | tf_op jit(solution)/shard_map/ppermute | solution.py:553
  45.5 0.1 shard_map.76
  45.6 0.6 copy-done.5
  46.3 8.1 %collective-permute-start.14 = (bf16[128,1024]{1,0:T(8,128)(2,1)S(1)}, bf16[128,1024]{1,0:T(8,128)(2,1)S(1)}, u32[]{:S(2)}, u32[]{:S(2)}) collective-permute-start(bf16[128,1024]{1,0:T(8,128)(2,1)S(1)} %shard_map.77), channel_id=1, source_target_pairs={{0,4},{4,0},{8,12},{12,8},{1,5},{5,1},{9,13},{13,9},{2,6},{6,2},{1... | collective-permute-start | bytes 786440 | tf_op jit(solution)/shard_map/ppermute | solution.py:553
  54.5 1.4 %shard_map.79 = bf16[192,1024]{1,0:T(8,128)(2,1)S(1)} custom-call(f32[192,1024]{1,0:T(8,128)} %get-tuple-element.58.total, bf16[192,1024]{1,0:T(8,128)(2,1)S(1)} %collective-permute-done.11.arrived), custom_call_target="tpu_custom_call" | custom-call | flops 1024 | bytes 1024 | tf_op jit(solution)/shard_map/pallas_call | solution.py:480
  55.9 4.1 %collective-permute-start.19 = (bf16[192,1024]{1,0:T(8,128)(2,1)S(1)}, bf16[192,1024]{1,0:T(8,128)(2,1)S(1)}, u32[]{:S(2)}, u32[]{:S(2)}) collective-permute-start(bf16[192,1024]{1,0:T(8,128)(2,1)S(1)} %shard_map.79), channel_id=1, source_target_pairs={{0,4},{4,0},{8,12},{12,8},{1,5},{5,1},{9,13},{13,9},{2,6},{6,2},{1... | collective-permute-start | bytes 1179656 | tf_op jit(solution)/shard_map/ppermute | solution.py:553
  60.0 5.6 %shard_map.80 = (f32[320,1024]{1,0:T(8,128)S(1)}, bf16[320,1024]{1,0:T(8,128)(2,1)S(1)}) custom-call(s32[1]{0:T(128)} %bitcast.outer.flag, f32[8,128]{1,0:T(8,128)S(1)} %select_select_fusion.refs_0_.refs_1_.consts, f32[1,640]{1,0:T(1,128)S(1)} %add_convert_fusion.refs_1_.refs_2_.labels, bf16[320,1024]{1,0:T(8,128)(2,1)} %s_mine.1, ...), custom_call_target="tpu_custom_call" | custom-call | flops 1024 | bytes 1024 | tf_op jit(solution)/shard_map/pallas_call | solution.py:428
  65.8 0.5 collective-permute-start.16
  66.3 1.5 %collective-permute-done.17.rest_2_ = bf16[96,1024]{1,0:T(8,128)(2,1)S(1)} collective-permute-done((bf16[96,1024]{1,0:T(8,128)(2,1)S(1)}, bf16[96,1024]{1,0:T(8,128)(2,1)S(1)}, u32[]{:S(2)}, u32[]{:S(2)}) %collective-permute-start.17) | collective-permute-done | bytes 196640 | tf_op jit(solution)/shard_map/ppermute | solution.py:21
  67.9 2.2 %shard_map.82 = (bf16[320,1024]{1,0:T(8,128)(2,1)}, f32[320,1024]{1,0:T(8,128)S(1)}, bf16[128,1024]{1,0:T(8,128)(2,1)S(1)}) custom-call(f32[320,1024]{1,0:T(8,128)S(1)} %get-tuple-element.66.mine_s, f32[320,1024]{1,0:T(8,128)} %shard_map.78.away, bf16[128,1024]{1,0:T(8,128)(2,1)S(1)} %collective-permute-done.14.inside, ...), custom_call_target="tpu_custom_call" | custom-call | flops 1024 | bytes 1024 | tf_op jit(solution)/shard_map/pallas_call | solution.py:505
  70.0 0.9 %shard_map.83 = bf16[320,1024]{1,0:T(8,128)(2,1)} custom-call(s32[1]{0:T(128)} %bitcast.outer.flag, f32[320,1024]{1,0:T(8,128)S(1)} %get-tuple-element.72.here_total, bf16[320,1024]{1,0:T(8,128)(2,1)S(1)} %collective-permute-done.18.across_back, bf16[128,1024]{1,0:T(8,128)(2,1)S(1)} %get-tuple-element.75.inside_a, ...), custom_call_target="tpu_custom_call" | custom-call | flops 1024 | bytes 1024 | tf_op jit(solution)/shard_map/pallas_call | solution.py:534
  (50 shorter events, 1.1 us)
Async XLA Ops:
  0.6 17.3 %collective-permute-start.3 = (bf16[320,1024]{1,0:T(8,128)(2,1)}, bf16[320,1024]{1,0:T(8,128)(2,1)}, u32[]{:S(2)}, u32[]{:S(2)}) collective-permute-start(bf16[320,1024]{1,0:T(8,128)(2,1)} %here), channel_id=1, source_target_pairs={{4,8},{8,4},{0,1},{12,13},{5,9},{9,5},{1,0},{13,12},{6,10},{10,6},... | collective-permute-start | bytes 1966088 | tf_op jit(solution)/shard_map/ppermute | solution.py:553
  1.1 19.6 %collective-permute-start.2 = (bf16[320,1024]{1,0:T(8,128)(2,1)}, bf16[320,1024]{1,0:T(8,128)(2,1)S(1)}, u32[]{:S(2)}, u32[]{:S(2)}) collective-permute-start(bf16[320,1024]{1,0:T(8,128)(2,1)} %here), channel_id=1, source_target_pairs={{0,4},{4,0},{8,12},{12,8},{1,5},{5,1},{9,13},{13,9},{2,6},{6,2},{1... | collective-permute-start | bytes 1966088 | tf_op jit(solution)/shard_map/ppermute | solution.py:553
  6.0 6.8 %collective-permute-start = (s32[1,320]{1,0:T(1,128)S(1)}, s32[1,320]{1,0:T(1,128)S(1)}, u32[]{:S(2)}, u32[]{:S(2)}) collective-permute-start(s32[1,320]{1,0:T(1,128)S(1)} %concatenate.19), channel_id=1, source_target_pairs={{1,0},{0,1},{3,2},{2,3},{5,4},{4,5},{7,6},{6,7},{9,8},{8,9},{11,10... | collective-permute-start | bytes 3848 | tf_op jit(solution)/shard_map/ppermute | solution.py:21
  6.0 6.9 %collective-permute-start.1 = (bf16[320,1024]{1,0:T(8,128)(2,1)}, bf16[320,1024]{1,0:T(8,128)(2,1)S(1)}, u32[]{:S(2)}, u32[]{:S(2)}) collective-permute-start(bf16[320,1024]{1,0:T(8,128)(2,1)} %s_mine.1), channel_id=1, source_target_pairs={{1,0},{0,1},{3,2},{2,3},{5,4},{4,5},{7,6},{6,7},{9,8},{8,9},{11,10... | collective-permute-start | bytes 1966088 | tf_op jit(solution)/shard_map/ppermute | solution.py:21
  9.3 24.7 %collective-permute-start.4 = (bf16[336,1024]{1,0:T(8,128)(2,1)}, bf16[336,1024]{1,0:T(8,128)(2,1)S(1)}, u32[]{:S(2)}, u32[]{:S(2)}) collective-permute-start(bf16[336,1024]{1,0:T(8,128)(2,1)} %pad_maximum_fusion), channel_id=1, source_target_pairs={{0,4},{12,8},{1,5},{13,9},{2,6},{14,10},{3,7},{15,11},{16,20},{28,... | collective-permute-start | bytes 2064392 | tf_op jit(solution)/shard_map/ppermute | solution.py:553
  12.8 0.8 %copy-start.3 = (bf16[320,1024]{1,0:T(8,128)(2,1)}, bf16[320,1024]{1,0:T(8,128)(2,1)S(1)}, u32[]{:S(2)}) copy-start(bf16[320,1024]{1,0:T(8,128)(2,1)S(1)} %collective-permute-done.1.refs_3_.refs_4_.s_other) | copy-start | bytes 1966084
  18.0 19.1 %collective-permute-start.10 = (bf16[320,1024]{1,0:T(8,128)(2,1)}, bf16[320,1024]{1,0:T(8,128)(2,1)}, u32[]{:S(2)}, u32[]{:S(2)}) collective-permute-start(bf16[320,1024]{1,0:T(8,128)(2,1)} %collective-permute-done.3.refs_5_.across), channel_id=1, source_target_pairs={{4,0},{8,12},{5,1},{9,13},{6,2},{10,14},{7,3},{11,15},{20,16},{24,... | collective-permute-start | bytes 1966088 | tf_op jit(solution)/shard_map/ppermute | solution.py:553
  20.8 0.8 %copy-start = (bf16[320,1024]{1,0:T(8,128)(2,1)}, bf16[320,1024]{1,0:T(8,128)(2,1)S(1)}, u32[]{:S(2)}) copy-start(bf16[320,1024]{1,0:T(8,128)(2,1)S(1)} %collective-permute-done.2.refs_4_.whole.refs_5_.side) | copy-start | bytes 1966084
  20.8 6.4 %collective-permute-start.5 = (bf16[128,1024]{1,0:T(8,128)(2,1)S(1)}, bf16[128,1024]{1,0:T(8,128)(2,1)S(1)}, u32[]{:S(2)}, u32[]{:S(2)}) collective-permute-start(bf16[128,1024]{1,0:T(8,128)(2,1)S(1)} %get-tuple-element.45), channel_id=1, source_target_pairs={{4,8},{8,4},{0,1},{12,13},{5,9},{9,5},{1,0},{13,12},{6,10},{10,6},... | collective-permute-start | bytes 786440 | tf_op jit(solution)/shard_map/ppermute | solution.py:553
  20.9 16.2 %collective-permute-start.9 = (bf16[192,1024]{1,0:T(8,128)(2,1)S(1)}, bf16[192,1024]{1,0:T(8,128)(2,1)S(1)}, u32[]{:S(2)}, u32[]{:S(2)}) collective-permute-start(bf16[192,1024]{1,0:T(8,128)(2,1)S(1)} %get-tuple-element.51), channel_id=1, source_target_pairs={{4,8},{8,4},{0,1},{12,13},{5,9},{9,5},{1,0},{13,12},{6,10},{10,6},... | collective-permute-start | bytes 1179656 | tf_op jit(solution)/shard_map/ppermute | solution.py:553
  27.2 9.9 %copy-start.1 = (bf16[128,1024]{1,0:T(8,128)(2,1)}, bf16[128,1024]{1,0:T(8,128)(2,1)S(1)}, u32[]{:S(2)}) copy-start(bf16[128,1024]{1,0:T(8,128)(2,1)S(1)} %collective-permute-done.5.refs_5_.rest_1_) | copy-start | bytes 786436
  34.1 3.0 %collective-permute-start.6 = (bf16[176,1024]{1,0:T(8,128)(2,1)S(1)}, bf16[176,1024]{1,0:T(8,128)(2,1)S(1)}, u32[]{:S(2)}, u32[]{:S(2)}) collective-permute-start(bf16[176,1024]{1,0:T(8,128)(2,1)S(1)} %get-tuple-element.49), channel_id=1, source_target_pairs={{1,0},{0,1},{3,2},{2,3},{5,4},{4,5},{7,6},{6,7},{9,8},{8,9},{11,10... | collective-permute-start | bytes 1081352 | tf_op jit(solution)/shard_map/ppermute | solution.py:21
  34.2 2.9 %collective-permute-start.7 = (bf16[160,1024]{1,0:T(8,128)(2,1)S(1)}, bf16[160,1024]{1,0:T(8,128)(2,1)S(1)}, u32[]{:S(2)}, u32[]{:S(2)}) collective-permute-start(bf16[160,1024]{1,0:T(8,128)(2,1)S(1)} %get-tuple-element.50), channel_id=1, source_target_pairs={{1,0},{0,1},{3,2},{2,3},{5,4},{4,5},{7,6},{6,7},{9,8},{8,9},{11,10... | collective-permute-start | bytes 983048 | tf_op jit(solution)/shard_map/ppermute | solution.py:21
  34.7 10.8 %collective-permute-start.8 = (bf16[128,1024]{1,0:T(8,128)(2,1)S(1)}, bf16[128,1024]{1,0:T(8,128)(2,1)S(1)}, u32[]{:S(2)}, u32[]{:S(2)}) collective-permute-start(bf16[128,1024]{1,0:T(8,128)(2,1)S(1)} %collective-permute-done.5.refs_5_.rest_1_), channel_id=1, source_target_pairs={{0,4},{4,0},{8,12},{12,8},{1,5},{5,1},{9,13},{13,9},{2,6},{6,2},{1... | collective-permute-start | bytes 786440 | tf_op jit(solution)/shard_map/ppermute | solution.py:553
  37.1 0.9 %copy-start.2 = (bf16[192,1024]{1,0:T(8,128)(2,1)}, bf16[192,1024]{1,0:T(8,128)(2,1)S(1)}, u32[]{:S(2)}) copy-start(bf16[192,1024]{1,0:T(8,128)(2,1)S(1)} %collective-permute-done.9.refs_8_.rest_2_) | copy-start | bytes 1179652
  37.2 9.0 %collective-permute-start.13 = (bf16[128,1024]{1,0:T(8,128)(2,1)S(1)}, bf16[128,1024]{1,0:T(8,128)(2,1)S(1)}, u32[]{:S(2)}, u32[]{:S(2)}) collective-permute-start(bf16[128,1024]{1,0:T(8,128)(2,1)S(1)} %shard_map.73), channel_id=1, source_target_pairs={{4,8},{8,4},{0,1},{12,13},{5,9},{9,5},{1,0},{13,12},{6,10},{10,6},... | collective-permute-start | bytes 786440 | tf_op jit(solution)/shard_map/ppermute | solution.py:553
  37.4 17.1 %collective-permute-start.11 = (bf16[192,1024]{1,0:T(8,128)(2,1)S(1)}, bf16[192,1024]{1,0:T(8,128)(2,1)S(1)}, u32[]{:S(2)}, u32[]{:S(2)}) collective-permute-start(bf16[192,1024]{1,0:T(8,128)(2,1)S(1)} %shard_map.74), channel_id=1, source_target_pairs={{4,8},{8,4},{0,1},{12,13},{5,9},{9,5},{1,0},{13,12},{6,10},{10,6},... | collective-permute-start | bytes 1179656 | tf_op jit(solution)/shard_map/ppermute | solution.py:553
  37.9 16.5 %collective-permute-start.12 = (bf16[192,1024]{1,0:T(8,128)(2,1)S(1)}, bf16[192,1024]{1,0:T(8,128)(2,1)S(1)}, u32[]{:S(2)}, u32[]{:S(2)}) collective-permute-start(bf16[192,1024]{1,0:T(8,128)(2,1)S(1)} %collective-permute-done.9.refs_8_.rest_2_), channel_id=1, source_target_pairs={{0,4},{4,0},{8,12},{12,8},{1,5},{5,1},{9,13},{13,9},{2,6},{6,2},{1... | collective-permute-start | bytes 1179656 | tf_op jit(solution)/shard_map/ppermute | solution.py:553
  45.5 0.7 %copy-start.5 = (bf16[128,1024]{1,0:T(8,128)(2,1)}, bf16[128,1024]{1,0:T(8,128)(2,1)S(1)}, u32[]{:S(2)}) copy-start(bf16[128,1024]{1,0:T(8,128)(2,1)S(1)} %collective-permute-done.8.rest_3_) | copy-start | bytes 786436
  46.2 23.8 %collective-permute-start.18 = (bf16[320,1024]{1,0:T(8,128)(2,1)S(1)}, bf16[320,1024]{1,0:T(8,128)(2,1)S(1)}, u32[]{:S(2)}, u32[]{:S(2)}) collective-permute-start(bf16[320,1024]{1,0:T(8,128)(2,1)S(1)} %shard_map.75), channel_id=1, source_target_pairs={{4,8},{8,4},{0,1},{12,13},{5,9},{9,5},{1,0},{13,12},{6,10},{10,6},... | collective-permute-start | bytes 1966088 | tf_op jit(solution)/shard_map/ppermute | solution.py:553
  46.3 19.9 %collective-permute-start.14 = (bf16[128,1024]{1,0:T(8,128)(2,1)S(1)}, bf16[128,1024]{1,0:T(8,128)(2,1)S(1)}, u32[]{:S(2)}, u32[]{:S(2)}) collective-permute-start(bf16[128,1024]{1,0:T(8,128)(2,1)S(1)} %shard_map.77), channel_id=1, source_target_pairs={{0,4},{4,0},{8,12},{12,8},{1,5},{5,1},{9,13},{13,9},{2,6},{6,2},{1... | collective-permute-start | bytes 786440 | tf_op jit(solution)/shard_map/ppermute | solution.py:553
  54.5 1.4 %copy-start.4 = (bf16[192,1024]{1,0:T(8,128)(2,1)}, bf16[192,1024]{1,0:T(8,128)(2,1)S(1)}, u32[]{:S(2)}) copy-start(bf16[192,1024]{1,0:T(8,128)(2,1)S(1)} %collective-permute-done.12.rest_4_) | copy-start | bytes 1179652
  55.9 14.2 %collective-permute-start.19 = (bf16[192,1024]{1,0:T(8,128)(2,1)S(1)}, bf16[192,1024]{1,0:T(8,128)(2,1)S(1)}, u32[]{:S(2)}, u32[]{:S(2)}) collective-permute-start(bf16[192,1024]{1,0:T(8,128)(2,1)S(1)} %shard_map.79), channel_id=1, source_target_pairs={{0,4},{4,0},{8,12},{12,8},{1,5},{5,1},{9,13},{13,9},{2,6},{6,2},{1... | collective-permute-start | bytes 1179656 | tf_op jit(solution)/shard_map/ppermute | solution.py:553
  65.7 2.2 %collective-permute-start.15 = (bf16[112,1024]{1,0:T(8,128)(2,1)S(1)}, bf16[112,1024]{1,0:T(8,128)(2,1)S(1)}, u32[]{:S(2)}, u32[]{:S(2)}) collective-permute-start(bf16[112,1024]{1,0:T(8,128)(2,1)S(1)} %get-tuple-element.68), channel_id=1, source_target_pairs={{1,0},{0,1},{3,2},{2,3},{5,4},{4,5},{7,6},{6,7},{9,8},{8,9},{11,10... | collective-permute-start | bytes 688136 | tf_op jit(solution)/shard_map/ppermute | solution.py:21
  65.8 2.1 %collective-permute-start.16 = (bf16[112,1024]{1,0:T(8,128)(2,1)S(1)}, bf16[112,1024]{1,0:T(8,128)(2,1)S(1)}, u32[]{:S(2)}, u32[]{:S(2)}) collective-permute-start(bf16[112,1024]{1,0:T(8,128)(2,1)S(1)} %get-tuple-element.69), channel_id=1, source_target_pairs={{1,0},{0,1},{3,2},{2,3},{5,4},{4,5},{7,6},{6,7},{9,8},{8,9},{11,10... | collective-permute-start | bytes 688136 | tf_op jit(solution)/shard_map/ppermute | solution.py:21
  66.3 1.6 %collective-permute-start.17 = (bf16[96,1024]{1,0:T(8,128)(2,1)S(1)}, bf16[96,1024]{1,0:T(8,128)(2,1)S(1)}, u32[]{:S(2)}, u32[]{:S(2)}) collective-permute-start(bf16[96,1024]{1,0:T(8,128)(2,1)S(1)} %get-tuple-element.70), channel_id=1, source_target_pairs={{1,0},{0,1},{3,2},{2,3},{5,4},{4,5},{7,6},{6,7},{9,8},{8,9},{11,10... | collective-permute-start | bytes 589832 | tf_op jit(solution)/shard_map/ppermute | solution.py:21

commit v13 on v12

--- a/solution.py
+++ b/solution.py
@@ -129,7 +129,7 @@
     ends = take_if(plan.ends)
     held = take(len(blocks))
     prior_held = [take_if(b.prior == "kept") for b in blocks]
-    out_held = [take_if(b.out in ("kept", "kept scaled", "split")) for b in blocks]
+    out_held = [take_if(b.out in ("kept", "split")) for b in blocks]
     coef_held = [take_if(b.coef) for b in blocks]
     (sems,) = take(1)
     used = 0
@@ -217,8 +217,8 @@
                 total = total + prior_held[i][...]
             elif block.prior:
                 total = total + priors[i][...]
-            if block.out.startswith("kept"):
-                out_held[i][...] = scale * total if block.out == "kept scaled" else total
+            if block.out == "kept":
+                out_held[i][...] = total
                 leaving.append(move(out_held[i], outs[i][0]))
             elif block.out == "split":
                 cut = outs[i][0].shape[0]
@@ -227,6 +227,8 @@
                 leaving.append(move(out_held[i], outs[i][1]))
             elif block.out == "total":
                 outs[i][0][...] = total
+            elif block.out == "scaled":
+                outs[i][0][...] = scale * total
             elif block.out:
                 outs[i][0][...] = (scale * total).astype(jnp.bfloat16)
 
@@ -320,7 +322,7 @@
             get((count - shape.cut, width), jnp.float32, True)
         elif shape.out:
             kind = jnp.bfloat16 if shape.out == "rounded" else jnp.float32
-            get((count, width), kind, shape.out.startswith("kept"))
+            get((count, width), kind, shape.out == "kept")
     for shape, count in zip(shapes, counts):
         if shape.coef:
             get((count, 2 * rows), jnp.bfloat16, True)
@@ -333,7 +335,7 @@
     scratch += [pltpu.VMEM((n, width), jnp.bfloat16) for n in counts]
     scratch += [pltpu.VMEM((n, width), jnp.float32) for n, b in zip(counts, shapes) if b.prior == "kept"]
     for n, b in zip(counts, shapes):
-        if b.out in ("kept", "kept scaled", "split"):
+        if b.out in ("kept", "split"):
             scratch.append(pltpu.VMEM((n - b.cut, width), jnp.float32))
     scratch += [pltpu.VMEM((n, 2 * rows), jnp.bfloat16) for n, b in zip(counts, shapes) if b.coef]
     scratch.append(pltpu.SemaphoreType.DMA((len(operands) + len(outs),)))
@@ -488,33 +490,28 @@
     )(in_hbm(total.array) if away else in_vmem(total), in_vmem(arrived))
 
 
-def finish_spectra_body(mine_s, away, inside, *rest):
-    others, (out, near, inside_near, sem) = rest[:-4], rest[-4:]
-    copy = pltpu.make_async_copy(away, near, sem)
-    copy.start()
+def finish_spectra_body(mine_s, inside, *rest):
+    others, (out, near) = rest[:-2], rest[-2:]
     at = 0
     for other in others:
         where = pl.ds(at, other.shape[0])
         out[where] = (mine_s[where] + other[...].astype(jnp.float32)).astype(jnp.bfloat16)
         at += other.shape[0]
-    inside_near[...] = inside[...]
-    copy.wait()
-
-
-def finish_spectra(mine_s, others, away, inside):
+    near[...] = inside[...]
+
+
+def finish_spectra(mine_s, others, inside):
     return pl.pallas_call(
         finish_spectra_body,
         out_shape=[
             jax.ShapeDtypeStruct(mine_s.shape, jnp.bfloat16),
-            vmem_out(away.shape, away.dtype),
             vmem_out(inside.shape, inside.dtype),
         ],
-        in_specs=[VMEM_SPEC, HBM_SPEC] + [VMEM_SPEC] * (1 + len(others)),
-        out_specs=[VMEM_SPEC] * 3,
-        scratch_shapes=[pltpu.SemaphoreType.DMA],
+        in_specs=[VMEM_SPEC] * (2 + len(others)),
+        out_specs=[VMEM_SPEC] * 2,
         cost_estimate=SMALL_COST,
         compiler_params=params(),
-    )(in_vmem(mine_s), in_hbm(away), *[in_vmem(a) for a in [inside] + others])
+    )(*[in_vmem(a) for a in [mine_s, inside] + others])
 
 
 def finish_structures_body(flag, here_total, across_back, inside_a, inside_b, out):
@@ -669,14 +666,7 @@
     total_a = add_rounded(side_total_a, back_a)
     inside_a = permute(total_a, sides)
     across_back = permute(after(across_out, total_a), middle)
-    (here_total,) = pair_work(
-        consts,
-        [(Block(here_at, ("ends",), "kept scaled", prior="kept"), Away(after(glycans, total_a)), here_g)],
-        rows,
-        wanted=~outer,
-        ends=ends,
-    )
-    back_b, last_b = lax.optimization_barrier((back_b, last_b, here_total))[:2]
+    back_b, last_b = lax.optimization_barrier((back_b, last_b, total_a))[:2]
     total_b = add_rounded(Away(side_total_b), back_b)
     inside_b = permute(total_b, sides)
 
@@ -694,7 +684,16 @@
         (last_a, last_b),
     )
     others = [swap_inner(x) for x in split(other_s, (piece, piece, rows - 2 * piece))]
-    grad_spectra, here_total, inside_a = finish_spectra(mine_s, others, here_total, inside_a)
+    late, inside_a = lax.optimization_barrier((glycans, inside_a, mine_s))[:2]
+    (here_total,) = pair_work(
+        consts,
+        [(Block(here_at, ("ends",), "scaled", prior="kept"), Away(late), here_g)],
+        rows,
+        wanted=~outer,
+        ends=ends,
+    )
+    others[0] = after(others[0], here_total)
+    grad_spectra, inside_a = finish_spectra(mine_s, others, inside_a)
     across_back = after(across_back, grad_spectra)
     return grad_spectra, finish_structures(outer, here_total, across_back, inside_a, inside_b)
 

time: 71.4 us -> 72.1 us (level)
  Pallas kernels: 20.6 us -> 23 us
  starting transfers between devices: 32.9 us -> 31.1 us
    ppermute x13, starting transfers between devices: 31.2 us -> 29.4 us  [permute(): return lax.ppermute(block, ('blk', 'inner'), pairs)]
    pallas_call x2, Pallas kernels: 1.4 us -> 2.84 us  [add_rounded(): pl.pallas_call(add_body, out_shape=vmem_out(arrived.shape, jnp.bfloat16),...]
    pallas_call x1, Pallas kernels: 0.9 us -> 1.88 us  [finish_structures(): pl.pallas_call(finish_structures_body, out_shape=jax.ShapeDtypeStruct(her...]
  transfers between devices with their start and end apart: 20 -> 20, of which waited for: 3 -> 4; matrix products, arithmetic and copies ran while one was open for 5% -> 5% of each run, Pallas kernels for 28% -> 29%
where the time goes in v13:
time: 72.1 us; the launch traced here: 71.5 us
  starting transfers between devices  31.1 us (43%)
  Pallas kernels  23 us (32%)
  waiting for transfers between devices  9.74 us (14%)
  other arithmetic  2.98 us (4%)
  local copies, waits for them, and re-layouts  2.45 us (3%)
  between operations  2.28 us (3%)
    ppermute x13, starting transfers between devices, permute(): return lax.ppermute(block, ('blk', 'inner'), pairs)  29.4 us
    pallas_call x8, Pallas kernels, pair_work(): pl.pallas_call(functools.partial(pair_body, plan), out_shape=outs, in_spe...  10.3 us
    ppermute x13, waiting for transfers between devices, permute(): return lax.ppermute(block, ('blk', 'inner'), pairs)  8.31 us
    pallas_call x1, Pallas kernels, spectra_work(): pl.pallas_call(functools.partial(spectra_body, plan), out_shape=[vmem_out...  5.83 us
    pallas_call x2, Pallas kernels, add_rounded(): pl.pallas_call(add_body, out_shape=vmem_out(arrived.shape, jnp.bfloat16),...  2.84 us
    concatenate x1, other arithmetic, along_line(): end_mine = permute(jnp.concatenate([spectra, coded]), inward)  2 us
    pallas_call x1, Pallas kernels, finish_spectra(): pl.pallas_call(finish_spectra_body, out_shape=[jax.ShapeDtypeStruct(mine_...  1.96 us
    pallas_call x1, Pallas kernels, finish_structures(): pl.pallas_call(finish_structures_body, out_shape=jax.ShapeDtypeStruct(her...  1.88 us
  transfers between devices with their start and end apart: 20, of which 4 were waited for; matrix products, arithmetic and copies ran while one was open for 5% of the time, Pallas kernels for 29%

profile of v13, /device:TPU:0, one launch (start us, length us, event | category | flops | bytes accessed | tf_op | source)
XLA Modules:
  0.0 71.5 jit_solution(18091457241672786631)
XLA Ops:
  0.6 0.5 collective-permute-start.3
  1.1 4.1 %collective-permute-start.2 = (bf16[320,1024]{1,0:T(8,128)(2,1)}, bf16[320,1024]{1,0:T(8,128)(2,1)S(1)}, u32[]{:S(2)}, u32[]{:S(2)}) collective-permute-start(bf16[320,1024]{1,0:T(8,128)(2,1)} %refs_5_), channel_id=1, source_target_pairs={{0,4},{4,0},{8,12},{12,8},{1,5},{5,1},{9,13},{13,9},{2,6},{6,2},{1... | collective-permute-start | bytes 1966088 | tf_op jit(solution)/shard_map/ppermute | solution.py:550
  5.3 0.7 concatenate.19
  6.0 0.5 collective-permute-start.1
  6.5 0.7 fusion.28
  7.2 0.1 fusion.14
  7.3 2.0 %pad_maximum_fusion = bf16[336,1024]{1,0:T(8,128)(2,1)} fusion(bf16[16,1024]{1,0:T(8,128)(2,1)S(1)} %fusion.14, bf16[320,1024]{1,0:T(8,128)(2,1)} %s_mine.1), kind=kLoop, calls=%fused_computation | loop fusion | flops 1376256 | bytes 1376256 | tf_op jit(solution)/shard_map/concatenate | solution.py:591
  9.3 1.9 %collective-permute-start.4 = (bf16[336,1024]{1,0:T(8,128)(2,1)}, bf16[336,1024]{1,0:T(8,128)(2,1)S(1)}, u32[]{:S(2)}, u32[]{:S(2)}) collective-permute-start(bf16[336,1024]{1,0:T(8,128)(2,1)} %pad_maximum_fusion), channel_id=1, source_target_pairs={{0,4},{12,8},{1,5},{13,9},{2,6},{14,10},{3,7},{15,11},{16,20},{28,... | collective-permute-start | bytes 2064392 | tf_op jit(solution)/shard_map/ppermute | solution.py:550
  12.8 0.8 %copy-done.3 = bf16[320,1024]{1,0:T(8,128)(2,1)} copy-done((bf16[320,1024]{1,0:T(8,128)(2,1)}, bf16[320,1024]{1,0:T(8,128)(2,1)S(1)}, u32[]{:S(2)}) %copy-start.3) | copy-done | bytes 655384
  13.7 4.3 %shard_map.68 = (f32[320,1024]{1,0:T(8,128)}, bf16[320,640]{1,0:T(8,128)(2,1)}) custom-call(f32[8,128]{1,0:T(8,128)S(1)} %select_select_fusion.refs_0_.refs_1_.consts, f32[1,640]{1,0:T(1,128)S(1)} %add_convert_fusion.refs_1_.refs_2_.labels, bf16[320,1024]{1,0:T(8,128)(2,1)} %s_mine.1, bf16[320,1024]{1,0:T(8,128)(2,1)} %copy-done.3, bf16[320,1024]{1,0:T(8,128)(2,1)} %refs_5_), custom_call_target="tpu_custom_call" | custom-call | flops 1024 | bytes 1024 | tf_op jit(solution)/shard_map/pallas_call | solution.py:342
  18.0 1.3 %collective-permute-start.10 = (bf16[320,1024]{1,0:T(8,128)(2,1)}, bf16[320,1024]{1,0:T(8,128)(2,1)}, u32[]{:S(2)}, u32[]{:S(2)}) collective-permute-start(bf16[320,1024]{1,0:T(8,128)(2,1)} %collective-permute-done.3.refs_5_.across), channel_id=1, source_target_pairs={{4,0},{8,12},{5,1},{9,13},{6,2},{10,14},{7,3},{11,15},{20,16},{24,... | collective-permute-start | bytes 1966088 | tf_op jit(solution)/shard_map/ppermute | solution.py:550
  19.3 1.5 %collective-permute-done.2.refs_4_.whole.refs_5_.side = bf16[320,1024]{1,0:T(8,128)(2,1)S(1)} collective-permute-done((bf16[320,1024]{1,0:T(8,128)(2,1)}, bf16[320,1024]{1,0:T(8,128)(2,1)S(1)}, u32[]{:S(2)}, u32[]{:S(2)}) %collective-permute-start.2) | collective-permute-done | bytes 655392 | tf_op jit(solution)/shard_map/ppermute | solution.py:550
  20.9 0.5 collective-permute-start.9
  21.4 0.2 copy-done
  21.6 5.6 %shard_map.69 = (f32[320,1024]{1,0:T(8,128)}, f32[320,1024]{1,0:T(8,128)}, bf16[320,640]{1,0:T(8,128)(2,1)}, bf16[320,640]{1,0:T(8,128)(2,1)}) custom-call(f32[8,128]{1,0:T(8,128)S(1)} %select_select_fusion.refs_0_.refs_1_.consts, f32[1,640]{1,0:T(1,128)S(1)} %add_convert_fusion.refs_1_.refs_2_.labels, bf16[320,1024]{1,0:T(8,128)(2,1)} %s_mine.1, ...), custom_call_target="tpu_custom_call" | custom-call | flops 1024 | bytes 1024 | tf_op jit(solution)/shard_map/pallas_call | solution.py:342
  27.3 6.8 %collective-permute-done.4.whole.refs_2_.refs_5_ = bf16[336,1024]{1,0:T(8,128)(2,1)S(1)} collective-permute-done((bf16[336,1024]{1,0:T(8,128)(2,1)}, bf16[336,1024]{1,0:T(8,128)(2,1)S(1)}, u32[]{:S(2)}, u32[]{:S(2)}) %collective-permute-start.4) | collective-permute-done | bytes 688160 | tf_op jit(solution)/shard_map/ppermute | solution.py:550
  34.2 0.5 collective-permute-start.7
  34.7 2.4 %collective-permute-start.8 = (bf16[128,1024]{1,0:T(8,128)(2,1)S(1)}, bf16[128,1024]{1,0:T(8,128)(2,1)S(1)}, u32[]{:S(2)}, u32[]{:S(2)}) collective-permute-start(bf16[128,1024]{1,0:T(8,128)(2,1)S(1)} %collective-permute-done.5.refs_5_.rest_1_), channel_id=1, source_target_pairs={{0,4},{4,0},{8,12},{12,8},{1,5},{5,1},{9,13},{13,9},{2,6},{6,2},{1... | collective-permute-start | bytes 786440 | tf_op jit(solution)/shard_map/ppermute | solution.py:550
  37.3 0.1 shard_map.74
  37.4 0.6 collective-permute-start.11
  37.9 7.4 %collective-permute-start.12 = (bf16[192,1024]{1,0:T(8,128)(2,1)S(1)}, bf16[192,1024]{1,0:T(8,128)(2,1)S(1)}, u32[]{:S(2)}, u32[]{:S(2)}) collective-permute-start(bf16[192,1024]{1,0:T(8,128)(2,1)S(1)} %collective-permute-done.9.refs_8_.rest_2_), channel_id=1, source_target_pairs={{0,4},{4,0},{8,12},{12,8},{1,5},{5,1},{9,13},{13,9},{2,6},{6,2},{1... | collective-permute-start | bytes 1179656 | tf_op jit(solution)/shard_map/ppermute | solution.py:550
  45.5 0.7 copy-done.5
  46.3 0.8 %shard_map.77 = bf16[128,1024]{1,0:T(8,128)(2,1)} custom-call(f32[128,1024]{1,0:T(8,128)S(1)} %get-tuple-element.60.total, bf16[128,1024]{1,0:T(8,128)(2,1)S(1)} %collective-permute-done.13.arrived), custom_call_target="tpu_custom_call" | custom-call | flops 1024 | bytes 1024 | tf_op jit(solution)/shard_map/pallas_call | solution.py:482
  47.0 8.6 %collective-permute-start.14 = (bf16[128,1024]{1,0:T(8,128)(2,1)}, bf16[128,1024]{1,0:T(8,128)(2,1)}, u32[]{:S(2)}, u32[]{:S(2)}) collective-permute-start(bf16[128,1024]{1,0:T(8,128)(2,1)} %shard_map.77), channel_id=1, source_target_pairs={{0,4},{4,0},{8,12},{12,8},{1,5},{5,1},{9,13},{13,9},{2,6},{6,2},{1... | collective-permute-start | bytes 786440 | tf_op jit(solution)/shard_map/ppermute | solution.py:550
  55.6 2.1 %shard_map.78 = bf16[192,1024]{1,0:T(8,128)(2,1)} custom-call(f32[192,1024]{1,0:T(8,128)} %get-tuple-element.59.total, bf16[192,1024]{1,0:T(8,128)(2,1)S(1)} %collective-permute-done.11.arrived), custom_call_target="tpu_custom_call" | custom-call | flops 1024 | bytes 1024 | tf_op jit(solution)/shard_map/pallas_call | solution.py:482
  57.7 1.9 %collective-permute-start.19 = (bf16[192,1024]{1,0:T(8,128)(2,1)}, bf16[192,1024]{1,0:T(8,128)(2,1)}, u32[]{:S(2)}, u32[]{:S(2)}) collective-permute-start(bf16[192,1024]{1,0:T(8,128)(2,1)} %shard_map.78), channel_id=1, source_target_pairs={{0,4},{4,0},{8,12},{12,8},{1,5},{5,1},{9,13},{13,9},{2,6},{6,2},{1... | collective-permute-start | bytes 1179656 | tf_op jit(solution)/shard_map/ppermute | solution.py:550
  59.6 5.8 %shard_map.79 = (f32[320,1024]{1,0:T(8,128)S(1)}, bf16[320,1024]{1,0:T(8,128)(2,1)S(1)}) custom-call(s32[1]{0:T(128)} %bitcast.outer.flag, f32[8,128]{1,0:T(8,128)S(1)} %select_select_fusion.refs_0_.refs_1_.consts, f32[1,640]{1,0:T(1,128)S(1)} %add_convert_fusion.refs_1_.refs_2_.labels, bf16[320,1024]{1,0:T(8,128)(2,1)} %s_mine.1, ...), custom_call_target="tpu_custom_call" | custom-call | flops 1024 | bytes 1024 | tf_op jit(solution)/shard_map/pallas_call | solution.py:430
  65.6 0.5 collective-permute-start.16
  66.3 0.8 %collective-permute-done.15.rest_0_ = bf16[112,1024]{1,0:T(8,128)(2,1)S(1)} collective-permute-done((bf16[112,1024]{1,0:T(8,128)(2,1)S(1)}, bf16[112,1024]{1,0:T(8,128)(2,1)S(1)}, u32[]{:S(2)}, u32[]{:S(2)}) %collective-permute-start.15) | collective-permute-done | bytes 229408 | tf_op jit(solution)/shard_map/ppermute | solution.py:21
  67.1 0.6 collective-permute-done.17.rest_2_
  67.7 2.0 %shard_map.82 = (bf16[320,1024]{1,0:T(8,128)(2,1)}, bf16[128,1024]{1,0:T(8,128)(2,1)S(1)}) custom-call(f32[320,1024]{1,0:T(8,128)S(1)} %get-tuple-element.66.mine_s, bf16[128,1024]{1,0:T(8,128)(2,1)} %collective-permute-done.14.inside, bf16[112,1024]{1,0:T(8,128)(2,1)S(1)} %collective-permute-done.15.rest_0_, ...), custom_call_target="tpu_custom_call" | custom-call | flops 1024 | bytes 1024 | tf_op jit(solution)/shard_map/pallas_call | solution.py:504
  69.7 1.9 %shard_map.83 = bf16[320,1024]{1,0:T(8,128)(2,1)} custom-call(s32[1]{0:T(128)} %bitcast.outer.flag, f32[320,1024]{1,0:T(8,128)S(1)} %shard_map.81.here_total, bf16[320,1024]{1,0:T(8,128)(2,1)S(1)} %collective-permute-done.18.across_back, bf16[128,1024]{1,0:T(8,128)(2,1)S(1)} %get-tuple-element.77.inside_a, bf16[192,1024]{1,0:T(8,128)(2,1)} %collective-permute-done.19.inside_b), custom_call_target="tpu_custom_call" | custom-call | flops 1024 | bytes 1024 | tf_op jit(solution)/shard_map/pallas_call | solution.py:531
  (50 shorter events, 1.1 us)
Async XLA Ops:
  0.6 17.3 %collective-permute-start.3 = (bf16[320,1024]{1,0:T(8,128)(2,1)}, bf16[320,1024]{1,0:T(8,128)(2,1)}, u32[]{:S(2)}, u32[]{:S(2)}) collective-permute-start(bf16[320,1024]{1,0:T(8,128)(2,1)} %refs_5_), channel_id=1, source_target_pairs={{4,8},{8,4},{0,1},{12,13},{5,9},{9,5},{1,0},{13,12},{6,10},{10,6},... | collective-permute-start | bytes 1966088 | tf_op jit(solution)/shard_map/ppermute | solution.py:550
  1.1 19.6 %collective-permute-start.2 = (bf16[320,1024]{1,0:T(8,128)(2,1)}, bf16[320,1024]{1,0:T(8,128)(2,1)S(1)}, u32[]{:S(2)}, u32[]{:S(2)}) collective-permute-start(bf16[320,1024]{1,0:T(8,128)(2,1)} %refs_5_), channel_id=1, source_target_pairs={{0,4},{4,0},{8,12},{12,8},{1,5},{5,1},{9,13},{13,9},{2,6},{6,2},{1... | collective-permute-start | bytes 1966088 | tf_op jit(solution)/shard_map/ppermute | solution.py:550
  6.0 6.8 %collective-permute-start = (s32[1,320]{1,0:T(1,128)S(1)}, s32[1,320]{1,0:T(1,128)S(1)}, u32[]{:S(2)}, u32[]{:S(2)}) collective-permute-start(s32[1,320]{1,0:T(1,128)S(1)} %concatenate.19), channel_id=1, source_target_pairs={{1,0},{0,1},{3,2},{2,3},{5,4},{4,5},{7,6},{6,7},{9,8},{8,9},{11,10... | collective-permute-start | bytes 3848 | tf_op jit(solution)/shard_map/ppermute | solution.py:21
  6.0 6.9 %collective-permute-start.1 = (bf16[320,1024]{1,0:T(8,128)(2,1)}, bf16[320,1024]{1,0:T(8,128)(2,1)S(1)}, u32[]{:S(2)}, u32[]{:S(2)}) collective-permute-start(bf16[320,1024]{1,0:T(8,128)(2,1)} %s_mine.1), channel_id=1, source_target_pairs={{1,0},{0,1},{3,2},{2,3},{5,4},{4,5},{7,6},{6,7},{9,8},{8,9},{11,10... | collective-permute-start | bytes 1966088 | tf_op jit(solution)/shard_map/ppermute | solution.py:21
  9.3 24.7 %collective-permute-start.4 = (bf16[336,1024]{1,0:T(8,128)(2,1)}, bf16[336,1024]{1,0:T(8,128)(2,1)S(1)}, u32[]{:S(2)}, u32[]{:S(2)}) collective-permute-start(bf16[336,1024]{1,0:T(8,128)(2,1)} %pad_maximum_fusion), channel_id=1, source_target_pairs={{0,4},{12,8},{1,5},{13,9},{2,6},{14,10},{3,7},{15,11},{16,20},{28,... | collective-permute-start | bytes 2064392 | tf_op jit(solution)/shard_map/ppermute | solution.py:550
  12.8 0.8 %copy-start.3 = (bf16[320,1024]{1,0:T(8,128)(2,1)}, bf16[320,1024]{1,0:T(8,128)(2,1)S(1)}, u32[]{:S(2)}) copy-start(bf16[320,1024]{1,0:T(8,128)(2,1)S(1)} %collective-permute-done.1.refs_3_.refs_4_.s_other) | copy-start | bytes 1966084
  18.0 19.1 %collective-permute-start.10 = (bf16[320,1024]{1,0:T(8,128)(2,1)}, bf16[320,1024]{1,0:T(8,128)(2,1)}, u32[]{:S(2)}, u32[]{:S(2)}) collective-permute-start(bf16[320,1024]{1,0:T(8,128)(2,1)} %collective-permute-done.3.refs_5_.across), channel_id=1, source_target_pairs={{4,0},{8,12},{5,1},{9,13},{6,2},{10,14},{7,3},{11,15},{20,16},{24,... | collective-permute-start | bytes 1966088 | tf_op jit(solution)/shard_map/ppermute | solution.py:550
  20.8 0.8 %copy-start = (bf16[320,1024]{1,0:T(8,128)(2,1)}, bf16[320,1024]{1,0:T(8,128)(2,1)S(1)}, u32[]{:S(2)}) copy-start(bf16[320,1024]{1,0:T(8,128)(2,1)S(1)} %collective-permute-done.2.refs_4_.whole.refs_5_.side) | copy-start | bytes 1966084
  20.8 6.4 %collective-permute-start.5 = (bf16[128,1024]{1,0:T(8,128)(2,1)S(1)}, bf16[128,1024]{1,0:T(8,128)(2,1)S(1)}, u32[]{:S(2)}, u32[]{:S(2)}) collective-permute-start(bf16[128,1024]{1,0:T(8,128)(2,1)S(1)} %get-tuple-element.46), channel_id=1, source_target_pairs={{4,8},{8,4},{0,1},{12,13},{5,9},{9,5},{1,0},{13,12},{6,10},{10,6},... | collective-permute-start | bytes 786440 | tf_op jit(solution)/shard_map/ppermute | solution.py:550
  20.9 16.2 %collective-permute-start.9 = (bf16[192,1024]{1,0:T(8,128)(2,1)S(1)}, bf16[192,1024]{1,0:T(8,128)(2,1)S(1)}, u32[]{:S(2)}, u32[]{:S(2)}) collective-permute-start(bf16[192,1024]{1,0:T(8,128)(2,1)S(1)} %get-tuple-element.52), channel_id=1, source_target_pairs={{4,8},{8,4},{0,1},{12,13},{5,9},{9,5},{1,0},{13,12},{6,10},{10,6},... | collective-permute-start | bytes 1179656 | tf_op jit(solution)/shard_map/ppermute | solution.py:550
  27.2 9.9 %copy-start.1 = (bf16[128,1024]{1,0:T(8,128)(2,1)}, bf16[128,1024]{1,0:T(8,128)(2,1)S(1)}, u32[]{:S(2)}) copy-start(bf16[128,1024]{1,0:T(8,128)(2,1)S(1)} %collective-permute-done.5.refs_5_.rest_1_) | copy-start | bytes 786436
  34.1 3.0 %collective-permute-start.6 = (bf16[176,1024]{1,0:T(8,128)(2,1)S(1)}, bf16[176,1024]{1,0:T(8,128)(2,1)S(1)}, u32[]{:S(2)}, u32[]{:S(2)}) collective-permute-start(bf16[176,1024]{1,0:T(8,128)(2,1)S(1)} %get-tuple-element.50), channel_id=1, source_target_pairs={{1,0},{0,1},{3,2},{2,3},{5,4},{4,5},{7,6},{6,7},{9,8},{8,9},{11,10... | collective-permute-start | bytes 1081352 | tf_op jit(solution)/shard_map/ppermute | solution.py:21
  34.2 2.9 %collective-permute-start.7 = (bf16[160,1024]{1,0:T(8,128)(2,1)S(1)}, bf16[160,1024]{1,0:T(8,128)(2,1)S(1)}, u32[]{:S(2)}, u32[]{:S(2)}) collective-permute-start(bf16[160,1024]{1,0:T(8,128)(2,1)S(1)} %get-tuple-element.51), channel_id=1, source_target_pairs={{1,0},{0,1},{3,2},{2,3},{5,4},{4,5},{7,6},{6,7},{9,8},{8,9},{11,10... | collective-permute-start | bytes 983048 | tf_op jit(solution)/shard_map/ppermute | solution.py:21
  34.7 10.8 %collective-permute-start.8 = (bf16[128,1024]{1,0:T(8,128)(2,1)S(1)}, bf16[128,1024]{1,0:T(8,128)(2,1)S(1)}, u32[]{:S(2)}, u32[]{:S(2)}) collective-permute-start(bf16[128,1024]{1,0:T(8,128)(2,1)S(1)} %collective-permute-done.5.refs_5_.rest_1_), channel_id=1, source_target_pairs={{0,4},{4,0},{8,12},{12,8},{1,5},{5,1},{9,13},{13,9},{2,6},{6,2},{1... | collective-permute-start | bytes 786440 | tf_op jit(solution)/shard_map/ppermute | solution.py:550
  37.1 0.9 %copy-start.2 = (bf16[192,1024]{1,0:T(8,128)(2,1)}, bf16[192,1024]{1,0:T(8,128)(2,1)S(1)}, u32[]{:S(2)}) copy-start(bf16[192,1024]{1,0:T(8,128)(2,1)S(1)} %collective-permute-done.9.refs_8_.rest_2_) | copy-start | bytes 1179652
  37.2 9.1 %collective-permute-start.13 = (bf16[128,1024]{1,0:T(8,128)(2,1)S(1)}, bf16[128,1024]{1,0:T(8,128)(2,1)S(1)}, u32[]{:S(2)}, u32[]{:S(2)}) collective-permute-start(bf16[128,1024]{1,0:T(8,128)(2,1)S(1)} %shard_map.73), channel_id=1, source_target_pairs={{4,8},{8,4},{0,1},{12,13},{5,9},{9,5},{1,0},{13,12},{6,10},{10,6},... | collective-permute-start | bytes 786440 | tf_op jit(solution)/shard_map/ppermute | solution.py:550
  37.4 18.2 %collective-permute-start.11 = (bf16[192,1024]{1,0:T(8,128)(2,1)S(1)}, bf16[192,1024]{1,0:T(8,128)(2,1)S(1)}, u32[]{:S(2)}, u32[]{:S(2)}) collective-permute-start(bf16[192,1024]{1,0:T(8,128)(2,1)S(1)} %shard_map.74), channel_id=1, source_target_pairs={{4,8},{8,4},{0,1},{12,13},{5,9},{9,5},{1,0},{13,12},{6,10},{10,6},... | collective-permute-start | bytes 1179656 | tf_op jit(solution)/shard_map/ppermute | solution.py:550
  37.9 17.7 %collective-permute-start.12 = (bf16[192,1024]{1,0:T(8,128)(2,1)S(1)}, bf16[192,1024]{1,0:T(8,128)(2,1)S(1)}, u32[]{:S(2)}, u32[]{:S(2)}) collective-permute-start(bf16[192,1024]{1,0:T(8,128)(2,1)S(1)} %collective-permute-done.9.refs_8_.rest_2_), channel_id=1, source_target_pairs={{0,4},{4,0},{8,12},{12,8},{1,5},{5,1},{9,13},{13,9},{2,6},{6,2},{1... | collective-permute-start | bytes 1179656 | tf_op jit(solution)/shard_map/ppermute | solution.py:550
  45.5 0.7 copy-start.5
  47.0 22.6 %collective-permute-start.18 = (bf16[320,1024]{1,0:T(8,128)(2,1)S(1)}, bf16[320,1024]{1,0:T(8,128)(2,1)S(1)}, u32[]{:S(2)}, u32[]{:S(2)}) collective-permute-start(bf16[320,1024]{1,0:T(8,128)(2,1)S(1)} %shard_map.75), channel_id=1, source_target_pairs={{4,8},{8,4},{0,1},{12,13},{5,9},{9,5},{1,0},{13,12},{6,10},{10,6},... | collective-permute-start | bytes 1966088 | tf_op jit(solution)/shard_map/ppermute | solution.py:550
  47.0 19.1 %collective-permute-start.14 = (bf16[128,1024]{1,0:T(8,128)(2,1)}, bf16[128,1024]{1,0:T(8,128)(2,1)}, u32[]{:S(2)}, u32[]{:S(2)}) collective-permute-start(bf16[128,1024]{1,0:T(8,128)(2,1)} %shard_map.77), channel_id=1, source_target_pairs={{0,4},{4,0},{8,12},{12,8},{1,5},{5,1},{9,13},{13,9},{2,6},{6,2},{1... | collective-permute-start | bytes 786440 | tf_op jit(solution)/shard_map/ppermute | solution.py:550
  55.6 2.1 %copy-start.4 = (bf16[192,1024]{1,0:T(8,128)(2,1)}, bf16[192,1024]{1,0:T(8,128)(2,1)S(1)}, u32[]{:S(2)}) copy-start(bf16[192,1024]{1,0:T(8,128)(2,1)S(1)} %collective-permute-done.12.rest_4_) | copy-start | bytes 1179652
  57.7 11.9 %collective-permute-start.19 = (bf16[192,1024]{1,0:T(8,128)(2,1)}, bf16[192,1024]{1,0:T(8,128)(2,1)}, u32[]{:S(2)}, u32[]{:S(2)}) collective-permute-start(bf16[192,1024]{1,0:T(8,128)(2,1)} %shard_map.78), channel_id=1, source_target_pairs={{0,4},{4,0},{8,12},{12,8},{1,5},{5,1},{9,13},{13,9},{2,6},{6,2},{1... | collective-permute-start | bytes 1179656 | tf_op jit(solution)/shard_map/ppermute | solution.py:550
  65.5 1.6 %collective-permute-start.15 = (bf16[112,1024]{1,0:T(8,128)(2,1)S(1)}, bf16[112,1024]{1,0:T(8,128)(2,1)S(1)}, u32[]{:S(2)}, u32[]{:S(2)}) collective-permute-start(bf16[112,1024]{1,0:T(8,128)(2,1)S(1)} %get-tuple-element.69), channel_id=1, source_target_pairs={{1,0},{0,1},{3,2},{2,3},{5,4},{4,5},{7,6},{6,7},{9,8},{8,9},{11,10... | collective-permute-start | bytes 688136 | tf_op jit(solution)/shard_map/ppermute | solution.py:21
  65.6 2.1 %collective-permute-start.16 = (bf16[112,1024]{1,0:T(8,128)(2,1)S(1)}, bf16[112,1024]{1,0:T(8,128)(2,1)S(1)}, u32[]{:S(2)}, u32[]{:S(2)}) collective-permute-start(bf16[112,1024]{1,0:T(8,128)(2,1)S(1)} %get-tuple-element.72), channel_id=1, source_target_pairs={{1,0},{0,1},{3,2},{2,3},{5,4},{4,5},{7,6},{6,7},{9,8},{8,9},{11,10... | collective-permute-start | bytes 688136 | tf_op jit(solution)/shard_map/ppermute | solution.py:21
  66.1 1.6 %collective-permute-start.17 = (bf16[96,1024]{1,0:T(8,128)(2,1)S(1)}, bf16[96,1024]{1,0:T(8,128)(2,1)S(1)}, u32[]{:S(2)}, u32[]{:S(2)}) collective-permute-start(bf16[96,1024]{1,0:T(8,128)(2,1)S(1)} %get-tuple-element.73), channel_id=1, source_target_pairs={{1,0},{0,1},{3,2},{2,3},{5,4},{4,5},{7,6},{6,7},{9,8},{8,9},{11,10... | collective-permute-start | bytes 589832 | tf_op jit(solution)/shard_map/ppermute | solution.py:21

commit v14 on v13

--- a/solution.py
+++ b/solution.py
@@ -12,7 +12,7 @@
 LINE = 4
 LABEL_ROWS = 16
 FAR_ROW, KEEP_ROW, LAST_ROW = 5, 6, 7
-VMEM_BYTES = 20 * 1024 * 1024
+VMEM_BYTES = 10 * 1024 * 1024
 
 
 def from_behind(block, axis, distance):

time: 72.1 us -> 72.1 us (level)
  no operation moved by 1% of the time
where the time goes in v14:
time: 72.1 us; the launch traced here: 71.5 us
  starting transfers between devices  31.1 us (43%)
  Pallas kernels  23 us (32%)
  waiting for transfers between devices  9.74 us (14%)
  other arithmetic  2.98 us (4%)
  local copies, waits for them, and re-layouts  2.45 us (3%)
  between operations  2.28 us (3%)
    ppermute x13, starting transfers between devices, permute(): return lax.ppermute(block, ('blk', 'inner'), pairs)  29.4 us
    pallas_call x8, Pallas kernels, pair_work(): pl.pallas_call(functools.partial(pair_body, plan), out_shape=outs, in_spe...  10.3 us
    ppermute x13, waiting for transfers between devices, permute(): return lax.ppermute(block, ('blk', 'inner'), pairs)  8.31 us
    pallas_call x1, Pallas kernels, spectra_work(): pl.pallas_call(functools.partial(spectra_body, plan), out_shape=[vmem_out...  5.83 us
    pallas_call x2, Pallas kernels, add_rounded(): pl.pallas_call(add_body, out_shape=vmem_out(arrived.shape, jnp.bfloat16),...  2.84 us
    concatenate x1, other arithmetic, along_line(): end_mine = permute(jnp.concatenate([spectra, coded]), inward)  2 us
    pallas_call x1, Pallas kernels, finish_spectra(): pl.pallas_call(finish_spectra_body, out_shape=[jax.ShapeDtypeStruct(mine_...  1.96 us
    pallas_call x1, Pallas kernels, finish_structures(): pl.pallas_call(finish_structures_body, out_shape=jax.ShapeDtypeStruct(her...  1.88 us
  transfers between devices with their start and end apart: 20, of which 4 were waited for; matrix products, arithmetic and copies ran while one was open for 5% of the time, Pallas kernels for 29%

profile of v14, /device:TPU:0, one launch (start us, length us, event | category | flops | bytes accessed | tf_op | source)
XLA Modules:
  0.0 71.5 jit_solution(9199368395330352291)
XLA Ops:
  0.6 0.5 collective-permute-start.3
  1.1 4.1 %collective-permute-start.2 = (bf16[320,1024]{1,0:T(8,128)(2,1)}, bf16[320,1024]{1,0:T(8,128)(2,1)S(1)}, u32[]{:S(2)}, u32[]{:S(2)}) collective-permute-start(bf16[320,1024]{1,0:T(8,128)(2,1)} %refs_5_), channel_id=1, source_target_pairs={{0,4},{4,0},{8,12},{12,8},{1,5},{5,1},{9,13},{13,9},{2,6},{6,2},{1... | collective-permute-start | bytes 1966088 | tf_op jit(solution)/shard_map/ppermute | solution.py:550
  5.3 0.7 concatenate.19
  6.0 0.5 collective-permute-start.1
  6.5 0.7 fusion.28
  7.2 0.1 fusion.14
  7.3 2.0 %pad_maximum_fusion = bf16[336,1024]{1,0:T(8,128)(2,1)} fusion(bf16[16,1024]{1,0:T(8,128)(2,1)S(1)} %fusion.14, bf16[320,1024]{1,0:T(8,128)(2,1)} %s_mine.1), kind=kLoop, calls=%fused_computation | loop fusion | flops 1376256 | bytes 1376256 | tf_op jit(solution)/shard_map/concatenate | solution.py:591
  9.3 1.9 %collective-permute-start.4 = (bf16[336,1024]{1,0:T(8,128)(2,1)}, bf16[336,1024]{1,0:T(8,128)(2,1)S(1)}, u32[]{:S(2)}, u32[]{:S(2)}) collective-permute-start(bf16[336,1024]{1,0:T(8,128)(2,1)} %pad_maximum_fusion), channel_id=1, source_target_pairs={{0,4},{12,8},{1,5},{13,9},{2,6},{14,10},{3,7},{15,11},{16,20},{28,... | collective-permute-start | bytes 2064392 | tf_op jit(solution)/shard_map/ppermute | solution.py:550
  12.8 0.8 %copy-done.3 = bf16[320,1024]{1,0:T(8,128)(2,1)} copy-done((bf16[320,1024]{1,0:T(8,128)(2,1)}, bf16[320,1024]{1,0:T(8,128)(2,1)S(1)}, u32[]{:S(2)}) %copy-start.3) | copy-done | bytes 655384
  13.7 4.3 %shard_map.68 = (f32[320,1024]{1,0:T(8,128)}, bf16[320,640]{1,0:T(8,128)(2,1)}) custom-call(f32[8,128]{1,0:T(8,128)S(1)} %select_select_fusion.refs_0_.refs_1_.consts, f32[1,640]{1,0:T(1,128)S(1)} %add_convert_fusion.refs_1_.refs_2_.labels, bf16[320,1024]{1,0:T(8,128)(2,1)} %s_mine.1, bf16[320,1024]{1,0:T(8,128)(2,1)} %copy-done.3, bf16[320,1024]{1,0:T(8,128)(2,1)} %refs_5_), custom_call_target="tpu_custom_call" | custom-call | flops 1024 | bytes 1024 | tf_op jit(solution)/shard_map/pallas_call | solution.py:342
  18.0 1.3 %collective-permute-start.10 = (bf16[320,1024]{1,0:T(8,128)(2,1)}, bf16[320,1024]{1,0:T(8,128)(2,1)}, u32[]{:S(2)}, u32[]{:S(2)}) collective-permute-start(bf16[320,1024]{1,0:T(8,128)(2,1)} %collective-permute-done.3.refs_5_.across), channel_id=1, source_target_pairs={{4,0},{8,12},{5,1},{9,13},{6,2},{10,14},{7,3},{11,15},{20,16},{24,... | collective-permute-start | bytes 1966088 | tf_op jit(solution)/shard_map/ppermute | solution.py:550
  19.3 1.5 %collective-permute-done.2.refs_4_.whole.refs_5_.side = bf16[320,1024]{1,0:T(8,128)(2,1)S(1)} collective-permute-done((bf16[320,1024]{1,0:T(8,128)(2,1)}, bf16[320,1024]{1,0:T(8,128)(2,1)S(1)}, u32[]{:S(2)}, u32[]{:S(2)}) %collective-permute-start.2) | collective-permute-done | bytes 655392 | tf_op jit(solution)/shard_map/ppermute | solution.py:550
  20.9 0.5 collective-permute-start.9
  21.4 0.2 copy-done
  21.6 5.6 %shard_map.69 = (f32[320,1024]{1,0:T(8,128)}, f32[320,1024]{1,0:T(8,128)}, bf16[320,640]{1,0:T(8,128)(2,1)}, bf16[320,640]{1,0:T(8,128)(2,1)}) custom-call(f32[8,128]{1,0:T(8,128)S(1)} %select_select_fusion.refs_0_.refs_1_.consts, f32[1,640]{1,0:T(1,128)S(1)} %add_convert_fusion.refs_1_.refs_2_.labels, bf16[320,1024]{1,0:T(8,128)(2,1)} %s_mine.1, ...), custom_call_target="tpu_custom_call" | custom-call | flops 1024 | bytes 1024 | tf_op jit(solution)/shard_map/pallas_call | solution.py:342
  27.3 6.8 %collective-permute-done.4.whole.refs_2_.refs_5_ = bf16[336,1024]{1,0:T(8,128)(2,1)S(1)} collective-permute-done((bf16[336,1024]{1,0:T(8,128)(2,1)}, bf16[336,1024]{1,0:T(8,128)(2,1)S(1)}, u32[]{:S(2)}, u32[]{:S(2)}) %collective-permute-start.4) | collective-permute-done | bytes 688160 | tf_op jit(solution)/shard_map/ppermute | solution.py:550
  34.2 0.5 collective-permute-start.7
  34.7 2.4 %collective-permute-start.8 = (bf16[128,1024]{1,0:T(8,128)(2,1)S(1)}, bf16[128,1024]{1,0:T(8,128)(2,1)S(1)}, u32[]{:S(2)}, u32[]{:S(2)}) collective-permute-start(bf16[128,1024]{1,0:T(8,128)(2,1)S(1)} %collective-permute-done.5.refs_5_.rest_1_), channel_id=1, source_target_pairs={{0,4},{4,0},{8,12},{12,8},{1,5},{5,1},{9,13},{13,9},{2,6},{6,2},{1... | collective-permute-start | bytes 786440 | tf_op jit(solution)/shard_map/ppermute | solution.py:550
  37.3 0.1 shard_map.74
  37.4 0.6 collective-permute-start.11
  37.9 7.4 %collective-permute-start.12 = (bf16[192,1024]{1,0:T(8,128)(2,1)S(1)}, bf16[192,1024]{1,0:T(8,128)(2,1)S(1)}, u32[]{:S(2)}, u32[]{:S(2)}) collective-permute-start(bf16[192,1024]{1,0:T(8,128)(2,1)S(1)} %collective-permute-done.9.refs_8_.rest_2_), channel_id=1, source_target_pairs={{0,4},{4,0},{8,12},{12,8},{1,5},{5,1},{9,13},{13,9},{2,6},{6,2},{1... | collective-permute-start | bytes 1179656 | tf_op jit(solution)/shard_map/ppermute | solution.py:550
  45.5 0.7 copy-done.5
  46.3 0.8 %shard_map.77 = bf16[128,1024]{1,0:T(8,128)(2,1)} custom-call(f32[128,1024]{1,0:T(8,128)S(1)} %get-tuple-element.60.total, bf16[128,1024]{1,0:T(8,128)(2,1)S(1)} %collective-permute-done.13.arrived), custom_call_target="tpu_custom_call" | custom-call | flops 1024 | bytes 1024 | tf_op jit(solution)/shard_map/pallas_call | solution.py:482
  47.0 8.6 %collective-permute-start.14 = (bf16[128,1024]{1,0:T(8,128)(2,1)}, bf16[128,1024]{1,0:T(8,128)(2,1)}, u32[]{:S(2)}, u32[]{:S(2)}) collective-permute-start(bf16[128,1024]{1,0:T(8,128)(2,1)} %shard_map.77), channel_id=1, source_target_pairs={{0,4},{4,0},{8,12},{12,8},{1,5},{5,1},{9,13},{13,9},{2,6},{6,2},{1... | collective-permute-start | bytes 786440 | tf_op jit(solution)/shard_map/ppermute | solution.py:550
  55.6 2.1 %shard_map.78 = bf16[192,1024]{1,0:T(8,128)(2,1)} custom-call(f32[192,1024]{1,0:T(8,128)} %get-tuple-element.59.total, bf16[192,1024]{1,0:T(8,128)(2,1)S(1)} %collective-permute-done.11.arrived), custom_call_target="tpu_custom_call" | custom-call | flops 1024 | bytes 1024 | tf_op jit(solution)/shard_map/pallas_call | solution.py:482
  57.7 1.9 %collective-permute-start.19 = (bf16[192,1024]{1,0:T(8,128)(2,1)}, bf16[192,1024]{1,0:T(8,128)(2,1)}, u32[]{:S(2)}, u32[]{:S(2)}) collective-permute-start(bf16[192,1024]{1,0:T(8,128)(2,1)} %shard_map.78), channel_id=1, source_target_pairs={{0,4},{4,0},{8,12},{12,8},{1,5},{5,1},{9,13},{13,9},{2,6},{6,2},{1... | collective-permute-start | bytes 1179656 | tf_op jit(solution)/shard_map/ppermute | solution.py:550
  59.6 5.8 %shard_map.79 = (f32[320,1024]{1,0:T(8,128)S(1)}, bf16[320,1024]{1,0:T(8,128)(2,1)S(1)}) custom-call(s32[1]{0:T(128)} %bitcast.outer.flag, f32[8,128]{1,0:T(8,128)S(1)} %select_select_fusion.refs_0_.refs_1_.consts, f32[1,640]{1,0:T(1,128)S(1)} %add_convert_fusion.refs_1_.refs_2_.labels, bf16[320,1024]{1,0:T(8,128)(2,1)} %s_mine.1, ...), custom_call_target="tpu_custom_call" | custom-call | flops 1024 | bytes 1024 | tf_op jit(solution)/shard_map/pallas_call | solution.py:430
  65.6 0.5 collective-permute-start.16
  66.3 0.8 %collective-permute-done.15.rest_0_ = bf16[112,1024]{1,0:T(8,128)(2,1)S(1)} collective-permute-done((bf16[112,1024]{1,0:T(8,128)(2,1)S(1)}, bf16[112,1024]{1,0:T(8,128)(2,1)S(1)}, u32[]{:S(2)}, u32[]{:S(2)}) %collective-permute-start.15) | collective-permute-done | bytes 229408 | tf_op jit(solution)/shard_map/ppermute | solution.py:21
  67.1 0.6 collective-permute-done.17.rest_2_
  67.7 2.0 %shard_map.82 = (bf16[320,1024]{1,0:T(8,128)(2,1)}, bf16[128,1024]{1,0:T(8,128)(2,1)S(1)}) custom-call(f32[320,1024]{1,0:T(8,128)S(1)} %get-tuple-element.66.mine_s, bf16[128,1024]{1,0:T(8,128)(2,1)} %collective-permute-done.14.inside, bf16[112,1024]{1,0:T(8,128)(2,1)S(1)} %collective-permute-done.15.rest_0_, ...), custom_call_target="tpu_custom_call" | custom-call | flops 1024 | bytes 1024 | tf_op jit(solution)/shard_map/pallas_call | solution.py:504
  69.7 1.9 %shard_map.83 = bf16[320,1024]{1,0:T(8,128)(2,1)} custom-call(s32[1]{0:T(128)} %bitcast.outer.flag, f32[320,1024]{1,0:T(8,128)S(1)} %shard_map.81.here_total, bf16[320,1024]{1,0:T(8,128)(2,1)S(1)} %collective-permute-done.18.across_back, bf16[128,1024]{1,0:T(8,128)(2,1)S(1)} %get-tuple-element.77.inside_a, bf16[192,1024]{1,0:T(8,128)(2,1)} %collective-permute-done.19.inside_b), custom_call_target="tpu_custom_call" | custom-call | flops 1024 | bytes 1024 | tf_op jit(solution)/shard_map/pallas_call | solution.py:531
  (50 shorter events, 1.1 us)
Async XLA Ops:
  0.6 17.3 %collective-permute-start.3 = (bf16[320,1024]{1,0:T(8,128)(2,1)}, bf16[320,1024]{1,0:T(8,128)(2,1)}, u32[]{:S(2)}, u32[]{:S(2)}) collective-permute-start(bf16[320,1024]{1,0:T(8,128)(2,1)} %refs_5_), channel_id=1, source_target_pairs={{4,8},{8,4},{0,1},{12,13},{5,9},{9,5},{1,0},{13,12},{6,10},{10,6},... | collective-permute-start | bytes 1966088 | tf_op jit(solution)/shard_map/ppermute | solution.py:550
  1.1 19.6 %collective-permute-start.2 = (bf16[320,1024]{1,0:T(8,128)(2,1)}, bf16[320,1024]{1,0:T(8,128)(2,1)S(1)}, u32[]{:S(2)}, u32[]{:S(2)}) collective-permute-start(bf16[320,1024]{1,0:T(8,128)(2,1)} %refs_5_), channel_id=1, source_target_pairs={{0,4},{4,0},{8,12},{12,8},{1,5},{5,1},{9,13},{13,9},{2,6},{6,2},{1... | collective-permute-start | bytes 1966088 | tf_op jit(solution)/shard_map/ppermute | solution.py:550
  6.0 6.8 %collective-permute-start = (s32[1,320]{1,0:T(1,128)S(1)}, s32[1,320]{1,0:T(1,128)S(1)}, u32[]{:S(2)}, u32[]{:S(2)}) collective-permute-start(s32[1,320]{1,0:T(1,128)S(1)} %concatenate.19), channel_id=1, source_target_pairs={{1,0},{0,1},{3,2},{2,3},{5,4},{4,5},{7,6},{6,7},{9,8},{8,9},{11,10... | collective-permute-start | bytes 3848 | tf_op jit(solution)/shard_map/ppermute | solution.py:21
  6.0 6.9 %collective-permute-start.1 = (bf16[320,1024]{1,0:T(8,128)(2,1)}, bf16[320,1024]{1,0:T(8,128)(2,1)S(1)}, u32[]{:S(2)}, u32[]{:S(2)}) collective-permute-start(bf16[320,1024]{1,0:T(8,128)(2,1)} %s_mine.1), channel_id=1, source_target_pairs={{1,0},{0,1},{3,2},{2,3},{5,4},{4,5},{7,6},{6,7},{9,8},{8,9},{11,10... | collective-permute-start | bytes 1966088 | tf_op jit(solution)/shard_map/ppermute | solution.py:21
  9.3 24.7 %collective-permute-start.4 = (bf16[336,1024]{1,0:T(8,128)(2,1)}, bf16[336,1024]{1,0:T(8,128)(2,1)S(1)}, u32[]{:S(2)}, u32[]{:S(2)}) collective-permute-start(bf16[336,1024]{1,0:T(8,128)(2,1)} %pad_maximum_fusion), channel_id=1, source_target_pairs={{0,4},{12,8},{1,5},{13,9},{2,6},{14,10},{3,7},{15,11},{16,20},{28,... | collective-permute-start | bytes 2064392 | tf_op jit(solution)/shard_map/ppermute | solution.py:550
  12.8 0.8 %copy-start.3 = (bf16[320,1024]{1,0:T(8,128)(2,1)}, bf16[320,1024]{1,0:T(8,128)(2,1)S(1)}, u32[]{:S(2)}) copy-start(bf16[320,1024]{1,0:T(8,128)(2,1)S(1)} %collective-permute-done.1.refs_3_.refs_4_.s_other) | copy-start | bytes 1966084
  18.0 19.1 %collective-permute-start.10 = (bf16[320,1024]{1,0:T(8,128)(2,1)}, bf16[320,1024]{1,0:T(8,128)(2,1)}, u32[]{:S(2)}, u32[]{:S(2)}) collective-permute-start(bf16[320,1024]{1,0:T(8,128)(2,1)} %collective-permute-done.3.refs_5_.across), channel_id=1, source_target_pairs={{4,0},{8,12},{5,1},{9,13},{6,2},{10,14},{7,3},{11,15},{20,16},{24,... | collective-permute-start | bytes 1966088 | tf_op jit(solution)/shard_map/ppermute | solution.py:550
  20.8 0.8 %copy-start = (bf16[320,1024]{1,0:T(8,128)(2,1)}, bf16[320,1024]{1,0:T(8,128)(2,1)S(1)}, u32[]{:S(2)}) copy-start(bf16[320,1024]{1,0:T(8,128)(2,1)S(1)} %collective-permute-done.2.refs_4_.whole.refs_5_.side) | copy-start | bytes 1966084
  20.8 6.4 %collective-permute-start.5 = (bf16[128,1024]{1,0:T(8,128)(2,1)S(1)}, bf16[128,1024]{1,0:T(8,128)(2,1)S(1)}, u32[]{:S(2)}, u32[]{:S(2)}) collective-permute-start(bf16[128,1024]{1,0:T(8,128)(2,1)S(1)} %get-tuple-element.46), channel_id=1, source_target_pairs={{4,8},{8,4},{0,1},{12,13},{5,9},{9,5},{1,0},{13,12},{6,10},{10,6},... | collective-permute-start | bytes 786440 | tf_op jit(solution)/shard_map/ppermute | solution.py:550
  20.9 16.2 %collective-permute-start.9 = (bf16[192,1024]{1,0:T(8,128)(2,1)S(1)}, bf16[192,1024]{1,0:T(8,128)(2,1)S(1)}, u32[]{:S(2)}, u32[]{:S(2)}) collective-permute-start(bf16[192,1024]{1,0:T(8,128)(2,1)S(1)} %get-tuple-element.52), channel_id=1, source_target_pairs={{4,8},{8,4},{0,1},{12,13},{5,9},{9,5},{1,0},{13,12},{6,10},{10,6},... | collective-permute-start | bytes 1179656 | tf_op jit(solution)/shard_map/ppermute | solution.py:550
  27.2 9.9 %copy-start.1 = (bf16[128,1024]{1,0:T(8,128)(2,1)}, bf16[128,1024]{1,0:T(8,128)(2,1)S(1)}, u32[]{:S(2)}) copy-start(bf16[128,1024]{1,0:T(8,128)(2,1)S(1)} %collective-permute-done.5.refs_5_.rest_1_) | copy-start | bytes 786436
  34.1 3.0 %collective-permute-start.6 = (bf16[176,1024]{1,0:T(8,128)(2,1)S(1)}, bf16[176,1024]{1,0:T(8,128)(2,1)S(1)}, u32[]{:S(2)}, u32[]{:S(2)}) collective-permute-start(bf16[176,1024]{1,0:T(8,128)(2,1)S(1)} %get-tuple-element.50), channel_id=1, source_target_pairs={{1,0},{0,1},{3,2},{2,3},{5,4},{4,5},{7,6},{6,7},{9,8},{8,9},{11,10... | collective-permute-start | bytes 1081352 | tf_op jit(solution)/shard_map/ppermute | solution.py:21
  34.2 2.9 %collective-permute-start.7 = (bf16[160,1024]{1,0:T(8,128)(2,1)S(1)}, bf16[160,1024]{1,0:T(8,128)(2,1)S(1)}, u32[]{:S(2)}, u32[]{:S(2)}) collective-permute-start(bf16[160,1024]{1,0:T(8,128)(2,1)S(1)} %get-tuple-element.51), channel_id=1, source_target_pairs={{1,0},{0,1},{3,2},{2,3},{5,4},{4,5},{7,6},{6,7},{9,8},{8,9},{11,10... | collective-permute-start | bytes 983048 | tf_op jit(solution)/shard_map/ppermute | solution.py:21
  34.7 10.8 %collective-permute-start.8 = (bf16[128,1024]{1,0:T(8,128)(2,1)S(1)}, bf16[128,1024]{1,0:T(8,128)(2,1)S(1)}, u32[]{:S(2)}, u32[]{:S(2)}) collective-permute-start(bf16[128,1024]{1,0:T(8,128)(2,1)S(1)} %collective-permute-done.5.refs_5_.rest_1_), channel_id=1, source_target_pairs={{0,4},{4,0},{8,12},{12,8},{1,5},{5,1},{9,13},{13,9},{2,6},{6,2},{1... | collective-permute-start | bytes 786440 | tf_op jit(solution)/shard_map/ppermute | solution.py:550
  37.1 0.9 %copy-start.2 = (bf16[192,1024]{1,0:T(8,128)(2,1)}, bf16[192,1024]{1,0:T(8,128)(2,1)S(1)}, u32[]{:S(2)}) copy-start(bf16[192,1024]{1,0:T(8,128)(2,1)S(1)} %collective-permute-done.9.refs_8_.rest_2_) | copy-start | bytes 1179652
  37.2 9.1 %collective-permute-start.13 = (bf16[128,1024]{1,0:T(8,128)(2,1)S(1)}, bf16[128,1024]{1,0:T(8,128)(2,1)S(1)}, u32[]{:S(2)}, u32[]{:S(2)}) collective-permute-start(bf16[128,1024]{1,0:T(8,128)(2,1)S(1)} %shard_map.73), channel_id=1, source_target_pairs={{4,8},{8,4},{0,1},{12,13},{5,9},{9,5},{1,0},{13,12},{6,10},{10,6},... | collective-permute-start | bytes 786440 | tf_op jit(solution)/shard_map/ppermute | solution.py:550
  37.4 18.2 %collective-permute-start.11 = (bf16[192,1024]{1,0:T(8,128)(2,1)S(1)}, bf16[192,1024]{1,0:T(8,128)(2,1)S(1)}, u32[]{:S(2)}, u32[]{:S(2)}) collective-permute-start(bf16[192,1024]{1,0:T(8,128)(2,1)S(1)} %shard_map.74), channel_id=1, source_target_pairs={{4,8},{8,4},{0,1},{12,13},{5,9},{9,5},{1,0},{13,12},{6,10},{10,6},... | collective-permute-start | bytes 1179656 | tf_op jit(solution)/shard_map/ppermute | solution.py:550
  37.9 17.7 %collective-permute-start.12 = (bf16[192,1024]{1,0:T(8,128)(2,1)S(1)}, bf16[192,1024]{1,0:T(8,128)(2,1)S(1)}, u32[]{:S(2)}, u32[]{:S(2)}) collective-permute-start(bf16[192,1024]{1,0:T(8,128)(2,1)S(1)} %collective-permute-done.9.refs_8_.rest_2_), channel_id=1, source_target_pairs={{0,4},{4,0},{8,12},{12,8},{1,5},{5,1},{9,13},{13,9},{2,6},{6,2},{1... | collective-permute-start | bytes 1179656 | tf_op jit(solution)/shard_map/ppermute | solution.py:550
  45.5 0.7 copy-start.5
  47.0 22.6 %collective-permute-start.18 = (bf16[320,1024]{1,0:T(8,128)(2,1)S(1)}, bf16[320,1024]{1,0:T(8,128)(2,1)S(1)}, u32[]{:S(2)}, u32[]{:S(2)}) collective-permute-start(bf16[320,1024]{1,0:T(8,128)(2,1)S(1)} %shard_map.75), channel_id=1, source_target_pairs={{4,8},{8,4},{0,1},{12,13},{5,9},{9,5},{1,0},{13,12},{6,10},{10,6},... | collective-permute-start | bytes 1966088 | tf_op jit(solution)/shard_map/ppermute | solution.py:550
  47.0 19.1 %collective-permute-start.14 = (bf16[128,1024]{1,0:T(8,128)(2,1)}, bf16[128,1024]{1,0:T(8,128)(2,1)}, u32[]{:S(2)}, u32[]{:S(2)}) collective-permute-start(bf16[128,1024]{1,0:T(8,128)(2,1)} %shard_map.77), channel_id=1, source_target_pairs={{0,4},{4,0},{8,12},{12,8},{1,5},{5,1},{9,13},{13,9},{2,6},{6,2},{1... | collective-permute-start | bytes 786440 | tf_op jit(solution)/shard_map/ppermute | solution.py:550
  55.6 2.1 %copy-start.4 = (bf16[192,1024]{1,0:T(8,128)(2,1)}, bf16[192,1024]{1,0:T(8,128)(2,1)S(1)}, u32[]{:S(2)}) copy-start(bf16[192,1024]{1,0:T(8,128)(2,1)S(1)} %collective-permute-done.12.rest_4_) | copy-start | bytes 1179652
  57.7 11.9 %collective-permute-start.19 = (bf16[192,1024]{1,0:T(8,128)(2,1)}, bf16[192,1024]{1,0:T(8,128)(2,1)}, u32[]{:S(2)}, u32[]{:S(2)}) collective-permute-start(bf16[192,1024]{1,0:T(8,128)(2,1)} %shard_map.78), channel_id=1, source_target_pairs={{0,4},{4,0},{8,12},{12,8},{1,5},{5,1},{9,13},{13,9},{2,6},{6,2},{1... | collective-permute-start | bytes 1179656 | tf_op jit(solution)/shard_map/ppermute | solution.py:550
  65.5 1.6 %collective-permute-start.15 = (bf16[112,1024]{1,0:T(8,128)(2,1)S(1)}, bf16[112,1024]{1,0:T(8,128)(2,1)S(1)}, u32[]{:S(2)}, u32[]{:S(2)}) collective-permute-start(bf16[112,1024]{1,0:T(8,128)(2,1)S(1)} %get-tuple-element.69), channel_id=1, source_target_pairs={{1,0},{0,1},{3,2},{2,3},{5,4},{4,5},{7,6},{6,7},{9,8},{8,9},{11,10... | collective-permute-start | bytes 688136 | tf_op jit(solution)/shard_map/ppermute | solution.py:21
  65.6 2.1 %collective-permute-start.16 = (bf16[112,1024]{1,0:T(8,128)(2,1)S(1)}, bf16[112,1024]{1,0:T(8,128)(2,1)S(1)}, u32[]{:S(2)}, u32[]{:S(2)}) collective-permute-start(bf16[112,1024]{1,0:T(8,128)(2,1)S(1)} %get-tuple-element.72), channel_id=1, source_target_pairs={{1,0},{0,1},{3,2},{2,3},{5,4},{4,5},{7,6},{6,7},{9,8},{8,9},{11,10... | collective-permute-start | bytes 688136 | tf_op jit(solution)/shard_map/ppermute | solution.py:21
  66.1 1.6 %collective-permute-start.17 = (bf16[96,1024]{1,0:T(8,128)(2,1)S(1)}, bf16[96,1024]{1,0:T(8,128)(2,1)S(1)}, u32[]{:S(2)}, u32[]{:S(2)}) collective-permute-start(bf16[96,1024]{1,0:T(8,128)(2,1)S(1)} %get-tuple-element.73), channel_id=1, source_target_pairs={{1,0},{0,1},{3,2},{2,3},{5,4},{4,5},{7,6},{6,7},{9,8},{8,9},{11,10... | collective-permute-start | bytes 589832 | tf_op jit(solution)/shard_map/ppermute | solution.py:21

commit v15 on v14

--- a/solution.py
+++ b/solution.py
@@ -490,52 +490,64 @@
     )(in_hbm(total.array) if away else in_vmem(total), in_vmem(arrived))
 
 
-def finish_spectra_body(mine_s, inside, *rest):
-    others, (out, near) = rest[:-2], rest[-2:]
+def finish_spectra_body(mine_s, *rest):
+    others, out = rest[:-1], rest[-1]
     at = 0
     for other in others:
         where = pl.ds(at, other.shape[0])
         out[where] = (mine_s[where] + other[...].astype(jnp.float32)).astype(jnp.bfloat16)
         at += other.shape[0]
-    near[...] = inside[...]
-
-
-def finish_spectra(mine_s, others, inside):
+
+
+def finish_spectra(mine_s, others):
     return pl.pallas_call(
         finish_spectra_body,
-        out_shape=[
-            jax.ShapeDtypeStruct(mine_s.shape, jnp.bfloat16),
-            vmem_out(inside.shape, inside.dtype),
-        ],
-        in_specs=[VMEM_SPEC] * (2 + len(others)),
-        out_specs=[VMEM_SPEC] * 2,
+        out_shape=jax.ShapeDtypeStruct(mine_s.shape, jnp.bfloat16),
+        in_specs=[VMEM_SPEC] * (1 + len(others)),
+        out_specs=VMEM_SPEC,
         cost_estimate=SMALL_COST,
         compiler_params=params(),
-    )(*[in_vmem(a) for a in [mine_s, inside] + others])
-
-
-def finish_structures_body(flag, here_total, across_back, inside_a, inside_b, out):
+    )(*[in_vmem(a) for a in [mine_s] + others])
+
+
+def finish_structures_body(flag, here_total, across_back, inside_a, inside_b, out, held, sems):
+    cut = inside_a.shape[0]
+
     @pl.when(flag[0] != 0)
     def _():
-        out[pl.ds(0, inside_a.shape[0])] = inside_a[...]
-        out[pl.ds(inside_a.shape[0], inside_b.shape[0])] = inside_b[...]
+        first = pltpu.make_async_copy(inside_a, out.at[pl.ds(0, cut)], sems.at[0])
+        second = pltpu.make_async_copy(inside_b, out.at[pl.ds(cut, inside_b.shape[0])], sems.at[1])
+        first.start()
+        second.start()
+        first.wait()
+        second.wait()
 
     @pl.when(flag[0] == 0)
     def _():
         total = here_total[...] + across_back[...].astype(jnp.float32)
-        out[...] = total.astype(jnp.bfloat16)
+        held[...] = total.astype(jnp.bfloat16)
+        copy = pltpu.make_async_copy(held, out, sems.at[0])
+        copy.start()
+        copy.wait()
 
 
 def finish_structures(flag, here_total, across_back, inside_a, inside_b):
-    arrays = [here_total, across_back, inside_a, inside_b]
+    shape = here_total.shape
     return pl.pallas_call(
         finish_structures_body,
-        out_shape=jax.ShapeDtypeStruct(here_total.shape, jnp.bfloat16),
-        in_specs=[SMEM_SPEC] + [VMEM_SPEC] * len(arrays),
-        out_specs=VMEM_SPEC,
+        out_shape=jax.ShapeDtypeStruct(shape, jnp.bfloat16),
+        in_specs=[SMEM_SPEC, VMEM_SPEC, VMEM_SPEC, HBM_SPEC, HBM_SPEC],
+        out_specs=HBM_SPEC,
+        scratch_shapes=[pltpu.VMEM(shape, jnp.bfloat16), pltpu.SemaphoreType.DMA((2,))],
         cost_estimate=SMALL_COST,
         compiler_params=params(),
-    )(jnp.int32(flag).reshape(1), *[in_vmem(a) for a in arrays])
+    )(
+        jnp.int32(flag).reshape(1),
+        in_vmem(here_total),
+        in_vmem(across_back),
+        in_hbm(inside_a),
+        in_hbm(inside_b),
+    )
 
 
 def along_line(spectra, glycans, labels, scale, shift):
@@ -693,7 +705,7 @@
         ends=ends,
     )
     others[0] = after(others[0], here_total)
-    grad_spectra, inside_a = finish_spectra(mine_s, others, inside_a)
+    grad_spectra = finish_spectra(mine_s, others)
     across_back = after(across_back, grad_spectra)
     return grad_spectra, finish_structures(outer, here_total, across_back, inside_a, inside_b)
 

time: 72.1 us -> 90.4 us (1.25)
  Pallas kernels: 23 us -> 41.1 us
    pallas_call x2, Pallas kernels: 3.84 us -> 22 us  [the longest x1 21 us: finish_structures(): pl.pallas_call(finish_structures_body, out_shape=jax.ShapeDtypeStruct(sha...]
  transfers between devices with their start and end apart: 20 -> 20, of which waited for: 4 -> 5; matrix products, arithmetic and copies ran while one was open for 5% -> 4% of each run, Pallas kernels for 29% -> 22%
where the time goes in v15:
time: 90.4 us; the launch traced here: 89.9 us
  Pallas kernels  41.1 us (45%)
  starting transfers between devices  31.1 us (34%)
  waiting for transfers between devices  9.87 us (11%)
  other arithmetic  2.97 us (3%)
  local copies, waits for them, and re-layouts  2.48 us (3%)
  between operations  2.44 us (3%)
    ppermute x13, starting transfers between devices, permute(): return lax.ppermute(block, ('blk', 'inner'), pairs)  29.4 us
    pallas_call x1, Pallas kernels, finish_structures(): pl.pallas_call(finish_structures_body, out_shape=jax.ShapeDtypeStruct(sha...  21 us
    pallas_call x8, Pallas kernels, pair_work(): pl.pallas_call(functools.partial(pair_body, plan), out_shape=outs, in_spe...  10.3 us
    ppermute x13, waiting for transfers between devices, permute(): return lax.ppermute(block, ('blk', 'inner'), pairs)  8.44 us
    pallas_call x1, Pallas kernels, spectra_work(): pl.pallas_call(functools.partial(spectra_body, plan), out_shape=[vmem_out...  5.83 us
    pallas_call x2, Pallas kernels, add_rounded(): pl.pallas_call(add_body, out_shape=vmem_out(arrived.shape, jnp.bfloat16),...  2.86 us
    concatenate x1, other arithmetic, along_line(): end_mine = permute(jnp.concatenate([spectra, coded]), inward)  1.99 us
  transfers between devices with their start and end apart: 20, of which 5 were waited for; matrix products, arithmetic and copies ran while one was open for 4% of the time, Pallas kernels for 22%

profile of v15, /device:TPU:0, one launch (start us, length us, event | category | flops | bytes accessed | tf_op | source)
XLA Modules:
  0.0 89.9 jit_solution(2949066684291863498)
XLA Ops:
  0.6 0.5 collective-permute-start.3
  1.1 4.1 %collective-permute-start.2 = (bf16[320,1024]{1,0:T(8,128)(2,1)}, bf16[320,1024]{1,0:T(8,128)(2,1)S(1)}, u32[]{:S(2)}, u32[]{:S(2)}) collective-permute-start(bf16[320,1024]{1,0:T(8,128)(2,1)} %refs_5_), channel_id=1, source_target_pairs={{0,4},{4,0},{8,12},{12,8},{1,5},{5,1},{9,13},{13,9},{2,6},{6,2},{1... | collective-permute-start | bytes 1966088 | tf_op jit(solution)/shard_map/ppermute | solution.py:562
  5.3 0.7 concatenate.19
  6.0 0.5 collective-permute-start.1
  6.5 0.7 fusion.28
  7.3 2.0 %pad_maximum_fusion = bf16[336,1024]{1,0:T(8,128)(2,1)} fusion(bf16[16,1024]{1,0:T(8,128)(2,1)S(1)} %fusion.14, bf16[320,1024]{1,0:T(8,128)(2,1)} %s_mine.1), kind=kLoop, calls=%fused_computation | loop fusion | flops 1376256 | bytes 1376256 | tf_op jit(solution)/shard_map/concatenate | solution.py:603
  9.3 1.9 %collective-permute-start.4 = (bf16[336,1024]{1,0:T(8,128)(2,1)}, bf16[336,1024]{1,0:T(8,128)(2,1)S(1)}, u32[]{:S(2)}, u32[]{:S(2)}) collective-permute-start(bf16[336,1024]{1,0:T(8,128)(2,1)} %pad_maximum_fusion), channel_id=1, source_target_pairs={{0,4},{12,8},{1,5},{13,9},{2,6},{14,10},{3,7},{15,11},{16,20},{28,... | collective-permute-start | bytes 2064392 | tf_op jit(solution)/shard_map/ppermute | solution.py:562
  12.8 0.8 copy-done.3
  13.7 4.3 %shard_map.68 = (f32[320,1024]{1,0:T(8,128)}, bf16[320,640]{1,0:T(8,128)(2,1)}) custom-call(f32[8,128]{1,0:T(8,128)S(1)} %select_select_fusion.refs_0_.refs_1_.consts, f32[1,640]{1,0:T(1,128)S(1)} %add_convert_fusion.refs_1_.refs_2_.labels, bf16[320,1024]{1,0:T(8,128)(2,1)} %s_mine.1, bf16[320,1024]{1,0:T(8,128)(2,1)} %copy-done.3, bf16[320,1024]{1,0:T(8,128)(2,1)} %refs_5_), custom_call_target="tpu_custom_call" | custom-call | flops 1024 | bytes 1024 | tf_op jit(solution)/shard_map/pallas_call | solution.py:342
  18.0 1.3 %collective-permute-start.10 = (bf16[320,1024]{1,0:T(8,128)(2,1)}, bf16[320,1024]{1,0:T(8,128)(2,1)}, u32[]{:S(2)}, u32[]{:S(2)}) collective-permute-start(bf16[320,1024]{1,0:T(8,128)(2,1)} %collective-permute-done.3.refs_5_.across), channel_id=1, source_target_pairs={{4,0},{8,12},{5,1},{9,13},{6,2},{10,14},{7,3},{11,15},{20,16},{24,... | collective-permute-start | bytes 1966088 | tf_op jit(solution)/shard_map/ppermute | solution.py:562
  19.3 1.5 %collective-permute-done.2.refs_4_.whole.refs_5_.side = bf16[320,1024]{1,0:T(8,128)(2,1)S(1)} collective-permute-done((bf16[320,1024]{1,0:T(8,128)(2,1)}, bf16[320,1024]{1,0:T(8,128)(2,1)S(1)}, u32[]{:S(2)}, u32[]{:S(2)}) %collective-permute-start.2) | collective-permute-done | bytes 655392 | tf_op jit(solution)/shard_map/ppermute | solution.py:562
  20.9 0.5 collective-permute-start.9
  21.4 0.2 copy-done
  21.6 5.5 %shard_map.69 = (f32[320,1024]{1,0:T(8,128)}, f32[320,1024]{1,0:T(8,128)}, bf16[320,640]{1,0:T(8,128)(2,1)}, bf16[320,640]{1,0:T(8,128)(2,1)}) custom-call(f32[8,128]{1,0:T(8,128)S(1)} %select_select_fusion.refs_0_.refs_1_.consts, f32[1,640]{1,0:T(1,128)S(1)} %add_convert_fusion.refs_1_.refs_2_.labels, bf16[320,1024]{1,0:T(8,128)(2,1)} %s_mine.1, ...), custom_call_target="tpu_custom_call" | custom-call | flops 1024 | bytes 1024 | tf_op jit(solution)/shard_map/pallas_call | solution.py:342
  27.3 6.8 %collective-permute-done.4.whole.refs_2_.refs_5_ = bf16[336,1024]{1,0:T(8,128)(2,1)S(1)} collective-permute-done((bf16[336,1024]{1,0:T(8,128)(2,1)}, bf16[336,1024]{1,0:T(8,128)(2,1)S(1)}, u32[]{:S(2)}, u32[]{:S(2)}) %collective-permute-start.4) | collective-permute-done | bytes 688160 | tf_op jit(solution)/shard_map/ppermute | solution.py:562
  34.2 0.5 collective-permute-start.7
  34.7 2.4 %collective-permute-start.8 = (bf16[128,1024]{1,0:T(8,128)(2,1)S(1)}, bf16[128,1024]{1,0:T(8,128)(2,1)S(1)}, u32[]{:S(2)}, u32[]{:S(2)}) collective-permute-start(bf16[128,1024]{1,0:T(8,128)(2,1)S(1)} %collective-permute-done.5.refs_5_.rest_1_), channel_id=1, source_target_pairs={{0,4},{4,0},{8,12},{12,8},{1,5},{5,1},{9,13},{13,9},{2,6},{6,2},{1... | collective-permute-start | bytes 786440 | tf_op jit(solution)/shard_map/ppermute | solution.py:562
  37.3 0.1 shard_map.74
  37.4 0.6 collective-permute-start.11
  37.9 7.4 %collective-permute-start.12 = (bf16[192,1024]{1,0:T(8,128)(2,1)S(1)}, bf16[192,1024]{1,0:T(8,128)(2,1)S(1)}, u32[]{:S(2)}, u32[]{:S(2)}) collective-permute-start(bf16[192,1024]{1,0:T(8,128)(2,1)S(1)} %collective-permute-done.9.refs_8_.rest_2_), channel_id=1, source_target_pairs={{0,4},{4,0},{8,12},{12,8},{1,5},{5,1},{9,13},{13,9},{2,6},{6,2},{1... | collective-permute-start | bytes 1179656 | tf_op jit(solution)/shard_map/ppermute | solution.py:562
  45.5 0.7 copy-done.5
  46.3 0.7 shard_map.77
  47.0 8.6 %collective-permute-start.15 = (bf16[128,1024]{1,0:T(8,128)(2,1)}, bf16[128,1024]{1,0:T(8,128)(2,1)}, u32[]{:S(2)}, u32[]{:S(2)}) collective-permute-start(bf16[128,1024]{1,0:T(8,128)(2,1)} %shard_map.77), channel_id=1, source_target_pairs={{0,4},{4,0},{8,12},{12,8},{1,5},{5,1},{9,13},{13,9},{2,6},{6,2},{1... | collective-permute-start | bytes 786440 | tf_op jit(solution)/shard_map/ppermute | solution.py:562
  55.6 2.1 %shard_map.78 = bf16[192,1024]{1,0:T(8,128)(2,1)} custom-call(f32[192,1024]{1,0:T(8,128)} %get-tuple-element.57.total, bf16[192,1024]{1,0:T(8,128)(2,1)S(1)} %collective-permute-done.11.arrived), custom_call_target="tpu_custom_call" | custom-call | flops 1024 | bytes 1024 | tf_op jit(solution)/shard_map/pallas_call | solution.py:482
  57.7 1.9 %collective-permute-start.19 = (bf16[192,1024]{1,0:T(8,128)(2,1)}, bf16[192,1024]{1,0:T(8,128)(2,1)}, u32[]{:S(2)}, u32[]{:S(2)}) collective-permute-start(bf16[192,1024]{1,0:T(8,128)(2,1)} %shard_map.78), channel_id=1, source_target_pairs={{0,4},{4,0},{8,12},{12,8},{1,5},{5,1},{9,13},{13,9},{2,6},{6,2},{1... | collective-permute-start | bytes 1179656 | tf_op jit(solution)/shard_map/ppermute | solution.py:562
  59.6 5.8 %shard_map.79 = (f32[320,1024]{1,0:T(8,128)S(1)}, bf16[320,1024]{1,0:T(8,128)(2,1)S(1)}) custom-call(s32[1]{0:T(128)} %bitcast.outer.flag, f32[8,128]{1,0:T(8,128)S(1)} %select_select_fusion.refs_0_.refs_1_.consts, f32[1,640]{1,0:T(1,128)S(1)} %add_convert_fusion.refs_1_.refs_2_.labels, bf16[320,1024]{1,0:T(8,128)(2,1)} %s_mine.1, ...), custom_call_target="tpu_custom_call" | custom-call | flops 1024 | bytes 1024 | tf_op jit(solution)/shard_map/pallas_call | solution.py:430
  65.6 0.5 collective-permute-start.16
  66.3 0.8 collective-permute-done.14.rest_0_
  67.1 0.6 collective-permute-done.17.rest_2_
  67.7 1.0 %shard_map.82 = bf16[320,1024]{1,0:T(8,128)(2,1)} custom-call(f32[320,1024]{1,0:T(8,128)S(1)} %get-tuple-element.64.mine_s, bf16[112,1024]{1,0:T(8,128)(2,1)S(1)} %collective-permute-done.14.rest_0_, bf16[112,1024]{1,0:T(8,128)(2,1)S(1)} %collective-permute-done.16.rest_1_, bf16[96,1024]{1,0:T(8,128)(2,1)S(1)} %collective-permute-done.17.rest_2_), custom_call_target="tpu_custom_call" | custom-call | flops 1024 | bytes 1024 | tf_op jit(solution)/shard_map/pallas_call | solution.py:503
  68.7 0.1 collective-permute-done.19.inside_b
  68.8 21.0 %shard_map.83 = bf16[320,1024]{1,0:T(8,128)(2,1)} custom-call(s32[1]{0:T(128)} %bitcast.outer.flag, f32[320,1024]{1,0:T(8,128)S(1)} %shard_map.81.here_total, bf16[320,1024]{1,0:T(8,128)(2,1)S(1)} %collective-permute-done.18.across_back, bf16[128,1024]{1,0:T(8,128)(2,1)} %collective-permute-done.15.inside_a, bf16[192,1024]{1,0:T(8,128)(2,1)} %collective-permute-done.19.inside_b), custom_call_target="tpu_custom_call" | custom-call | flops 1024 | bytes 1024 | tf_op jit(solution)/shard_map/pallas_call | solution.py:536
  (50 shorter events, 1.2 us)
Async XLA Ops:
  0.6 17.3 %collective-permute-start.3 = (bf16[320,1024]{1,0:T(8,128)(2,1)}, bf16[320,1024]{1,0:T(8,128)(2,1)}, u32[]{:S(2)}, u32[]{:S(2)}) collective-permute-start(bf16[320,1024]{1,0:T(8,128)(2,1)} %refs_5_), channel_id=1, source_target_pairs={{4,8},{8,4},{0,1},{12,13},{5,9},{9,5},{1,0},{13,12},{6,10},{10,6},... | collective-permute-start | bytes 1966088 | tf_op jit(solution)/shard_map/ppermute | solution.py:562
  1.1 19.6 %collective-permute-start.2 = (bf16[320,1024]{1,0:T(8,128)(2,1)}, bf16[320,1024]{1,0:T(8,128)(2,1)S(1)}, u32[]{:S(2)}, u32[]{:S(2)}) collective-permute-start(bf16[320,1024]{1,0:T(8,128)(2,1)} %refs_5_), channel_id=1, source_target_pairs={{0,4},{4,0},{8,12},{12,8},{1,5},{5,1},{9,13},{13,9},{2,6},{6,2},{1... | collective-permute-start | bytes 1966088 | tf_op jit(solution)/shard_map/ppermute | solution.py:562
  6.0 6.8 %collective-permute-start = (s32[1,320]{1,0:T(1,128)S(1)}, s32[1,320]{1,0:T(1,128)S(1)}, u32[]{:S(2)}, u32[]{:S(2)}) collective-permute-start(s32[1,320]{1,0:T(1,128)S(1)} %concatenate.19), channel_id=1, source_target_pairs={{1,0},{0,1},{3,2},{2,3},{5,4},{4,5},{7,6},{6,7},{9,8},{8,9},{11,10... | collective-permute-start | bytes 3848 | tf_op jit(solution)/shard_map/ppermute | solution.py:21
  6.0 6.9 %collective-permute-start.1 = (bf16[320,1024]{1,0:T(8,128)(2,1)}, bf16[320,1024]{1,0:T(8,128)(2,1)S(1)}, u32[]{:S(2)}, u32[]{:S(2)}) collective-permute-start(bf16[320,1024]{1,0:T(8,128)(2,1)} %s_mine.1), channel_id=1, source_target_pairs={{1,0},{0,1},{3,2},{2,3},{5,4},{4,5},{7,6},{6,7},{9,8},{8,9},{11,10... | collective-permute-start | bytes 1966088 | tf_op jit(solution)/shard_map/ppermute | solution.py:21
  9.3 24.8 %collective-permute-start.4 = (bf16[336,1024]{1,0:T(8,128)(2,1)}, bf16[336,1024]{1,0:T(8,128)(2,1)S(1)}, u32[]{:S(2)}, u32[]{:S(2)}) collective-permute-start(bf16[336,1024]{1,0:T(8,128)(2,1)} %pad_maximum_fusion), channel_id=1, source_target_pairs={{0,4},{12,8},{1,5},{13,9},{2,6},{14,10},{3,7},{15,11},{16,20},{28,... | collective-permute-start | bytes 2064392 | tf_op jit(solution)/shard_map/ppermute | solution.py:562
  12.8 0.8 copy-start.3
  18.0 19.1 %collective-permute-start.10 = (bf16[320,1024]{1,0:T(8,128)(2,1)}, bf16[320,1024]{1,0:T(8,128)(2,1)}, u32[]{:S(2)}, u32[]{:S(2)}) collective-permute-start(bf16[320,1024]{1,0:T(8,128)(2,1)} %collective-permute-done.3.refs_5_.across), channel_id=1, source_target_pairs={{4,0},{8,12},{5,1},{9,13},{6,2},{10,14},{7,3},{11,15},{20,16},{24,... | collective-permute-start | bytes 1966088 | tf_op jit(solution)/shard_map/ppermute | solution.py:562
  20.8 0.8 copy-start
  20.8 6.3 %collective-permute-start.5 = (bf16[128,1024]{1,0:T(8,128)(2,1)S(1)}, bf16[128,1024]{1,0:T(8,128)(2,1)S(1)}, u32[]{:S(2)}, u32[]{:S(2)}) collective-permute-start(bf16[128,1024]{1,0:T(8,128)(2,1)S(1)} %get-tuple-element.44), channel_id=1, source_target_pairs={{4,8},{8,4},{0,1},{12,13},{5,9},{9,5},{1,0},{13,12},{6,10},{10,6},... | collective-permute-start | bytes 786440 | tf_op jit(solution)/shard_map/ppermute | solution.py:562
  20.9 16.2 %collective-permute-start.9 = (bf16[192,1024]{1,0:T(8,128)(2,1)S(1)}, bf16[192,1024]{1,0:T(8,128)(2,1)S(1)}, u32[]{:S(2)}, u32[]{:S(2)}) collective-permute-start(bf16[192,1024]{1,0:T(8,128)(2,1)S(1)} %get-tuple-element.50), channel_id=1, source_target_pairs={{4,8},{8,4},{0,1},{12,13},{5,9},{9,5},{1,0},{13,12},{6,10},{10,6},... | collective-permute-start | bytes 1179656 | tf_op jit(solution)/shard_map/ppermute | solution.py:562
  27.2 9.9 %copy-start.1 = (bf16[128,1024]{1,0:T(8,128)(2,1)}, bf16[128,1024]{1,0:T(8,128)(2,1)S(1)}, u32[]{:S(2)}) copy-start(bf16[128,1024]{1,0:T(8,128)(2,1)S(1)} %collective-permute-done.5.refs_5_.rest_1_) | copy-start | bytes 786436
  34.1 3.0 %collective-permute-start.6 = (bf16[176,1024]{1,0:T(8,128)(2,1)S(1)}, bf16[176,1024]{1,0:T(8,128)(2,1)S(1)}, u32[]{:S(2)}, u32[]{:S(2)}) collective-permute-start(bf16[176,1024]{1,0:T(8,128)(2,1)S(1)} %get-tuple-element.48), channel_id=1, source_target_pairs={{1,0},{0,1},{3,2},{2,3},{5,4},{4,5},{7,6},{6,7},{9,8},{8,9},{11,10... | collective-permute-start | bytes 1081352 | tf_op jit(solution)/shard_map/ppermute | solution.py:21
  34.2 2.9 %collective-permute-start.7 = (bf16[160,1024]{1,0:T(8,128)(2,1)S(1)}, bf16[160,1024]{1,0:T(8,128)(2,1)S(1)}, u32[]{:S(2)}, u32[]{:S(2)}) collective-permute-start(bf16[160,1024]{1,0:T(8,128)(2,1)S(1)} %get-tuple-element.49), channel_id=1, source_target_pairs={{1,0},{0,1},{3,2},{2,3},{5,4},{4,5},{7,6},{6,7},{9,8},{8,9},{11,10... | collective-permute-start | bytes 983048 | tf_op jit(solution)/shard_map/ppermute | solution.py:21
  34.7 10.8 %collective-permute-start.8 = (bf16[128,1024]{1,0:T(8,128)(2,1)S(1)}, bf16[128,1024]{1,0:T(8,128)(2,1)S(1)}, u32[]{:S(2)}, u32[]{:S(2)}) collective-permute-start(bf16[128,1024]{1,0:T(8,128)(2,1)S(1)} %collective-permute-done.5.refs_5_.rest_1_), channel_id=1, source_target_pairs={{0,4},{4,0},{8,12},{12,8},{1,5},{5,1},{9,13},{13,9},{2,6},{6,2},{1... | collective-permute-start | bytes 786440 | tf_op jit(solution)/shard_map/ppermute | solution.py:562
  37.1 0.9 copy-start.2
  37.2 9.1 %collective-permute-start.13 = (bf16[128,1024]{1,0:T(8,128)(2,1)S(1)}, bf16[128,1024]{1,0:T(8,128)(2,1)S(1)}, u32[]{:S(2)}, u32[]{:S(2)}) collective-permute-start(bf16[128,1024]{1,0:T(8,128)(2,1)S(1)} %shard_map.73), channel_id=1, source_target_pairs={{4,8},{8,4},{0,1},{12,13},{5,9},{9,5},{1,0},{13,12},{6,10},{10,6},... | collective-permute-start | bytes 786440 | tf_op jit(solution)/shard_map/ppermute | solution.py:562
  37.4 18.2 %collective-permute-start.11 = (bf16[192,1024]{1,0:T(8,128)(2,1)S(1)}, bf16[192,1024]{1,0:T(8,128)(2,1)S(1)}, u32[]{:S(2)}, u32[]{:S(2)}) collective-permute-start(bf16[192,1024]{1,0:T(8,128)(2,1)S(1)} %shard_map.74), channel_id=1, source_target_pairs={{4,8},{8,4},{0,1},{12,13},{5,9},{9,5},{1,0},{13,12},{6,10},{10,6},... | collective-permute-start | bytes 1179656 | tf_op jit(solution)/shard_map/ppermute | solution.py:562
  37.9 17.7 %collective-permute-start.12 = (bf16[192,1024]{1,0:T(8,128)(2,1)S(1)}, bf16[192,1024]{1,0:T(8,128)(2,1)S(1)}, u32[]{:S(2)}, u32[]{:S(2)}) collective-permute-start(bf16[192,1024]{1,0:T(8,128)(2,1)S(1)} %collective-permute-done.9.refs_8_.rest_2_), channel_id=1, source_target_pairs={{0,4},{4,0},{8,12},{12,8},{1,5},{5,1},{9,13},{13,9},{2,6},{6,2},{1... | collective-permute-start | bytes 1179656 | tf_op jit(solution)/shard_map/ppermute | solution.py:562
  45.5 0.7 copy-start.5
  47.0 21.7 %collective-permute-start.18 = (bf16[320,1024]{1,0:T(8,128)(2,1)S(1)}, bf16[320,1024]{1,0:T(8,128)(2,1)S(1)}, u32[]{:S(2)}, u32[]{:S(2)}) collective-permute-start(bf16[320,1024]{1,0:T(8,128)(2,1)S(1)} %shard_map.75), channel_id=1, source_target_pairs={{4,8},{8,4},{0,1},{12,13},{5,9},{9,5},{1,0},{13,12},{6,10},{10,6},... | collective-permute-start | bytes 1966088 | tf_op jit(solution)/shard_map/ppermute | solution.py:562
  47.0 19.1 %collective-permute-start.15 = (bf16[128,1024]{1,0:T(8,128)(2,1)}, bf16[128,1024]{1,0:T(8,128)(2,1)}, u32[]{:S(2)}, u32[]{:S(2)}) collective-permute-start(bf16[128,1024]{1,0:T(8,128)(2,1)} %shard_map.77), channel_id=1, source_target_pairs={{0,4},{4,0},{8,12},{12,8},{1,5},{5,1},{9,13},{13,9},{2,6},{6,2},{1... | collective-permute-start | bytes 786440 | tf_op jit(solution)/shard_map/ppermute | solution.py:562
  55.6 2.1 %copy-start.4 = (bf16[192,1024]{1,0:T(8,128)(2,1)}, bf16[192,1024]{1,0:T(8,128)(2,1)S(1)}, u32[]{:S(2)}) copy-start(bf16[192,1024]{1,0:T(8,128)(2,1)S(1)} %collective-permute-done.12.rest_4_) | copy-start | bytes 1179652
  57.7 11.1 %collective-permute-start.19 = (bf16[192,1024]{1,0:T(8,128)(2,1)}, bf16[192,1024]{1,0:T(8,128)(2,1)}, u32[]{:S(2)}, u32[]{:S(2)}) collective-permute-start(bf16[192,1024]{1,0:T(8,128)(2,1)} %shard_map.78), channel_id=1, source_target_pairs={{0,4},{4,0},{8,12},{12,8},{1,5},{5,1},{9,13},{13,9},{2,6},{6,2},{1... | collective-permute-start | bytes 1179656 | tf_op jit(solution)/shard_map/ppermute | solution.py:562
  65.5 1.6 %collective-permute-start.14 = (bf16[112,1024]{1,0:T(8,128)(2,1)S(1)}, bf16[112,1024]{1,0:T(8,128)(2,1)S(1)}, u32[]{:S(2)}, u32[]{:S(2)}) collective-permute-start(bf16[112,1024]{1,0:T(8,128)(2,1)S(1)} %get-tuple-element.66), channel_id=1, source_target_pairs={{1,0},{0,1},{3,2},{2,3},{5,4},{4,5},{7,6},{6,7},{9,8},{8,9},{11,10... | collective-permute-start | bytes 688136 | tf_op jit(solution)/shard_map/ppermute | solution.py:21
  65.6 2.1 %collective-permute-start.16 = (bf16[112,1024]{1,0:T(8,128)(2,1)S(1)}, bf16[112,1024]{1,0:T(8,128)(2,1)S(1)}, u32[]{:S(2)}, u32[]{:S(2)}) collective-permute-start(bf16[112,1024]{1,0:T(8,128)(2,1)S(1)} %get-tuple-element.69), channel_id=1, source_target_pairs={{1,0},{0,1},{3,2},{2,3},{5,4},{4,5},{7,6},{6,7},{9,8},{8,9},{11,10... | collective-permute-start | bytes 688136 | tf_op jit(solution)/shard_map/ppermute | solution.py:21
  66.1 1.6 %collective-permute-start.17 = (bf16[96,1024]{1,0:T(8,128)(2,1)S(1)}, bf16[96,1024]{1,0:T(8,128)(2,1)S(1)}, u32[]{:S(2)}, u32[]{:S(2)}) collective-permute-start(bf16[96,1024]{1,0:T(8,128)(2,1)S(1)} %get-tuple-element.70), channel_id=1, source_target_pairs={{1,0},{0,1},{3,2},{2,3},{5,4},{4,5},{7,6},{6,7},{9,8},{8,9},{11,10... | collective-permute-start | bytes 589832 | tf_op jit(solution)/shard_map/ppermute | solution.py:21

commit v16 on v15

--- a/solution.py
+++ b/solution.py
@@ -515,8 +515,9 @@
 
     @pl.when(flag[0] != 0)
     def _():
-        first = pltpu.make_async_copy(inside_a, out.at[pl.ds(0, cut)], sems.at[0])
-        second = pltpu.make_async_copy(inside_b, out.at[pl.ds(cut, inside_b.shape[0])], sems.at[1])
+        first = pltpu.make_async_copy(inside_a, held.at[pl.ds(0, cut)], sems.at[0])
+        rest = pl.ds(cut, inside_b.shape[0])
+        second = pltpu.make_async_copy(inside_b, held.at[rest], sems.at[1])
         first.start()
         second.start()
         first.wait()
@@ -526,9 +527,10 @@
     def _():
         total = here_total[...] + across_back[...].astype(jnp.float32)
         held[...] = total.astype(jnp.bfloat16)
-        copy = pltpu.make_async_copy(held, out, sems.at[0])
-        copy.start()
-        copy.wait()
+
+    copy = pltpu.make_async_copy(held, out, sems.at[0])
+    copy.start()
+    copy.wait()
 
 
 def finish_structures(flag, here_total, across_back, inside_a, inside_b):

time: 90.4 us -> 71.4 us (0.79)
  Pallas kernels: 41.1 us -> 22.1 us
    pallas_call x1, Pallas kernels: 21 us -> 1.93 us  [finish_structures(): pl.pallas_call(finish_structures_body, out_shape=jax.ShapeDtypeStruct(sha...]
  transfers between devices with their start and end apart: 20 -> 20, of which waited for: 5 -> 5; matrix products, arithmetic and copies ran while one was open for 4% -> 5% of each run, Pallas kernels for 22% -> 28%
where the time goes in v16:
time: 71.4 us; the launch traced here: 70.9 us
  starting transfers between devices  31.1 us (44%)
  Pallas kernels  22.1 us (31%)
  waiting for transfers between devices  9.87 us (14%)
  other arithmetic  2.97 us (4%)
  local copies, waits for them, and re-layouts  2.48 us (3%)
  between operations  2.44 us (3%)
    ppermute x13, starting transfers between devices, permute(): return lax.ppermute(block, ('blk', 'inner'), pairs)  29.4 us
    pallas_call x8, Pallas kernels, pair_work(): pl.pallas_call(functools.partial(pair_body, plan), out_shape=outs, in_spe...  10.3 us
    ppermute x13, waiting for transfers between devices, permute(): return lax.ppermute(block, ('blk', 'inner'), pairs)  8.44 us
    pallas_call x1, Pallas kernels, spectra_work(): pl.pallas_call(functools.partial(spectra_body, plan), out_shape=[vmem_out...  5.83 us
    pallas_call x2, Pallas kernels, add_rounded(): pl.pallas_call(add_body, out_shape=vmem_out(arrived.shape, jnp.bfloat16),...  2.86 us
    concatenate x1, other arithmetic, along_line(): end_mine = permute(jnp.concatenate([spectra, coded]), inward)  1.99 us
    pallas_call x1, Pallas kernels, finish_structures(): pl.pallas_call(finish_structures_body, out_shape=jax.ShapeDtypeStruct(sha...  1.93 us
    unnamed x12, local copies, waits for them, and re-layouts  1.78 us
  transfers between devices with their start and end apart: 20, of which 5 were waited for; matrix products, arithmetic and copies ran while one was open for 5% of the time, Pallas kernels for 28%

profile of v16, /device:TPU:0, one launch (start us, length us, event | category | flops | bytes accessed | tf_op | source)
XLA Modules:
  0.0 70.9 jit_solution(7323299008578780005)
XLA Ops:
  0.6 0.5 collective-permute-start.3
  1.1 4.1 %collective-permute-start.2 = (bf16[320,1024]{1,0:T(8,128)(2,1)}, bf16[320,1024]{1,0:T(8,128)(2,1)S(1)}, u32[]{:S(2)}, u32[]{:S(2)}) collective-permute-start(bf16[320,1024]{1,0:T(8,128)(2,1)} %refs_5_), channel_id=1, source_target_pairs={{0,4},{4,0},{8,12},{12,8},{1,5},{5,1},{9,13},{13,9},{2,6},{6,2},{1... | collective-permute-start | bytes 1966088 | tf_op jit(solution)/shard_map/ppermute | solution.py:564
  5.3 0.7 concatenate.19
  6.0 0.5 collective-permute-start.1
  6.5 0.7 fusion.28
  7.3 2.0 %pad_maximum_fusion = bf16[336,1024]{1,0:T(8,128)(2,1)} fusion(bf16[16,1024]{1,0:T(8,128)(2,1)S(1)} %fusion.14, bf16[320,1024]{1,0:T(8,128)(2,1)} %s_mine.1), kind=kLoop, calls=%fused_computation | loop fusion | flops 1376256 | bytes 1376256 | tf_op jit(solution)/shard_map/concatenate | solution.py:605
  9.3 1.9 %collective-permute-start.4 = (bf16[336,1024]{1,0:T(8,128)(2,1)}, bf16[336,1024]{1,0:T(8,128)(2,1)S(1)}, u32[]{:S(2)}, u32[]{:S(2)}) collective-permute-start(bf16[336,1024]{1,0:T(8,128)(2,1)} %pad_maximum_fusion), channel_id=1, source_target_pairs={{0,4},{12,8},{1,5},{13,9},{2,6},{14,10},{3,7},{15,11},{16,20},{28,... | collective-permute-start | bytes 2064392 | tf_op jit(solution)/shard_map/ppermute | solution.py:564
  12.8 0.8 %copy-done.3 = bf16[320,1024]{1,0:T(8,128)(2,1)} copy-done((bf16[320,1024]{1,0:T(8,128)(2,1)}, bf16[320,1024]{1,0:T(8,128)(2,1)S(1)}, u32[]{:S(2)}) %copy-start.3) | copy-done | bytes 655384
  13.7 4.3 %shard_map.68 = (f32[320,1024]{1,0:T(8,128)}, bf16[320,640]{1,0:T(8,128)(2,1)}) custom-call(f32[8,128]{1,0:T(8,128)S(1)} %select_select_fusion.refs_0_.refs_1_.consts, f32[1,640]{1,0:T(1,128)S(1)} %add_convert_fusion.refs_1_.refs_2_.labels, bf16[320,1024]{1,0:T(8,128)(2,1)} %s_mine.1, bf16[320,1024]{1,0:T(8,128)(2,1)} %copy-done.3, bf16[320,1024]{1,0:T(8,128)(2,1)} %refs_5_), custom_call_target="tpu_custom_call" | custom-call | flops 1024 | bytes 1024 | tf_op jit(solution)/shard_map/pallas_call | solution.py:342
  18.0 1.3 %collective-permute-start.10 = (bf16[320,1024]{1,0:T(8,128)(2,1)}, bf16[320,1024]{1,0:T(8,128)(2,1)}, u32[]{:S(2)}, u32[]{:S(2)}) collective-permute-start(bf16[320,1024]{1,0:T(8,128)(2,1)} %collective-permute-done.3.refs_5_.across), channel_id=1, source_target_pairs={{4,0},{8,12},{5,1},{9,13},{6,2},{10,14},{7,3},{11,15},{20,16},{24,... | collective-permute-start | bytes 1966088 | tf_op jit(solution)/shard_map/ppermute | solution.py:564
  19.3 1.5 %collective-permute-done.2.refs_4_.whole.refs_5_.side = bf16[320,1024]{1,0:T(8,128)(2,1)S(1)} collective-permute-done((bf16[320,1024]{1,0:T(8,128)(2,1)}, bf16[320,1024]{1,0:T(8,128)(2,1)S(1)}, u32[]{:S(2)}, u32[]{:S(2)}) %collective-permute-start.2) | collective-permute-done | bytes 655392 | tf_op jit(solution)/shard_map/ppermute | solution.py:564
  20.9 0.5 collective-permute-start.9
  21.4 0.2 copy-done
  21.6 5.5 %shard_map.69 = (f32[320,1024]{1,0:T(8,128)}, f32[320,1024]{1,0:T(8,128)}, bf16[320,640]{1,0:T(8,128)(2,1)}, bf16[320,640]{1,0:T(8,128)(2,1)}) custom-call(f32[8,128]{1,0:T(8,128)S(1)} %select_select_fusion.refs_0_.refs_1_.consts, f32[1,640]{1,0:T(1,128)S(1)} %add_convert_fusion.refs_1_.refs_2_.labels, bf16[320,1024]{1,0:T(8,128)(2,1)} %s_mine.1, ...), custom_call_target="tpu_custom_call" | custom-call | flops 1024 | bytes 1024 | tf_op jit(solution)/shard_map/pallas_call | solution.py:342
  27.3 6.8 %collective-permute-done.4.whole.refs_2_.refs_5_ = bf16[336,1024]{1,0:T(8,128)(2,1)S(1)} collective-permute-done((bf16[336,1024]{1,0:T(8,128)(2,1)}, bf16[336,1024]{1,0:T(8,128)(2,1)S(1)}, u32[]{:S(2)}, u32[]{:S(2)}) %collective-permute-start.4) | collective-permute-done | bytes 688160 | tf_op jit(solution)/shard_map/ppermute | solution.py:564
  34.2 0.5 collective-permute-start.7
  34.7 2.4 %collective-permute-start.8 = (bf16[128,1024]{1,0:T(8,128)(2,1)S(1)}, bf16[128,1024]{1,0:T(8,128)(2,1)S(1)}, u32[]{:S(2)}, u32[]{:S(2)}) collective-permute-start(bf16[128,1024]{1,0:T(8,128)(2,1)S(1)} %collective-permute-done.5.refs_5_.rest_1_), channel_id=1, source_target_pairs={{0,4},{4,0},{8,12},{12,8},{1,5},{5,1},{9,13},{13,9},{2,6},{6,2},{1... | collective-permute-start | bytes 786440 | tf_op jit(solution)/shard_map/ppermute | solution.py:564
  37.3 0.1 shard_map.74
  37.4 0.6 collective-permute-start.11
  37.9 7.4 %collective-permute-start.12 = (bf16[192,1024]{1,0:T(8,128)(2,1)S(1)}, bf16[192,1024]{1,0:T(8,128)(2,1)S(1)}, u32[]{:S(2)}, u32[]{:S(2)}) collective-permute-start(bf16[192,1024]{1,0:T(8,128)(2,1)S(1)} %collective-permute-done.9.refs_8_.rest_2_), channel_id=1, source_target_pairs={{0,4},{4,0},{8,12},{12,8},{1,5},{5,1},{9,13},{13,9},{2,6},{6,2},{1... | collective-permute-start | bytes 1179656 | tf_op jit(solution)/shard_map/ppermute | solution.py:564
  45.5 0.7 %copy-done.5 = bf16[128,1024]{1,0:T(8,128)(2,1)} copy-done((bf16[128,1024]{1,0:T(8,128)(2,1)}, bf16[128,1024]{1,0:T(8,128)(2,1)S(1)}, u32[]{:S(2)}) %copy-start.5) | copy-done | bytes 262168
  46.3 0.7 %shard_map.77 = bf16[128,1024]{1,0:T(8,128)(2,1)} custom-call(f32[128,1024]{1,0:T(8,128)S(1)} %get-tuple-element.58.total, bf16[128,1024]{1,0:T(8,128)(2,1)S(1)} %collective-permute-done.13.arrived), custom_call_target="tpu_custom_call" | custom-call | flops 1024 | bytes 1024 | tf_op jit(solution)/shard_map/pallas_call | solution.py:482
  47.0 8.6 %collective-permute-start.15 = (bf16[128,1024]{1,0:T(8,128)(2,1)}, bf16[128,1024]{1,0:T(8,128)(2,1)}, u32[]{:S(2)}, u32[]{:S(2)}) collective-permute-start(bf16[128,1024]{1,0:T(8,128)(2,1)} %shard_map.77), channel_id=1, source_target_pairs={{0,4},{4,0},{8,12},{12,8},{1,5},{5,1},{9,13},{13,9},{2,6},{6,2},{1... | collective-permute-start | bytes 786440 | tf_op jit(solution)/shard_map/ppermute | solution.py:564
  55.6 2.1 %shard_map.78 = bf16[192,1024]{1,0:T(8,128)(2,1)} custom-call(f32[192,1024]{1,0:T(8,128)} %get-tuple-element.57.total, bf16[192,1024]{1,0:T(8,128)(2,1)S(1)} %collective-permute-done.11.arrived), custom_call_target="tpu_custom_call" | custom-call | flops 1024 | bytes 1024 | tf_op jit(solution)/shard_map/pallas_call | solution.py:482
  57.7 1.9 %collective-permute-start.19 = (bf16[192,1024]{1,0:T(8,128)(2,1)}, bf16[192,1024]{1,0:T(8,128)(2,1)}, u32[]{:S(2)}, u32[]{:S(2)}) collective-permute-start(bf16[192,1024]{1,0:T(8,128)(2,1)} %shard_map.78), channel_id=1, source_target_pairs={{0,4},{4,0},{8,12},{12,8},{1,5},{5,1},{9,13},{13,9},{2,6},{6,2},{1... | collective-permute-start | bytes 1179656 | tf_op jit(solution)/shard_map/ppermute | solution.py:564
  59.6 5.8 %shard_map.79 = (f32[320,1024]{1,0:T(8,128)S(1)}, bf16[320,1024]{1,0:T(8,128)(2,1)S(1)}) custom-call(s32[1]{0:T(128)} %bitcast.outer.flag, f32[8,128]{1,0:T(8,128)S(1)} %select_select_fusion.refs_0_.refs_1_.consts, f32[1,640]{1,0:T(1,128)S(1)} %add_convert_fusion.refs_1_.refs_2_.labels, bf16[320,1024]{1,0:T(8,128)(2,1)} %s_mine.1, ...), custom_call_target="tpu_custom_call" | custom-call | flops 1024 | bytes 1024 | tf_op jit(solution)/shard_map/pallas_call | solution.py:430
  65.6 0.5 collective-permute-start.16
  66.3 0.8 %collective-permute-done.14.rest_0_ = bf16[112,1024]{1,0:T(8,128)(2,1)S(1)} collective-permute-done((bf16[112,1024]{1,0:T(8,128)(2,1)S(1)}, bf16[112,1024]{1,0:T(8,128)(2,1)S(1)}, u32[]{:S(2)}, u32[]{:S(2)}) %collective-permute-start.14) | collective-permute-done | bytes 229408 | tf_op jit(solution)/shard_map/ppermute | solution.py:21
  67.1 0.6 collective-permute-done.17.rest_2_
  67.7 1.0 %shard_map.82 = bf16[320,1024]{1,0:T(8,128)(2,1)} custom-call(f32[320,1024]{1,0:T(8,128)S(1)} %get-tuple-element.64.mine_s, bf16[112,1024]{1,0:T(8,128)(2,1)S(1)} %collective-permute-done.14.rest_0_, bf16[112,1024]{1,0:T(8,128)(2,1)S(1)} %collective-permute-done.16.rest_1_, bf16[96,1024]{1,0:T(8,128)(2,1)S(1)} %collective-permute-done.17.rest_2_), custom_call_target="tpu_custom_call" | custom-call | flops 1024 | bytes 1024 | tf_op jit(solution)/shard_map/pallas_call | solution.py:503
  68.7 0.1 collective-permute-done.19.inside_b
  68.8 1.9 %shard_map.83 = bf16[320,1024]{1,0:T(8,128)(2,1)} custom-call(s32[1]{0:T(128)} %bitcast.outer.flag, f32[320,1024]{1,0:T(8,128)S(1)} %shard_map.81.here_total, bf16[320,1024]{1,0:T(8,128)(2,1)S(1)} %collective-permute-done.18.across_back, bf16[128,1024]{1,0:T(8,128)(2,1)} %collective-permute-done.15.inside_a, bf16[192,1024]{1,0:T(8,128)(2,1)} %collective-permute-done.19.inside_b), custom_call_target="tpu_custom_call" | custom-call | flops 1024 | bytes 1024 | tf_op jit(solution)/shard_map/pallas_call | solution.py:538
  (50 shorter events, 1.2 us)
Async XLA Ops:
  0.6 17.3 %collective-permute-start.3 = (bf16[320,1024]{1,0:T(8,128)(2,1)}, bf16[320,1024]{1,0:T(8,128)(2,1)}, u32[]{:S(2)}, u32[]{:S(2)}) collective-permute-start(bf16[320,1024]{1,0:T(8,128)(2,1)} %refs_5_), channel_id=1, source_target_pairs={{4,8},{8,4},{0,1},{12,13},{5,9},{9,5},{1,0},{13,12},{6,10},{10,6},... | collective-permute-start | bytes 1966088 | tf_op jit(solution)/shard_map/ppermute | solution.py:564
  1.1 19.6 %collective-permute-start.2 = (bf16[320,1024]{1,0:T(8,128)(2,1)}, bf16[320,1024]{1,0:T(8,128)(2,1)S(1)}, u32[]{:S(2)}, u32[]{:S(2)}) collective-permute-start(bf16[320,1024]{1,0:T(8,128)(2,1)} %refs_5_), channel_id=1, source_target_pairs={{0,4},{4,0},{8,12},{12,8},{1,5},{5,1},{9,13},{13,9},{2,6},{6,2},{1... | collective-permute-start | bytes 1966088 | tf_op jit(solution)/shard_map/ppermute | solution.py:564
  6.0 6.8 %collective-permute-start = (s32[1,320]{1,0:T(1,128)S(1)}, s32[1,320]{1,0:T(1,128)S(1)}, u32[]{:S(2)}, u32[]{:S(2)}) collective-permute-start(s32[1,320]{1,0:T(1,128)S(1)} %concatenate.19), channel_id=1, source_target_pairs={{1,0},{0,1},{3,2},{2,3},{5,4},{4,5},{7,6},{6,7},{9,8},{8,9},{11,10... | collective-permute-start | bytes 3848 | tf_op jit(solution)/shard_map/ppermute | solution.py:21
  6.0 6.9 %collective-permute-start.1 = (bf16[320,1024]{1,0:T(8,128)(2,1)}, bf16[320,1024]{1,0:T(8,128)(2,1)S(1)}, u32[]{:S(2)}, u32[]{:S(2)}) collective-permute-start(bf16[320,1024]{1,0:T(8,128)(2,1)} %s_mine.1), channel_id=1, source_target_pairs={{1,0},{0,1},{3,2},{2,3},{5,4},{4,5},{7,6},{6,7},{9,8},{8,9},{11,10... | collective-permute-start | bytes 1966088 | tf_op jit(solution)/shard_map/ppermute | solution.py:21
  9.3 24.8 %collective-permute-start.4 = (bf16[336,1024]{1,0:T(8,128)(2,1)}, bf16[336,1024]{1,0:T(8,128)(2,1)S(1)}, u32[]{:S(2)}, u32[]{:S(2)}) collective-permute-start(bf16[336,1024]{1,0:T(8,128)(2,1)} %pad_maximum_fusion), channel_id=1, source_target_pairs={{0,4},{12,8},{1,5},{13,9},{2,6},{14,10},{3,7},{15,11},{16,20},{28,... | collective-permute-start | bytes 2064392 | tf_op jit(solution)/shard_map/ppermute | solution.py:564
  12.8 0.8 %copy-start.3 = (bf16[320,1024]{1,0:T(8,128)(2,1)}, bf16[320,1024]{1,0:T(8,128)(2,1)S(1)}, u32[]{:S(2)}) copy-start(bf16[320,1024]{1,0:T(8,128)(2,1)S(1)} %collective-permute-done.1.refs_3_.refs_4_.s_other) | copy-start | bytes 1966084
  18.0 19.1 %collective-permute-start.10 = (bf16[320,1024]{1,0:T(8,128)(2,1)}, bf16[320,1024]{1,0:T(8,128)(2,1)}, u32[]{:S(2)}, u32[]{:S(2)}) collective-permute-start(bf16[320,1024]{1,0:T(8,128)(2,1)} %collective-permute-done.3.refs_5_.across), channel_id=1, source_target_pairs={{4,0},{8,12},{5,1},{9,13},{6,2},{10,14},{7,3},{11,15},{20,16},{24,... | collective-permute-start | bytes 1966088 | tf_op jit(solution)/shard_map/ppermute | solution.py:564
  20.8 0.8 %copy-start = (bf16[320,1024]{1,0:T(8,128)(2,1)}, bf16[320,1024]{1,0:T(8,128)(2,1)S(1)}, u32[]{:S(2)}) copy-start(bf16[320,1024]{1,0:T(8,128)(2,1)S(1)} %collective-permute-done.2.refs_4_.whole.refs_5_.side) | copy-start | bytes 1966084
  20.8 6.3 %collective-permute-start.5 = (bf16[128,1024]{1,0:T(8,128)(2,1)S(1)}, bf16[128,1024]{1,0:T(8,128)(2,1)S(1)}, u32[]{:S(2)}, u32[]{:S(2)}) collective-permute-start(bf16[128,1024]{1,0:T(8,128)(2,1)S(1)} %get-tuple-element.44), channel_id=1, source_target_pairs={{4,8},{8,4},{0,1},{12,13},{5,9},{9,5},{1,0},{13,12},{6,10},{10,6},... | collective-permute-start | bytes 786440 | tf_op jit(solution)/shard_map/ppermute | solution.py:564
  20.9 16.2 %collective-permute-start.9 = (bf16[192,1024]{1,0:T(8,128)(2,1)S(1)}, bf16[192,1024]{1,0:T(8,128)(2,1)S(1)}, u32[]{:S(2)}, u32[]{:S(2)}) collective-permute-start(bf16[192,1024]{1,0:T(8,128)(2,1)S(1)} %get-tuple-element.50), channel_id=1, source_target_pairs={{4,8},{8,4},{0,1},{12,13},{5,9},{9,5},{1,0},{13,12},{6,10},{10,6},... | collective-permute-start | bytes 1179656 | tf_op jit(solution)/shard_map/ppermute | solution.py:564
  27.2 9.9 %copy-start.1 = (bf16[128,1024]{1,0:T(8,128)(2,1)}, bf16[128,1024]{1,0:T(8,128)(2,1)S(1)}, u32[]{:S(2)}) copy-start(bf16[128,1024]{1,0:T(8,128)(2,1)S(1)} %collective-permute-done.5.refs_5_.rest_1_) | copy-start | bytes 786436
  34.1 3.0 %collective-permute-start.6 = (bf16[176,1024]{1,0:T(8,128)(2,1)S(1)}, bf16[176,1024]{1,0:T(8,128)(2,1)S(1)}, u32[]{:S(2)}, u32[]{:S(2)}) collective-permute-start(bf16[176,1024]{1,0:T(8,128)(2,1)S(1)} %get-tuple-element.48), channel_id=1, source_target_pairs={{1,0},{0,1},{3,2},{2,3},{5,4},{4,5},{7,6},{6,7},{9,8},{8,9},{11,10... | collective-permute-start | bytes 1081352 | tf_op jit(solution)/shard_map/ppermute | solution.py:21
  34.2 2.9 %collective-permute-start.7 = (bf16[160,1024]{1,0:T(8,128)(2,1)S(1)}, bf16[160,1024]{1,0:T(8,128)(2,1)S(1)}, u32[]{:S(2)}, u32[]{:S(2)}) collective-permute-start(bf16[160,1024]{1,0:T(8,128)(2,1)S(1)} %get-tuple-element.49), channel_id=1, source_target_pairs={{1,0},{0,1},{3,2},{2,3},{5,4},{4,5},{7,6},{6,7},{9,8},{8,9},{11,10... | collective-permute-start | bytes 983048 | tf_op jit(solution)/shard_map/ppermute | solution.py:21
  34.7 10.8 %collective-permute-start.8 = (bf16[128,1024]{1,0:T(8,128)(2,1)S(1)}, bf16[128,1024]{1,0:T(8,128)(2,1)S(1)}, u32[]{:S(2)}, u32[]{:S(2)}) collective-permute-start(bf16[128,1024]{1,0:T(8,128)(2,1)S(1)} %collective-permute-done.5.refs_5_.rest_1_), channel_id=1, source_target_pairs={{0,4},{4,0},{8,12},{12,8},{1,5},{5,1},{9,13},{13,9},{2,6},{6,2},{1... | collective-permute-start | bytes 786440 | tf_op jit(solution)/shard_map/ppermute | solution.py:564
  37.1 0.9 %copy-start.2 = (bf16[192,1024]{1,0:T(8,128)(2,1)}, bf16[192,1024]{1,0:T(8,128)(2,1)S(1)}, u32[]{:S(2)}) copy-start(bf16[192,1024]{1,0:T(8,128)(2,1)S(1)} %collective-permute-done.9.refs_8_.rest_2_) | copy-start | bytes 1179652
  37.2 9.1 %collective-permute-start.13 = (bf16[128,1024]{1,0:T(8,128)(2,1)S(1)}, bf16[128,1024]{1,0:T(8,128)(2,1)S(1)}, u32[]{:S(2)}, u32[]{:S(2)}) collective-permute-start(bf16[128,1024]{1,0:T(8,128)(2,1)S(1)} %shard_map.73), channel_id=1, source_target_pairs={{4,8},{8,4},{0,1},{12,13},{5,9},{9,5},{1,0},{13,12},{6,10},{10,6},... | collective-permute-start | bytes 786440 | tf_op jit(solution)/shard_map/ppermute | solution.py:564
  37.4 18.2 %collective-permute-start.11 = (bf16[192,1024]{1,0:T(8,128)(2,1)S(1)}, bf16[192,1024]{1,0:T(8,128)(2,1)S(1)}, u32[]{:S(2)}, u32[]{:S(2)}) collective-permute-start(bf16[192,1024]{1,0:T(8,128)(2,1)S(1)} %shard_map.74), channel_id=1, source_target_pairs={{4,8},{8,4},{0,1},{12,13},{5,9},{9,5},{1,0},{13,12},{6,10},{10,6},... | collective-permute-start | bytes 1179656 | tf_op jit(solution)/shard_map/ppermute | solution.py:564
  37.9 17.7 %collective-permute-start.12 = (bf16[192,1024]{1,0:T(8,128)(2,1)S(1)}, bf16[192,1024]{1,0:T(8,128)(2,1)S(1)}, u32[]{:S(2)}, u32[]{:S(2)}) collective-permute-start(bf16[192,1024]{1,0:T(8,128)(2,1)S(1)} %collective-permute-done.9.refs_8_.rest_2_), channel_id=1, source_target_pairs={{0,4},{4,0},{8,12},{12,8},{1,5},{5,1},{9,13},{13,9},{2,6},{6,2},{1... | collective-permute-start | bytes 1179656 | tf_op jit(solution)/shard_map/ppermute | solution.py:564
  45.5 0.7 %copy-start.5 = (bf16[128,1024]{1,0:T(8,128)(2,1)}, bf16[128,1024]{1,0:T(8,128)(2,1)S(1)}, u32[]{:S(2)}) copy-start(bf16[128,1024]{1,0:T(8,128)(2,1)S(1)} %collective-permute-done.8.rest_3_) | copy-start | bytes 786436
  47.0 21.7 %collective-permute-start.18 = (bf16[320,1024]{1,0:T(8,128)(2,1)S(1)}, bf16[320,1024]{1,0:T(8,128)(2,1)S(1)}, u32[]{:S(2)}, u32[]{:S(2)}) collective-permute-start(bf16[320,1024]{1,0:T(8,128)(2,1)S(1)} %shard_map.75), channel_id=1, source_target_pairs={{4,8},{8,4},{0,1},{12,13},{5,9},{9,5},{1,0},{13,12},{6,10},{10,6},... | collective-permute-start | bytes 1966088 | tf_op jit(solution)/shard_map/ppermute | solution.py:564
  47.0 19.1 %collective-permute-start.15 = (bf16[128,1024]{1,0:T(8,128)(2,1)}, bf16[128,1024]{1,0:T(8,128)(2,1)}, u32[]{:S(2)}, u32[]{:S(2)}) collective-permute-start(bf16[128,1024]{1,0:T(8,128)(2,1)} %shard_map.77), channel_id=1, source_target_pairs={{0,4},{4,0},{8,12},{12,8},{1,5},{5,1},{9,13},{13,9},{2,6},{6,2},{1... | collective-permute-start | bytes 786440 | tf_op jit(solution)/shard_map/ppermute | solution.py:564
  55.6 2.1 %copy-start.4 = (bf16[192,1024]{1,0:T(8,128)(2,1)}, bf16[192,1024]{1,0:T(8,128)(2,1)S(1)}, u32[]{:S(2)}) copy-start(bf16[192,1024]{1,0:T(8,128)(2,1)S(1)} %collective-permute-done.12.rest_4_) | copy-start | bytes 1179652
  57.7 11.1 %collective-permute-start.19 = (bf16[192,1024]{1,0:T(8,128)(2,1)}, bf16[192,1024]{1,0:T(8,128)(2,1)}, u32[]{:S(2)}, u32[]{:S(2)}) collective-permute-start(bf16[192,1024]{1,0:T(8,128)(2,1)} %shard_map.78), channel_id=1, source_target_pairs={{0,4},{4,0},{8,12},{12,8},{1,5},{5,1},{9,13},{13,9},{2,6},{6,2},{1... | collective-permute-start | bytes 1179656 | tf_op jit(solution)/shard_map/ppermute | solution.py:564
  65.5 1.6 %collective-permute-start.14 = (bf16[112,1024]{1,0:T(8,128)(2,1)S(1)}, bf16[112,1024]{1,0:T(8,128)(2,1)S(1)}, u32[]{:S(2)}, u32[]{:S(2)}) collective-permute-start(bf16[112,1024]{1,0:T(8,128)(2,1)S(1)} %get-tuple-element.66), channel_id=1, source_target_pairs={{1,0},{0,1},{3,2},{2,3},{5,4},{4,5},{7,6},{6,7},{9,8},{8,9},{11,10... | collective-permute-start | bytes 688136 | tf_op jit(solution)/shard_map/ppermute | solution.py:21
  65.6 2.1 %collective-permute-start.16 = (bf16[112,1024]{1,0:T(8,128)(2,1)S(1)}, bf16[112,1024]{1,0:T(8,128)(2,1)S(1)}, u32[]{:S(2)}, u32[]{:S(2)}) collective-permute-start(bf16[112,1024]{1,0:T(8,128)(2,1)S(1)} %get-tuple-element.69), channel_id=1, source_target_pairs={{1,0},{0,1},{3,2},{2,3},{5,4},{4,5},{7,6},{6,7},{9,8},{8,9},{11,10... | collective-permute-start | bytes 688136 | tf_op jit(solution)/shard_map/ppermute | solution.py:21
  66.1 1.6 %collective-permute-start.17 = (bf16[96,1024]{1,0:T(8,128)(2,1)S(1)}, bf16[96,1024]{1,0:T(8,128)(2,1)S(1)}, u32[]{:S(2)}, u32[]{:S(2)}) collective-permute-start(bf16[96,1024]{1,0:T(8,128)(2,1)S(1)} %get-tuple-element.70), channel_id=1, source_target_pairs={{1,0},{0,1},{3,2},{2,3},{5,4},{4,5},{7,6},{6,7},{9,8},{8,9},{11,10... | collective-permute-start | bytes 589832 | tf_op jit(solution)/shard_map/ppermute | solution.py:21

commit v17 on v12

--- a/solution.py
+++ b/solution.py
@@ -488,33 +488,48 @@
     )(in_hbm(total.array) if away else in_vmem(total), in_vmem(arrived))
 
 
-def finish_spectra_body(mine_s, away, inside, *rest):
-    others, (out, near, inside_near, sem) = rest[:-4], rest[-4:]
-    copy = pltpu.make_async_copy(away, near, sem)
-    copy.start()
+def finish_spectra_body(mine_s, inside, *rest):
+    others, (out, near) = rest[:-2], rest[-2:]
     at = 0
     for other in others:
         where = pl.ds(at, other.shape[0])
         out[where] = (mine_s[where] + other[...].astype(jnp.float32)).astype(jnp.bfloat16)
         at += other.shape[0]
-    inside_near[...] = inside[...]
-    copy.wait()
-
-
-def finish_spectra(mine_s, others, away, inside):
+    near[...] = inside[...]
+
+
+def finish_spectra(mine_s, others, inside):
     return pl.pallas_call(
         finish_spectra_body,
         out_shape=[
             jax.ShapeDtypeStruct(mine_s.shape, jnp.bfloat16),
-            vmem_out(away.shape, away.dtype),
             vmem_out(inside.shape, inside.dtype),
         ],
-        in_specs=[VMEM_SPEC, HBM_SPEC] + [VMEM_SPEC] * (1 + len(others)),
-        out_specs=[VMEM_SPEC] * 3,
+        in_specs=[VMEM_SPEC] * (2 + len(others)),
+        out_specs=[VMEM_SPEC] * 2,
+        cost_estimate=SMALL_COST,
+        compiler_params=params(),
+    )(*[in_vmem(a) for a in [mine_s, inside] + others])
+
+
+def bring_body(wanted, away, near, sem):
+    @pl.when(wanted[0] != 0)
+    def _():
+        copy = pltpu.make_async_copy(away, near, sem)
+        copy.start()
+        copy.wait()
+
+
+def bring(wanted, away):
+    return pl.pallas_call(
+        bring_body,
+        out_shape=vmem_out(away.shape, away.dtype),
+        in_specs=[SMEM_SPEC, HBM_SPEC],
+        out_specs=VMEM_SPEC,
         scratch_shapes=[pltpu.SemaphoreType.DMA],
         cost_estimate=SMALL_COST,
         compiler_params=params(),
-    )(in_vmem(mine_s), in_hbm(away), *[in_vmem(a) for a in [inside] + others])
+    )(jnp.int32(wanted).reshape(1), in_hbm(away))
 
 
 def finish_structures_body(flag, here_total, across_back, inside_a, inside_b, out):
@@ -694,8 +709,9 @@
         (last_a, last_b),
     )
     others = [swap_inner(x) for x in split(other_s, (piece, piece, rows - 2 * piece))]
-    grad_spectra, here_total, inside_a = finish_spectra(mine_s, others, here_total, inside_a)
-    across_back = after(across_back, grad_spectra)
+    grad_spectra, inside_a = finish_spectra(mine_s, others, inside_a)
+    here_total = bring(~outer, after(here_total, grad_spectra))
+    across_back = after(across_back, here_total)
     return grad_spectra, finish_structures(outer, here_total, across_back, inside_a, inside_b)
 
 

time: 71.4 us -> 70.2 us (0.983)
  Pallas kernels: 20.6 us -> 19.4 us
    pallas_call x1, Pallas kernels: 2.16 us -> 0.96 us  [finish_spectra(): pl.pallas_call(finish_spectra_body, out_shape=[jax.ShapeDtypeStruct(mine_...]
  transfers between devices with their start and end apart: 20 -> 20, of which waited for: 3 -> 3; matrix products, arithmetic and copies ran while one was open for 5% -> 5% of each run, Pallas kernels for 28% -> 26%
where the time goes in v17:
time: 70.2 us; the launch traced here: 69.8 us
  starting transfers between devices  32.9 us (47%)
  Pallas kernels  19.4 us (28%)
  waiting for transfers between devices  9.83 us (14%)
  other arithmetic  2.98 us (4%)
  local copies, waits for them, and re-layouts  2.36 us (3%)
  between operations  2.33 us (3%)
    ppermute x13, starting transfers between devices, permute(): return lax.ppermute(block, ('blk', 'inner'), pairs)  31.2 us
    pallas_call x8, Pallas kernels, pair_work(): pl.pallas_call(functools.partial(pair_body, plan), out_shape=outs, in_spe...  10.3 us
    ppermute x13, waiting for transfers between devices, permute(): return lax.ppermute(block, ('blk', 'inner'), pairs)  8.31 us
    pallas_call x1, Pallas kernels, spectra_work(): pl.pallas_call(functools.partial(spectra_body, plan), out_shape=[vmem_out...  5.64 us
    concatenate x1, other arithmetic, along_line(): end_mine = permute(jnp.concatenate([spectra, coded]), inward)  2 us
    ppermute x7, starting transfers between devices, from_behind(): return lax.ppermute(block, axis, route)  1.72 us
    unnamed x12, local copies, waits for them, and re-layouts  1.67 us
    ppermute x7, waiting for transfers between devices, from_behind(): return lax.ppermute(block, axis, route)  1.52 us
  transfers between devices with their start and end apart: 20, of which 3 were waited for; matrix products, arithmetic and copies ran while one was open for 5% of the time, Pallas kernels for 26%

profile of v17, /device:TPU:0, one launch (start us, length us, event | category | flops | bytes accessed | tf_op | source)
XLA Modules:
  0.0 69.8 jit_solution(14611245218041148695)
XLA Ops:
  0.6 0.5 collective-permute-start.3
  1.1 4.1 %collective-permute-start.2 = (bf16[320,1024]{1,0:T(8,128)(2,1)}, bf16[320,1024]{1,0:T(8,128)(2,1)S(1)}, u32[]{:S(2)}, u32[]{:S(2)}) collective-permute-start(bf16[320,1024]{1,0:T(8,128)(2,1)} %here), channel_id=1, source_target_pairs={{0,4},{4,0},{8,12},{12,8},{1,5},{5,1},{9,13},{13,9},{2,6},{6,2},{1... | collective-permute-start | bytes 1966088 | tf_op jit(solution)/shard_map/ppermute | solution.py:568
  5.3 0.7 concatenate.19
  6.0 0.5 collective-permute-start.1
  6.5 0.7 %fusion.28 = (bf16[320]{0:T(512)(128)(2,1)S(1)}, bf16[320]{0:T(512)(128)(2,1)S(1)}, bf16[320]{0:T(512)(128)(2,1)S(1)}) fusion(s32[320]{0:T(512)} %param.7), kind=kLoop, calls=%fused_computation.44 | loop fusion | flops 13760 | bytes 3200 | tf_op jit(solution)/shard_map/convert.7
  7.2 0.1 fusion.14
  7.3 2.0 %pad_maximum_fusion = bf16[336,1024]{1,0:T(8,128)(2,1)} fusion(bf16[16,1024]{1,0:T(8,128)(2,1)S(1)} %fusion.14, bf16[320,1024]{1,0:T(8,128)(2,1)} %s_mine.1), kind=kLoop, calls=%fused_computation | loop fusion | flops 1376256 | bytes 1376256 | tf_op jit(solution)/shard_map/concatenate | solution.py:609
  9.3 1.9 %collective-permute-start.4 = (bf16[336,1024]{1,0:T(8,128)(2,1)}, bf16[336,1024]{1,0:T(8,128)(2,1)S(1)}, u32[]{:S(2)}, u32[]{:S(2)}) collective-permute-start(bf16[336,1024]{1,0:T(8,128)(2,1)} %pad_maximum_fusion), channel_id=1, source_target_pairs={{0,4},{12,8},{1,5},{13,9},{2,6},{14,10},{3,7},{15,11},{16,20},{28,... | collective-permute-start | bytes 2064392 | tf_op jit(solution)/shard_map/ppermute | solution.py:568
  12.7 0.1 select_select_fusion.refs_0_.refs_1_.consts
  12.8 0.8 %copy-done.3 = bf16[320,1024]{1,0:T(8,128)(2,1)} copy-done((bf16[320,1024]{1,0:T(8,128)(2,1)}, bf16[320,1024]{1,0:T(8,128)(2,1)S(1)}, u32[]{:S(2)}) %copy-start.3) | copy-done | bytes 655384
  13.7 4.3 %shard_map.68 = (f32[320,1024]{1,0:T(8,128)}, bf16[320,640]{1,0:T(8,128)(2,1)}) custom-call(f32[8,128]{1,0:T(8,128)S(1)} %select_select_fusion.refs_0_.refs_1_.consts, f32[1,640]{1,0:T(1,128)S(1)} %add_convert_fusion.refs_1_.refs_2_.labels, bf16[320,1024]{1,0:T(8,128)(2,1)} %s_mine.1, bf16[320,1024]{1,0:T(8,128)(2,1)} %copy-done.3, bf16[320,1024]{1,0:T(8,128)(2,1)} %here), custom_call_target="tpu_custom_call" | custom-call | flops 1024 | bytes 1024 | tf_op jit(solution)/shard_map/pallas_call | solution.py:340
  18.0 1.3 %collective-permute-start.10 = (bf16[320,1024]{1,0:T(8,128)(2,1)}, bf16[320,1024]{1,0:T(8,128)(2,1)}, u32[]{:S(2)}, u32[]{:S(2)}) collective-permute-start(bf16[320,1024]{1,0:T(8,128)(2,1)} %collective-permute-done.3.refs_5_.across), channel_id=1, source_target_pairs={{4,0},{8,12},{5,1},{9,13},{6,2},{10,14},{7,3},{11,15},{20,16},{24,... | collective-permute-start | bytes 1966088 | tf_op jit(solution)/shard_map/ppermute | solution.py:568
  19.3 1.5 %collective-permute-done.2.refs_4_.whole.refs_5_.side = bf16[320,1024]{1,0:T(8,128)(2,1)S(1)} collective-permute-done((bf16[320,1024]{1,0:T(8,128)(2,1)}, bf16[320,1024]{1,0:T(8,128)(2,1)S(1)}, u32[]{:S(2)}, u32[]{:S(2)}) %collective-permute-start.2) | collective-permute-done | bytes 655392 | tf_op jit(solution)/shard_map/ppermute | solution.py:568
  20.9 0.5 collective-permute-start.9
  21.4 0.2 copy-done
  21.6 5.6 %shard_map.69 = (f32[320,1024]{1,0:T(8,128)}, f32[320,1024]{1,0:T(8,128)}, bf16[320,640]{1,0:T(8,128)(2,1)}, bf16[320,640]{1,0:T(8,128)(2,1)}) custom-call(f32[8,128]{1,0:T(8,128)S(1)} %select_select_fusion.refs_0_.refs_1_.consts, f32[1,640]{1,0:T(1,128)S(1)} %add_convert_fusion.refs_1_.refs_2_.labels, bf16[320,1024]{1,0:T(8,128)(2,1)} %s_mine.1, ...), custom_call_target="tpu_custom_call" | custom-call | flops 1024 | bytes 1024 | tf_op jit(solution)/shard_map/pallas_call | solution.py:340
  27.3 6.8 %collective-permute-done.4.whole.refs_2_.refs_5_ = bf16[336,1024]{1,0:T(8,128)(2,1)S(1)} collective-permute-done((bf16[336,1024]{1,0:T(8,128)(2,1)}, bf16[336,1024]{1,0:T(8,128)(2,1)S(1)}, u32[]{:S(2)}, u32[]{:S(2)}) %collective-permute-start.4) | collective-permute-done | bytes 688160 | tf_op jit(solution)/shard_map/ppermute | solution.py:568
  34.2 0.5 collective-permute-start.7
  34.7 2.4 %collective-permute-start.8 = (bf16[128,1024]{1,0:T(8,128)(2,1)S(1)}, bf16[128,1024]{1,0:T(8,128)(2,1)S(1)}, u32[]{:S(2)}, u32[]{:S(2)}) collective-permute-start(bf16[128,1024]{1,0:T(8,128)(2,1)S(1)} %collective-permute-done.5.refs_5_.rest_1_), channel_id=1, source_target_pairs={{0,4},{4,0},{8,12},{12,8},{1,5},{5,1},{9,13},{13,9},{2,6},{6,2},{1... | collective-permute-start | bytes 786440 | tf_op jit(solution)/shard_map/ppermute | solution.py:568
  37.3 0.1 shard_map.74
  37.4 0.6 collective-permute-start.11
  37.9 7.4 %collective-permute-start.12 = (bf16[192,1024]{1,0:T(8,128)(2,1)S(1)}, bf16[192,1024]{1,0:T(8,128)(2,1)S(1)}, u32[]{:S(2)}, u32[]{:S(2)}) collective-permute-start(bf16[192,1024]{1,0:T(8,128)(2,1)S(1)} %collective-permute-done.9.refs_8_.rest_2_), channel_id=1, source_target_pairs={{0,4},{4,0},{8,12},{12,8},{1,5},{5,1},{9,13},{13,9},{2,6},{6,2},{1... | collective-permute-start | bytes 1179656 | tf_op jit(solution)/shard_map/ppermute | solution.py:568
  45.5 0.1 shard_map.76
  45.6 0.6 copy-done.5
  46.3 8.1 %collective-permute-start.14 = (bf16[128,1024]{1,0:T(8,128)(2,1)S(1)}, bf16[128,1024]{1,0:T(8,128)(2,1)S(1)}, u32[]{:S(2)}, u32[]{:S(2)}) collective-permute-start(bf16[128,1024]{1,0:T(8,128)(2,1)S(1)} %shard_map.77), channel_id=1, source_target_pairs={{0,4},{4,0},{8,12},{12,8},{1,5},{5,1},{9,13},{13,9},{2,6},{6,2},{1... | collective-permute-start | bytes 786440 | tf_op jit(solution)/shard_map/ppermute | solution.py:568
  54.5 1.4 %shard_map.79 = bf16[192,1024]{1,0:T(8,128)(2,1)S(1)} custom-call(f32[192,1024]{1,0:T(8,128)} %get-tuple-element.58.total, bf16[192,1024]{1,0:T(8,128)(2,1)S(1)} %collective-permute-done.11.arrived), custom_call_target="tpu_custom_call" | custom-call | flops 1024 | bytes 1024 | tf_op jit(solution)/shard_map/pallas_call | solution.py:480
  55.9 4.1 %collective-permute-start.19 = (bf16[192,1024]{1,0:T(8,128)(2,1)S(1)}, bf16[192,1024]{1,0:T(8,128)(2,1)S(1)}, u32[]{:S(2)}, u32[]{:S(2)}) collective-permute-start(bf16[192,1024]{1,0:T(8,128)(2,1)S(1)} %shard_map.79), channel_id=1, source_target_pairs={{0,4},{4,0},{8,12},{12,8},{1,5},{5,1},{9,13},{13,9},{2,6},{6,2},{1... | collective-permute-start | bytes 1179656 | tf_op jit(solution)/shard_map/ppermute | solution.py:568
  60.0 5.6 %shard_map.80 = (f32[320,1024]{1,0:T(8,128)S(1)}, bf16[320,1024]{1,0:T(8,128)(2,1)S(1)}) custom-call(s32[1]{0:T(128)} %bitcast.outer.flag, f32[8,128]{1,0:T(8,128)S(1)} %select_select_fusion.refs_0_.refs_1_.consts, f32[1,640]{1,0:T(1,128)S(1)} %add_convert_fusion.refs_1_.refs_2_.labels, bf16[320,1024]{1,0:T(8,128)(2,1)} %s_mine.1, ...), custom_call_target="tpu_custom_call" | custom-call | flops 1024 | bytes 1024 | tf_op jit(solution)/shard_map/pallas_call | solution.py:428
  65.8 0.5 collective-permute-start.16
  66.3 1.5 %collective-permute-done.17.rest_2_ = bf16[96,1024]{1,0:T(8,128)(2,1)S(1)} collective-permute-done((bf16[96,1024]{1,0:T(8,128)(2,1)S(1)}, bf16[96,1024]{1,0:T(8,128)(2,1)S(1)}, u32[]{:S(2)}, u32[]{:S(2)}) %collective-permute-start.17) | collective-permute-done | bytes 196640 | tf_op jit(solution)/shard_map/ppermute | solution.py:21
  67.9 1.0 %shard_map.82 = (bf16[320,1024]{1,0:T(8,128)(2,1)}, bf16[128,1024]{1,0:T(8,128)(2,1)S(1)}) custom-call(f32[320,1024]{1,0:T(8,128)S(1)} %get-tuple-element.66.mine_s, bf16[128,1024]{1,0:T(8,128)(2,1)S(1)} %collective-permute-done.14.inside, bf16[112,1024]{1,0:T(8,128)(2,1)S(1)} %collective-permute-done.15.rest_0_, ...), custom_call_target="tpu_custom_call" | custom-call | flops 1024 | bytes 1024 | tf_op jit(solution)/shard_map/pallas_call | solution.py:502
  68.9 0.9 %shard_map.84 = bf16[320,1024]{1,0:T(8,128)(2,1)} custom-call(s32[1]{0:T(128)} %bitcast.outer.flag, f32[320,1024]{1,0:T(8,128)S(1)} %shard_map.83.here_total, bf16[320,1024]{1,0:T(8,128)(2,1)S(1)} %collective-permute-done.18.across_back, bf16[128,1024]{1,0:T(8,128)(2,1)S(1)} %get-tuple-element.75.inside_a, bf16[192,1024]{1,0:T(8,128)(2,1)S(1)} %collective-permute-done.19.inside_b), custom_call_target="tpu_custom_call" | custom-call | flops 1024 | bytes 1024 | tf_op jit(solution)/shard_map/pallas_call | solution.py:549
  (51 shorter events, 1.1 us)
Async XLA Ops:
  0.6 17.3 %collective-permute-start.3 = (bf16[320,1024]{1,0:T(8,128)(2,1)}, bf16[320,1024]{1,0:T(8,128)(2,1)}, u32[]{:S(2)}, u32[]{:S(2)}) collective-permute-start(bf16[320,1024]{1,0:T(8,128)(2,1)} %here), channel_id=1, source_target_pairs={{4,8},{8,4},{0,1},{12,13},{5,9},{9,5},{1,0},{13,12},{6,10},{10,6},... | collective-permute-start | bytes 1966088 | tf_op jit(solution)/shard_map/ppermute | solution.py:568
  1.1 19.6 %collective-permute-start.2 = (bf16[320,1024]{1,0:T(8,128)(2,1)}, bf16[320,1024]{1,0:T(8,128)(2,1)S(1)}, u32[]{:S(2)}, u32[]{:S(2)}) collective-permute-start(bf16[320,1024]{1,0:T(8,128)(2,1)} %here), channel_id=1, source_target_pairs={{0,4},{4,0},{8,12},{12,8},{1,5},{5,1},{9,13},{13,9},{2,6},{6,2},{1... | collective-permute-start | bytes 1966088 | tf_op jit(solution)/shard_map/ppermute | solution.py:568
  6.0 6.8 %collective-permute-start = (s32[1,320]{1,0:T(1,128)S(1)}, s32[1,320]{1,0:T(1,128)S(1)}, u32[]{:S(2)}, u32[]{:S(2)}) collective-permute-start(s32[1,320]{1,0:T(1,128)S(1)} %concatenate.19), channel_id=1, source_target_pairs={{1,0},{0,1},{3,2},{2,3},{5,4},{4,5},{7,6},{6,7},{9,8},{8,9},{11,10... | collective-permute-start | bytes 3848 | tf_op jit(solution)/shard_map/ppermute | solution.py:21
  6.0 6.9 %collective-permute-start.1 = (bf16[320,1024]{1,0:T(8,128)(2,1)}, bf16[320,1024]{1,0:T(8,128)(2,1)S(1)}, u32[]{:S(2)}, u32[]{:S(2)}) collective-permute-start(bf16[320,1024]{1,0:T(8,128)(2,1)} %s_mine.1), channel_id=1, source_target_pairs={{1,0},{0,1},{3,2},{2,3},{5,4},{4,5},{7,6},{6,7},{9,8},{8,9},{11,10... | collective-permute-start | bytes 1966088 | tf_op jit(solution)/shard_map/ppermute | solution.py:21
  9.3 24.7 %collective-permute-start.4 = (bf16[336,1024]{1,0:T(8,128)(2,1)}, bf16[336,1024]{1,0:T(8,128)(2,1)S(1)}, u32[]{:S(2)}, u32[]{:S(2)}) collective-permute-start(bf16[336,1024]{1,0:T(8,128)(2,1)} %pad_maximum_fusion), channel_id=1, source_target_pairs={{0,4},{12,8},{1,5},{13,9},{2,6},{14,10},{3,7},{15,11},{16,20},{28,... | collective-permute-start | bytes 2064392 | tf_op jit(solution)/shard_map/ppermute | solution.py:568
  12.8 0.8 %copy-start.3 = (bf16[320,1024]{1,0:T(8,128)(2,1)}, bf16[320,1024]{1,0:T(8,128)(2,1)S(1)}, u32[]{:S(2)}) copy-start(bf16[320,1024]{1,0:T(8,128)(2,1)S(1)} %collective-permute-done.1.refs_3_.refs_4_.s_other) | copy-start | bytes 1966084
  18.0 19.1 %collective-permute-start.10 = (bf16[320,1024]{1,0:T(8,128)(2,1)}, bf16[320,1024]{1,0:T(8,128)(2,1)}, u32[]{:S(2)}, u32[]{:S(2)}) collective-permute-start(bf16[320,1024]{1,0:T(8,128)(2,1)} %collective-permute-done.3.refs_5_.across), channel_id=1, source_target_pairs={{4,0},{8,12},{5,1},{9,13},{6,2},{10,14},{7,3},{11,15},{20,16},{24,... | collective-permute-start | bytes 1966088 | tf_op jit(solution)/shard_map/ppermute | solution.py:568
  20.8 0.8 %copy-start = (bf16[320,1024]{1,0:T(8,128)(2,1)}, bf16[320,1024]{1,0:T(8,128)(2,1)S(1)}, u32[]{:S(2)}) copy-start(bf16[320,1024]{1,0:T(8,128)(2,1)S(1)} %collective-permute-done.2.refs_4_.whole.refs_5_.side) | copy-start | bytes 1966084
  20.8 6.4 %collective-permute-start.5 = (bf16[128,1024]{1,0:T(8,128)(2,1)S(1)}, bf16[128,1024]{1,0:T(8,128)(2,1)S(1)}, u32[]{:S(2)}, u32[]{:S(2)}) collective-permute-start(bf16[128,1024]{1,0:T(8,128)(2,1)S(1)} %get-tuple-element.45), channel_id=1, source_target_pairs={{4,8},{8,4},{0,1},{12,13},{5,9},{9,5},{1,0},{13,12},{6,10},{10,6},... | collective-permute-start | bytes 786440 | tf_op jit(solution)/shard_map/ppermute | solution.py:568
  20.9 16.2 %collective-permute-start.9 = (bf16[192,1024]{1,0:T(8,128)(2,1)S(1)}, bf16[192,1024]{1,0:T(8,128)(2,1)S(1)}, u32[]{:S(2)}, u32[]{:S(2)}) collective-permute-start(bf16[192,1024]{1,0:T(8,128)(2,1)S(1)} %get-tuple-element.51), channel_id=1, source_target_pairs={{4,8},{8,4},{0,1},{12,13},{5,9},{9,5},{1,0},{13,12},{6,10},{10,6},... | collective-permute-start | bytes 1179656 | tf_op jit(solution)/shard_map/ppermute | solution.py:568
  27.2 9.9 %copy-start.1 = (bf16[128,1024]{1,0:T(8,128)(2,1)}, bf16[128,1024]{1,0:T(8,128)(2,1)S(1)}, u32[]{:S(2)}) copy-start(bf16[128,1024]{1,0:T(8,128)(2,1)S(1)} %collective-permute-done.5.refs_5_.rest_1_) | copy-start | bytes 786436
  34.1 3.0 %collective-permute-start.6 = (bf16[176,1024]{1,0:T(8,128)(2,1)S(1)}, bf16[176,1024]{1,0:T(8,128)(2,1)S(1)}, u32[]{:S(2)}, u32[]{:S(2)}) collective-permute-start(bf16[176,1024]{1,0:T(8,128)(2,1)S(1)} %get-tuple-element.49), channel_id=1, source_target_pairs={{1,0},{0,1},{3,2},{2,3},{5,4},{4,5},{7,6},{6,7},{9,8},{8,9},{11,10... | collective-permute-start | bytes 1081352 | tf_op jit(solution)/shard_map/ppermute | solution.py:21
  34.2 2.9 %collective-permute-start.7 = (bf16[160,1024]{1,0:T(8,128)(2,1)S(1)}, bf16[160,1024]{1,0:T(8,128)(2,1)S(1)}, u32[]{:S(2)}, u32[]{:S(2)}) collective-permute-start(bf16[160,1024]{1,0:T(8,128)(2,1)S(1)} %get-tuple-element.50), channel_id=1, source_target_pairs={{1,0},{0,1},{3,2},{2,3},{5,4},{4,5},{7,6},{6,7},{9,8},{8,9},{11,10... | collective-permute-start | bytes 983048 | tf_op jit(solution)/shard_map/ppermute | solution.py:21
  34.7 10.8 %collective-permute-start.8 = (bf16[128,1024]{1,0:T(8,128)(2,1)S(1)}, bf16[128,1024]{1,0:T(8,128)(2,1)S(1)}, u32[]{:S(2)}, u32[]{:S(2)}) collective-permute-start(bf16[128,1024]{1,0:T(8,128)(2,1)S(1)} %collective-permute-done.5.refs_5_.rest_1_), channel_id=1, source_target_pairs={{0,4},{4,0},{8,12},{12,8},{1,5},{5,1},{9,13},{13,9},{2,6},{6,2},{1... | collective-permute-start | bytes 786440 | tf_op jit(solution)/shard_map/ppermute | solution.py:568
  37.1 0.9 %copy-start.2 = (bf16[192,1024]{1,0:T(8,128)(2,1)}, bf16[192,1024]{1,0:T(8,128)(2,1)S(1)}, u32[]{:S(2)}) copy-start(bf16[192,1024]{1,0:T(8,128)(2,1)S(1)} %collective-permute-done.9.refs_8_.rest_2_) | copy-start | bytes 1179652
  37.2 9.0 %collective-permute-start.13 = (bf16[128,1024]{1,0:T(8,128)(2,1)S(1)}, bf16[128,1024]{1,0:T(8,128)(2,1)S(1)}, u32[]{:S(2)}, u32[]{:S(2)}) collective-permute-start(bf16[128,1024]{1,0:T(8,128)(2,1)S(1)} %shard_map.73), channel_id=1, source_target_pairs={{4,8},{8,4},{0,1},{12,13},{5,9},{9,5},{1,0},{13,12},{6,10},{10,6},... | collective-permute-start | bytes 786440 | tf_op jit(solution)/shard_map/ppermute | solution.py:568
  37.4 17.1 %collective-permute-start.11 = (bf16[192,1024]{1,0:T(8,128)(2,1)S(1)}, bf16[192,1024]{1,0:T(8,128)(2,1)S(1)}, u32[]{:S(2)}, u32[]{:S(2)}) collective-permute-start(bf16[192,1024]{1,0:T(8,128)(2,1)S(1)} %shard_map.74), channel_id=1, source_target_pairs={{4,8},{8,4},{0,1},{12,13},{5,9},{9,5},{1,0},{13,12},{6,10},{10,6},... | collective-permute-start | bytes 1179656 | tf_op jit(solution)/shard_map/ppermute | solution.py:568
  37.9 16.5 %collective-permute-start.12 = (bf16[192,1024]{1,0:T(8,128)(2,1)S(1)}, bf16[192,1024]{1,0:T(8,128)(2,1)S(1)}, u32[]{:S(2)}, u32[]{:S(2)}) collective-permute-start(bf16[192,1024]{1,0:T(8,128)(2,1)S(1)} %collective-permute-done.9.refs_8_.rest_2_), channel_id=1, source_target_pairs={{0,4},{4,0},{8,12},{12,8},{1,5},{5,1},{9,13},{13,9},{2,6},{6,2},{1... | collective-permute-start | bytes 1179656 | tf_op jit(solution)/shard_map/ppermute | solution.py:568
  45.5 0.7 %copy-start.5 = (bf16[128,1024]{1,0:T(8,128)(2,1)}, bf16[128,1024]{1,0:T(8,128)(2,1)S(1)}, u32[]{:S(2)}) copy-start(bf16[128,1024]{1,0:T(8,128)(2,1)S(1)} %collective-permute-done.8.rest_3_) | copy-start | bytes 786436
  46.2 22.6 %collective-permute-start.18 = (bf16[320,1024]{1,0:T(8,128)(2,1)S(1)}, bf16[320,1024]{1,0:T(8,128)(2,1)S(1)}, u32[]{:S(2)}, u32[]{:S(2)}) collective-permute-start(bf16[320,1024]{1,0:T(8,128)(2,1)S(1)} %shard_map.75), channel_id=1, source_target_pairs={{4,8},{8,4},{0,1},{12,13},{5,9},{9,5},{1,0},{13,12},{6,10},{10,6},... | collective-permute-start | bytes 1966088 | tf_op jit(solution)/shard_map/ppermute | solution.py:568
  46.3 19.9 %collective-permute-start.14 = (bf16[128,1024]{1,0:T(8,128)(2,1)S(1)}, bf16[128,1024]{1,0:T(8,128)(2,1)S(1)}, u32[]{:S(2)}, u32[]{:S(2)}) collective-permute-start(bf16[128,1024]{1,0:T(8,128)(2,1)S(1)} %shard_map.77), channel_id=1, source_target_pairs={{0,4},{4,0},{8,12},{12,8},{1,5},{5,1},{9,13},{13,9},{2,6},{6,2},{1... | collective-permute-start | bytes 786440 | tf_op jit(solution)/shard_map/ppermute | solution.py:568
  54.5 1.4 %copy-start.4 = (bf16[192,1024]{1,0:T(8,128)(2,1)}, bf16[192,1024]{1,0:T(8,128)(2,1)S(1)}, u32[]{:S(2)}) copy-start(bf16[192,1024]{1,0:T(8,128)(2,1)S(1)} %collective-permute-done.12.rest_4_) | copy-start | bytes 1179652
  55.9 13.0 %collective-permute-start.19 = (bf16[192,1024]{1,0:T(8,128)(2,1)S(1)}, bf16[192,1024]{1,0:T(8,128)(2,1)S(1)}, u32[]{:S(2)}, u32[]{:S(2)}) collective-permute-start(bf16[192,1024]{1,0:T(8,128)(2,1)S(1)} %shard_map.79), channel_id=1, source_target_pairs={{0,4},{4,0},{8,12},{12,8},{1,5},{5,1},{9,13},{13,9},{2,6},{6,2},{1... | collective-permute-start | bytes 1179656 | tf_op jit(solution)/shard_map/ppermute | solution.py:568
  65.7 2.2 %collective-permute-start.15 = (bf16[112,1024]{1,0:T(8,128)(2,1)S(1)}, bf16[112,1024]{1,0:T(8,128)(2,1)S(1)}, u32[]{:S(2)}, u32[]{:S(2)}) collective-permute-start(bf16[112,1024]{1,0:T(8,128)(2,1)S(1)} %get-tuple-element.68), channel_id=1, source_target_pairs={{1,0},{0,1},{3,2},{2,3},{5,4},{4,5},{7,6},{6,7},{9,8},{8,9},{11,10... | collective-permute-start | bytes 688136 | tf_op jit(solution)/shard_map/ppermute | solution.py:21
  65.8 2.1 %collective-permute-start.16 = (bf16[112,1024]{1,0:T(8,128)(2,1)S(1)}, bf16[112,1024]{1,0:T(8,128)(2,1)S(1)}, u32[]{:S(2)}, u32[]{:S(2)}) collective-permute-start(bf16[112,1024]{1,0:T(8,128)(2,1)S(1)} %get-tuple-element.69), channel_id=1, source_target_pairs={{1,0},{0,1},{3,2},{2,3},{5,4},{4,5},{7,6},{6,7},{9,8},{8,9},{11,10... | collective-permute-start | bytes 688136 | tf_op jit(solution)/shard_map/ppermute | solution.py:21
  66.3 1.6 %collective-permute-start.17 = (bf16[96,1024]{1,0:T(8,128)(2,1)S(1)}, bf16[96,1024]{1,0:T(8,128)(2,1)S(1)}, u32[]{:S(2)}, u32[]{:S(2)}) collective-permute-start(bf16[96,1024]{1,0:T(8,128)(2,1)S(1)} %get-tuple-element.70), channel_id=1, source_target_pairs={{1,0},{0,1},{3,2},{2,3},{5,4},{4,5},{7,6},{6,7},{9,8},{8,9},{11,10... | collective-permute-start | bytes 589832 | tf_op jit(solution)/shard_map/ppermute | solution.py:21

commit v18 on v17

--- a/solution.py
+++ b/solution.py
@@ -389,7 +389,7 @@
         for copy in fill(list(nexts) + list(lasts), held, 2 * rows):
             copy.wait()
 
-    for copy in moves:
+    for copy in moves[:2]:
         copy.wait()
     scale, shift = consts[0:1, 0:1], consts[1:2, 0:1]
 
@@ -411,6 +411,8 @@
         work_out(2 * rows, FAR_ROW)
 
     work_out(3 * rows, LAST_ROW)
+    for copy in moves[2:]:
+        copy.wait()
     for i, out in enumerate((mine_out, other_out)):
         total = lax.dot_general(
             coefs[:, i * rows : (i + 1) * rows],

time: 70.2 us -> 70.4 us (level)
  transfers between devices with their start and end apart: 20 -> 20, of which waited for: 3 -> 3; matrix products, arithmetic and copies ran while one was open for 5% -> 5% of each run, Pallas kernels for 26% -> 27%
where the time goes in v18:
time: 70.4 us; the launch traced here: 69.9 us
  starting transfers between devices  32.9 us (47%)
  Pallas kernels  19.5 us (28%)
  waiting for transfers between devices  9.83 us (14%)
  other arithmetic  2.98 us (4%)
  local copies, waits for them, and re-layouts  2.36 us (3%)
  between operations  2.33 us (3%)
    ppermute x13, starting transfers between devices, permute(): return lax.ppermute(block, ('blk', 'inner'), pairs)  31.2 us
    pallas_call x8, Pallas kernels, pair_work(): pl.pallas_call(functools.partial(pair_body, plan), out_shape=outs, in_spe...  10.3 us
    ppermute x13, waiting for transfers between devices, permute(): return lax.ppermute(block, ('blk', 'inner'), pairs)  8.31 us
    pallas_call x1, Pallas kernels, spectra_work(): pl.pallas_call(functools.partial(spectra_body, plan), out_shape=[vmem_out...  5.82 us
    concatenate x1, other arithmetic, along_line(): end_mine = permute(jnp.concatenate([spectra, coded]), inward)  2 us
    ppermute x7, starting transfers between devices, from_behind(): return lax.ppermute(block, axis, route)  1.72 us
    unnamed x12, local copies, waits for them, and re-layouts  1.67 us
    ppermute x7, waiting for transfers between devices, from_behind(): return lax.ppermute(block, axis, route)  1.52 us
  transfers between devices with their start and end apart: 20, of which 3 were waited for; matrix products, arithmetic and copies ran while one was open for 5% of the time, Pallas kernels for 27%

profile of v18, /device:TPU:0, one launch (start us, length us, event | category | flops | bytes accessed | tf_op | source)
XLA Modules:
  0.0 69.9 jit_solution(14598230962172523763)
XLA Ops:
  0.6 0.5 collective-permute-start.3
  1.1 4.1 %collective-permute-start.2 = (bf16[320,1024]{1,0:T(8,128)(2,1)}, bf16[320,1024]{1,0:T(8,128)(2,1)S(1)}, u32[]{:S(2)}, u32[]{:S(2)}) collective-permute-start(bf16[320,1024]{1,0:T(8,128)(2,1)} %here), channel_id=1, source_target_pairs={{0,4},{4,0},{8,12},{12,8},{1,5},{5,1},{9,13},{13,9},{2,6},{6,2},{1... | collective-permute-start | bytes 1966088 | tf_op jit(solution)/shard_map/ppermute | solution.py:570
  5.3 0.7 concatenate.19
  6.0 0.5 collective-permute-start.1
  6.5 0.7 fusion.28
  7.2 0.1 fusion.14
  7.3 2.0 %pad_maximum_fusion = bf16[336,1024]{1,0:T(8,128)(2,1)} fusion(bf16[16,1024]{1,0:T(8,128)(2,1)S(1)} %fusion.14, bf16[320,1024]{1,0:T(8,128)(2,1)} %s_mine.1), kind=kLoop, calls=%fused_computation | loop fusion | flops 1376256 | bytes 1376256 | tf_op jit(solution)/shard_map/concatenate | solution.py:611
  9.3 1.9 %collective-permute-start.4 = (bf16[336,1024]{1,0:T(8,128)(2,1)}, bf16[336,1024]{1,0:T(8,128)(2,1)S(1)}, u32[]{:S(2)}, u32[]{:S(2)}) collective-permute-start(bf16[336,1024]{1,0:T(8,128)(2,1)} %pad_maximum_fusion), channel_id=1, source_target_pairs={{0,4},{12,8},{1,5},{13,9},{2,6},{14,10},{3,7},{15,11},{16,20},{28,... | collective-permute-start | bytes 2064392 | tf_op jit(solution)/shard_map/ppermute | solution.py:570
  12.7 0.1 select_select_fusion.refs_0_.refs_1_.consts
  12.8 0.8 %copy-done.3 = bf16[320,1024]{1,0:T(8,128)(2,1)} copy-done((bf16[320,1024]{1,0:T(8,128)(2,1)}, bf16[320,1024]{1,0:T(8,128)(2,1)S(1)}, u32[]{:S(2)}) %copy-start.3) | copy-done | bytes 655384
  13.7 4.3 %shard_map.68 = (f32[320,1024]{1,0:T(8,128)}, bf16[320,640]{1,0:T(8,128)(2,1)}) custom-call(f32[8,128]{1,0:T(8,128)S(1)} %select_select_fusion.refs_0_.refs_1_.consts, f32[1,640]{1,0:T(1,128)S(1)} %add_convert_fusion.refs_1_.refs_2_.labels, bf16[320,1024]{1,0:T(8,128)(2,1)} %s_mine.1, bf16[320,1024]{1,0:T(8,128)(2,1)} %copy-done.3, bf16[320,1024]{1,0:T(8,128)(2,1)} %here), custom_call_target="tpu_custom_call" | custom-call | flops 1024 | bytes 1024 | tf_op jit(solution)/shard_map/pallas_call | solution.py:340
  18.0 1.3 %collective-permute-start.10 = (bf16[320,1024]{1,0:T(8,128)(2,1)}, bf16[320,1024]{1,0:T(8,128)(2,1)}, u32[]{:S(2)}, u32[]{:S(2)}) collective-permute-start(bf16[320,1024]{1,0:T(8,128)(2,1)} %collective-permute-done.3.refs_5_.across), channel_id=1, source_target_pairs={{4,0},{8,12},{5,1},{9,13},{6,2},{10,14},{7,3},{11,15},{20,16},{24,... | collective-permute-start | bytes 1966088 | tf_op jit(solution)/shard_map/ppermute | solution.py:570
  19.3 1.5 %collective-permute-done.2.refs_4_.whole.refs_5_.side = bf16[320,1024]{1,0:T(8,128)(2,1)S(1)} collective-permute-done((bf16[320,1024]{1,0:T(8,128)(2,1)}, bf16[320,1024]{1,0:T(8,128)(2,1)S(1)}, u32[]{:S(2)}, u32[]{:S(2)}) %collective-permute-start.2) | collective-permute-done | bytes 655392 | tf_op jit(solution)/shard_map/ppermute | solution.py:570
  20.9 0.5 collective-permute-start.9
  21.4 0.2 copy-done
  21.6 5.6 %shard_map.69 = (f32[320,1024]{1,0:T(8,128)}, f32[320,1024]{1,0:T(8,128)}, bf16[320,640]{1,0:T(8,128)(2,1)}, bf16[320,640]{1,0:T(8,128)(2,1)}) custom-call(f32[8,128]{1,0:T(8,128)S(1)} %select_select_fusion.refs_0_.refs_1_.consts, f32[1,640]{1,0:T(1,128)S(1)} %add_convert_fusion.refs_1_.refs_2_.labels, bf16[320,1024]{1,0:T(8,128)(2,1)} %s_mine.1, ...), custom_call_target="tpu_custom_call" | custom-call | flops 1024 | bytes 1024 | tf_op jit(solution)/shard_map/pallas_call | solution.py:340
  27.3 6.8 %collective-permute-done.4.whole.refs_2_.refs_5_ = bf16[336,1024]{1,0:T(8,128)(2,1)S(1)} collective-permute-done((bf16[336,1024]{1,0:T(8,128)(2,1)}, bf16[336,1024]{1,0:T(8,128)(2,1)S(1)}, u32[]{:S(2)}, u32[]{:S(2)}) %collective-permute-start.4) | collective-permute-done | bytes 688160 | tf_op jit(solution)/shard_map/ppermute | solution.py:570
  34.2 0.5 collective-permute-start.7
  34.7 2.4 %collective-permute-start.8 = (bf16[128,1024]{1,0:T(8,128)(2,1)S(1)}, bf16[128,1024]{1,0:T(8,128)(2,1)S(1)}, u32[]{:S(2)}, u32[]{:S(2)}) collective-permute-start(bf16[128,1024]{1,0:T(8,128)(2,1)S(1)} %collective-permute-done.5.refs_5_.rest_1_), channel_id=1, source_target_pairs={{0,4},{4,0},{8,12},{12,8},{1,5},{5,1},{9,13},{13,9},{2,6},{6,2},{1... | collective-permute-start | bytes 786440 | tf_op jit(solution)/shard_map/ppermute | solution.py:570
  37.3 0.1 shard_map.74
  37.4 0.6 collective-permute-start.11
  37.9 7.4 %collective-permute-start.12 = (bf16[192,1024]{1,0:T(8,128)(2,1)S(1)}, bf16[192,1024]{1,0:T(8,128)(2,1)S(1)}, u32[]{:S(2)}, u32[]{:S(2)}) collective-permute-start(bf16[192,1024]{1,0:T(8,128)(2,1)S(1)} %collective-permute-done.9.refs_8_.rest_2_), channel_id=1, source_target_pairs={{0,4},{4,0},{8,12},{12,8},{1,5},{5,1},{9,13},{13,9},{2,6},{6,2},{1... | collective-permute-start | bytes 1179656 | tf_op jit(solution)/shard_map/ppermute | solution.py:570
  45.5 0.1 shard_map.76
  45.6 0.6 copy-done.5
  46.3 8.1 %collective-permute-start.14 = (bf16[128,1024]{1,0:T(8,128)(2,1)S(1)}, bf16[128,1024]{1,0:T(8,128)(2,1)S(1)}, u32[]{:S(2)}, u32[]{:S(2)}) collective-permute-start(bf16[128,1024]{1,0:T(8,128)(2,1)S(1)} %shard_map.77), channel_id=1, source_target_pairs={{0,4},{4,0},{8,12},{12,8},{1,5},{5,1},{9,13},{13,9},{2,6},{6,2},{1... | collective-permute-start | bytes 786440 | tf_op jit(solution)/shard_map/ppermute | solution.py:570
  54.5 1.4 %shard_map.79 = bf16[192,1024]{1,0:T(8,128)(2,1)S(1)} custom-call(f32[192,1024]{1,0:T(8,128)} %get-tuple-element.58.total, bf16[192,1024]{1,0:T(8,128)(2,1)S(1)} %collective-permute-done.11.arrived), custom_call_target="tpu_custom_call" | custom-call | flops 1024 | bytes 1024 | tf_op jit(solution)/shard_map/pallas_call | solution.py:482
  55.9 4.1 %collective-permute-start.19 = (bf16[192,1024]{1,0:T(8,128)(2,1)S(1)}, bf16[192,1024]{1,0:T(8,128)(2,1)S(1)}, u32[]{:S(2)}, u32[]{:S(2)}) collective-permute-start(bf16[192,1024]{1,0:T(8,128)(2,1)S(1)} %shard_map.79), channel_id=1, source_target_pairs={{0,4},{4,0},{8,12},{12,8},{1,5},{5,1},{9,13},{13,9},{2,6},{6,2},{1... | collective-permute-start | bytes 1179656 | tf_op jit(solution)/shard_map/ppermute | solution.py:570
  60.0 5.8 %shard_map.80 = (f32[320,1024]{1,0:T(8,128)S(1)}, bf16[320,1024]{1,0:T(8,128)(2,1)S(1)}) custom-call(s32[1]{0:T(128)} %bitcast.outer.flag, f32[8,128]{1,0:T(8,128)S(1)} %select_select_fusion.refs_0_.refs_1_.consts, f32[1,640]{1,0:T(1,128)S(1)} %add_convert_fusion.refs_1_.refs_2_.labels, bf16[320,1024]{1,0:T(8,128)(2,1)} %s_mine.1, ...), custom_call_target="tpu_custom_call" | custom-call | flops 1024 | bytes 1024 | tf_op jit(solution)/shard_map/pallas_call | solution.py:430
  65.9 0.5 collective-permute-start.16
  66.5 1.5 %collective-permute-done.17.rest_2_ = bf16[96,1024]{1,0:T(8,128)(2,1)S(1)} collective-permute-done((bf16[96,1024]{1,0:T(8,128)(2,1)S(1)}, bf16[96,1024]{1,0:T(8,128)(2,1)S(1)}, u32[]{:S(2)}, u32[]{:S(2)}) %collective-permute-start.17) | collective-permute-done | bytes 196640 | tf_op jit(solution)/shard_map/ppermute | solution.py:21
  68.0 1.0 %shard_map.82 = (bf16[320,1024]{1,0:T(8,128)(2,1)}, bf16[128,1024]{1,0:T(8,128)(2,1)S(1)}) custom-call(f32[320,1024]{1,0:T(8,128)S(1)} %get-tuple-element.66.mine_s, bf16[128,1024]{1,0:T(8,128)(2,1)S(1)} %collective-permute-done.14.inside, bf16[112,1024]{1,0:T(8,128)(2,1)S(1)} %collective-permute-done.15.rest_0_, ...), custom_call_target="tpu_custom_call" | custom-call | flops 1024 | bytes 1024 | tf_op jit(solution)/shard_map/pallas_call | solution.py:504
  69.0 0.9 %shard_map.84 = bf16[320,1024]{1,0:T(8,128)(2,1)} custom-call(s32[1]{0:T(128)} %bitcast.outer.flag, f32[320,1024]{1,0:T(8,128)S(1)} %shard_map.83.here_total, bf16[320,1024]{1,0:T(8,128)(2,1)S(1)} %collective-permute-done.18.across_back, bf16[128,1024]{1,0:T(8,128)(2,1)S(1)} %get-tuple-element.75.inside_a, bf16[192,1024]{1,0:T(8,128)(2,1)S(1)} %collective-permute-done.19.inside_b), custom_call_target="tpu_custom_call" | custom-call | flops 1024 | bytes 1024 | tf_op jit(solution)/shard_map/pallas_call | solution.py:551
  (51 shorter events, 1.1 us)
Async XLA Ops:
  0.6 17.3 %collective-permute-start.3 = (bf16[320,1024]{1,0:T(8,128)(2,1)}, bf16[320,1024]{1,0:T(8,128)(2,1)}, u32[]{:S(2)}, u32[]{:S(2)}) collective-permute-start(bf16[320,1024]{1,0:T(8,128)(2,1)} %here), channel_id=1, source_target_pairs={{4,8},{8,4},{0,1},{12,13},{5,9},{9,5},{1,0},{13,12},{6,10},{10,6},... | collective-permute-start | bytes 1966088 | tf_op jit(solution)/shard_map/ppermute | solution.py:570
  1.1 19.6 %collective-permute-start.2 = (bf16[320,1024]{1,0:T(8,128)(2,1)}, bf16[320,1024]{1,0:T(8,128)(2,1)S(1)}, u32[]{:S(2)}, u32[]{:S(2)}) collective-permute-start(bf16[320,1024]{1,0:T(8,128)(2,1)} %here), channel_id=1, source_target_pairs={{0,4},{4,0},{8,12},{12,8},{1,5},{5,1},{9,13},{13,9},{2,6},{6,2},{1... | collective-permute-start | bytes 1966088 | tf_op jit(solution)/shard_map/ppermute | solution.py:570
  6.0 6.8 %collective-permute-start = (s32[1,320]{1,0:T(1,128)S(1)}, s32[1,320]{1,0:T(1,128)S(1)}, u32[]{:S(2)}, u32[]{:S(2)}) collective-permute-start(s32[1,320]{1,0:T(1,128)S(1)} %concatenate.19), channel_id=1, source_target_pairs={{1,0},{0,1},{3,2},{2,3},{5,4},{4,5},{7,6},{6,7},{9,8},{8,9},{11,10... | collective-permute-start | bytes 3848 | tf_op jit(solution)/shard_map/ppermute | solution.py:21
  6.0 6.9 %collective-permute-start.1 = (bf16[320,1024]{1,0:T(8,128)(2,1)}, bf16[320,1024]{1,0:T(8,128)(2,1)S(1)}, u32[]{:S(2)}, u32[]{:S(2)}) collective-permute-start(bf16[320,1024]{1,0:T(8,128)(2,1)} %s_mine.1), channel_id=1, source_target_pairs={{1,0},{0,1},{3,2},{2,3},{5,4},{4,5},{7,6},{6,7},{9,8},{8,9},{11,10... | collective-permute-start | bytes 1966088 | tf_op jit(solution)/shard_map/ppermute | solution.py:21
  9.3 24.7 %collective-permute-start.4 = (bf16[336,1024]{1,0:T(8,128)(2,1)}, bf16[336,1024]{1,0:T(8,128)(2,1)S(1)}, u32[]{:S(2)}, u32[]{:S(2)}) collective-permute-start(bf16[336,1024]{1,0:T(8,128)(2,1)} %pad_maximum_fusion), channel_id=1, source_target_pairs={{0,4},{12,8},{1,5},{13,9},{2,6},{14,10},{3,7},{15,11},{16,20},{28,... | collective-permute-start | bytes 2064392 | tf_op jit(solution)/shard_map/ppermute | solution.py:570
  12.8 0.8 %copy-start.3 = (bf16[320,1024]{1,0:T(8,128)(2,1)}, bf16[320,1024]{1,0:T(8,128)(2,1)S(1)}, u32[]{:S(2)}) copy-start(bf16[320,1024]{1,0:T(8,128)(2,1)S(1)} %collective-permute-done.1.refs_3_.refs_4_.s_other) | copy-start | bytes 1966084
  18.0 19.1 %collective-permute-start.10 = (bf16[320,1024]{1,0:T(8,128)(2,1)}, bf16[320,1024]{1,0:T(8,128)(2,1)}, u32[]{:S(2)}, u32[]{:S(2)}) collective-permute-start(bf16[320,1024]{1,0:T(8,128)(2,1)} %collective-permute-done.3.refs_5_.across), channel_id=1, source_target_pairs={{4,0},{8,12},{5,1},{9,13},{6,2},{10,14},{7,3},{11,15},{20,16},{24,... | collective-permute-start | bytes 1966088 | tf_op jit(solution)/shard_map/ppermute | solution.py:570
  20.8 0.8 %copy-start = (bf16[320,1024]{1,0:T(8,128)(2,1)}, bf16[320,1024]{1,0:T(8,128)(2,1)S(1)}, u32[]{:S(2)}) copy-start(bf16[320,1024]{1,0:T(8,128)(2,1)S(1)} %collective-permute-done.2.refs_4_.whole.refs_5_.side) | copy-start | bytes 1966084
  20.8 6.4 %collective-permute-start.5 = (bf16[128,1024]{1,0:T(8,128)(2,1)S(1)}, bf16[128,1024]{1,0:T(8,128)(2,1)S(1)}, u32[]{:S(2)}, u32[]{:S(2)}) collective-permute-start(bf16[128,1024]{1,0:T(8,128)(2,1)S(1)} %get-tuple-element.45), channel_id=1, source_target_pairs={{4,8},{8,4},{0,1},{12,13},{5,9},{9,5},{1,0},{13,12},{6,10},{10,6},... | collective-permute-start | bytes 786440 | tf_op jit(solution)/shard_map/ppermute | solution.py:570
  20.9 16.2 %collective-permute-start.9 = (bf16[192,1024]{1,0:T(8,128)(2,1)S(1)}, bf16[192,1024]{1,0:T(8,128)(2,1)S(1)}, u32[]{:S(2)}, u32[]{:S(2)}) collective-permute-start(bf16[192,1024]{1,0:T(8,128)(2,1)S(1)} %get-tuple-element.51), channel_id=1, source_target_pairs={{4,8},{8,4},{0,1},{12,13},{5,9},{9,5},{1,0},{13,12},{6,10},{10,6},... | collective-permute-start | bytes 1179656 | tf_op jit(solution)/shard_map/ppermute | solution.py:570
  27.2 9.9 %copy-start.1 = (bf16[128,1024]{1,0:T(8,128)(2,1)}, bf16[128,1024]{1,0:T(8,128)(2,1)S(1)}, u32[]{:S(2)}) copy-start(bf16[128,1024]{1,0:T(8,128)(2,1)S(1)} %collective-permute-done.5.refs_5_.rest_1_) | copy-start | bytes 786436
  34.1 3.0 %collective-permute-start.6 = (bf16[176,1024]{1,0:T(8,128)(2,1)S(1)}, bf16[176,1024]{1,0:T(8,128)(2,1)S(1)}, u32[]{:S(2)}, u32[]{:S(2)}) collective-permute-start(bf16[176,1024]{1,0:T(8,128)(2,1)S(1)} %get-tuple-element.49), channel_id=1, source_target_pairs={{1,0},{0,1},{3,2},{2,3},{5,4},{4,5},{7,6},{6,7},{9,8},{8,9},{11,10... | collective-permute-start | bytes 1081352 | tf_op jit(solution)/shard_map/ppermute | solution.py:21
  34.2 2.9 %collective-permute-start.7 = (bf16[160,1024]{1,0:T(8,128)(2,1)S(1)}, bf16[160,1024]{1,0:T(8,128)(2,1)S(1)}, u32[]{:S(2)}, u32[]{:S(2)}) collective-permute-start(bf16[160,1024]{1,0:T(8,128)(2,1)S(1)} %get-tuple-element.50), channel_id=1, source_target_pairs={{1,0},{0,1},{3,2},{2,3},{5,4},{4,5},{7,6},{6,7},{9,8},{8,9},{11,10... | collective-permute-start | bytes 983048 | tf_op jit(solution)/shard_map/ppermute | solution.py:21
  34.7 10.8 %collective-permute-start.8 = (bf16[128,1024]{1,0:T(8,128)(2,1)S(1)}, bf16[128,1024]{1,0:T(8,128)(2,1)S(1)}, u32[]{:S(2)}, u32[]{:S(2)}) collective-permute-start(bf16[128,1024]{1,0:T(8,128)(2,1)S(1)} %collective-permute-done.5.refs_5_.rest_1_), channel_id=1, source_target_pairs={{0,4},{4,0},{8,12},{12,8},{1,5},{5,1},{9,13},{13,9},{2,6},{6,2},{1... | collective-permute-start | bytes 786440 | tf_op jit(solution)/shard_map/ppermute | solution.py:570
  37.1 0.9 %copy-start.2 = (bf16[192,1024]{1,0:T(8,128)(2,1)}, bf16[192,1024]{1,0:T(8,128)(2,1)S(1)}, u32[]{:S(2)}) copy-start(bf16[192,1024]{1,0:T(8,128)(2,1)S(1)} %collective-permute-done.9.refs_8_.rest_2_) | copy-start | bytes 1179652
  37.2 9.0 %collective-permute-start.13 = (bf16[128,1024]{1,0:T(8,128)(2,1)S(1)}, bf16[128,1024]{1,0:T(8,128)(2,1)S(1)}, u32[]{:S(2)}, u32[]{:S(2)}) collective-permute-start(bf16[128,1024]{1,0:T(8,128)(2,1)S(1)} %shard_map.73), channel_id=1, source_target_pairs={{4,8},{8,4},{0,1},{12,13},{5,9},{9,5},{1,0},{13,12},{6,10},{10,6},... | collective-permute-start | bytes 786440 | tf_op jit(solution)/shard_map/ppermute | solution.py:570
  37.4 17.1 %collective-permute-start.11 = (bf16[192,1024]{1,0:T(8,128)(2,1)S(1)}, bf16[192,1024]{1,0:T(8,128)(2,1)S(1)}, u32[]{:S(2)}, u32[]{:S(2)}) collective-permute-start(bf16[192,1024]{1,0:T(8,128)(2,1)S(1)} %shard_map.74), channel_id=1, source_target_pairs={{4,8},{8,4},{0,1},{12,13},{5,9},{9,5},{1,0},{13,12},{6,10},{10,6},... | collective-permute-start | bytes 1179656 | tf_op jit(solution)/shard_map/ppermute | solution.py:570
  37.9 16.5 %collective-permute-start.12 = (bf16[192,1024]{1,0:T(8,128)(2,1)S(1)}, bf16[192,1024]{1,0:T(8,128)(2,1)S(1)}, u32[]{:S(2)}, u32[]{:S(2)}) collective-permute-start(bf16[192,1024]{1,0:T(8,128)(2,1)S(1)} %collective-permute-done.9.refs_8_.rest_2_), channel_id=1, source_target_pairs={{0,4},{4,0},{8,12},{12,8},{1,5},{5,1},{9,13},{13,9},{2,6},{6,2},{1... | collective-permute-start | bytes 1179656 | tf_op jit(solution)/shard_map/ppermute | solution.py:570
  45.5 0.7 %copy-start.5 = (bf16[128,1024]{1,0:T(8,128)(2,1)}, bf16[128,1024]{1,0:T(8,128)(2,1)S(1)}, u32[]{:S(2)}) copy-start(bf16[128,1024]{1,0:T(8,128)(2,1)S(1)} %collective-permute-done.8.rest_3_) | copy-start | bytes 786436
  46.2 22.8 %collective-permute-start.18 = (bf16[320,1024]{1,0:T(8,128)(2,1)S(1)}, bf16[320,1024]{1,0:T(8,128)(2,1)S(1)}, u32[]{:S(2)}, u32[]{:S(2)}) collective-permute-start(bf16[320,1024]{1,0:T(8,128)(2,1)S(1)} %shard_map.75), channel_id=1, source_target_pairs={{4,8},{8,4},{0,1},{12,13},{5,9},{9,5},{1,0},{13,12},{6,10},{10,6},... | collective-permute-start | bytes 1966088 | tf_op jit(solution)/shard_map/ppermute | solution.py:570
  46.3 20.1 %collective-permute-start.14 = (bf16[128,1024]{1,0:T(8,128)(2,1)S(1)}, bf16[128,1024]{1,0:T(8,128)(2,1)S(1)}, u32[]{:S(2)}, u32[]{:S(2)}) collective-permute-start(bf16[128,1024]{1,0:T(8,128)(2,1)S(1)} %shard_map.77), channel_id=1, source_target_pairs={{0,4},{4,0},{8,12},{12,8},{1,5},{5,1},{9,13},{13,9},{2,6},{6,2},{1... | collective-permute-start | bytes 786440 | tf_op jit(solution)/shard_map/ppermute | solution.py:570
  54.5 1.4 %copy-start.4 = (bf16[192,1024]{1,0:T(8,128)(2,1)}, bf16[192,1024]{1,0:T(8,128)(2,1)S(1)}, u32[]{:S(2)}) copy-start(bf16[192,1024]{1,0:T(8,128)(2,1)S(1)} %collective-permute-done.12.rest_4_) | copy-start | bytes 1179652
  55.9 13.2 %collective-permute-start.19 = (bf16[192,1024]{1,0:T(8,128)(2,1)S(1)}, bf16[192,1024]{1,0:T(8,128)(2,1)S(1)}, u32[]{:S(2)}, u32[]{:S(2)}) collective-permute-start(bf16[192,1024]{1,0:T(8,128)(2,1)S(1)} %shard_map.79), channel_id=1, source_target_pairs={{0,4},{4,0},{8,12},{12,8},{1,5},{5,1},{9,13},{13,9},{2,6},{6,2},{1... | collective-permute-start | bytes 1179656 | tf_op jit(solution)/shard_map/ppermute | solution.py:570
  65.9 2.2 %collective-permute-start.15 = (bf16[112,1024]{1,0:T(8,128)(2,1)S(1)}, bf16[112,1024]{1,0:T(8,128)(2,1)S(1)}, u32[]{:S(2)}, u32[]{:S(2)}) collective-permute-start(bf16[112,1024]{1,0:T(8,128)(2,1)S(1)} %get-tuple-element.68), channel_id=1, source_target_pairs={{1,0},{0,1},{3,2},{2,3},{5,4},{4,5},{7,6},{6,7},{9,8},{8,9},{11,10... | collective-permute-start | bytes 688136 | tf_op jit(solution)/shard_map/ppermute | solution.py:21
  65.9 2.1 %collective-permute-start.16 = (bf16[112,1024]{1,0:T(8,128)(2,1)S(1)}, bf16[112,1024]{1,0:T(8,128)(2,1)S(1)}, u32[]{:S(2)}, u32[]{:S(2)}) collective-permute-start(bf16[112,1024]{1,0:T(8,128)(2,1)S(1)} %get-tuple-element.69), channel_id=1, source_target_pairs={{1,0},{0,1},{3,2},{2,3},{5,4},{4,5},{7,6},{6,7},{9,8},{8,9},{11,10... | collective-permute-start | bytes 688136 | tf_op jit(solution)/shard_map/ppermute | solution.py:21
  66.4 1.6 %collective-permute-start.17 = (bf16[96,1024]{1,0:T(8,128)(2,1)S(1)}, bf16[96,1024]{1,0:T(8,128)(2,1)S(1)}, u32[]{:S(2)}, u32[]{:S(2)}) collective-permute-start(bf16[96,1024]{1,0:T(8,128)(2,1)S(1)} %get-tuple-element.70), channel_id=1, source_target_pairs={{1,0},{0,1},{3,2},{2,3},{5,4},{4,5},{7,6},{6,7},{9,8},{8,9},{11,10... | collective-permute-start | bytes 589832 | tf_op jit(solution)/shard_map/ppermute | solution.py:21
